TPU v7x, 256 devices: a whole 4x4x8 slice. The times are simulated.
256 devices in a mesh: row: 16 (over y, x), col: 16 (over z, core).
Axes of the slice: x: 4, y: 4, z: 8, core: 2. Of those that a mesh axis runs over, the one named last changes fastest.
Arguments:
- tiles: float32 [16, 16, 64, 128, 128], P('row', 'col'), may hold values from -0.125 to 0.125
- tile_rows: int32 [16, 16, 64], P('row', 'col'), may hold values from 0 to 63
- tile_cols: int32 [16, 16, 64], P('row', 'col'), may hold values from 0 to 127
- tile_count: int32 [16, 16], P('row', 'col'), may hold values from 32 to 64, as said below
- row_types: int32 [16, 64, 128], P('row', 'col'), may hold values from 0 to 1
- var_types: int32 [16, 128, 128], P('col', 'row'), may hold values from 0 to 1
- rhs: float32 [16, 64, 128], P('row', 'col'), may hold values from -6 to 6
- cost: float32 [16, 128, 128], P('col', 'row'), may hold values from -6 to 6
- primal_start: float32 [16, 128, 128], P('col', 'row'), may hold values from 0 to 1
- dual_start: float32 [16, 64, 128], P('row', 'col'), may hold values from -3 to 3
Outputs:
- primal_out: float32 [16, 128, 128], P('col', 'row')
- dual_out: float32 [16, 64, 128], P('row', 'col')
- primal_residual: float32 [2], replicated
- dual_residual: float32 [2], replicated
- gap: float32 [2], replicated
Inputs may be any that keep to these rules, and one draw needn't show every extreme that they name: Slots from tile_count on hold entries that are not part of the matrix; in every draw some device uses all 64 slots.
All inputs are finite; a program needn't handle non-finite values.
Results may differ from a plain program's by a relative error of at most 0.0001.
Values sent between devices are 32-bit elements; how exact they have to be, the bound alone decides.
No kernel may reach another device: no remote copies, remote signals or barrier semaphores. Data moves between devices by JAX's collectives and lax.ppermute only.
A program may use at most 64 MiB of HBM per device.

v0:
```python
import jax
import jax.numpy as jnp
from jax import lax
from jax.sharding import PartitionSpec as P

ITERS = 2


def forward_tiles(blocks, row_index, col_index, filled, vectors, out_blocks):
    block_size = min(16, blocks.shape[0])
    turns = (filled + block_size - 1) // block_size

    def forward_add_block(turn, total):
        first_slot = turn * block_size
        picked_tiles = lax.dynamic_slice_in_dim(blocks, first_slot, block_size, 0)
        rows_here = lax.dynamic_slice_in_dim(row_index, first_slot, block_size, 0)
        cols_here = lax.dynamic_slice_in_dim(col_index, first_slot, block_size, 0)
        live_mask = (first_slot + jnp.arange(block_size) < filled).astype(jnp.float32)
        picked = vectors[:, cols_here, :]
        product = jnp.einsum("tij,vtj->vti", picked_tiles, picked, precision=lax.Precision.HIGHEST)
        return total.at[:, rows_here, :].add(product * live_mask[None, :, None])

    result = jnp.zeros((vectors.shape[0], out_blocks, vectors.shape[2]), jnp.float32)
    return lax.fori_loop(0, turns, forward_add_block, result)


def adjoint_tiles(blocks, row_index, col_index, filled, vectors, out_blocks):
    block_size = min(16, blocks.shape[0])
    turns = (filled + block_size - 1) // block_size

    def adjoint_add_block(turn, total):
        first_slot = turn * block_size
        picked_tiles = lax.dynamic_slice_in_dim(blocks, first_slot, block_size, 0)
        rows_here = lax.dynamic_slice_in_dim(row_index, first_slot, block_size, 0)
        cols_here = lax.dynamic_slice_in_dim(col_index, first_slot, block_size, 0)
        live_mask = (first_slot + jnp.arange(block_size) < filled).astype(jnp.float32)
        picked = vectors[:, rows_here, :]
        product = jnp.einsum("tij,vti->vtj", picked_tiles, picked, precision=lax.Precision.HIGHEST)
        return total.at[:, cols_here, :].add(product * live_mask[None, :, None])

    result = jnp.zeros((vectors.shape[0], out_blocks, vectors.shape[2]), jnp.float32)
    return lax.fori_loop(0, turns, adjoint_add_block, result)


def clamp_primal(values, var_free):
    return jnp.where(var_free > 0.5, jnp.maximum(values, 0.0), jnp.clip(values, 0.0, 1.0))


def clamp_dual(values, row_ineq):
    return jnp.where(row_ineq > 0.5, jnp.maximum(values, 0.0), values)


def shards(
    tiles,
    tile_rows,
    tile_cols,
    tile_count,
    row_types,
    var_types,
    rhs,
    cost,
    primal_start,
    dual_start,
):
    blocks = tiles.reshape(tiles.shape[2:])
    row_index = tile_rows.reshape(-1)
    col_index = tile_cols.reshape(-1)
    filled = tile_count.reshape(())
    rows_share = rhs.shape[1]
    cols_share = cost.shape[1]
    row_blocks = rows_share * lax.axis_size("col")
    col_blocks = cols_share * lax.axis_size("row")
    rows_total = float(rhs.shape[0] * row_blocks * rhs.shape[2] * lax.axis_size("row"))
    cols_total = float(cost.shape[0] * col_blocks * cost.shape[2] * lax.axis_size("col"))
    var_free = var_types.astype(jnp.float32)
    row_ineq = row_types.astype(jnp.float32)
    cost_used, free_used, primal = (cost, var_free, primal_start)
    rhs_used, ineq_used, dual = (rhs, row_ineq, dual_start)

    def primal_full(vectors):
        return lax.all_gather(vectors, "row", axis=1, tiled=True)

    def dual_full(vectors):
        return lax.all_gather(vectors, "col", axis=1, tiled=True)

    def adjoint_reduce(partial_terms):
        return lax.psum_scatter(partial_terms, "row", scatter_dimension=1, tiled=True)

    def forward_reduce(partial_terms):
        return lax.psum_scatter(partial_terms, "col", scatter_dimension=1, tiled=True)

    history = []
    for turn in range(ITERS):
        gradient = adjoint_reduce(
            adjoint_tiles(blocks, row_index, col_index, filled, dual_full(dual), col_blocks)
        )
        primal_next = clamp_primal(primal - 0.4 * (cost_used - gradient), free_used)
        extended = primal_full(2.0 * primal_next - primal)
        image = forward_reduce(
            forward_tiles(blocks, row_index, col_index, filled, extended, row_blocks)
        )
        dual_next = clamp_dual(dual + 0.4 * (rhs_used - image), ineq_used)
        primal, dual = (primal_next, dual_next)
        history.append((primal, dual))
    pair_primal = jnp.concatenate([primal, 0.5 * (history[0][0] + history[1][0])], 0)
    pair_dual = jnp.concatenate([dual, 0.5 * (history[0][1] + history[1][1])], 0)
    forward_pair = forward_reduce(
        forward_tiles(blocks, row_index, col_index, filled, primal_full(pair_primal), row_blocks)
    )
    residual = rhs - forward_pair
    residual = jnp.where(row_ineq > 0.5, jnp.maximum(residual, 0.0), residual)
    primal_square = jnp.sum(residual * residual, axis=(1, 2))
    rhs_dot = jnp.sum(rhs * pair_dual, axis=(1, 2))
    primal_square, rhs_dot = lax.psum((primal_square, rhs_dot), ("row", "col"))
    adjoint_pair = adjoint_reduce(
        adjoint_tiles(blocks, row_index, col_index, filled, dual_full(pair_dual), col_blocks)
    )
    reduced = cost - adjoint_pair
    violation = jnp.where(var_free > 0.5, jnp.minimum(reduced, 0.0), 0.0)
    dual_square = jnp.sum(violation * violation, axis=(1, 2))
    cost_dot = jnp.sum(cost * pair_primal, axis=(1, 2))
    box_term = jnp.sum(jnp.where(var_free < 0.5, jnp.minimum(reduced, 0.0), 0.0), axis=(1, 2))
    dual_square, cost_dot, box_term = lax.psum((dual_square, cost_dot, box_term), ("row", "col"))
    primal_residual = primal_square / rows_total
    dual_residual = dual_square / cols_total
    gap = (cost_dot - rhs_dot - box_term) / cols_total
    return (primal, dual, primal_residual, dual_residual, gap)


def solution(mesh):
    in_specs = (
        P("row", "col", None, None, None),
        P("row", "col", None),
        P("row", "col", None),
        P("row", "col"),
        P("row", "col", None),
        P("col", "row", None),
        P("row", "col", None),
        P("col", "row", None),
        P("col", "row", None),
        P("row", "col", None),
    )
    out_specs = (P("col", "row", None), P("row", "col", None), P(), P(), P())
    return jax.shard_map(shards, mesh=mesh, in_specs=in_specs, out_specs=out_specs, check_vma=False)
```

profile of v0, /device:TPU:1, one launch (start us, length us, event | category | flops | bytes accessed | tf_op | source)
XLA Modules:
  0.0 791.8 jit_solution(3903101194418176924)
XLA Ops:
  7.9 21.6 %all_gather.18 = f32[1,64,128]{2,0,1:T(1,128)S(1)} all-gather(f32[1,4,128]{2,0,1:T(1,128)} %bitcast.150), channel_id=1, replica_groups=mesh['row'=16,'col'=16] {'col'}, dimensions={1}, use_global_device_ids=true | all-gather | bytes 34816 | tf_op jit(solution)/shard_map/all_gather | solution.py:84
  29.6 14.9 %while.60 = (s32[]{:T(128)}, f32[1,128,128]{2,1,0:T(8,128)S(1)}, s32[]{:T(128)}, s32[64]{0:T(128)}, s32[64]{0:T(128)}, /*index=5*/f32[1,64,128]{2,1,0:T(8,128)S(...) while((s32[]{:T(128)}, f32[1,128,128]{2,1,0:T(8,128)S(1)}, ...), condition=%wide.region_2.3_spmd, body=%wide.region_0.2_spmd.sunk | while | flops 3150998 | bytes 1160307 | solution.py:42
  47.7 89.6 %all-reduce.10.cloned.1.call-done = f32[1,128,128]{2,1,0:T(8,128)} async-done(((f32[1,128,128]{2,1,0:T(8,128)}), f32[1,128,128]{2,1,0:T(8,128)}) %all-reduce.10.cloned.1.call-update) | async-done | bytes 65552
  137.9 17.5 %all_gather.19 = f32[1,128,128]{2,1,0:T(8,128)S(1)} all-gather(f32[1,8,128]{2,1,0:T(8,128)S(1)} %get-tuple-element.421), channel_id=1, replica_groups=mesh['row'=16,'col'=16] {'row'}, dimensions={1}, use_global_device_ids=true | all-gather | bytes 69632 | tf_op jit(solution)/shard_map/all_gather | solution.py:81
  155.4 17.3 %while.61 = (s32[]{:T(128)}, f32[1,64,128]{2,1,0:T(8,128)S(1)}, s32[]{:T(128)}, s32[64]{0:T(128)}, s32[64]{0:T(128)}, /*index=5*/f32[1,128,128]{2,1,0:T(8,128)S(...) while((s32[]{:T(128)}, f32[1,64,128]{2,1,0:T(8,128)S(1)}, ...), condition=%wide.region_6.7_spmd, body=%wide.region_4.6_spmd.sunk | while | flops 3150998 | bytes 1127539 | solution.py:24
  156.7 3.0 fusion.72
  162.5 3.0 fusion.72
  168.2 3.0 fusion.72
  172.7 56.0 %all-reduce.1 = f32[1,64,128]{2,1,0:T(8,128)S(1)} all-reduce(f32[1,64,128]{2,1,0:T(8,128)S(1)} %get-tuple-element.264), channel_id=3, replica_groups=mesh['row'=16,'col'=16] {'col'}, use_global_device_ids=true, to_apply=%region_7.8.clone | all-reduce | flops 8192 | bytes 65536
  228.7 18.2 %all_gather.20 = f32[1,64,128]{2,0,1:T(1,128)S(1)} all-gather(f32[1,4,128]{2,0,1:T(1,128)S(1)} %bitcast.147), channel_id=1, replica_groups=mesh['row'=16,'col'=16] {'col'}, dimensions={1}, use_global_device_ids=true | all-gather | bytes 34816 | tf_op jit(solution)/shard_map/all_gather | solution.py:84
  246.9 14.9 %while.62 = (s32[]{:T(128)}, f32[1,128,128]{2,1,0:T(8,128)S(1)}, s32[]{:T(128)}, s32[64]{0:T(128)}, s32[64]{0:T(128)}, /*index=5*/f32[1,64,128]{2,1,0:T(8,128)S(...) while((s32[]{:T(128)}, f32[1,128,128]{2,1,0:T(8,128)S(1)}, ...), condition=%wide.region_10.11_spmd, body=%wide.region_8.10_spmd.sunk | while | flops 3150998 | bytes 1160307 | solution.py:42
  262.5 92.2 %all-reduce.12.cloned.1.call-done = f32[1,128,128]{2,1,0:T(8,128)} async-done(((f32[1,128,128]{2,1,0:T(8,128)}), f32[1,128,128]{2,1,0:T(8,128)}) %all-reduce.12.cloned.1.call-update) | async-done | bytes 65552
  355.4 17.5 %all_gather.21 = f32[1,128,128]{2,1,0:T(8,128)S(1)} all-gather(f32[1,8,128]{2,1,0:T(8,128)S(1)} %multiply_subtract_fusion), channel_id=1, replica_groups=mesh['row'=16,'col'=16] {'row'}, dimensions={1}, use_global_device_ids=true | all-gather | bytes 69632 | tf_op jit(solution)/shard_map/all_gather | solution.py:81
  372.9 17.2 %while.63 = (s32[]{:T(128)}, f32[1,64,128]{2,1,0:T(8,128)S(1)}, s32[]{:T(128)}, s32[64]{0:T(128)}, s32[64]{0:T(128)}, /*index=5*/f32[1,128,128]{2,1,0:T(8,128)S(...) while((s32[]{:T(128)}, f32[1,64,128]{2,1,0:T(8,128)S(1)}, ...), condition=%wide.region_14.15_spmd, body=%wide.region_12.14_spmd.sunk | while | flops 3150998 | bytes 1127539 | solution.py:24
  374.2 3.0 fusion.80
  380.0 3.0 fusion.80
  390.1 56.0 %all-reduce.3 = f32[1,64,128]{2,1,0:T(8,128)S(1)} all-reduce(f32[1,64,128]{2,1,0:T(8,128)S(1)} %get-tuple-element.266), channel_id=5, replica_groups=mesh['row'=16,'col'=16] {'col'}, use_global_device_ids=true, to_apply=%region_15.16.clone | all-reduce | flops 8192 | bytes 65536
  446.2 18.3 %all_gather.23 = f32[2,64,128]{2,0,1:T(2,128)S(1)} all-gather(f32[2,4,128]{2,0,1:T(2,128)S(1)} %copy.29), channel_id=1, replica_groups=mesh['row'=16,'col'=16] {'col'}, dimensions={1}, use_global_device_ids=true | all-gather | bytes 69632 | tf_op jit(solution)/shard_map/all_gather | solution.py:84
  464.5 16.0 %while.65 = (s32[]{:T(128)}, f32[2,128,128]{2,0,1:T(2,128)S(1)}, s32[]{:T(128)}, s32[64]{0:T(128)}, s32[64]{0:T(128)}, /*index=5*/f32[2,64,128]{2,0,1:T(2,128)S(...) while((s32[]{:T(128)}, f32[2,128,128]{2,0,1:T(2,128)S(1)}, ...), condition=%wide.region_24.25_spmd, body=%wide.region_22.24_spmd.sunk | while | flops 6300822 | bytes 1168115 | solution.py:42
  481.3 76.6 %reduce-scatter.7.cloned.1.call-done = f32[2,8,128]{2,1,0:T(8,128)} async-done(((f32[2,128,128]{2,1,0:T(8,128)}), f32[2,8,128]{2,1,0:T(8,128)}) %reduce-scatter.7.cloned.1.call-update) | async-done | bytes 8208 | tf_op jit(solution)/shard_map/reduce_scatter | solution.py:87
  558.7 17.3 %all_gather.22 = f32[2,128,128]{2,1,0:T(8,128)S(1)} all-gather(f32[2,8,128]{2,1,0:T(8,128)S(1)} %get-tuple-element.436), channel_id=1, replica_groups=mesh['row'=16,'col'=16] {'row'}, dimensions={1}, use_global_device_ids=true | all-gather | bytes 139264 | tf_op jit(solution)/shard_map/all_gather | solution.py:81
  576.1 18.3 %while.64 = (s32[]{:T(128)}, f32[2,64,128]{2,0,1:T(2,128)S(1)}, s32[]{:T(128)}, s32[64]{0:T(128)}, s32[64]{0:T(128)}, /*index=5*/f32[2,128,128]{2,0,1:T(2,128)S(...) while((s32[]{:T(128)}, f32[2,64,128]{2,0,1:T(2,128)S(1)}, ...), condition=%wide.region_18.19_spmd, body=%wide.region_16.18_spmd.sunk | while | flops 6300822 | bytes 1168115 | solution.py:24
  595.0 111.8 %all-reduce.14.cloned.1.call-done = f32[2,64,128]{2,1,0:T(8,128)} async-done(((f32[2,64,128]{2,1,0:T(8,128)}), f32[2,64,128]{2,1,0:T(8,128)}) %all-reduce.14.cloned.1.call-update) | async-done | bytes 65552
  707.6 76.6 %all-reduce.5 = (f32[2]{0:T(128)S(1)}, f32[2]{0:T(128)S(1)}, f32[2]{0:T(128)S(1)}, f32[2]{0:T(128)S(1)}, f32[2]{0:T(128)S(1)}) all-reduce(f32[2]{0:T(128)S(1)} %get-tuple-element.313, f32[2]{0:T(128)S(1)} %get-tuple-element.310, f32[2]{0:T(128)S(1)} %get-tuple-element.309, ...), channel_id=1, replica_groups=mesh['row'=16,'col'=16] {'row','col'}, use_global_device_ids=true, to_apply=%region_21.22 | all-reduce | flops 10 | bytes 80 | tf_op jit(solution)/shard_map/psum | solution.py:114
  (158 shorter events, 91.2 us)
Async XLA Ops:
  7.2 38.0 %copy-start.11 = (u32[256]{0:T(256)S(1)}, u32[256]{0:T(256)}, u32[]{:S(2)}) copy-start(u32[256]{0:T(256)} %constant.141) | copy-start | bytes 3076
  7.2 38.6 %copy-start.10 = (u32[256]{0:T(256)S(1)}, u32[256]{0:T(256)}, u32[]{:S(2)}) copy-start(u32[256]{0:T(256)} %constant.145) | copy-start | bytes 3076
  7.2 130.0 %copy-start.6 = (s32[1,8,128]{2,1,0:T(8,128)S(1)}, s32[1,8,128]{2,1,0:T(8,128)}, u32[]{:S(2)}) copy-start(s32[1,8,128]{2,1,0:T(8,128)} %param.27) | copy-start | bytes 12292
  7.2 130.0 %copy-start.2 = (f32[1,8,128]{2,1,0:T(8,128)S(1)}, f32[1,8,128]{2,1,0:T(8,128)}, u32[]{:S(2)}) copy-start(f32[1,8,128]{2,1,0:T(8,128)} %param.29) | copy-start | bytes 12292
  7.2 130.0 %copy-start.8 = (f32[1,8,128]{2,1,0:T(8,128)S(1)}, f32[1,8,128]{2,1,0:T(8,128)}, u32[]{:S(2)}) copy-start(f32[1,8,128]{2,1,0:T(8,128)} %param.30) | copy-start | bytes 12292
  7.2 130.0 %all-reduce.10.cloned.1.call-start = ((), (), s32[]{:S(2)}) async-start(), calls=%async_computation.2 | async-start | bytes 131072
  44.5 0.6 copy-start
  44.5 184.2 %copy-start.4 = (f32[1,4,128]{2,1,0:T(4,128)S(1)}, f32[1,4,128]{2,1,0:T(4,128)}, u32[]{:S(2)}) copy-start(f32[1,4,128]{2,1,0:T(4,128)} %param.28) | copy-start | bytes 6148
  44.5 184.1 %copy-start.7 = (f32[1,4,128]{2,1,0:T(4,128)S(1)}, f32[1,4,128]{2,1,0:T(4,128)}, u32[]{:S(2)}) copy-start(f32[1,4,128]{2,1,0:T(4,128)} %param.31) | copy-start | bytes 6148
  44.5 184.1 %copy-start.9 = (s32[1,4,128]{2,1,0:T(4,128)S(1)}, s32[1,4,128]{2,1,0:T(4,128)}, u32[]{:S(2)}) copy-start(s32[1,4,128]{2,1,0:T(4,128)} %param.26) | copy-start | bytes 6148
  45.1 309.6 %all-reduce.12.cloned.1.call-start = ((), (), s32[]{:S(2)}) async-start(), calls=%async_computation.3 | async-start | bytes 131072
  261.8 0.6 copy-start.1
  262.5 295.4 %reduce-scatter.7.cloned.1.call-start = ((), (), s32[]{:S(2)}) async-start(), calls=%async_computation.1 | async-start | bytes 139264 | tf_op jit(solution)/shard_map/reduce_scatter | solution.py:87
  355.4 202.5 %copy-start.3 = (f32[1,8,128]{2,1,0:T(8,128)}, f32[1,8,128]{2,1,0:T(8,128)S(1)}, u32[]{:S(2)}) copy-start(f32[1,8,128]{2,1,0:T(8,128)S(1)} %get-tuple-element.416) | copy-start | bytes 12292
  446.2 260.7 %copy-start.5 = (f32[1,4,128]{2,1,0:T(4,128)}, f32[1,4,128]{2,1,0:T(4,128)S(1)}, u32[]{:S(2)}) copy-start(f32[1,4,128]{2,1,0:T(4,128)S(1)} %get-tuple-element.418) | copy-start | bytes 6148
  481.2 225.6 %all-reduce.14.cloned.1.call-start = ((), (), s32[]{:S(2)}) async-start(), calls=%async_computation.4 | async-start | bytes 131072
Sparse Core Ops, SparseCore 0:
  45.3 91.9 all-reduce.9
  262.6 92.0 all-reduce.11
  481.3 76.4 reduce-scatter.6
  595.2 111.6 all-reduce.13
where the time goes:
time: 794 us; the launch traced here: 792 us
  waiting for transfers between devices  370 us (47%)
  blocking collectives  299 us (38%)
  matrix products  46.3 us (6%)
  other arithmetic  45.4 us (6%)
  between operations  15.9 us (2%)
  local copies, waits for them, and re-layouts  14.1 us (2%)
    unnamed x7, waiting for transfers between devices  294 us
    unnamed x2, blocking collectives  112 us
    reduce_scatter x1, waiting for transfers between devices, adjoint_reduce(): lax.psum_scatter(partial_terms, 'row', scatter_dimension=1, tiled=True)  76.6 us
    psum x1, blocking collectives, shards(): primal_square, rhs_dot = lax.psum((primal_square, rhs_dot), ('row', 'col'))  76.6 us
    all_gather x3, blocking collectives, dual_full(): return lax.all_gather(vectors, 'col', axis=1, tiled=True)  58.2 us
    all_gather x3, blocking collectives, primal_full(): return lax.all_gather(vectors, 'row', axis=1, tiled=True)  52.2 us
    dot_general x9, matrix products, forward_add_block(): jnp.einsum('tij,vtj->vti', picked_tiles, picked, precision=lax.Precision....  26.6 us
    dot_general x9, matrix products, adjoint_add_block(): jnp.einsum('tij,vti->vtj', picked_tiles, picked, precision=lax.Precision....  19.7 us
  transfers between devices with their start and end apart: 4, of which 4 were waited for; matrix products, arithmetic and copies ran while one was open for 0% of the time, Pallas kernels for 0%

commit v1 on v0

v1 whole, which is shorter than its diff:
```python
import jax
import jax.numpy as jnp
from jax import lax
from jax.experimental import pallas as pl
from jax.experimental.pallas import tpu as pltpu
from jax.sharding import PartitionSpec as P

N = 16
TILE = 128
ROW_BLOCKS = 64
COL_BLOCKS = 128
SLOTS = 64
ROWS_SHARE = ROW_BLOCKS // N
COLS_SHARE = COL_BLOCKS // N
NROWS = float(N * ROW_BLOCKS * TILE)
NCOLS = float(N * COL_BLOCKS * TILE)
UNROLL = 8
F32, BF16 = jnp.float32, jnp.bfloat16

ROW_MASKS = (1, 3, 4, 12)

VMEM = pl.BlockSpec(memory_space=pltpu.VMEM)
SMEM = pl.BlockSpec(memory_space=pltpu.SMEM)


def call(kernel, name, out_shapes, args, smem=0, smem_out=False, scratch=()):
    shapes = tuple(jax.ShapeDtypeStruct(s, d) for s, d in out_shapes)
    return pl.pallas_call(
        kernel,
        name=name,
        out_shape=shapes,
        in_specs=[SMEM] * smem + [VMEM] * (len(args) - smem),
        out_specs=tuple([SMEM if smem_out else VMEM] * len(shapes)),
        scratch_shapes=list(scratch),
        compiler_params=pltpu.CompilerParams(vmem_limit_bytes=32 * 2**20),
    )(*args)


def split(vector, copies):
    wide = jnp.broadcast_to(vector, (copies, TILE))
    lead = wide.astype(BF16).astype(F32)
    return [lead, wide - lead]


def adjoint_product(rows, cols, tile_pair, dual_ref, total):
    total[...] = jnp.zeros_like(total)

    def body(slot, carry):
        lhs = jnp.concatenate(split(dual_ref[pl.ds(rows[slot], 1), :], 8), 0).astype(BF16)
        lhs = jnp.concatenate([lhs, lhs], 1)
        product = jnp.dot(lhs, tile_pair(slot), preferred_element_type=F32)
        total[cols[slot]] += product[0:8] + product[8:16]
        return carry

    lax.fori_loop(0, SLOTS, body, 0, unroll=UNROLL)


def forward_product(rows, cols, tile_pair, primal_refs, total):
    total[...] = jnp.zeros_like(total)
    copies = 8 // len(primal_refs)

    def body(slot, carry):
        parts = [split(ref[pl.ds(cols[slot], 1), :], copies) for ref in primal_refs]
        lhs = jnp.concatenate([p[0] for p in parts] + [p[1] for p in parts], 0).astype(BF16)
        product = lax.dot_general(
            lhs, tile_pair(slot), (((1,), (1,)), ((), ())), preferred_element_type=F32
        )
        product = product[:, :TILE] + product[:, TILE:]
        total[rows[slot]] += product[0:8] + product[8:16]
        return carry

    lax.fori_loop(0, SLOTS, body, 0, unroll=UNROLL)


def clamp_primal(values, free):
    floor = jnp.maximum(values, 0.0)
    return jnp.where(free > 0.5, floor, jnp.minimum(floor, 1.0))


def clamp_dual(values, ineq):
    return jnp.where(ineq > 0.5, jnp.maximum(values, 0.0), values)


def first_adjoint(count, rows, cols, dual, tiles, gradient, pairs, total):
    def tile_pair(slot):
        tile = jnp.where(slot < count[0], tiles[slot], 0.0)
        lead = tile.astype(BF16)
        pair = jnp.concatenate([lead, (tile - lead.astype(F32)).astype(BF16)], 0)
        pairs[slot] = pair
        return pair

    adjoint_product(rows, cols, tile_pair, dual, total)
    gradient[...] = total[:, 0, :]


def first_forward(
    where, rows, cols, own, other, gathered, pairs, image, primal, start, cost, free, extended, total
):
    for place in range(N):
        device = where[0]
        for step, mask in enumerate(ROW_MASKS):
            if place >> step & 1:
                device = device ^ mask
        block = pl.ds(pl.multiple_of(device * COLS_SHARE, COLS_SHARE), COLS_SHARE)
        for k, ref in enumerate((start, cost, free)):
            ref[block, :] = gathered[place, k]
    gradient = own[...] + other[...]
    primal[...] = clamp_primal(start[...] - 0.4 * (cost[...] - gradient), free[...])
    extended[...] = 2.0 * primal[...] - start[...]
    forward_product(rows, cols, lambda slot: pairs[slot], [extended], total)
    image[...] = total[:, 0, :]


def second_adjoint(rows, cols, images, start, rhs, ineq, pairs, gradient, dual, total):
    image = jnp.sum(images[...], 0)
    dual[...] = clamp_dual(start[...] + 0.4 * (rhs[...] - image), ineq[...])
    adjoint_product(rows, cols, lambda slot: pairs[slot], dual, total)
    gradient[...] = total[:, 0, :]


def second_forward(
    where, rows, cols, own, other, before, cost, free, pairs, image, plain, primal, gradient, mine, extended, total
):
    gradient[...] = own[...] + other[...]
    primal[...] = clamp_primal(before[...] - 0.4 * (cost[...] - gradient[...]), free[...])
    extended[...] = 2.0 * primal[...] - before[...]
    mine[...] = primal[pl.ds(pl.multiple_of(where[0] * COLS_SHARE, COLS_SHARE), COLS_SHARE), :]
    forward_product(rows, cols, lambda slot: pairs[slot], [extended, primal], total)
    image[...] = total[:, 0, :]
    plain[...] = total[:, 4, :]


def third_adjoint(where, rows, cols, images, before, rhs, ineq, pairs, payload, mine, dual, total):
    image = images[0]
    plain = images[1]
    for k in range(1, N // 2):
        image = image + images[2 * k]
        plain = plain + images[2 * k + 1]
    earlier, bound, kind = before[...], rhs[...], ineq[...]
    dual[...] = clamp_dual(earlier + 0.4 * (bound - image), kind)
    mine[...] = dual[pl.ds(where[1] * ROWS_SHARE, ROWS_SHARE), :]
    adjoint_product(rows, cols, lambda slot: pairs[slot], dual, total)
    payload[0:COL_BLOCKS, :] = total[:, 0, :]
    terms = []
    for product in (plain, 0.5 * (3.0 * plain - image)):
        residual = bound - product
        residual = jnp.where(kind > 0.5, jnp.maximum(residual, 0.0), residual)
        terms.append(jnp.sum(residual * residual, 0, keepdims=True))
    for value in (dual[...], 0.5 * (earlier + dual[...])):
        terms.append(jnp.sum(bound * value, 0, keepdims=True))
    payload[COL_BLOCKS : COL_BLOCKS + 8, :] = jnp.concatenate(terms + terms, 0)


def column_terms(own, other, earlier, before, primal, cost, free, terms, row_terms):
    adjoint = own[0:COL_BLOCKS, :] + other[0:COL_BLOCKS, :]
    row_terms[...] = own[COL_BLOCKS:, :] + other[COL_BLOCKS:, :]
    price, kind = cost[...], free[...]
    rows = []
    for gradient, value in (
        (adjoint, primal[...]),
        (0.5 * (earlier[...] + adjoint), 0.5 * (before[...] + primal[...])),
    ):
        low = jnp.minimum(price - gradient, 0.0)
        violation = jnp.where(kind > 0.5, low, 0.0)
        box = jnp.where(kind > 0.5, 0.0, low)
        rows.append(jnp.sum(violation * violation, 0, keepdims=True))
        rows.append(jnp.sum(price * value, 0, keepdims=True))
        rows.append(jnp.sum(box, 0, keepdims=True))
    terms[...] = jnp.concatenate(rows + rows[:2], 0)


def measures(gathered, row_terms, primal_residual, dual_residual, gap):
    columns = jnp.sum(gathered[...], 0)
    rows = row_terms[...]
    for k in range(2):
        primal_residual[k] = jnp.sum(rows[k : k + 1]) * (1.0 / NROWS)
        dual_residual[k] = jnp.sum(columns[3 * k : 3 * k + 1]) * (1.0 / NCOLS)
        total = columns[3 * k + 1 : 3 * k + 2] - columns[3 * k + 2 : 3 * k + 3] - rows[2 + k : 3 + k]
        gap[k] = jnp.sum(total) * (1.0 / NCOLS)


def swap(values, axis, mask):
    return lax.ppermute(values, axis, [(i, i ^ mask) for i in range(N)])


def sum_over_row(values):
    for mask in ROW_MASKS[:-1]:
        values = values + swap(values, "row", mask)
    return values, swap(values, "row", ROW_MASKS[-1])


def shards(
    tiles, tile_rows, tile_cols, tile_count, row_types, var_types, rhs, cost, primal_start, dual_start
):
    tiles = tiles.reshape(SLOTS, TILE, TILE)
    rows, cols = tile_rows.reshape(-1), tile_cols.reshape(-1)
    count = tile_count.reshape(1)
    where = jnp.stack([lax.axis_index("row"), lax.axis_index("col")]).astype(jnp.int32)
    blocks = (ROW_BLOCKS, TILE)
    columns = (COL_BLOCKS, TILE)
    row_total = [pltpu.VMEM((ROW_BLOCKS, 8, TILE), F32)]
    col_total = [pltpu.VMEM((COL_BLOCKS, 8, TILE), F32)]

    row_side = jnp.concatenate([dual_start, rhs, row_types.astype(F32)], 0)
    row_side = lax.all_gather(row_side, "col", axis=1, tiled=True)
    dual0, rhs_full, ineq = row_side[0], row_side[1], row_side[2]

    gradient, pairs = call(
        first_adjoint,
        "first_adjoint",
        [(columns, F32), ((SLOTS, 2 * TILE, TILE), BF16)],
        (count, rows, cols, dual0, tiles),
        smem=3,
        scratch=col_total,
    )

    gathered = jnp.concatenate([primal_start, cost, var_types.astype(F32)], 0)
    gathered = gathered.reshape(3 * COLS_SHARE, TILE)
    for step, mask in enumerate(ROW_MASKS):
        other = swap(jnp.concatenate([gradient, gathered], 0), "row", mask)
        gathered = jnp.concatenate([gathered, other[COL_BLOCKS:]], 0)
        other = other[:COL_BLOCKS]
        if step < len(ROW_MASKS) - 1:
            gradient = gradient + other
    gathered = gathered.reshape(N, 3, COLS_SHARE, TILE)

    image, primal1, start_full, cost_full, free = call(
        first_forward,
        "first_forward",
        [(blocks, F32)] + [(columns, F32)] * 4,
        (where, rows, cols, gradient, other, gathered, pairs),
        smem=3,
        scratch=[pltpu.VMEM(columns, F32)] + row_total,
    )

    images = lax.all_gather(image, "col", axis=0, tiled=False)
    gradient, dual1 = call(
        second_adjoint,
        "second_adjoint",
        [(columns, F32), (blocks, F32)],
        (rows, cols, images, dual0, rhs_full, ineq, pairs),
        smem=2,
        scratch=col_total,
    )
    gradient, other = sum_over_row(gradient)

    image, plain, primal2, gradient2, primal_mine = call(
        second_forward,
        "second_forward",
        [(blocks, F32)] * 2 + [(columns, F32)] * 2 + [((COLS_SHARE, TILE), F32)],
        (where, rows, cols, gradient, other, primal1, cost_full, free, pairs),
        smem=3,
        scratch=[pltpu.VMEM(columns, F32)] + row_total,
    )

    second = where[1] % 2 == 1
    kept = jnp.where(second, plain, image)
    given = jnp.where(second, image, plain)
    images = lax.all_gather(kept + swap(given, "col", 1), "col", axis=0, tiled=False)

    payload, dual_mine, dual2 = call(
        third_adjoint,
        "third_adjoint",
        [((COL_BLOCKS + 8, TILE), F32), ((ROWS_SHARE, TILE), F32), (blocks, F32)],
        (where, rows, cols, images, dual1, rhs_full, ineq, pairs),
        smem=3,
        scratch=col_total,
    )
    payload, other = sum_over_row(payload)
    terms, row_terms = call(
        column_terms,
        "column_terms",
        [((8, TILE), F32)] * 2,
        (payload, other, gradient2, primal1, primal2, cost_full, free),
    )
    terms = lax.all_gather(terms, "col", axis=0, tiled=False)
    primal_residual, dual_residual, gap = call(
        measures, "measures", [((2,), F32)] * 3, (terms, row_terms), smem_out=True
    )
    return primal_mine[None], dual_mine[None], primal_residual, dual_residual, gap


def solution(mesh):
    in_specs = (
        P("row", "col", None, None, None),
        P("row", "col", None),
        P("row", "col", None),
        P("row", "col"),
        P("row", "col", None),
        P("col", "row", None),
        P("row", "col", None),
        P("col", "row", None),
        P("col", "row", None),
        P("row", "col", None),
    )
    out_specs = (P("col", "row", None), P("row", "col", None), P(), P(), P())
    return jax.shard_map(shards, mesh=mesh, in_specs=in_specs, out_specs=out_specs, check_vma=False)
```

time: 794 us -> 161 us (0.20)
  waiting for transfers between devices: 370 us -> 31 us
  blocking collectives: 299 us -> 77.8 us
  matrix products: 46.3 us -> 0 us
  other arithmetic: 45.4 us -> 3.01 us
  starting transfers between devices: 0.16 us -> 23.5 us
  between operations: 15.9 us -> 1.52 us
  Pallas kernels: 0 us -> 14.2 us
    unnamed x7 -> x0, waiting for transfers between devices: 294 us -> none
    unnamed x2 -> x0, blocking collectives: 112 us -> none
    reduce_scatter x1 -> x0, waiting for transfers between devices: 76.6 us -> none  [adjoint_reduce(): lax.psum_scatter(partial_terms, 'row', scatter_dimension=1, tiled=True)]
    psum x1 -> x0, blocking collectives: 76.6 us -> none  [shards(): primal_square, rhs_dot = lax.psum((primal_square, rhs_dot), ('row', 'col'))]
    dot_general x18 -> x0, matrix products: 46.3 us -> none  [the longest x9 26.6 us: forward_add_block(): jnp.einsum('tij,vtj->vti', picked_tiles, picked, precision=lax.Precision....]
    all_gather x6 -> x4, blocking collectives: 110 us -> 77.8 us  [the longest x1 21.7 us: shards(): row_side = lax.all_gather(row_side, 'col', axis=1, tiled=True)]
    ppermute x0 -> x13, waiting for transfers between devices: none -> 31 us  [swap(): return lax.ppermute(values, axis, [(i, i ^ mask) for i in range(N)])]
    ppermute x0 -> x13, starting transfers between devices: none -> 23.5 us  [swap(): return lax.ppermute(values, axis, [(i, i ^ mask) for i in range(N)])]
  transfers between devices with their start and end apart: 4 -> 13, of which waited for: 4 -> 13; matrix products, arithmetic and copies ran while one was open for 0% -> 0% of each run, Pallas kernels for 0% -> 0%
where the time goes in v1:
time: 161 us
  blocking collectives  77.8 us (48%)
  waiting for transfers between devices  31 us (19%)
  starting transfers between devices  23.5 us (15%)
  Pallas kernels  14.2 us (9%)
  local copies, waits for them, and re-layouts  9.96 us (6%)
  other arithmetic  3.01 us (2%)
    ppermute x13, waiting for transfers between devices, swap(): return lax.ppermute(values, axis, [(i, i ^ mask) for i in range(N)])  31 us
    ppermute x13, starting transfers between devices, swap(): return lax.ppermute(values, axis, [(i, i ^ mask) for i in range(N)])  23.5 us
    all_gather x1, blocking collectives, shards(): row_side = lax.all_gather(row_side, 'col', axis=1, tiled=True)  21.7 us
    all_gather x1, blocking collectives, shards(): images = lax.all_gather(image, 'col', axis=0, tiled=False)  19.9 us
    all_gather x1, blocking collectives, shards(): terms = lax.all_gather(terms, 'col', axis=0, tiled=False)  18.6 us
    all_gather x1, blocking collectives, shards(): lax.all_gather(kept + swap(given, 'col', 1), 'col', axis=0, tiled=False)  17.6 us
    pallas_call x7, Pallas kernels, call(): pl.pallas_call(kernel, name=name, out_shape=shapes, in_specs=[SMEM] * sme...  14.2 us
    unnamed x25, local copies, waits for them, and re-layouts  9.87 us
  transfers between devices with their start and end apart: 13, of which 13 were waited for; matrix products, arithmetic and copies ran while one was open for 0% of the time, Pallas kernels for 0%

profile of v1, /device:TPU:1, one launch (start us, length us, event | category | flops | bytes accessed | tf_op | source)
XLA Modules:
  0.0 160.9 jit_solution(7160013820864764434)
XLA Ops:
  2.1 21.7 %all_gather.21 = f32[3,64,128]{2,0,1:T(4,128)S(1)} all-gather(f32[3,4,128]{2,0,1:T(4,128)S(1)} %pad_maximum_fusion.3), channel_id=1, replica_groups=mesh['row'=16,'col'=16] {'col'}, dimensions={1}, use_global_device_ids=true | all-gather | bytes 104448 | tf_op jit(solution)/shard_map/all_gather | solution.py:205
  25.9 2.2 %copy-done.4 = f32[1,1,64,128,128]{4,3,2,1,0:T(8,128)S(1)} copy-done((f32[1,1,64,128,128]{4,3,2,1,0:T(8,128)S(1)}, f32[1,1,64,128,128]{4,3,2,1,0:T(8,128)}, u32[]{:S(2)}) %copy-start.4) | copy-done | bytes 4194328
  29.4 2.3 %first_adjoint.1 = (f32[128,128]{1,0:T(8,128)S(1)}, bf16[64,256,128]{2,1,0:T(8,128)(2,1)S(1)}) custom-call(s32[1]{0:T(128)} %bitcast.30.count, s32[64]{0:T(128)S(1)} %bitcast.42, s32[64]{0:T(128)S(1)} %bitcast.47, f32[64,128]{1,0:T(8,128)S(1)} %bitcast.38, f32[64,128,128]{2,1,0:T(8,128)S(1)} %bitcast.31), custom_call_target="tpu_custom_call" | custom-call | tf_op jit(solution)/shard_map/first_adjoint/pallas_call | solution.py:28
  34.8 2.6 %collective-permute-done = f32[152,128]{1,0:T(8,128)S(1)} collective-permute-done((f32[152,128]{1,0:T(8,128)S(1)}, f32[152,128]{1,0:T(8,128)S(1)}, u32[]{:S(2)}, u32[]{:S(2)}) %collective-permute-start) | collective-permute-done | bytes 77856 | tf_op jit(solution)/shard_map/ppermute | solution.py:183
  37.5 2.6 %collective-permute-start.1 = (f32[176,128]{1,0:T(8,128)S(1)}, f32[176,128]{1,0:T(8,128)S(1)}, u32[]{:S(2)}, u32[]{:S(2)}) collective-permute-start(f32[176,128]{1,0:T(8,128)S(1)} %pad_maximum_fusion.1), channel_id=1, source_target_pairs={{0,48},{16,32},{32,16},{48,0},{64,112},{80,96},{96,80},{112,64},{1... | collective-permute-start | bytes 270344 | tf_op jit(solution)/shard_map/ppermute | solution.py:183
  43.6 2.3 %collective-permute-done.2 = f32[224,128]{1,0:T(8,128)S(1)} collective-permute-done((f32[224,128]{1,0:T(8,128)S(1)}, f32[224,128]{1,0:T(8,128)S(1)}, u32[]{:S(2)}, u32[]{:S(2)}) %collective-permute-start.2) | collective-permute-done | bytes 114720 | tf_op jit(solution)/shard_map/ppermute | solution.py:183
  46.0 2.8 %collective-permute-start.3 = (f32[320,128]{1,0:T(8,128)S(1)}, f32[320,128]{1,0:T(8,128)S(1)}, u32[]{:S(2)}, u32[]{:S(2)}) collective-permute-start(f32[320,128]{1,0:T(8,128)S(1)} %get-tuple-element.51), channel_id=1, source_target_pairs={{0,192},{16,208},{32,224},{48,240},{64,128},{80,144},{96,160},{112... | collective-permute-start | bytes 491528 | tf_op jit(solution)/shard_map/ppermute | solution.py:183
  48.9 2.6 %collective-permute-done.3 = f32[320,128]{1,0:T(8,128)S(1)} collective-permute-done((f32[320,128]{1,0:T(8,128)S(1)}, f32[320,128]{1,0:T(8,128)S(1)}, u32[]{:S(2)}, u32[]{:S(2)}) %collective-permute-start.3) | collective-permute-done | bytes 163872 | tf_op jit(solution)/shard_map/ppermute | solution.py:183
  53.8 3.2 %first_forward.1 = (f32[64,128]{1,0:T(8,128)S(1)}, f32[128,128]{1,0:T(8,128)S(1)}, f32[128,128]{1,0:T(8,128)}, f32[128,128]{1,0:T(8,128)S(1)}, f32[128,128]{1,0:T(8,128)S(1)}) custom-call(s32[2]{0:T(128)S(1)} %pad_add_fusion.where, s32[64]{0:T(128)S(1)} %bitcast.43, s32[64]{0:T(128)S(1)} %bitcast.48, f32[128,128]{1,0:T(8,128)S(1)} %get-tuple-element.46.own, ...), custom_call_target="tpu_custom_call" | custom-call | tf_op jit(solution)/shard_map/first_forward/pallas_call | solution.py:28
  57.0 19.9 %all-gather = f32[1024,128]{1,0:T(8,128)S(1)} all-gather(f32[64,128]{1,0:T(8,128)S(1)} %get-tuple-element.27), channel_id=2, replica_groups=mesh['row'=16,'col'=16] {'col'}, dimensions={0}, use_global_device_ids=true | all-gather | bytes 557056 | tf_op jit(solution)/shard_map/all_gather | solution.py:236
  79.2 3.5 %collective-permute-done.4 = f32[128,128]{1,0:T(8,128)S(1)} collective-permute-done((f32[128,128]{1,0:T(8,128)S(1)}, f32[128,128]{1,0:T(8,128)S(1)}, u32[]{:S(2)}, u32[]{:S(2)}) %collective-permute-start.4) | collective-permute-done | bytes 65568 | tf_op jit(solution)/shard_map/ppermute | solution.py:183
  82.7 2.6 %collective-permute-start.5 = (f32[128,128]{1,0:T(8,128)S(1)}, f32[128,128]{1,0:T(8,128)S(1)}, u32[]{:S(2)}, u32[]{:S(2)}) collective-permute-start(f32[128,128]{1,0:T(8,128)S(1)} %add.37), channel_id=1, source_target_pairs={{0,48},{16,32},{32,16},{48,0},{64,112},{80,96},{96,80},{112,64},{1... | collective-permute-start | bytes 196616 | tf_op jit(solution)/shard_map/ppermute | solution.py:183
  87.3 3.0 %collective-permute-done.6 = f32[128,128]{1,0:T(8,128)S(1)} collective-permute-done((f32[128,128]{1,0:T(8,128)S(1)}, f32[128,128]{1,0:T(8,128)S(1)}, u32[]{:S(2)}, u32[]{:S(2)}) %collective-permute-start.6) | collective-permute-done | bytes 65568 | tf_op jit(solution)/shard_map/ppermute | solution.py:183
  90.4 2.8 %collective-permute-start.7 = (f32[128,128]{1,0:T(8,128)S(1)}, f32[128,128]{1,0:T(8,128)S(1)}, u32[]{:S(2)}, u32[]{:S(2)}) collective-permute-start(f32[128,128]{1,0:T(8,128)S(1)} %add.39.own), channel_id=1, source_target_pairs={{0,192},{16,208},{32,224},{48,240},{64,128},{80,144},{96,160},{112... | collective-permute-start | bytes 196616 | tf_op jit(solution)/shard_map/ppermute | solution.py:183
  94.8 2.2 %copy-done.3 = bf16[64,256,128]{2,1,0:T(8,128)(2,1)S(1)} copy-done((bf16[64,256,128]{2,1,0:T(8,128)(2,1)S(1)}, bf16[64,256,128]{2,1,0:T(8,128)(2,1)}, u32[]{:S(2)}) %copy-start.3) | copy-done | bytes 4194328
  97.0 3.0 %second_forward.1 = (f32[64,128]{1,0:T(8,128)S(1)}, f32[64,128]{1,0:T(8,128)S(1)}, f32[128,128]{1,0:T(8,128)S(1)}, f32[128,128]{1,0:T(8,128)S(1)}, f32[8,128]{1,0:T(8,128)}) custom-call(s32[2]{0:T(128)S(1)} %pad_add_fusion.where, s32[64]{0:T(128)S(1)} %bitcast.45, s32[64]{0:T(128)S(1)} %bitcast.50, f32[128,128]{1,0:T(8,128)S(1)} %add.39.own, ...), custom_call_target="tpu_custom_call" | custom-call | tf_op jit(solution)/shard_map/second_forward/pallas_call | solution.py:28
  100.0 4.3 %collective-permute-start.8 = (f32[64,128]{1,0:T(8,128)S(1)}, f32[64,128]{1,0:T(8,128)S(1)}, u32[]{:S(2)}, u32[]{:S(2)}) collective-permute-start(f32[64,128]{1,0:T(8,128)S(1)} %broadcast_select_fusion), channel_id=1, source_target_pairs={{0,1},{1,0},{2,3},{3,2},{4,5},{5,4},{6,7},{7,6},{8,9},{9,8},{10,11... | collective-permute-start | bytes 98312 | tf_op jit(solution)/shard_map/ppermute | solution.py:183
  105.3 17.6 %all-gather.1 = f32[1024,128]{1,0:T(8,128)S(1)} all-gather(f32[64,128]{1,0:T(8,128)S(1)} %select_add_fusion), channel_id=3, replica_groups=mesh['row'=16,'col'=16] {'col'}, dimensions={0}, use_global_device_ids=true | all-gather | bytes 557056 | tf_op jit(solution)/shard_map/all_gather | solution.py:259
  122.8 2.7 %third_adjoint.1 = (f32[136,128]{1,0:T(8,128)S(1)}, f32[4,128]{1,0:T(4,128)}, f32[64,128]{1,0:T(8,128)}) custom-call(s32[2]{0:T(128)S(1)} %pad_add_fusion.where, s32[64]{0:T(128)S(1)} %bitcast.46, s32[64]{0:T(128)S(1)} %bitcast.51, f32[16,64,128]{2,1,0:T(8,128)S(1)} %bitcast.32, f32[64,128]{1,0:T(8,128)S(1)} %get-tuple-element.35.before, ...), custom_call_target="tpu_custom_call" | custom-call | tf_op jit(solution)/shard_map/third_adjoint/pallas_call | solution.py:28
  125.6 3.6 %collective-permute-done.9 = f32[136,128]{1,0:T(8,128)S(1)} collective-permute-done((f32[136,128]{1,0:T(8,128)S(1)}, f32[136,128]{1,0:T(8,128)S(1)}, u32[]{:S(2)}, u32[]{:S(2)}) %collective-permute-start.9) | collective-permute-done | bytes 69664 | tf_op jit(solution)/shard_map/ppermute | solution.py:183
  129.2 2.6 %collective-permute-start.10 = (f32[136,128]{1,0:T(8,128)S(1)}, f32[136,128]{1,0:T(8,128)S(1)}, u32[]{:S(2)}, u32[]{:S(2)}) collective-permute-start(f32[136,128]{1,0:T(8,128)S(1)} %add.42), channel_id=1, source_target_pairs={{0,48},{16,32},{32,16},{48,0},{64,112},{80,96},{96,80},{112,64},{1... | collective-permute-start | bytes 208904 | tf_op jit(solution)/shard_map/ppermute | solution.py:183
  133.8 3.1 %collective-permute-done.11 = f32[136,128]{1,0:T(8,128)S(1)} collective-permute-done((f32[136,128]{1,0:T(8,128)S(1)}, f32[136,128]{1,0:T(8,128)S(1)}, u32[]{:S(2)}, u32[]{:S(2)}) %collective-permute-start.11) | collective-permute-done | bytes 69664 | tf_op jit(solution)/shard_map/ppermute | solution.py:183
  136.9 2.8 %collective-permute-start.12 = (f32[136,128]{1,0:T(8,128)S(1)}, f32[136,128]{1,0:T(8,128)S(1)}, u32[]{:S(2)}, u32[]{:S(2)}) collective-permute-start(f32[136,128]{1,0:T(8,128)S(1)} %add.44.own), channel_id=1, source_target_pairs={{0,192},{16,208},{32,224},{48,240},{64,128},{80,144},{96,160},{112... | collective-permute-start | bytes 208904 | tf_op jit(solution)/shard_map/ppermute | solution.py:183
  141.5 18.6 %all-gather.2 = f32[128,128]{1,0:T(8,128)S(1)} all-gather(f32[8,128]{1,0:T(8,128)S(1)} %get-tuple-element.40), channel_id=4, replica_groups=mesh['row'=16,'col'=16] {'col'}, dimensions={0}, use_global_device_ids=true | all-gather | bytes 69632 | tf_op jit(solution)/shard_map/all_gather | solution.py:276
  (63 shorter events, 24.5 us)
Async XLA Ops:
  0.6 45.3 %copy-start.9 = (f32[1,8,128]{2,1,0:T(8,128)S(1)}, f32[1,8,128]{2,1,0:T(8,128)}, u32[]{:S(2)}) copy-start(f32[1,8,128]{2,1,0:T(8,128)} %param.17) | copy-start | bytes 12292
  0.6 45.3 %copy-start.10 = (f32[1,8,128]{2,1,0:T(8,128)S(1)}, f32[1,8,128]{2,1,0:T(8,128)}, u32[]{:S(2)}) copy-start(f32[1,8,128]{2,1,0:T(8,128)} %param.18) | copy-start | bytes 12292
  0.7 50.9 %copy-start.6 = (s32[1,1,64]{2,1,0:T(1,128)S(1)}, s32[1,1,64]{2,1,0:T(1,128)}, u32[]{:S(2)}) copy-start(s32[1,1,64]{2,1,0:T(1,128)} %param.11) | copy-start | bytes 772
  0.7 50.9 %copy-start.8 = (s32[1,1,64]{2,1,0:T(1,128)S(1)}, s32[1,1,64]{2,1,0:T(1,128)}, u32[]{:S(2)}) copy-start(s32[1,1,64]{2,1,0:T(1,128)} %param.12) | copy-start | bytes 772
  25.9 2.2 %copy-start.4 = (f32[1,1,64,128,128]{4,3,2,1,0:T(8,128)S(1)}, f32[1,1,64,128,128]{4,3,2,1,0:T(8,128)}, u32[]{:S(2)}) copy-start(f32[1,1,64,128,128]{4,3,2,1,0:T(8,128)} %param.10) | copy-start | bytes 12582916
  28.1 0.7 copy-start.5
  28.7 0.7 copy-start.7
  31.7 2.0 %copy-start = (bf16[64,256,128]{2,1,0:T(8,128)(2,1)}, bf16[64,256,128]{2,1,0:T(8,128)(2,1)S(1)}, u32[]{:S(2)}) copy-start(bf16[64,256,128]{2,1,0:T(8,128)(2,1)S(1)} %get-tuple-element.26.pairs) | copy-start | bytes 12582916
  33.6 3.8 %collective-permute-start = (f32[152,128]{1,0:T(8,128)S(1)}, f32[152,128]{1,0:T(8,128)S(1)}, u32[]{:S(2)}, u32[]{:S(2)}) collective-permute-start(f32[152,128]{1,0:T(8,128)S(1)} %pad_maximum_fusion.2), channel_id=1, source_target_pairs={{0,16},{16,0},{32,48},{48,32},{64,80},{80,64},{96,112},{112,96},{1... | collective-permute-start | bytes 233480 | tf_op jit(solution)/shard_map/ppermute | solution.py:183
  37.5 4.7 %collective-permute-start.1 = (f32[176,128]{1,0:T(8,128)S(1)}, f32[176,128]{1,0:T(8,128)S(1)}, u32[]{:S(2)}, u32[]{:S(2)}) collective-permute-start(f32[176,128]{1,0:T(8,128)S(1)} %pad_maximum_fusion.1), channel_id=1, source_target_pairs={{0,48},{16,32},{32,16},{48,0},{64,112},{80,96},{96,80},{112,64},{1... | collective-permute-start | bytes 270344 | tf_op jit(solution)/shard_map/ppermute | solution.py:183
  42.2 3.7 %collective-permute-start.2 = (f32[224,128]{1,0:T(8,128)S(1)}, f32[224,128]{1,0:T(8,128)S(1)}, u32[]{:S(2)}, u32[]{:S(2)}) collective-permute-start(f32[224,128]{1,0:T(8,128)S(1)} %pad_maximum_fusion), channel_id=1, source_target_pairs={{0,64},{16,80},{32,96},{48,112},{64,0},{80,16},{96,32},{112,48},{1... | collective-permute-start | bytes 344072 | tf_op jit(solution)/shard_map/ppermute | solution.py:183
  46.0 5.5 %collective-permute-start.3 = (f32[320,128]{1,0:T(8,128)S(1)}, f32[320,128]{1,0:T(8,128)S(1)}, u32[]{:S(2)}, u32[]{:S(2)}) collective-permute-start(f32[320,128]{1,0:T(8,128)S(1)} %get-tuple-element.51), channel_id=1, source_target_pairs={{0,192},{16,208},{32,224},{48,240},{64,128},{80,144},{96,160},{112... | collective-permute-start | bytes 491528 | tf_op jit(solution)/shard_map/ppermute | solution.py:183
  51.6 2.2 %copy-start.1 = (bf16[64,256,128]{2,1,0:T(8,128)(2,1)S(1)}, bf16[64,256,128]{2,1,0:T(8,128)(2,1)}, u32[]{:S(2)}) copy-start(bf16[64,256,128]{2,1,0:T(8,128)(2,1)} %copy-done) | copy-start | bytes 12582916
  53.8 23.1 %copy-start.2 = (bf16[64,256,128]{2,1,0:T(8,128)(2,1)S(1)}, bf16[64,256,128]{2,1,0:T(8,128)(2,1)}, u32[]{:S(2)}) copy-start(bf16[64,256,128]{2,1,0:T(8,128)(2,1)} %copy-done) | copy-start | bytes 12582916
  79.1 3.6 %collective-permute-start.4 = (f32[128,128]{1,0:T(8,128)S(1)}, f32[128,128]{1,0:T(8,128)S(1)}, u32[]{:S(2)}, u32[]{:S(2)}) collective-permute-start(f32[128,128]{1,0:T(8,128)S(1)} %get-tuple-element.28), channel_id=1, source_target_pairs={{0,16},{16,0},{32,48},{48,32},{64,80},{80,64},{96,112},{112,96},{1... | collective-permute-start | bytes 196616 | tf_op jit(solution)/shard_map/ppermute | solution.py:183
  82.7 4.4 %collective-permute-start.5 = (f32[128,128]{1,0:T(8,128)S(1)}, f32[128,128]{1,0:T(8,128)S(1)}, u32[]{:S(2)}, u32[]{:S(2)}) collective-permute-start(f32[128,128]{1,0:T(8,128)S(1)} %add.37), channel_id=1, source_target_pairs={{0,48},{16,32},{32,16},{48,0},{64,112},{80,96},{96,80},{112,64},{1... | collective-permute-start | bytes 196616 | tf_op jit(solution)/shard_map/ppermute | solution.py:183
  87.1 3.2 %collective-permute-start.6 = (f32[128,128]{1,0:T(8,128)S(1)}, f32[128,128]{1,0:T(8,128)S(1)}, u32[]{:S(2)}, u32[]{:S(2)}) collective-permute-start(f32[128,128]{1,0:T(8,128)S(1)} %add.38), channel_id=1, source_target_pairs={{0,64},{16,80},{32,96},{48,112},{64,0},{80,16},{96,32},{112,48},{1... | collective-permute-start | bytes 196616 | tf_op jit(solution)/shard_map/ppermute | solution.py:183
  90.4 4.5 %collective-permute-start.7 = (f32[128,128]{1,0:T(8,128)S(1)}, f32[128,128]{1,0:T(8,128)S(1)}, u32[]{:S(2)}, u32[]{:S(2)}) collective-permute-start(f32[128,128]{1,0:T(8,128)S(1)} %add.39.own), channel_id=1, source_target_pairs={{0,192},{16,208},{32,224},{48,240},{64,128},{80,144},{96,160},{112... | collective-permute-start | bytes 196616 | tf_op jit(solution)/shard_map/ppermute | solution.py:183
  94.8 2.2 %copy-start.3 = (bf16[64,256,128]{2,1,0:T(8,128)(2,1)S(1)}, bf16[64,256,128]{2,1,0:T(8,128)(2,1)}, u32[]{:S(2)}) copy-start(bf16[64,256,128]{2,1,0:T(8,128)(2,1)} %copy-done) | copy-start | bytes 12582916
  100.0 5.2 %collective-permute-start.8 = (f32[64,128]{1,0:T(8,128)S(1)}, f32[64,128]{1,0:T(8,128)S(1)}, u32[]{:S(2)}, u32[]{:S(2)}) collective-permute-start(f32[64,128]{1,0:T(8,128)S(1)} %broadcast_select_fusion), channel_id=1, source_target_pairs={{0,1},{1,0},{2,3},{3,2},{4,5},{5,4},{6,7},{7,6},{8,9},{9,8},{10,11... | collective-permute-start | bytes 98312 | tf_op jit(solution)/shard_map/ppermute | solution.py:183
  125.6 3.6 %collective-permute-start.9 = (f32[136,128]{1,0:T(8,128)S(1)}, f32[136,128]{1,0:T(8,128)S(1)}, u32[]{:S(2)}, u32[]{:S(2)}) collective-permute-start(f32[136,128]{1,0:T(8,128)S(1)} %get-tuple-element.37), channel_id=1, source_target_pairs={{0,16},{16,0},{32,48},{48,32},{64,80},{80,64},{96,112},{112,96},{1... | collective-permute-start | bytes 208904 | tf_op jit(solution)/shard_map/ppermute | solution.py:183
  129.2 4.5 %collective-permute-start.10 = (f32[136,128]{1,0:T(8,128)S(1)}, f32[136,128]{1,0:T(8,128)S(1)}, u32[]{:S(2)}, u32[]{:S(2)}) collective-permute-start(f32[136,128]{1,0:T(8,128)S(1)} %add.42), channel_id=1, source_target_pairs={{0,48},{16,32},{32,16},{48,0},{64,112},{80,96},{96,80},{112,64},{1... | collective-permute-start | bytes 208904 | tf_op jit(solution)/shard_map/ppermute | solution.py:183
  133.7 3.2 %collective-permute-start.11 = (f32[136,128]{1,0:T(8,128)S(1)}, f32[136,128]{1,0:T(8,128)S(1)}, u32[]{:S(2)}, u32[]{:S(2)}) collective-permute-start(f32[136,128]{1,0:T(8,128)S(1)} %add.43), channel_id=1, source_target_pairs={{0,64},{16,80},{32,96},{48,112},{64,0},{80,16},{96,32},{112,48},{1... | collective-permute-start | bytes 208904 | tf_op jit(solution)/shard_map/ppermute | solution.py:183
  136.9 4.5 %collective-permute-start.12 = (f32[136,128]{1,0:T(8,128)S(1)}, f32[136,128]{1,0:T(8,128)S(1)}, u32[]{:S(2)}, u32[]{:S(2)}) collective-permute-start(f32[136,128]{1,0:T(8,128)S(1)} %add.44.own), channel_id=1, source_target_pairs={{0,192},{16,208},{32,224},{48,240},{64,128},{80,144},{96,160},{112... | collective-permute-start | bytes 208904 | tf_op jit(solution)/shard_map/ppermute | solution.py:183

commit v2 on v1

v2 whole, which is shorter than its diff:
```python
import jax
import jax.numpy as jnp
from jax import lax
from jax.experimental import pallas as pl
from jax.experimental.pallas import tpu as pltpu
from jax.sharding import Mesh
from jax.sharding import PartitionSpec as P

N = 16
TILE = 128
ROW_BLOCKS = 64
COL_BLOCKS = 128
SLOTS = 64
ROWS_SHARE = ROW_BLOCKS // N
COLS_SHARE = COL_BLOCKS // N
HALF = ROW_BLOCKS // 2
NROWS = float(N * ROW_BLOCKS * TILE)
NCOLS = float(N * COL_BLOCKS * TILE)
UNROLL = 8
F32, BF16 = jnp.float32, jnp.bfloat16

SLOT_ROWS, SLOT_COLS, COUNT, AT_Y, AT_X, AT_Z, AT_CORE = range(7)

VMEM = pl.BlockSpec(memory_space=pltpu.VMEM)
SMEM = pl.BlockSpec(memory_space=pltpu.SMEM)


def call(kernel, name, out_shapes, args, smem=0, smem_out=False, scratch=()):
    shapes = tuple(jax.ShapeDtypeStruct(s, d) for s, d in out_shapes)
    return pl.pallas_call(
        kernel,
        name=name,
        out_shape=shapes,
        in_specs=[SMEM] * smem + [VMEM] * (len(args) - smem),
        out_specs=tuple([SMEM if smem_out else VMEM] * len(shapes)),
        scratch_shapes=list(scratch),
        compiler_params=pltpu.CompilerParams(vmem_limit_bytes=8 * 2**20),
    )(*args)


def split(vector, copies):
    wide = jnp.broadcast_to(vector, (copies, TILE))
    lead = wide.astype(BF16).astype(F32)
    return [lead, wide - lead]


def adjoint_product(table, tile_pair, dual_ref, total):
    total[...] = jnp.zeros_like(total)

    def body(slot, carry):
        lhs = jnp.concatenate(split(dual_ref[pl.ds(table[SLOT_ROWS, slot], 1), :], 8), 0).astype(BF16)
        lhs = jnp.concatenate([lhs, lhs], 1)
        product = jnp.dot(lhs, tile_pair(slot), preferred_element_type=F32)
        total[table[SLOT_COLS, slot]] += product[0:8] + product[8:16]
        return carry

    lax.fori_loop(0, SLOTS, body, 0, unroll=UNROLL)


def forward_product(table, tile_pair, primal_refs, total):
    total[...] = jnp.zeros_like(total)
    copies = 8 // len(primal_refs)

    def body(slot, carry):
        parts = [split(ref[pl.ds(table[SLOT_COLS, slot], 1), :], copies) for ref in primal_refs]
        lhs = jnp.concatenate([p[0] for p in parts] + [p[1] for p in parts], 0).astype(BF16)
        product = lax.dot_general(
            lhs, tile_pair(slot), (((1,), (1,)), ((), ())), preferred_element_type=F32
        )
        product = product[:, :TILE] + product[:, TILE:]
        total[table[SLOT_ROWS, slot]] += product[0:8] + product[8:16]
        return carry

    lax.fori_loop(0, SLOTS, body, 0, unroll=UNROLL)


def clamp_primal(values, free):
    floor = jnp.maximum(values, 0.0)
    return jnp.where(free > 0.5, floor, jnp.minimum(floor, 1.0))


def clamp_dual(values, ineq):
    return jnp.where(ineq > 0.5, jnp.maximum(values, 0.0), values)


def index_row(table):
    return table[AT_Y, 0] * 4 + table[AT_X, 0]


def index_col(table):
    return table[AT_Z, 0] * 2 + table[AT_CORE, 0]


def sum_four(refs, rows):
    own, opposite, right, left = (ref[rows, :] for ref in refs)
    return (own + opposite) + (right + left)


def pack(place, count, rows, cols, kinds, rhs, start, table, row_side):
    table[...] = jnp.zeros_like(table)
    table[SLOT_ROWS : SLOT_ROWS + 1, 0:SLOTS] = rows[...]
    table[SLOT_COLS : SLOT_COLS + 1, 0:SLOTS] = cols[...]
    table[COUNT : COUNT + 1, :] = jnp.full((1, TILE), count[0], jnp.int32)
    for k in range(4):
        table[AT_Y + k : AT_Y + k + 1, :] = jnp.full((1, TILE), place[k], jnp.int32)
    side = jnp.concatenate(
        [start[...], rhs[...], kinds[...].astype(F32), jnp.zeros((ROWS_SHARE, TILE), F32)], 0
    )
    row_side[...] = jnp.broadcast_to(side[None], row_side.shape)


def first_adjoint(
    table, row_side, start, cost, kinds, tiles, payload, dual, rhs, ineq, pairs, total
):
    for k in range(N):
        block = slice(k * ROWS_SHARE, (k + 1) * ROWS_SHARE)
        for j, ref in enumerate((dual, rhs, ineq)):
            ref[block, :] = row_side[k, j * ROWS_SHARE : (j + 1) * ROWS_SHARE, :]

    def tile_pair(slot):
        tile = jnp.where(slot < table[COUNT, 0], tiles[slot], 0.0)
        lead = tile.astype(BF16)
        pair = jnp.concatenate([lead, (tile - lead.astype(F32)).astype(BF16)], 0)
        pairs[slot] = pair
        return pair

    adjoint_product(table, tile_pair, dual, total)
    payload[0:COL_BLOCKS, :] = total[:, 0, :]
    payload[COL_BLOCKS:, :] = jnp.concatenate(
        [start[...], cost[...], kinds[...].astype(F32)], 0
    )


def first_forward(
    table, own, opposite, right, left, pairs, kept, given, primal, start, cost, free, extended, total
):
    y, x = table[AT_Y, 0], table[AT_X, 0]
    for j, (ref, dy) in enumerate(((own, 0), (opposite, 2), (right, 3), (left, 1))):
        for k, dx in enumerate((0, 2, 3, 1)):
            device = ((y + dy) & 3) * 4 + ((x + dx) & 3)
            block = pl.ds(pl.multiple_of(device * COLS_SHARE, COLS_SHARE), COLS_SHARE)
            for m, out in enumerate((start, cost, free)):
                first = COL_BLOCKS + (3 * k + m) * COLS_SHARE
                out[block, :] = ref[first : first + COLS_SHARE, :]
    gradient = sum_four((own, opposite, right, left), slice(0, COL_BLOCKS))
    primal[...] = clamp_primal(start[...] - 0.4 * (cost[...] - gradient), free[...])
    extended[...] = 2.0 * primal[...] - start[...]
    forward_product(table, lambda slot: pairs[slot], [extended], total)
    mine = pl.multiple_of(table[AT_CORE, 0] * HALF, HALF)
    kept[...] = total[pl.ds(mine, HALF), 0, :]
    given[...] = total[pl.ds(HALF - mine, HALF), 0, :]


def second_adjoint(
    table, half, other, start, rhs, ineq, pairs, gradient, dual, image, total
):
    mine = pl.multiple_of(table[AT_CORE, 0] * HALF, HALF)
    image[pl.ds(mine, HALF), :] = half[...]
    image[pl.ds(HALF - mine, HALF), :] = other[...]
    dual[...] = clamp_dual(start[...] + 0.4 * (rhs[...] - image[...]), ineq[...])
    adjoint_product(table, lambda slot: pairs[slot], dual, total)
    gradient[...] = total[:, 0, :]


def second_forward(
    table, own, opposite, right, left, before, cost, free, pairs, kept, given, primal, gradient, mine, extended, total
):
    gradient[...] = sum_four((own, opposite, right, left), slice(0, COL_BLOCKS))
    primal[...] = clamp_primal(before[...] - 0.4 * (cost[...] - gradient[...]), free[...])
    extended[...] = 2.0 * primal[...] - before[...]
    mine[...] = primal[
        pl.ds(pl.multiple_of(index_row(table) * COLS_SHARE, COLS_SHARE), COLS_SHARE), :
    ]
    forward_product(table, lambda slot: pairs[slot], [extended, primal], total)
    first = table[AT_CORE, 0] == 0
    image, plain = total[:, 0, :], total[:, 4, :]
    kept[...] = jnp.where(first, image, plain)
    given[...] = jnp.where(first, plain, image)


def third_adjoint(
    table, held, other, before, rhs, ineq, pairs, payload, mine, dual, total
):
    first = table[AT_CORE, 0] == 0
    image = jnp.where(first, held[...], other[...])
    plain = jnp.where(first, other[...], held[...])
    earlier, bound, kind = before[...], rhs[...], ineq[...]
    dual[...] = clamp_dual(earlier + 0.4 * (bound - image), kind)
    mine[...] = dual[pl.ds(index_col(table) * ROWS_SHARE, ROWS_SHARE), :]
    adjoint_product(table, lambda slot: pairs[slot], dual, total)
    payload[0:COL_BLOCKS, :] = total[:, 0, :]
    terms = []
    for product in (plain, 0.5 * (3.0 * plain - image)):
        residual = bound - product
        residual = jnp.where(kind > 0.5, jnp.maximum(residual, 0.0), residual)
        terms.append(jnp.sum(residual * residual, 0, keepdims=True))
    for value in (dual[...], 0.5 * (earlier + dual[...])):
        terms.append(jnp.sum(bound * value, 0, keepdims=True))
    payload[COL_BLOCKS : COL_BLOCKS + 8, :] = jnp.concatenate(terms + terms, 0)


def column_terms(
    own, opposite, right, left, earlier, before, primal, cost, free, terms, row_terms
):
    four = (own, opposite, right, left)
    adjoint = sum_four(four, slice(0, COL_BLOCKS))
    row_terms[...] = sum_four(four, slice(COL_BLOCKS, COL_BLOCKS + 8))
    price, kind = cost[...], free[...]
    rows = []
    for gradient, value in (
        (adjoint, primal[...]),
        (0.5 * (earlier[...] + adjoint), 0.5 * (before[...] + primal[...])),
    ):
        low = jnp.minimum(price - gradient, 0.0)
        violation = jnp.where(kind > 0.5, low, 0.0)
        box = jnp.where(kind > 0.5, 0.0, low)
        rows.append(jnp.sum(violation * violation, 0, keepdims=True))
        rows.append(jnp.sum(price * value, 0, keepdims=True))
        rows.append(jnp.sum(box, 0, keepdims=True))
    rows = jnp.concatenate(rows + rows[:2], 0)
    terms[...] = jnp.broadcast_to(rows[None], terms.shape)


def measures(gathered, row_terms, primal_residual, dual_residual, gap):
    columns = jnp.sum(gathered[...], 0)
    rows = row_terms[...]
    for k in range(2):
        primal_residual[k] = jnp.sum(rows[k : k + 1]) * (1.0 / NROWS)
        dual_residual[k] = jnp.sum(columns[3 * k : 3 * k + 1]) * (1.0 / NCOLS)
        total = columns[3 * k + 1 : 3 * k + 2] - columns[3 * k + 2 : 3 * k + 3] - rows[2 + k : 3 + k]
        gap[k] = jnp.sum(total) * (1.0 / NCOLS)


def shift(values, axis, step):
    return lax.ppermute(values, axis, [(k, (k + step) % 4) for k in range(4)])


def four_of(values, axis):
    return values, shift(values, axis, 2), shift(values, axis, 1), shift(values, axis, -1)


def four_over_row(values):
    own, opposite, right, left = four_of(values, "x")
    return four_of((own + opposite) + (right + left), "y")


def swap_cores(values):
    return lax.ppermute(values, "core", [(0, 1), (1, 0)])


def exchange(copies, axes):
    return lax.all_to_all(copies, axes, 0, 0)


def sum_over_z(values):
    copies = jnp.broadcast_to(values[None], (8,) + values.shape)
    return jnp.sum(exchange(copies, "z"), 0)


def shards(
    tiles, tile_rows, tile_cols, tile_count, row_types, var_types, rhs, cost, primal_start, dual_start
):
    tiles = tiles.reshape(SLOTS, TILE, TILE)
    place = jnp.stack([lax.axis_index(a) for a in ("y", "x", "z", "core")]).astype(jnp.int32)
    blocks, columns, half = (ROW_BLOCKS, TILE), (COL_BLOCKS, TILE), (HALF, TILE)
    row_total = [pltpu.VMEM((ROW_BLOCKS, 8, TILE), F32)]
    col_total = [pltpu.VMEM((COL_BLOCKS, 8, TILE), F32)]

    table, row_side = call(
        pack,
        "pack",
        [((8, TILE), jnp.int32), ((N, 4 * ROWS_SHARE, TILE), F32)],
        (
            place,
            tile_count.reshape(1),
            tile_rows.reshape(1, SLOTS),
            tile_cols.reshape(1, SLOTS),
            row_types[0],
            rhs[0],
            dual_start[0],
        ),
        smem=2,
    )
    row_side = exchange(row_side, ("z", "core"))

    payload, dual0, rhs_full, ineq, pairs = call(
        first_adjoint,
        "first_adjoint",
        [((COL_BLOCKS + 3 * COLS_SHARE, TILE), F32)]
        + [(blocks, F32)] * 3
        + [((SLOTS, 2 * TILE, TILE), BF16)],
        (table, row_side, primal_start[0], cost[0], var_types[0], tiles),
        smem=1,
        scratch=col_total,
    )
    four = four_of(payload, "x")
    gradient = (four[0] + four[1]) + (four[2] + four[3])
    payload = jnp.concatenate([gradient[:COL_BLOCKS]] + [p[COL_BLOCKS:] for p in four], 0)
    four = four_of(payload, "y")

    kept, given, primal1, start_full, cost_full, free = call(
        first_forward,
        "first_forward",
        [(half, F32)] * 2 + [(columns, F32)] * 4,
        (table, *four, pairs),
        smem=1,
        scratch=[pltpu.VMEM(columns, F32)] + row_total,
    )
    held = sum_over_z(kept + swap_cores(given))

    gradient, dual1 = call(
        second_adjoint,
        "second_adjoint",
        [(columns, F32), (blocks, F32)],
        (table, held, swap_cores(held), dual0, rhs_full, ineq, pairs),
        smem=1,
        scratch=[pltpu.VMEM(blocks, F32)] + col_total,
    )

    kept, given, primal2, gradient2, primal_mine = call(
        second_forward,
        "second_forward",
        [(blocks, F32)] * 2 + [(columns, F32)] * 2 + [((COLS_SHARE, TILE), F32)],
        (table, *four_over_row(gradient), primal1, cost_full, free, pairs),
        smem=1,
        scratch=[pltpu.VMEM(columns, F32)] + row_total,
    )
    held = sum_over_z(kept + swap_cores(given))

    payload, dual_mine = call(
        third_adjoint,
        "third_adjoint",
        [((COL_BLOCKS + 8, TILE), F32), ((ROWS_SHARE, TILE), F32)],
        (table, held, swap_cores(held), dual1, rhs_full, ineq, pairs),
        smem=1,
        scratch=[pltpu.VMEM(blocks, F32)] + col_total,
    )
    terms, row_terms = call(
        column_terms,
        "column_terms",
        [((N, 8, TILE), F32), ((8, TILE), F32)],
        (*four_over_row(payload), gradient2, primal1, primal2, cost_full, free),
    )
    primal_residual, dual_residual, gap = call(
        measures,
        "measures",
        [((2,), F32)] * 3,
        (exchange(terms, ("z", "core")), row_terms),
        smem_out=True,
    )
    return primal_mine[None], dual_mine[None], primal_residual, dual_residual, gap


def solution(mesh):
    rings = Mesh(mesh.devices.reshape(4, 4, 8, 2), ("y", "x", "z", "core"))
    row, col = ("y", "x"), ("z", "core")
    in_specs = (
        P(row, col, None, None, None),
        P(row, col, None),
        P(row, col, None),
        P(row, col),
        P(row, col, None),
        P(col, row, None),
        P(row, col, None),
        P(col, row, None),
        P(col, row, None),
        P(row, col, None),
    )
    out_specs = (P(col, row, None), P(row, col, None), P(), P(), P())
    return jax.shard_map(shards, mesh=rings, in_specs=in_specs, out_specs=out_specs, check_vma=False)
```

time: 161 us -> 148 us (0.919)
  blocking collectives: 77.8 us -> 57 us
  starting transfers between devices: 23.5 us -> 28.9 us
  local copies, waits for them, and re-layouts: 9.96 us -> 14 us
  other arithmetic: 3.01 us -> 0.17 us
    all_gather x4 -> x0, blocking collectives: 77.8 us -> none  [the longest x1 21.7 us: shards(): row_side = lax.all_gather(row_side, 'col', axis=1, tiled=True)]
    all_to_all x0 -> x4, blocking collectives: none -> 57 us  [exchange(): return lax.all_to_all(copies, axes, 0, 0)]
    ppermute x13 -> x22, starting transfers between devices: 23.5 us -> 28.9 us  [the longest x18 21.3 us: shift(): return lax.ppermute(values, axis, [(k, (k + step) % 4) for k in range(4)])]
    unnamed x25 -> x29, local copies, waits for them, and re-layouts: 9.87 us -> 14 us
    pallas_call x7 -> x8, Pallas kernels: 14.2 us -> 15 us  [call(): pl.pallas_call(kernel, name=name, out_shape=shapes, in_specs=[SMEM] * sme...]
    ppermute x13 -> x22, waiting for transfers between devices: 31 us -> 30.9 us  [the longest x18 27.5 us: shift(): return lax.ppermute(values, axis, [(k, (k + step) % 4) for k in range(4)])]
  transfers between devices with their start and end apart: 13 -> 22, of which waited for: 13 -> 17; matrix products, arithmetic and copies ran while one was open for 0% -> 0% of each run, Pallas kernels for 0% -> 0%
where the time goes in v2:
time: 148 us
  blocking collectives  57 us (39%)
  waiting for transfers between devices  30.9 us (21%)
  starting transfers between devices  28.9 us (20%)
  Pallas kernels  15 us (10%)
  local copies, waits for them, and re-layouts  14 us (9%)
  between operations  1.56 us (1%)
    all_to_all x4, blocking collectives, exchange(): return lax.all_to_all(copies, axes, 0, 0)  57 us
    ppermute x18, waiting for transfers between devices, shift(): return lax.ppermute(values, axis, [(k, (k + step) % 4) for k in range(4)])  27.5 us
    ppermute x18, starting transfers between devices, shift(): return lax.ppermute(values, axis, [(k, (k + step) % 4) for k in range(4)])  21.3 us
    pallas_call x8, Pallas kernels, call(): pl.pallas_call(kernel, name=name, out_shape=shapes, in_specs=[SMEM] * sme...  15 us
    unnamed x29, local copies, waits for them, and re-layouts  14 us
    ppermute x4, starting transfers between devices, swap_cores(): return lax.ppermute(values, 'core', [(0, 1), (1, 0)])  7.62 us
    ppermute x4, waiting for transfers between devices, swap_cores(): return lax.ppermute(values, 'core', [(0, 1), (1, 0)])  3.4 us
  transfers between devices with their start and end apart: 22, of which 17 were waited for; matrix products, arithmetic and copies ran while one was open for 0% of the time, Pallas kernels for 0%

profile of v2, /device:TPU:1, one launch (start us, length us, event | category | flops | bytes accessed | tf_op | source)
XLA Modules:
  0.0 147.5 jit_solution(3105930498525768089)
XLA Ops:
  5.3 18.9 %all_to_all.20.row_side = f32[16,16,128]{2,1,0:T(8,128)S(1)} all-to-all(f32[16,16,128]{2,1,0:T(8,128)S(1)} %get-tuple-element.32), channel_id=1, replica_groups=mesh['y'=4,'x'=4,'z'=8,'core'=2] {'z','core'}, dimensions={0} | all-to-all | bytes 262144 | tf_op jit(solution)/shard_map/all_to_all | solution.py:252
  24.2 2.2 %copy-done.4 = f32[1,1,64,128,128]{4,3,2,1,0:T(8,128)S(1)} copy-done((f32[1,1,64,128,128]{4,3,2,1,0:T(8,128)S(1)}, f32[1,1,64,128,128]{4,3,2,1,0:T(8,128)}, u32[]{:S(2)}) %copy-start.4) | copy-done | bytes 4194328
  28.5 2.4 %first_adjoint.1 = (f32[152,128]{1,0:T(8,128)S(1)}, f32[64,128]{1,0:T(8,128)S(1)}, f32[64,128]{1,0:T(8,128)S(1)}, f32[64,128]{1,0:T(8,128)S(1)}, bf16[64,256,128]{2,1,0:T(8,128)(2,1)S(1)}) custom-call(s32[8,128]{1,0:T(8,128)S(1)} %get-tuple-element.31.table, f32[16,16,128]{2,1,0:T(8,128)S(1)} %all_to_all.20.row_side, f32[8,128]{1,0:T(8,128)S(1)} %bitcast.18, ...), custom_call_target="tpu_custom_call" | custom-call | tf_op jit(solution)/shard_map/first_adjoint/pallas_call | solution.py:30
  30.8 2.6 %collective-permute-start.2 = (f32[152,128]{1,0:T(8,128)S(1)}, f32[152,128]{1,0:T(8,128)S(1)}, u32[]{:S(2)}, u32[]{:S(2)}) collective-permute-start(f32[152,128]{1,0:T(8,128)S(1)} %get-tuple-element.33), channel_id=1, source_target_pairs={{0,48},{16,0},{32,16},{48,32},{1,49},{17,1},{33,17},{49,33},{2,50}... | collective-permute-start | bytes 233480 | tf_op jit(solution)/shard_map/ppermute | solution.py:235
  35.4 4.9 %collective-permute-done.1 = f32[152,128]{1,0:T(8,128)S(1)} collective-permute-done((f32[152,128]{1,0:T(8,128)S(1)}, f32[152,128]{1,0:T(8,128)S(1)}, u32[]{:S(2)}, u32[]{:S(2)}) %collective-permute-start.1) | collective-permute-done | bytes 77856 | tf_op jit(solution)/shard_map/ppermute | solution.py:235
  40.4 2.8 %collective-permute-start.5 = (f32[224,128]{1,0:T(8,128)S(1)}, f32[224,128]{1,0:T(8,128)S(1)}, u32[]{:S(2)}, u32[]{:S(2)}) collective-permute-start(f32[224,128]{1,0:T(8,128)S(1)} %slice_dynamic-update-slice_fusion.own), channel_id=1, source_target_pairs={{0,192},{64,0},{128,64},{192,128},{1,193},{65,1},{129,65},{193,129... | collective-permute-start | bytes 344072 | tf_op jit(solution)/shard_map/ppermute | solution.py:235
  45.0 5.4 %collective-permute-done.4.right = f32[224,128]{1,0:T(8,128)S(1)} collective-permute-done((f32[224,128]{1,0:T(8,128)S(1)}, f32[224,128]{1,0:T(8,128)S(1)}, u32[]{:S(2)}, u32[]{:S(2)}) %collective-permute-start.4) | collective-permute-done | bytes 114720 | tf_op jit(solution)/shard_map/ppermute | solution.py:235
  50.4 3.2 %first_forward.1 = (f32[32,128]{1,0:T(8,128)S(1)}, f32[32,128]{1,0:T(8,128)S(1)}, f32[128,128]{1,0:T(8,128)S(1)}, f32[128,128]{1,0:T(8,128)}, f32[128,128]{1,0:T(8,128)S(1)}, /*index=5*/f32[128,128]{1,0:T(8,128)S(1)}) custom-call(s32[8,128]{1,0:T(8,128)S(1)} %get-tuple-element.31.table, f32[224,128]{1,0:T(8,128)S(1)} %slice_dynamic-update-slice_fusion.own, ...), custom_call_target="tpu_custom_call" | custom-call | tf_op jit(solution)/shard_map/first_forward/pallas_call | solution.py:30
  55.5 2.1 %collective-permute-start.6 = (f32[32,128]{1,0:T(8,128)S(1)}, f32[32,128]{1,0:T(8,128)S(1)}, u32[]{:S(2)}, u32[]{:S(2)}) collective-permute-start(f32[32,128]{1,0:T(8,128)S(1)} %get-tuple-element.36), channel_id=1, source_target_pairs={{0,1},{1,0},{2,3},{3,2},{4,5},{5,4},{6,7},{7,6},{8,9},{9,8},{10,11... | collective-permute-start | bytes 49160 | tf_op jit(solution)/shard_map/ppermute | solution.py:248
  58.4 10.8 %all_to_all.21 = f32[8,32,128]{2,1,0:T(8,128)S(1)} all-to-all(f32[8,32,128]{2,1,0:T(8,128)S(1)} %broadcast_in_dim.8), channel_id=1, replica_groups=mesh['y'=4,'x'=4,'z'=8,'core'=2] {'z'}, dimensions={0} | all-to-all | bytes 262144 | tf_op jit(solution)/shard_map/all_to_all | solution.py:252
  71.8 2.2 %copy-done.1 = bf16[64,256,128]{2,1,0:T(8,128)(2,1)S(1)} copy-done((bf16[64,256,128]{2,1,0:T(8,128)(2,1)S(1)}, bf16[64,256,128]{2,1,0:T(8,128)(2,1)}, u32[]{:S(2)}) %copy-start.1) | copy-done | bytes 4194328
  74.0 2.2 %second_adjoint.1 = (f32[128,128]{1,0:T(8,128)S(1)}, f32[64,128]{1,0:T(8,128)S(1)}) custom-call(s32[8,128]{1,0:T(8,128)S(1)} %get-tuple-element.31.table, f32[32,128]{1,0:T(8,128)S(1)} %reduce_sum.18.half, f32[32,128]{1,0:T(8,128)S(1)} %collective-permute-done.7.other, f32[64,128]{1,0:T(8,128)S(1)} %get-tuple-element.37.start, ...), custom_call_target="tpu_custom_call" | custom-call | tf_op jit(solution)/shard_map/second_adjoint/pallas_call | solution.py:30
  79.4 2.2 %collective-permute-done.9 = f32[128,128]{1,0:T(8,128)S(1)} collective-permute-done((f32[128,128]{1,0:T(8,128)S(1)}, f32[128,128]{1,0:T(8,128)S(1)}, u32[]{:S(2)}, u32[]{:S(2)}) %collective-permute-start.9) | collective-permute-done | bytes 65568 | tf_op jit(solution)/shard_map/ppermute | solution.py:235
  85.6 3.6 %collective-permute-done.12.right = f32[128,128]{1,0:T(8,128)S(1)} collective-permute-done((f32[128,128]{1,0:T(8,128)S(1)}, f32[128,128]{1,0:T(8,128)S(1)}, u32[]{:S(2)}, u32[]{:S(2)}) %collective-permute-start.12) | collective-permute-done | bytes 65568 | tf_op jit(solution)/shard_map/ppermute | solution.py:235
  89.2 3.2 %second_forward.1 = (f32[64,128]{1,0:T(8,128)S(1)}, f32[64,128]{1,0:T(8,128)S(1)}, f32[128,128]{1,0:T(8,128)S(1)}, f32[128,128]{1,0:T(8,128)S(1)}, f32[8,128]{1,0:T(8,128)}) custom-call(s32[8,128]{1,0:T(8,128)S(1)} %get-tuple-element.31.table, f32[128,128]{1,0:T(8,128)S(1)} %add_add_fusion.1.own, f32[128,128]{1,0:T(8,128)S(1)} %collective-permute-done.11.opposite, ...), custom_call_target="tpu_custom_call" | custom-call | tf_op jit(solution)/shard_map/second_forward/pallas_call | solution.py:30
  92.4 3.2 %collective-permute-start.14 = (f32[64,128]{1,0:T(8,128)S(1)}, f32[64,128]{1,0:T(8,128)S(1)}, u32[]{:S(2)}, u32[]{:S(2)}) collective-permute-start(f32[64,128]{1,0:T(8,128)S(1)} %get-tuple-element.46), channel_id=1, source_target_pairs={{0,1},{1,0},{2,3},{3,2},{4,5},{5,4},{6,7},{7,6},{8,9},{9,8},{10,11... | collective-permute-start | bytes 98312 | tf_op jit(solution)/shard_map/ppermute | solution.py:248
  96.5 14.8 %all_to_all.22 = f32[8,64,128]{2,1,0:T(8,128)S(1)} all-to-all(f32[8,64,128]{2,1,0:T(8,128)S(1)} %broadcast_in_dim.20), channel_id=1, replica_groups=mesh['y'=4,'x'=4,'z'=8,'core'=2] {'z'}, dimensions={0} | all-to-all | bytes 524288 | tf_op jit(solution)/shard_map/all_to_all | solution.py:252
  112.8 2.2 %copy-done.3 = bf16[64,256,128]{2,1,0:T(8,128)(2,1)S(1)} copy-done((bf16[64,256,128]{2,1,0:T(8,128)(2,1)S(1)}, bf16[64,256,128]{2,1,0:T(8,128)(2,1)}, u32[]{:S(2)}) %copy-start.3) | copy-done | bytes 4194328
  115.0 2.7 %third_adjoint.1 = (f32[136,128]{1,0:T(8,128)S(1)}, f32[4,128]{1,0:T(4,128)}) custom-call(s32[8,128]{1,0:T(8,128)S(1)} %get-tuple-element.31.table, f32[64,128]{1,0:T(8,128)S(1)} %reduce_sum.19.held, f32[64,128]{1,0:T(8,128)S(1)} %collective-permute-done.15.other, f32[64,128]{1,0:T(8,128)S(1)} %get-tuple-element.47.before, ...), custom_call_target="tpu_custom_call" | custom-call | tf_op jit(solution)/shard_map/third_adjoint/pallas_call | solution.py:30
  117.7 2.1 %collective-permute-start.18 = (f32[136,128]{1,0:T(8,128)S(1)}, f32[136,128]{1,0:T(8,128)S(1)}, u32[]{:S(2)}, u32[]{:S(2)}) collective-permute-start(f32[136,128]{1,0:T(8,128)S(1)} %get-tuple-element.49), channel_id=1, source_target_pairs={{0,48},{16,0},{32,16},{48,32},{1,49},{17,1},{33,17},{49,33},{2,50}... | collective-permute-start | bytes 208904 | tf_op jit(solution)/shard_map/ppermute | solution.py:235
  121.2 5.1 %collective-permute-done.17 = f32[136,128]{1,0:T(8,128)S(1)} collective-permute-done((f32[136,128]{1,0:T(8,128)S(1)}, f32[136,128]{1,0:T(8,128)S(1)}, u32[]{:S(2)}, u32[]{:S(2)}) %collective-permute-start.17) | collective-permute-done | bytes 69664 | tf_op jit(solution)/shard_map/ppermute | solution.py:235
  126.4 2.6 %collective-permute-start.21 = (f32[136,128]{1,0:T(8,128)S(1)}, f32[136,128]{1,0:T(8,128)S(1)}, u32[]{:S(2)}, u32[]{:S(2)}) collective-permute-start(f32[136,128]{1,0:T(8,128)S(1)} %add_add_fusion.own), channel_id=1, source_target_pairs={{0,192},{64,0},{128,64},{192,128},{1,193},{65,1},{129,65},{193,129... | collective-permute-start | bytes 208904 | tf_op jit(solution)/shard_map/ppermute | solution.py:235
  130.4 3.7 %collective-permute-done.20.right = f32[136,128]{1,0:T(8,128)S(1)} collective-permute-done((f32[136,128]{1,0:T(8,128)S(1)}, f32[136,128]{1,0:T(8,128)S(1)}, u32[]{:S(2)}, u32[]{:S(2)}) %collective-permute-start.20) | collective-permute-done | bytes 69664 | tf_op jit(solution)/shard_map/ppermute | solution.py:235
  134.2 12.5 %all_to_all.23.gathered = f32[16,8,128]{2,1,0:T(8,128)S(1)} all-to-all(f32[16,8,128]{2,1,0:T(8,128)S(1)} %get-tuple-element.52), channel_id=1, replica_groups=mesh['y'=4,'x'=4,'z'=8,'core'=2] {'z','core'}, dimensions={0} | all-to-all | bytes 131072 | tf_op jit(solution)/shard_map/all_to_all | solution.py:252
  (72 shorter events, 28.5 us)
Async XLA Ops:
  24.2 2.2 %copy-start.4 = (f32[1,1,64,128,128]{4,3,2,1,0:T(8,128)S(1)}, f32[1,1,64,128,128]{4,3,2,1,0:T(8,128)}, u32[]{:S(2)}) copy-start(f32[1,1,64,128,128]{4,3,2,1,0:T(8,128)} %param.10) | copy-start | bytes 12582916
  30.8 4.6 %collective-permute-start.2 = (f32[152,128]{1,0:T(8,128)S(1)}, f32[152,128]{1,0:T(8,128)S(1)}, u32[]{:S(2)}, u32[]{:S(2)}) collective-permute-start(f32[152,128]{1,0:T(8,128)S(1)} %get-tuple-element.33), channel_id=1, source_target_pairs={{0,48},{16,0},{32,16},{48,32},{1,49},{17,1},{33,17},{49,33},{2,50}... | collective-permute-start | bytes 233480 | tf_op jit(solution)/shard_map/ppermute | solution.py:235
  33.4 6.9 %collective-permute-start.1 = (f32[152,128]{1,0:T(8,128)S(1)}, f32[152,128]{1,0:T(8,128)S(1)}, u32[]{:S(2)}, u32[]{:S(2)}) collective-permute-start(f32[152,128]{1,0:T(8,128)S(1)} %get-tuple-element.33), channel_id=1, source_target_pairs={{0,16},{16,32},{32,48},{48,0},{1,17},{17,33},{33,49},{49,1},{2,18}... | collective-permute-start | bytes 233480 | tf_op jit(solution)/shard_map/ppermute | solution.py:235
  33.4 6.9 %collective-permute-start = (f32[152,128]{1,0:T(8,128)S(1)}, f32[152,128]{1,0:T(8,128)S(1)}, u32[]{:S(2)}, u32[]{:S(2)}) collective-permute-start(f32[152,128]{1,0:T(8,128)S(1)} %get-tuple-element.33), channel_id=1, source_target_pairs={{0,32},{16,48},{32,0},{48,16},{1,33},{17,49},{33,1},{49,17},{2,34}... | collective-permute-start | bytes 233480 | tf_op jit(solution)/shard_map/ppermute | solution.py:235
  40.4 4.6 %collective-permute-start.5 = (f32[224,128]{1,0:T(8,128)S(1)}, f32[224,128]{1,0:T(8,128)S(1)}, u32[]{:S(2)}, u32[]{:S(2)}) collective-permute-start(f32[224,128]{1,0:T(8,128)S(1)} %slice_dynamic-update-slice_fusion.own), channel_id=1, source_target_pairs={{0,192},{64,0},{128,64},{192,128},{1,193},{65,1},{129,65},{193,129... | collective-permute-start | bytes 344072 | tf_op jit(solution)/shard_map/ppermute | solution.py:235
  43.2 7.2 %collective-permute-start.4 = (f32[224,128]{1,0:T(8,128)S(1)}, f32[224,128]{1,0:T(8,128)S(1)}, u32[]{:S(2)}, u32[]{:S(2)}) collective-permute-start(f32[224,128]{1,0:T(8,128)S(1)} %slice_dynamic-update-slice_fusion.own), channel_id=1, source_target_pairs={{0,64},{64,128},{128,192},{192,0},{1,65},{65,129},{129,193},{193,1... | collective-permute-start | bytes 344072 | tf_op jit(solution)/shard_map/ppermute | solution.py:235
  43.2 7.2 %collective-permute-start.3 = (f32[224,128]{1,0:T(8,128)S(1)}, f32[224,128]{1,0:T(8,128)S(1)}, u32[]{:S(2)}, u32[]{:S(2)}) collective-permute-start(f32[224,128]{1,0:T(8,128)S(1)} %slice_dynamic-update-slice_fusion.own), channel_id=1, source_target_pairs={{0,128},{64,192},{128,0},{192,64},{1,129},{65,193},{129,1},{193,65... | collective-permute-start | bytes 344072 | tf_op jit(solution)/shard_map/ppermute | solution.py:235
  55.5 2.9 %collective-permute-start.6 = (f32[32,128]{1,0:T(8,128)S(1)}, f32[32,128]{1,0:T(8,128)S(1)}, u32[]{:S(2)}, u32[]{:S(2)}) collective-permute-start(f32[32,128]{1,0:T(8,128)S(1)} %get-tuple-element.36), channel_id=1, source_target_pairs={{0,1},{1,0},{2,3},{3,2},{4,5},{5,4},{6,7},{7,6},{8,9},{9,8},{10,11... | collective-permute-start | bytes 49160 | tf_op jit(solution)/shard_map/ppermute | solution.py:248
  69.3 2.5 %collective-permute-start.7 = (f32[32,128]{1,0:T(8,128)S(1)}, f32[32,128]{1,0:T(8,128)S(1)}, u32[]{:S(2)}, u32[]{:S(2)}) collective-permute-start(f32[32,128]{1,0:T(8,128)S(1)} %reduce_sum.18.half), channel_id=1, source_target_pairs={{0,1},{1,0},{2,3},{3,2},{4,5},{5,4},{6,7},{7,6},{8,9},{9,8},{10,11... | collective-permute-start | bytes 49160 | tf_op jit(solution)/shard_map/ppermute | solution.py:248
  74.0 15.2 %copy-start.2 = (bf16[64,256,128]{2,1,0:T(8,128)(2,1)S(1)}, bf16[64,256,128]{2,1,0:T(8,128)(2,1)}, u32[]{:S(2)}) copy-start(bf16[64,256,128]{2,1,0:T(8,128)(2,1)} %copy-done) | copy-start | bytes 12582916
  76.2 3.2 %collective-permute-start.10 = (f32[128,128]{1,0:T(8,128)S(1)}, f32[128,128]{1,0:T(8,128)S(1)}, u32[]{:S(2)}, u32[]{:S(2)}) collective-permute-start(f32[128,128]{1,0:T(8,128)S(1)} %get-tuple-element.40), channel_id=1, source_target_pairs={{0,48},{16,0},{32,16},{48,32},{1,49},{17,1},{33,17},{49,33},{2,50}... | collective-permute-start | bytes 196616 | tf_op jit(solution)/shard_map/ppermute | solution.py:235
  77.2 4.3 %collective-permute-start.9 = (f32[128,128]{1,0:T(8,128)S(1)}, f32[128,128]{1,0:T(8,128)S(1)}, u32[]{:S(2)}, u32[]{:S(2)}) collective-permute-start(f32[128,128]{1,0:T(8,128)S(1)} %get-tuple-element.40), channel_id=1, source_target_pairs={{0,16},{16,32},{32,48},{48,0},{1,17},{17,33},{33,49},{49,1},{2,18}... | collective-permute-start | bytes 196616 | tf_op jit(solution)/shard_map/ppermute | solution.py:235
  77.7 4.7 %collective-permute-start.8 = (f32[128,128]{1,0:T(8,128)S(1)}, f32[128,128]{1,0:T(8,128)S(1)}, u32[]{:S(2)}, u32[]{:S(2)}) collective-permute-start(f32[128,128]{1,0:T(8,128)S(1)} %get-tuple-element.40), channel_id=1, source_target_pairs={{0,32},{16,48},{32,0},{48,16},{1,33},{17,49},{33,1},{49,17},{2,34}... | collective-permute-start | bytes 196616 | tf_op jit(solution)/shard_map/ppermute | solution.py:235
  82.4 3.2 %collective-permute-start.13 = (f32[128,128]{1,0:T(8,128)S(1)}, f32[128,128]{1,0:T(8,128)S(1)}, u32[]{:S(2)}, u32[]{:S(2)}) collective-permute-start(f32[128,128]{1,0:T(8,128)S(1)} %add_add_fusion.1.own), channel_id=1, source_target_pairs={{0,192},{64,0},{128,64},{192,128},{1,193},{65,1},{129,65},{193,129... | collective-permute-start | bytes 196616 | tf_op jit(solution)/shard_map/ppermute | solution.py:235
  84.1 5.0 %collective-permute-start.12 = (f32[128,128]{1,0:T(8,128)S(1)}, f32[128,128]{1,0:T(8,128)S(1)}, u32[]{:S(2)}, u32[]{:S(2)}) collective-permute-start(f32[128,128]{1,0:T(8,128)S(1)} %add_add_fusion.1.own), channel_id=1, source_target_pairs={{0,64},{64,128},{128,192},{192,0},{1,65},{65,129},{129,193},{193,1... | collective-permute-start | bytes 196616 | tf_op jit(solution)/shard_map/ppermute | solution.py:235
  84.1 5.0 %collective-permute-start.11 = (f32[128,128]{1,0:T(8,128)S(1)}, f32[128,128]{1,0:T(8,128)S(1)}, u32[]{:S(2)}, u32[]{:S(2)}) collective-permute-start(f32[128,128]{1,0:T(8,128)S(1)} %add_add_fusion.1.own), channel_id=1, source_target_pairs={{0,128},{64,192},{128,0},{192,64},{1,129},{65,193},{129,1},{193,65... | collective-permute-start | bytes 196616 | tf_op jit(solution)/shard_map/ppermute | solution.py:235
  92.4 4.0 %collective-permute-start.14 = (f32[64,128]{1,0:T(8,128)S(1)}, f32[64,128]{1,0:T(8,128)S(1)}, u32[]{:S(2)}, u32[]{:S(2)}) collective-permute-start(f32[64,128]{1,0:T(8,128)S(1)} %get-tuple-element.46), channel_id=1, source_target_pairs={{0,1},{1,0},{2,3},{3,2},{4,5},{5,4},{6,7},{7,6},{8,9},{9,8},{10,11... | collective-permute-start | bytes 98312 | tf_op jit(solution)/shard_map/ppermute | solution.py:248
  111.2 1.6 %collective-permute-start.15 = (f32[64,128]{1,0:T(8,128)S(1)}, f32[64,128]{1,0:T(8,128)S(1)}, u32[]{:S(2)}, u32[]{:S(2)}) collective-permute-start(f32[64,128]{1,0:T(8,128)S(1)} %reduce_sum.19.held), channel_id=1, source_target_pairs={{0,1},{1,0},{2,3},{3,2},{4,5},{5,4},{6,7},{7,6},{8,9},{9,8},{10,11... | collective-permute-start | bytes 98312 | tf_op jit(solution)/shard_map/ppermute | solution.py:248
  117.7 3.5 %collective-permute-start.18 = (f32[136,128]{1,0:T(8,128)S(1)}, f32[136,128]{1,0:T(8,128)S(1)}, u32[]{:S(2)}, u32[]{:S(2)}) collective-permute-start(f32[136,128]{1,0:T(8,128)S(1)} %get-tuple-element.49), channel_id=1, source_target_pairs={{0,48},{16,0},{32,16},{48,32},{1,49},{17,1},{33,17},{49,33},{2,50}... | collective-permute-start | bytes 208904 | tf_op jit(solution)/shard_map/ppermute | solution.py:235
  119.9 6.5 %collective-permute-start.17 = (f32[136,128]{1,0:T(8,128)S(1)}, f32[136,128]{1,0:T(8,128)S(1)}, u32[]{:S(2)}, u32[]{:S(2)}) collective-permute-start(f32[136,128]{1,0:T(8,128)S(1)} %get-tuple-element.49), channel_id=1, source_target_pairs={{0,16},{16,32},{32,48},{48,0},{1,17},{17,33},{33,49},{49,1},{2,18}... | collective-permute-start | bytes 208904 | tf_op jit(solution)/shard_map/ppermute | solution.py:235
  119.9 6.5 %collective-permute-start.16 = (f32[136,128]{1,0:T(8,128)S(1)}, f32[136,128]{1,0:T(8,128)S(1)}, u32[]{:S(2)}, u32[]{:S(2)}) collective-permute-start(f32[136,128]{1,0:T(8,128)S(1)} %get-tuple-element.49), channel_id=1, source_target_pairs={{0,32},{16,48},{32,0},{48,16},{1,33},{17,49},{33,1},{49,17},{2,34}... | collective-permute-start | bytes 208904 | tf_op jit(solution)/shard_map/ppermute | solution.py:235
  126.4 4.0 %collective-permute-start.21 = (f32[136,128]{1,0:T(8,128)S(1)}, f32[136,128]{1,0:T(8,128)S(1)}, u32[]{:S(2)}, u32[]{:S(2)}) collective-permute-start(f32[136,128]{1,0:T(8,128)S(1)} %add_add_fusion.own), channel_id=1, source_target_pairs={{0,192},{64,0},{128,64},{192,128},{1,193},{65,1},{129,65},{193,129... | collective-permute-start | bytes 208904 | tf_op jit(solution)/shard_map/ppermute | solution.py:235
  129.0 5.1 %collective-permute-start.20 = (f32[136,128]{1,0:T(8,128)S(1)}, f32[136,128]{1,0:T(8,128)S(1)}, u32[]{:S(2)}, u32[]{:S(2)}) collective-permute-start(f32[136,128]{1,0:T(8,128)S(1)} %add_add_fusion.own), channel_id=1, source_target_pairs={{0,64},{64,128},{128,192},{192,0},{1,65},{65,129},{129,193},{193,1... | collective-permute-start | bytes 208904 | tf_op jit(solution)/shard_map/ppermute | solution.py:235
  129.0 5.1 %collective-permute-start.19 = (f32[136,128]{1,0:T(8,128)S(1)}, f32[136,128]{1,0:T(8,128)S(1)}, u32[]{:S(2)}, u32[]{:S(2)}) collective-permute-start(f32[136,128]{1,0:T(8,128)S(1)} %add_add_fusion.own), channel_id=1, source_target_pairs={{0,128},{64,192},{128,0},{192,64},{1,129},{65,193},{129,1},{193,65... | collective-permute-start | bytes 208904 | tf_op jit(solution)/shard_map/ppermute | solution.py:235
  (11 other events, 11.8 us)

commit v3 on v2

--- a/solution.py
+++ b/solution.py
@@ -17,24 +17,29 @@
 NROWS = float(N * ROW_BLOCKS * TILE)
 NCOLS = float(N * COL_BLOCKS * TILE)
 UNROLL = 8
+PACK_VMEM = 60 * 2**20
+FIRST_VMEM = 48 * 2**20
+CHUNKS = 8
+CHUNK = SLOTS // CHUNKS
 F32, BF16 = jnp.float32, jnp.bfloat16
 
 SLOT_ROWS, SLOT_COLS, COUNT, AT_Y, AT_X, AT_Z, AT_CORE = range(7)
 
 VMEM = pl.BlockSpec(memory_space=pltpu.VMEM)
 SMEM = pl.BlockSpec(memory_space=pltpu.SMEM)
-
-
-def call(kernel, name, out_shapes, args, smem=0, smem_out=False, scratch=()):
+HBM = pl.BlockSpec(memory_space=pltpu.HBM)
+
+
+def call(kernel, name, out_shapes, args, smem=0, hbm=0, smem_out=False, scratch=(), vmem=8 * 2**20):
     shapes = tuple(jax.ShapeDtypeStruct(s, d) for s, d in out_shapes)
     return pl.pallas_call(
         kernel,
         name=name,
         out_shape=shapes,
-        in_specs=[SMEM] * smem + [VMEM] * (len(args) - smem),
+        in_specs=[SMEM] * smem + [HBM] * hbm + [VMEM] * (len(args) - smem - hbm),
         out_specs=tuple([SMEM if smem_out else VMEM] * len(shapes)),
         scratch_shapes=list(scratch),
-        compiler_params=pltpu.CompilerParams(vmem_limit_bytes=8 * 2**20),
+        compiler_params=pltpu.CompilerParams(vmem_limit_bytes=vmem),
     )(*args)
 
 
@@ -46,7 +51,10 @@
 
 def adjoint_product(table, tile_pair, dual_ref, total):
     total[...] = jnp.zeros_like(total)
-
+    adjoint_slots(table, tile_pair, dual_ref, total, 0, SLOTS)
+
+
+def adjoint_slots(table, tile_pair, dual_ref, total, first, slots):
     def body(slot, carry):
         lhs = jnp.concatenate(split(dual_ref[pl.ds(table[SLOT_ROWS, slot], 1), :], 8), 0).astype(BF16)
         lhs = jnp.concatenate([lhs, lhs], 1)
@@ -54,7 +62,7 @@
         total[table[SLOT_COLS, slot]] += product[0:8] + product[8:16]
         return carry
 
-    lax.fori_loop(0, SLOTS, body, 0, unroll=UNROLL)
+    lax.fori_loop(first, first + slots, body, 0, unroll=UNROLL)
 
 
 def forward_product(table, tile_pair, primal_refs, total):
@@ -96,39 +104,95 @@
     return (own + opposite) + (right + left)
 
 
-def pack(place, count, rows, cols, kinds, rhs, start, table, row_side):
+def pack(
+    count, rows, cols, row_kinds, rhs, dual, col_kinds, cost, primal,
+    table, row_side, column_side, places, side, kinds, done,
+):
+    copies = [
+        pltpu.make_async_copy(source, target, done.at[k])
+        for k, (source, target) in enumerate(
+            (
+                (rows.at[0], places.at[0:1]),
+                (cols.at[0], places.at[1:2]),
+                (dual.at[0], side.at[0]),
+                (rhs.at[0], side.at[1]),
+                (row_kinds.at[0], kinds.at[0:ROWS_SHARE]),
+                (primal.at[0], column_side.at[0:COLS_SHARE]),
+                (cost.at[0], column_side.at[COLS_SHARE : 2 * COLS_SHARE]),
+                (col_kinds.at[0], kinds.at[COLS_SHARE : 2 * COLS_SHARE]),
+            )
+        )
+    ]
+    for copy in copies:
+        copy.start()
     table[...] = jnp.zeros_like(table)
-    table[SLOT_ROWS : SLOT_ROWS + 1, 0:SLOTS] = rows[...]
-    table[SLOT_COLS : SLOT_COLS + 1, 0:SLOTS] = cols[...]
-    table[COUNT : COUNT + 1, :] = jnp.full((1, TILE), count[0], jnp.int32)
-    for k in range(4):
-        table[AT_Y + k : AT_Y + k + 1, :] = jnp.full((1, TILE), place[k], jnp.int32)
-    side = jnp.concatenate(
-        [start[...], rhs[...], kinds[...].astype(F32), jnp.zeros((ROWS_SHARE, TILE), F32)], 0
-    )
-    row_side[...] = jnp.broadcast_to(side[None], row_side.shape)
+    table[COUNT : COUNT + 1, :] = jnp.full((1, TILE), count[0, 0], jnp.int32)
+    for k, axis in ((AT_Y, "y"), (AT_X, "x"), (AT_Z, "z"), (AT_CORE, "core")):
+        table[k : k + 1, :] = jnp.full((1, TILE), lax.axis_index(axis), jnp.int32)
+    for copy in copies:
+        copy.wait()
+    table[SLOT_ROWS : SLOT_ROWS + 1, 0:SLOTS] = places[0:1, :]
+    table[SLOT_COLS : SLOT_COLS + 1, 0:SLOTS] = places[1:2, :]
+    packed = jnp.concatenate(
+        [
+            side[0],
+            side[1],
+            kinds[0:ROWS_SHARE, :].astype(F32),
+            jnp.zeros((ROWS_SHARE, TILE), F32),
+        ],
+        0,
+    )
+    column_side[2 * COLS_SHARE :, :] = kinds[COLS_SHARE:, :].astype(F32)
+    row_side[...] = jnp.broadcast_to(packed[None], row_side.shape)
+
+
+def x_sums(own, opposite, right, left, payload):
+    four = (own, opposite, right, left)
+    payload[0:COL_BLOCKS, :] = sum_four(four, slice(0, COL_BLOCKS))
+    share = 3 * COLS_SHARE
+    for k, ref in enumerate(four):
+        first = COL_BLOCKS + k * share
+        payload[first : first + share, :] = ref[COL_BLOCKS : COL_BLOCKS + share, :]
+
+
+def sums(own, opposite, right, left, total):
+    total[...] = sum_four((own, opposite, right, left), slice(None))
+
+
+def add_copies(kept, received, copies):
+    copies[...] = jnp.broadcast_to((kept[...] + received[...])[None], copies.shape)
+
+
+def sum_copies(pieces, total):
+    total[...] = jnp.sum(pieces[...], 0)
 
 
 def first_adjoint(
-    table, row_side, start, cost, kinds, tiles, payload, dual, rhs, ineq, pairs, total
-):
+    table, tiles, row_side, column_side, payload, dual, rhs, ineq, pairs, chunks, done, total
+):
+    copies = []
+    for k in range(CHUNKS):
+        part = pl.ds(k * CHUNK, CHUNK)
+        copies.append(pltpu.make_async_copy(tiles.at[part], chunks.at[part], done.at[k]))
+        copies[k].start()
     for k in range(N):
         block = slice(k * ROWS_SHARE, (k + 1) * ROWS_SHARE)
         for j, ref in enumerate((dual, rhs, ineq)):
             ref[block, :] = row_side[k, j * ROWS_SHARE : (j + 1) * ROWS_SHARE, :]
 
     def tile_pair(slot):
-        tile = jnp.where(slot < table[COUNT, 0], tiles[slot], 0.0)
+        tile = jnp.where(slot < table[COUNT, 0], chunks[slot], 0.0)
         lead = tile.astype(BF16)
         pair = jnp.concatenate([lead, (tile - lead.astype(F32)).astype(BF16)], 0)
         pairs[slot] = pair
         return pair
 
-    adjoint_product(table, tile_pair, dual, total)
+    total[...] = jnp.zeros_like(total)
+    for k in range(CHUNKS):
+        copies[k].wait()
+        adjoint_slots(table, tile_pair, dual, total, k * CHUNK, CHUNK)
     payload[0:COL_BLOCKS, :] = total[:, 0, :]
-    payload[COL_BLOCKS:, :] = jnp.concatenate(
-        [start[...], cost[...], kinds[...].astype(F32)], 0
-    )
+    payload[COL_BLOCKS:, :] = column_side[...]
 
 
 def first_forward(
@@ -240,8 +304,8 @@
 
 
 def four_over_row(values):
-    own, opposite, right, left = four_of(values, "x")
-    return four_of((own + opposite) + (right + left), "y")
+    total = call(sums, "sums", [(values.shape, F32)], four_of(values, "x"))
+    return four_of(total[0], "y")
 
 
 def swap_cores(values):
@@ -252,34 +316,38 @@
     return lax.all_to_all(copies, axes, 0, 0)
 
 
-def sum_over_z(values):
-    copies = jnp.broadcast_to(values[None], (8,) + values.shape)
-    return jnp.sum(exchange(copies, "z"), 0)
+def sum_over_col(kept, given):
+    copies = call(add_copies, "add_copies", [((8,) + kept.shape, F32)], (kept, swap_cores(given)))
+    total = call(sum_copies, "sum_copies", [(kept.shape, F32)], (exchange(copies[0], "z"),))
+    return total[0]
 
 
 def shards(
     tiles, tile_rows, tile_cols, tile_count, row_types, var_types, rhs, cost, primal_start, dual_start
 ):
     tiles = tiles.reshape(SLOTS, TILE, TILE)
-    place = jnp.stack([lax.axis_index(a) for a in ("y", "x", "z", "core")]).astype(jnp.int32)
     blocks, columns, half = (ROW_BLOCKS, TILE), (COL_BLOCKS, TILE), (HALF, TILE)
     row_total = [pltpu.VMEM((ROW_BLOCKS, 8, TILE), F32)]
     col_total = [pltpu.VMEM((COL_BLOCKS, 8, TILE), F32)]
 
-    table, row_side = call(
+    table, row_side, column_side = call(
         pack,
         "pack",
-        [((8, TILE), jnp.int32), ((N, 4 * ROWS_SHARE, TILE), F32)],
-        (
-            place,
-            tile_count.reshape(1),
-            tile_rows.reshape(1, SLOTS),
-            tile_cols.reshape(1, SLOTS),
-            row_types[0],
-            rhs[0],
-            dual_start[0],
-        ),
-        smem=2,
+        [
+            ((8, TILE), jnp.int32),
+            ((N, 4 * ROWS_SHARE, TILE), F32),
+            ((3 * COLS_SHARE, TILE), F32),
+        ],
+        (tile_count, tile_rows, tile_cols, row_types, rhs, dual_start, var_types, cost, primal_start),
+        smem=1,
+        hbm=8,
+        scratch=[
+            pltpu.VMEM((2, SLOTS), jnp.int32),
+            pltpu.VMEM((2, ROWS_SHARE, TILE), F32),
+            pltpu.VMEM((2 * COLS_SHARE, TILE), jnp.int32),
+            pltpu.SemaphoreType.DMA((8,)),
+        ],
+        vmem=PACK_VMEM,
     )
     row_side = exchange(row_side, ("z", "core"))
 
@@ -289,14 +357,15 @@
         [((COL_BLOCKS + 3 * COLS_SHARE, TILE), F32)]
         + [(blocks, F32)] * 3
         + [((SLOTS, 2 * TILE, TILE), BF16)],
-        (table, row_side, primal_start[0], cost[0], var_types[0], tiles),
-        smem=1,
-        scratch=col_total,
+        (table, tiles, row_side, column_side),
+        smem=1,
+        hbm=1,
+        scratch=[pltpu.VMEM((SLOTS, TILE, TILE), F32), pltpu.SemaphoreType.DMA((CHUNKS,))] + col_total,
+        vmem=FIRST_VMEM,
     )
     four = four_of(payload, "x")
-    gradient = (four[0] + four[1]) + (four[2] + four[3])
-    payload = jnp.concatenate([gradient[:COL_BLOCKS]] + [p[COL_BLOCKS:] for p in four], 0)
-    four = four_of(payload, "y")
+    payload = call(x_sums, "x_sums", [((COL_BLOCKS + 12 * COLS_SHARE, TILE), F32)], four)
+    four = four_of(payload[0], "y")
 
     kept, given, primal1, start_full, cost_full, free = call(
         first_forward,
@@ -306,7 +375,7 @@
         smem=1,
         scratch=[pltpu.VMEM(columns, F32)] + row_total,
     )
-    held = sum_over_z(kept + swap_cores(given))
+    held = sum_over_col(kept, given)
 
     gradient, dual1 = call(
         second_adjoint,
@@ -325,7 +394,7 @@
         smem=1,
         scratch=[pltpu.VMEM(columns, F32)] + row_total,
     )
-    held = sum_over_z(kept + swap_cores(given))
+    held = sum_over_col(kept, given)
 
     payload, dual_mine = call(
         third_adjoint,

time: 148 us -> 137 us (0.926)
  local copies, waits for them, and re-layouts: 14 us -> 1.39 us
  Pallas kernels: 15 us -> 17.1 us
    unnamed x29 -> x4, local copies, waits for them, and re-layouts: 14 us -> 1.39 us
    pallas_call x8 -> x15, Pallas kernels: 15 us -> 17.1 us  [call(): pl.pallas_call(kernel, name=name, out_shape=shapes, in_specs=[SMEM] * sme...]
where the time goes in v3:
time: 137 us
  blocking collectives  57.2 us (42%)
  waiting for transfers between devices  30.9 us (23%)
  starting transfers between devices  28.7 us (21%)
  Pallas kernels  17.1 us (12%)
  between operations  1.52 us (1%)
  local copies, waits for them, and re-layouts  1.39 us (1%)
    all_to_all x4, blocking collectives, exchange(): return lax.all_to_all(copies, axes, 0, 0)  57.2 us
    ppermute x18, waiting for transfers between devices, shift(): return lax.ppermute(values, axis, [(k, (k + step) % 4) for k in range(4)])  27.6 us
    ppermute x18, starting transfers between devices, shift(): return lax.ppermute(values, axis, [(k, (k + step) % 4) for k in range(4)])  21.3 us
    pallas_call x15, Pallas kernels, call(): pl.pallas_call(kernel, name=name, out_shape=shapes, in_specs=[SMEM] * sme...  17.1 us
    ppermute x4, starting transfers between devices, swap_cores(): return lax.ppermute(values, 'core', [(0, 1), (1, 0)])  7.45 us
    ppermute x4, waiting for transfers between devices, swap_cores(): return lax.ppermute(values, 'core', [(0, 1), (1, 0)])  3.4 us
  transfers between devices with their start and end apart: 22, of which 17 were waited for; matrix products, arithmetic and copies ran while one was open for 0% of the time, Pallas kernels for 0%

profile of v3, /device:TPU:1, one launch (start us, length us, event | category | flops | bytes accessed | tf_op | source)
XLA Modules:
  0.0 136.9 jit_solution(7857268418787769384)
XLA Ops:
  2.8 19.2 %all_to_all.20.row_side = f32[16,16,128]{2,1,0:T(8,128)S(1)} all-to-all(f32[16,16,128]{2,1,0:T(8,128)} %get-tuple-element.33), channel_id=1, replica_groups=mesh['y'=4,'x'=4,'z'=8,'core'=2] {'z','core'}, dimensions={0} | all-to-all | bytes 262144 | tf_op jit(solution)/shard_map/all_to_all | solution.py:316
  23.4 3.4 %first_adjoint.1 = (f32[152,128]{1,0:T(8,128)S(1)}, f32[64,128]{1,0:T(8,128)S(1)}, f32[64,128]{1,0:T(8,128)S(1)}, f32[64,128]{1,0:T(8,128)S(1)}, bf16[64,256,128]{2,1,0:T(8,128)(2,1)S(1)}) custom-call(s32[8,128]{1,0:T(8,128)S(1)} %copy-done, f32[64,128,128]{2,1,0:T(8,128)} %bitcast.3, f32[16,16,128]{2,1,0:T(8,128)S(1)} %all_to_all.20.row_side, ...), custom_call_target="tpu_custom_call" | custom-call | tf_op jit(solution)/shard_map/first_adjoint/pallas_call | solution.py:35
  26.8 2.6 %collective-permute-start.2 = (f32[152,128]{1,0:T(8,128)S(1)}, f32[152,128]{1,0:T(8,128)S(1)}, u32[]{:S(2)}, u32[]{:S(2)}) collective-permute-start(f32[152,128]{1,0:T(8,128)S(1)} %get-tuple-element.35.own), channel_id=1, source_target_pairs={{0,48},{16,0},{32,16},{48,32},{1,49},{17,1},{33,17},{49,33},{2,50}... | collective-permute-start | bytes 233480 | tf_op jit(solution)/shard_map/ppermute | solution.py:299
  29.4 1.7 %collective-permute-start = (f32[152,128]{1,0:T(8,128)S(1)}, f32[152,128]{1,0:T(8,128)S(1)}, u32[]{:S(2)}, u32[]{:S(2)}) collective-permute-start(f32[152,128]{1,0:T(8,128)S(1)} %get-tuple-element.35.own), channel_id=1, source_target_pairs={{0,32},{16,48},{32,0},{48,16},{1,33},{17,49},{33,1},{49,17},{2,34}... | collective-permute-start | bytes 233480 | tf_op jit(solution)/shard_map/ppermute | solution.py:299
  31.4 4.9 %collective-permute-done.1.right = f32[152,128]{1,0:T(8,128)S(1)} collective-permute-done((f32[152,128]{1,0:T(8,128)S(1)}, f32[152,128]{1,0:T(8,128)S(1)}, u32[]{:S(2)}, u32[]{:S(2)}) %collective-permute-start.1) | collective-permute-done | bytes 77856 | tf_op jit(solution)/shard_map/ppermute | solution.py:299
  36.3 2.8 %collective-permute-start.5 = (f32[224,128]{1,0:T(8,128)S(1)}, f32[224,128]{1,0:T(8,128)S(1)}, u32[]{:S(2)}, u32[]{:S(2)}) collective-permute-start(f32[224,128]{1,0:T(8,128)S(1)} %x_sums.1.own), channel_id=1, source_target_pairs={{0,192},{64,0},{128,64},{192,128},{1,193},{65,1},{129,65},{193,129... | collective-permute-start | bytes 344072 | tf_op jit(solution)/shard_map/ppermute | solution.py:299
  40.9 5.4 %collective-permute-done.4.right = f32[224,128]{1,0:T(8,128)S(1)} collective-permute-done((f32[224,128]{1,0:T(8,128)S(1)}, f32[224,128]{1,0:T(8,128)S(1)}, u32[]{:S(2)}, u32[]{:S(2)}) %collective-permute-start.4) | collective-permute-done | bytes 114720 | tf_op jit(solution)/shard_map/ppermute | solution.py:299
  46.3 3.2 %first_forward.1 = (f32[32,128]{1,0:T(8,128)S(1)}, f32[32,128]{1,0:T(8,128)S(1)}, f32[128,128]{1,0:T(8,128)S(1)}, f32[128,128]{1,0:T(8,128)}, f32[128,128]{1,0:T(8,128)S(1)}, /*index=5*/f32[128,128]{1,0:T(8,128)S(1)}) custom-call(s32[8,128]{1,0:T(8,128)S(1)} %copy-done, f32[224,128]{1,0:T(8,128)S(1)} %x_sums.1.own, ...), custom_call_target="tpu_custom_call" | custom-call | tf_op jit(solution)/shard_map/first_forward/pallas_call | solution.py:35
  49.5 2.1 %collective-permute-start.6 = (f32[32,128]{1,0:T(8,128)S(1)}, f32[32,128]{1,0:T(8,128)S(1)}, u32[]{:S(2)}, u32[]{:S(2)}) collective-permute-start(f32[32,128]{1,0:T(8,128)S(1)} %get-tuple-element.38), channel_id=1, source_target_pairs={{0,1},{1,0},{2,3},{3,2},{4,5},{5,4},{6,7},{7,6},{8,9},{9,8},{10,11... | collective-permute-start | bytes 49160 | tf_op jit(solution)/shard_map/ppermute | solution.py:312
  52.4 10.8 %all_to_all.21.pieces = f32[8,32,128]{2,1,0:T(8,128)S(1)} all-to-all(f32[8,32,128]{2,1,0:T(8,128)S(1)} %add_copies.2), channel_id=1, replica_groups=mesh['y'=4,'x'=4,'z'=8,'core'=2] {'z'}, dimensions={0} | all-to-all | bytes 262144 | tf_op jit(solution)/shard_map/all_to_all | solution.py:316
  63.2 1.7 %collective-permute-start.7 = (f32[32,128]{1,0:T(8,128)S(1)}, f32[32,128]{1,0:T(8,128)S(1)}, u32[]{:S(2)}, u32[]{:S(2)}) collective-permute-start(f32[32,128]{1,0:T(8,128)S(1)} %sum_copies.2.half), channel_id=1, source_target_pairs={{0,1},{1,0},{2,3},{3,2},{4,5},{5,4},{6,7},{7,6},{8,9},{9,8},{10,11... | collective-permute-start | bytes 49160 | tf_op jit(solution)/shard_map/ppermute | solution.py:312
  65.7 2.2 %second_adjoint.1 = (f32[128,128]{1,0:T(8,128)S(1)}, f32[64,128]{1,0:T(8,128)S(1)}) custom-call(s32[8,128]{1,0:T(8,128)S(1)} %copy-done, f32[32,128]{1,0:T(8,128)S(1)} %sum_copies.2.half, f32[32,128]{1,0:T(8,128)S(1)} %collective-permute-done.7.other, f32[64,128]{1,0:T(8,128)S(1)} %get-tuple-element.39.start, f32[64,128]{1,0:T(8,128)S(1)} %get-tuple-element.40.rhs, ...), custom_call_target="tpu_custom_call" | custom-call | tf_op jit(solution)/shard_map/second_adjoint/pallas_call | solution.py:35
  71.1 2.2 %collective-permute-done.9.right = f32[128,128]{1,0:T(8,128)S(1)} collective-permute-done((f32[128,128]{1,0:T(8,128)S(1)}, f32[128,128]{1,0:T(8,128)S(1)}, u32[]{:S(2)}, u32[]{:S(2)}) %collective-permute-start.9) | collective-permute-done | bytes 65568 | tf_op jit(solution)/shard_map/ppermute | solution.py:299
  74.2 1.7 %collective-permute-start.13 = (f32[128,128]{1,0:T(8,128)S(1)}, f32[128,128]{1,0:T(8,128)S(1)}, u32[]{:S(2)}, u32[]{:S(2)}) collective-permute-start(f32[128,128]{1,0:T(8,128)S(1)} %sums.2.own), channel_id=1, source_target_pairs={{0,192},{64,0},{128,64},{192,128},{1,193},{65,1},{129,65},{193,129... | collective-permute-start | bytes 196616 | tf_op jit(solution)/shard_map/ppermute | solution.py:299
  77.4 3.6 %collective-permute-done.12.right = f32[128,128]{1,0:T(8,128)S(1)} collective-permute-done((f32[128,128]{1,0:T(8,128)S(1)}, f32[128,128]{1,0:T(8,128)S(1)}, u32[]{:S(2)}, u32[]{:S(2)}) %collective-permute-start.12) | collective-permute-done | bytes 65568 | tf_op jit(solution)/shard_map/ppermute | solution.py:299
  80.9 3.2 %second_forward.1 = (f32[64,128]{1,0:T(8,128)S(1)}, f32[64,128]{1,0:T(8,128)S(1)}, f32[128,128]{1,0:T(8,128)S(1)}, f32[128,128]{1,0:T(8,128)S(1)}, f32[8,128]{1,0:T(8,128)}) custom-call(s32[8,128]{1,0:T(8,128)S(1)} %copy-done, f32[128,128]{1,0:T(8,128)S(1)} %sums.2.own, f32[128,128]{1,0:T(8,128)S(1)} %collective-permute-done.11.opposite, ...), custom_call_target="tpu_custom_call" | custom-call | tf_op jit(solution)/shard_map/second_forward/pallas_call | solution.py:35
  84.2 3.2 %collective-permute-start.14 = (f32[64,128]{1,0:T(8,128)S(1)}, f32[64,128]{1,0:T(8,128)S(1)}, u32[]{:S(2)}, u32[]{:S(2)}) collective-permute-start(f32[64,128]{1,0:T(8,128)S(1)} %get-tuple-element.48), channel_id=1, source_target_pairs={{0,1},{1,0},{2,3},{3,2},{4,5},{5,4},{6,7},{7,6},{8,9},{9,8},{10,11... | collective-permute-start | bytes 98312 | tf_op jit(solution)/shard_map/ppermute | solution.py:312
  88.2 14.8 %all_to_all.22.pieces = f32[8,64,128]{2,1,0:T(8,128)S(1)} all-to-all(f32[8,64,128]{2,1,0:T(8,128)S(1)} %add_copies.3), channel_id=1, replica_groups=mesh['y'=4,'x'=4,'z'=8,'core'=2] {'z'}, dimensions={0} | all-to-all | bytes 524288 | tf_op jit(solution)/shard_map/all_to_all | solution.py:316
  104.4 2.7 %third_adjoint.1 = (f32[136,128]{1,0:T(8,128)S(1)}, f32[4,128]{1,0:T(4,128)}) custom-call(s32[8,128]{1,0:T(8,128)S(1)} %copy-done, f32[64,128]{1,0:T(8,128)S(1)} %sum_copies.3.held, f32[64,128]{1,0:T(8,128)S(1)} %collective-permute-done.15.other, f32[64,128]{1,0:T(8,128)S(1)} %get-tuple-element.49.before, f32[64,128]{1,0:T(8,128)S(1)} %get-tuple-element.40.rhs, ...), custom_call_target="tpu_custom_call" | custom-call | tf_op jit(solution)/shard_map/third_adjoint/pallas_call | solution.py:35
  107.1 2.1 %collective-permute-start.18 = (f32[136,128]{1,0:T(8,128)S(1)}, f32[136,128]{1,0:T(8,128)S(1)}, u32[]{:S(2)}, u32[]{:S(2)}) collective-permute-start(f32[136,128]{1,0:T(8,128)S(1)} %get-tuple-element.51.own), channel_id=1, source_target_pairs={{0,48},{16,0},{32,16},{48,32},{1,49},{17,1},{33,17},{49,33},{2,50}... | collective-permute-start | bytes 208904 | tf_op jit(solution)/shard_map/ppermute | solution.py:299
  110.6 5.1 %collective-permute-done.17.right = f32[136,128]{1,0:T(8,128)S(1)} collective-permute-done((f32[136,128]{1,0:T(8,128)S(1)}, f32[136,128]{1,0:T(8,128)S(1)}, u32[]{:S(2)}, u32[]{:S(2)}) %collective-permute-start.17) | collective-permute-done | bytes 69664 | tf_op jit(solution)/shard_map/ppermute | solution.py:299
  115.8 2.6 %collective-permute-start.21 = (f32[136,128]{1,0:T(8,128)S(1)}, f32[136,128]{1,0:T(8,128)S(1)}, u32[]{:S(2)}, u32[]{:S(2)}) collective-permute-start(f32[136,128]{1,0:T(8,128)S(1)} %sums.3.own), channel_id=1, source_target_pairs={{0,192},{64,0},{128,64},{192,128},{1,193},{65,1},{129,65},{193,129... | collective-permute-start | bytes 208904 | tf_op jit(solution)/shard_map/ppermute | solution.py:299
  119.8 3.7 %collective-permute-done.20.right = f32[136,128]{1,0:T(8,128)S(1)} collective-permute-done((f32[136,128]{1,0:T(8,128)S(1)}, f32[136,128]{1,0:T(8,128)S(1)}, u32[]{:S(2)}, u32[]{:S(2)}) %collective-permute-start.20) | collective-permute-done | bytes 69664 | tf_op jit(solution)/shard_map/ppermute | solution.py:299
  123.6 12.5 %all_to_all.23.gathered = f32[16,8,128]{2,1,0:T(8,128)S(1)} all-to-all(f32[16,8,128]{2,1,0:T(8,128)S(1)} %get-tuple-element.54), channel_id=1, replica_groups=mesh['y'=4,'x'=4,'z'=8,'core'=2] {'z','core'}, dimensions={0} | all-to-all | bytes 131072 | tf_op jit(solution)/shard_map/all_to_all | solution.py:316
  (43 shorter events, 18.1 us)
Async XLA Ops:
  22.0 0.7 copy-start
  22.7 0.7 copy-start.1
  26.8 4.6 %collective-permute-start.2 = (f32[152,128]{1,0:T(8,128)S(1)}, f32[152,128]{1,0:T(8,128)S(1)}, u32[]{:S(2)}, u32[]{:S(2)}) collective-permute-start(f32[152,128]{1,0:T(8,128)S(1)} %get-tuple-element.35.own), channel_id=1, source_target_pairs={{0,48},{16,0},{32,16},{48,32},{1,49},{17,1},{33,17},{49,33},{2,50}... | collective-permute-start | bytes 233480 | tf_op jit(solution)/shard_map/ppermute | solution.py:299
  29.4 6.9 %collective-permute-start.1 = (f32[152,128]{1,0:T(8,128)S(1)}, f32[152,128]{1,0:T(8,128)S(1)}, u32[]{:S(2)}, u32[]{:S(2)}) collective-permute-start(f32[152,128]{1,0:T(8,128)S(1)} %get-tuple-element.35.own), channel_id=1, source_target_pairs={{0,16},{16,32},{32,48},{48,0},{1,17},{17,33},{33,49},{49,1},{2,18}... | collective-permute-start | bytes 233480 | tf_op jit(solution)/shard_map/ppermute | solution.py:299
  29.4 6.9 %collective-permute-start = (f32[152,128]{1,0:T(8,128)S(1)}, f32[152,128]{1,0:T(8,128)S(1)}, u32[]{:S(2)}, u32[]{:S(2)}) collective-permute-start(f32[152,128]{1,0:T(8,128)S(1)} %get-tuple-element.35.own), channel_id=1, source_target_pairs={{0,32},{16,48},{32,0},{48,16},{1,33},{17,49},{33,1},{49,17},{2,34}... | collective-permute-start | bytes 233480 | tf_op jit(solution)/shard_map/ppermute | solution.py:299
  36.3 4.6 %collective-permute-start.5 = (f32[224,128]{1,0:T(8,128)S(1)}, f32[224,128]{1,0:T(8,128)S(1)}, u32[]{:S(2)}, u32[]{:S(2)}) collective-permute-start(f32[224,128]{1,0:T(8,128)S(1)} %x_sums.1.own), channel_id=1, source_target_pairs={{0,192},{64,0},{128,64},{192,128},{1,193},{65,1},{129,65},{193,129... | collective-permute-start | bytes 344072 | tf_op jit(solution)/shard_map/ppermute | solution.py:299
  39.1 7.2 %collective-permute-start.4 = (f32[224,128]{1,0:T(8,128)S(1)}, f32[224,128]{1,0:T(8,128)S(1)}, u32[]{:S(2)}, u32[]{:S(2)}) collective-permute-start(f32[224,128]{1,0:T(8,128)S(1)} %x_sums.1.own), channel_id=1, source_target_pairs={{0,64},{64,128},{128,192},{192,0},{1,65},{65,129},{129,193},{193,1... | collective-permute-start | bytes 344072 | tf_op jit(solution)/shard_map/ppermute | solution.py:299
  39.2 7.2 %collective-permute-start.3 = (f32[224,128]{1,0:T(8,128)S(1)}, f32[224,128]{1,0:T(8,128)S(1)}, u32[]{:S(2)}, u32[]{:S(2)}) collective-permute-start(f32[224,128]{1,0:T(8,128)S(1)} %x_sums.1.own), channel_id=1, source_target_pairs={{0,128},{64,192},{128,0},{192,64},{1,129},{65,193},{129,1},{193,65... | collective-permute-start | bytes 344072 | tf_op jit(solution)/shard_map/ppermute | solution.py:299
  49.5 2.9 %collective-permute-start.6 = (f32[32,128]{1,0:T(8,128)S(1)}, f32[32,128]{1,0:T(8,128)S(1)}, u32[]{:S(2)}, u32[]{:S(2)}) collective-permute-start(f32[32,128]{1,0:T(8,128)S(1)} %get-tuple-element.38), channel_id=1, source_target_pairs={{0,1},{1,0},{2,3},{3,2},{4,5},{5,4},{6,7},{7,6},{8,9},{9,8},{10,11... | collective-permute-start | bytes 49160 | tf_op jit(solution)/shard_map/ppermute | solution.py:312
  63.2 2.5 %collective-permute-start.7 = (f32[32,128]{1,0:T(8,128)S(1)}, f32[32,128]{1,0:T(8,128)S(1)}, u32[]{:S(2)}, u32[]{:S(2)}) collective-permute-start(f32[32,128]{1,0:T(8,128)S(1)} %sum_copies.2.half), channel_id=1, source_target_pairs={{0,1},{1,0},{2,3},{3,2},{4,5},{5,4},{6,7},{7,6},{8,9},{9,8},{10,11... | collective-permute-start | bytes 49160 | tf_op jit(solution)/shard_map/ppermute | solution.py:312
  67.9 3.2 %collective-permute-start.10 = (f32[128,128]{1,0:T(8,128)S(1)}, f32[128,128]{1,0:T(8,128)S(1)}, u32[]{:S(2)}, u32[]{:S(2)}) collective-permute-start(f32[128,128]{1,0:T(8,128)S(1)} %get-tuple-element.42.own), channel_id=1, source_target_pairs={{0,48},{16,0},{32,16},{48,32},{1,49},{17,1},{33,17},{49,33},{2,50}... | collective-permute-start | bytes 196616 | tf_op jit(solution)/shard_map/ppermute | solution.py:299
  69.0 4.3 %collective-permute-start.9 = (f32[128,128]{1,0:T(8,128)S(1)}, f32[128,128]{1,0:T(8,128)S(1)}, u32[]{:S(2)}, u32[]{:S(2)}) collective-permute-start(f32[128,128]{1,0:T(8,128)S(1)} %get-tuple-element.42.own), channel_id=1, source_target_pairs={{0,16},{16,32},{32,48},{48,0},{1,17},{17,33},{33,49},{49,1},{2,18}... | collective-permute-start | bytes 196616 | tf_op jit(solution)/shard_map/ppermute | solution.py:299
  69.5 4.7 %collective-permute-start.8 = (f32[128,128]{1,0:T(8,128)S(1)}, f32[128,128]{1,0:T(8,128)S(1)}, u32[]{:S(2)}, u32[]{:S(2)}) collective-permute-start(f32[128,128]{1,0:T(8,128)S(1)} %get-tuple-element.42.own), channel_id=1, source_target_pairs={{0,32},{16,48},{32,0},{48,16},{1,33},{17,49},{33,1},{49,17},{2,34}... | collective-permute-start | bytes 196616 | tf_op jit(solution)/shard_map/ppermute | solution.py:299
  74.2 3.2 %collective-permute-start.13 = (f32[128,128]{1,0:T(8,128)S(1)}, f32[128,128]{1,0:T(8,128)S(1)}, u32[]{:S(2)}, u32[]{:S(2)}) collective-permute-start(f32[128,128]{1,0:T(8,128)S(1)} %sums.2.own), channel_id=1, source_target_pairs={{0,192},{64,0},{128,64},{192,128},{1,193},{65,1},{129,65},{193,129... | collective-permute-start | bytes 196616 | tf_op jit(solution)/shard_map/ppermute | solution.py:299
  75.9 5.0 %collective-permute-start.12 = (f32[128,128]{1,0:T(8,128)S(1)}, f32[128,128]{1,0:T(8,128)S(1)}, u32[]{:S(2)}, u32[]{:S(2)}) collective-permute-start(f32[128,128]{1,0:T(8,128)S(1)} %sums.2.own), channel_id=1, source_target_pairs={{0,64},{64,128},{128,192},{192,0},{1,65},{65,129},{129,193},{193,1... | collective-permute-start | bytes 196616 | tf_op jit(solution)/shard_map/ppermute | solution.py:299
  75.9 5.0 %collective-permute-start.11 = (f32[128,128]{1,0:T(8,128)S(1)}, f32[128,128]{1,0:T(8,128)S(1)}, u32[]{:S(2)}, u32[]{:S(2)}) collective-permute-start(f32[128,128]{1,0:T(8,128)S(1)} %sums.2.own), channel_id=1, source_target_pairs={{0,128},{64,192},{128,0},{192,64},{1,129},{65,193},{129,1},{193,65... | collective-permute-start | bytes 196616 | tf_op jit(solution)/shard_map/ppermute | solution.py:299
  84.2 4.0 %collective-permute-start.14 = (f32[64,128]{1,0:T(8,128)S(1)}, f32[64,128]{1,0:T(8,128)S(1)}, u32[]{:S(2)}, u32[]{:S(2)}) collective-permute-start(f32[64,128]{1,0:T(8,128)S(1)} %get-tuple-element.48), channel_id=1, source_target_pairs={{0,1},{1,0},{2,3},{3,2},{4,5},{5,4},{6,7},{7,6},{8,9},{9,8},{10,11... | collective-permute-start | bytes 98312 | tf_op jit(solution)/shard_map/ppermute | solution.py:312
  103.0 1.4 %collective-permute-start.15 = (f32[64,128]{1,0:T(8,128)S(1)}, f32[64,128]{1,0:T(8,128)S(1)}, u32[]{:S(2)}, u32[]{:S(2)}) collective-permute-start(f32[64,128]{1,0:T(8,128)S(1)} %sum_copies.3.held), channel_id=1, source_target_pairs={{0,1},{1,0},{2,3},{3,2},{4,5},{5,4},{6,7},{7,6},{8,9},{9,8},{10,11... | collective-permute-start | bytes 98312 | tf_op jit(solution)/shard_map/ppermute | solution.py:312
  107.1 3.5 %collective-permute-start.18 = (f32[136,128]{1,0:T(8,128)S(1)}, f32[136,128]{1,0:T(8,128)S(1)}, u32[]{:S(2)}, u32[]{:S(2)}) collective-permute-start(f32[136,128]{1,0:T(8,128)S(1)} %get-tuple-element.51.own), channel_id=1, source_target_pairs={{0,48},{16,0},{32,16},{48,32},{1,49},{17,1},{33,17},{49,33},{2,50}... | collective-permute-start | bytes 208904 | tf_op jit(solution)/shard_map/ppermute | solution.py:299
  109.3 6.5 %collective-permute-start.17 = (f32[136,128]{1,0:T(8,128)S(1)}, f32[136,128]{1,0:T(8,128)S(1)}, u32[]{:S(2)}, u32[]{:S(2)}) collective-permute-start(f32[136,128]{1,0:T(8,128)S(1)} %get-tuple-element.51.own), channel_id=1, source_target_pairs={{0,16},{16,32},{32,48},{48,0},{1,17},{17,33},{33,49},{49,1},{2,18}... | collective-permute-start | bytes 208904 | tf_op jit(solution)/shard_map/ppermute | solution.py:299
  109.3 6.5 %collective-permute-start.16 = (f32[136,128]{1,0:T(8,128)S(1)}, f32[136,128]{1,0:T(8,128)S(1)}, u32[]{:S(2)}, u32[]{:S(2)}) collective-permute-start(f32[136,128]{1,0:T(8,128)S(1)} %get-tuple-element.51.own), channel_id=1, source_target_pairs={{0,32},{16,48},{32,0},{48,16},{1,33},{17,49},{33,1},{49,17},{2,34}... | collective-permute-start | bytes 208904 | tf_op jit(solution)/shard_map/ppermute | solution.py:299
  115.8 4.0 %collective-permute-start.21 = (f32[136,128]{1,0:T(8,128)S(1)}, f32[136,128]{1,0:T(8,128)S(1)}, u32[]{:S(2)}, u32[]{:S(2)}) collective-permute-start(f32[136,128]{1,0:T(8,128)S(1)} %sums.3.own), channel_id=1, source_target_pairs={{0,192},{64,0},{128,64},{192,128},{1,193},{65,1},{129,65},{193,129... | collective-permute-start | bytes 208904 | tf_op jit(solution)/shard_map/ppermute | solution.py:299
  118.4 5.1 %collective-permute-start.20 = (f32[136,128]{1,0:T(8,128)S(1)}, f32[136,128]{1,0:T(8,128)S(1)}, u32[]{:S(2)}, u32[]{:S(2)}) collective-permute-start(f32[136,128]{1,0:T(8,128)S(1)} %sums.3.own), channel_id=1, source_target_pairs={{0,64},{64,128},{128,192},{192,0},{1,65},{65,129},{129,193},{193,1... | collective-permute-start | bytes 208904 | tf_op jit(solution)/shard_map/ppermute | solution.py:299
  118.4 5.1 %collective-permute-start.19 = (f32[136,128]{1,0:T(8,128)S(1)}, f32[136,128]{1,0:T(8,128)S(1)}, u32[]{:S(2)}, u32[]{:S(2)}) collective-permute-start(f32[136,128]{1,0:T(8,128)S(1)} %sums.3.own), channel_id=1, source_target_pairs={{0,128},{64,192},{128,0},{192,64},{1,129},{65,193},{129,1},{193,65... | collective-permute-start | bytes 208904 | tf_op jit(solution)/shard_map/ppermute | solution.py:299

commit v4 on v3

v4 whole, which is shorter than its diff:
```python
import jax
import jax.numpy as jnp
from jax import lax
from jax.experimental import pallas as pl
from jax.experimental.pallas import tpu as pltpu
from jax.sharding import Mesh
from jax.sharding import PartitionSpec as P

N = 16
TILE = 128
ROW_BLOCKS = 64
COL_BLOCKS = 128
SLOTS = 64
ROWS_SHARE = ROW_BLOCKS // N
COLS_SHARE = COL_BLOCKS // N
HALF = ROW_BLOCKS // 2
NROWS = float(N * ROW_BLOCKS * TILE)
NCOLS = float(N * COL_BLOCKS * TILE)
PACK_VMEM = 60 * 2**20
FIRST_VMEM = 48 * 2**20
PIECES = (4, 12, 16, 32)
F32, BF16 = jnp.float32, jnp.bfloat16

SLOT_ROWS, SLOT_COLS, COUNT, AT_Y, AT_X, AT_Z, AT_CORE = range(7)
COL_SIDE, ROW_SIDE, TABLE, SIDE = 0, 24, 32, 40

VMEM = pl.BlockSpec(memory_space=pltpu.VMEM)
SMEM = pl.BlockSpec(memory_space=pltpu.SMEM)
HBM = pl.BlockSpec(memory_space=pltpu.HBM)


def call(kernel, name, out_shapes, args, smem=0, hbm=0, smem_out=False, scratch=(), vmem=8 * 2**20):
    shapes = tuple(jax.ShapeDtypeStruct(s, d) for s, d in out_shapes)
    return pl.pallas_call(
        kernel,
        name=name,
        out_shape=shapes,
        in_specs=[SMEM] * smem + [HBM] * hbm + [VMEM] * (len(args) - smem - hbm),
        out_specs=tuple([SMEM if smem_out else VMEM] * len(shapes)),
        scratch_shapes=list(scratch),
        compiler_params=pltpu.CompilerParams(vmem_limit_bytes=vmem),
    )(*args)


def split(vector, copies):
    wide = jnp.broadcast_to(vector, (copies, TILE))
    lead = wide.astype(BF16).astype(F32)
    return [lead, wide - lead]


def adjoint_product(table, tile_pair, dual_ref, total):
    total[...] = jnp.zeros_like(total)
    adjoint_slots(table, tile_pair, dual_ref, total, 0, SLOTS)


def adjoint_slots(table, tile_pair, dual_ref, total, first, slots):
    def body(slot, carry):
        lhs = jnp.concatenate(split(dual_ref[pl.ds(table[SLOT_ROWS, slot], 1), :], 8), 0).astype(BF16)
        lhs = jnp.concatenate([lhs, lhs], 1)
        product = jnp.dot(lhs, tile_pair(slot), preferred_element_type=F32)
        total[table[SLOT_COLS, slot]] += product[0:8] + product[8:16]
        return carry

    lax.fori_loop(first, first + slots, body, 0, unroll=slots)


def forward_product(table, tile_pair, primal_refs, total):
    total[...] = jnp.zeros_like(total)
    copies = 8 // len(primal_refs)

    def body(slot, carry):
        parts = [split(ref[pl.ds(table[SLOT_COLS, slot], 1), :], copies) for ref in primal_refs]
        lhs = jnp.concatenate([p[0] for p in parts] + [p[1] for p in parts], 0).astype(BF16)
        product = lax.dot_general(
            lhs, tile_pair(slot), (((1,), (1,)), ((), ())), preferred_element_type=F32
        )
        product = product[:, :TILE] + product[:, TILE:]
        total[table[SLOT_ROWS, slot]] += product[0:8] + product[8:16]
        return carry

    lax.fori_loop(0, SLOTS, body, 0, unroll=SLOTS)


def clamp_primal(values, free):
    floor = jnp.maximum(values, 0.0)
    return jnp.where(free > 0.5, floor, jnp.minimum(floor, 1.0))


def clamp_dual(values, ineq):
    return jnp.where(ineq > 0.5, jnp.maximum(values, 0.0), values)


def index_row(table):
    return table[AT_Y, 0] * 4 + table[AT_X, 0]


def index_col(table):
    return table[AT_Z, 0] * 2 + table[AT_CORE, 0]


def sum_four(refs, rows):
    own, opposite, right, left = (ref[rows, :] for ref in refs)
    return (own + opposite) + (right + left)


def pack(
    count, rows, cols, row_kinds, rhs, dual, col_kinds, cost, primal, duals, side, places, kinds, start, done
):
    copies = [
        pltpu.make_async_copy(source, target, done.at[k])
        for k, (source, target) in enumerate(
            (
                (rows.at[0], places.at[0:1]),
                (cols.at[0], places.at[1:2]),
                (dual.at[0], start),
                (rhs.at[0], side.at[ROW_SIDE : ROW_SIDE + ROWS_SHARE]),
                (row_kinds.at[0], kinds.at[0:ROWS_SHARE]),
                (primal.at[0], side.at[0:COLS_SHARE]),
                (cost.at[0], side.at[COLS_SHARE : 2 * COLS_SHARE]),
                (col_kinds.at[0], kinds.at[COLS_SHARE : 2 * COLS_SHARE]),
            )
        )
    ]
    for copy in copies:
        copy.start()
    side[TABLE + COUNT :, :] = jnp.zeros((SIDE - TABLE - COUNT, TILE), F32)
    for k, value in (
        (COUNT, count[0, 0]),
        (AT_Y, lax.axis_index("y")),
        (AT_X, lax.axis_index("x")),
        (AT_Z, lax.axis_index("z")),
        (AT_CORE, lax.axis_index("core")),
    ):
        side[TABLE + k : TABLE + k + 1, :] = jnp.full((1, TILE), value, jnp.int32).astype(F32)
    side[TABLE : TABLE + COUNT, :] = jnp.zeros((COUNT, TILE), F32)
    for copy in copies:
        copy.wait()
    side[TABLE : TABLE + COUNT, 0:SLOTS] = places[...].astype(F32)
    side[2 * COLS_SHARE : ROW_SIDE, :] = kinds[COLS_SHARE:, :].astype(F32)
    side[ROW_SIDE + ROWS_SHARE : TABLE, :] = kinds[0:ROWS_SHARE, :].astype(F32)
    duals[...] = jnp.broadcast_to(start[...][None], duals.shape)


def x_sums(own, opposite, right, left, payload):
    four = (own, opposite, right, left)
    payload[0:COL_BLOCKS, :] = sum_four(four, slice(0, COL_BLOCKS))
    share = 3 * COLS_SHARE
    for k, ref in enumerate(four):
        first = COL_BLOCKS + k * share
        payload[first : first + share, :] = ref[COL_BLOCKS : COL_BLOCKS + share, :]


def sums(own, opposite, right, left, total):
    total[...] = sum_four((own, opposite, right, left), slice(None))


def image_copies(kept, received, side, copies):
    block = jnp.concatenate([kept[...] + received[...], side[ROW_SIDE:TABLE, :]], 0)
    copies[...] = jnp.broadcast_to(block[None], copies.shape)


def image_sums(pieces, held):
    held[0:HALF, :] = jnp.sum(pieces[:, 0:HALF, :], 0)
    for k in range(8):
        for j in range(2):
            first = HALF + j * ROWS_SHARE
            into = HALF * (1 + j) + k * ROWS_SHARE
            held[into : into + ROWS_SHARE, :] = pieces[k, first : first + ROWS_SHARE, :]


def pair_copies(kept, received, copies):
    both = kept[...] + received[...]
    for k in range(8):
        first = HALF + k * ROWS_SHARE
        copies[k, 0:HALF, :] = both[0:HALF]
        copies[k, HALF : HALF + 8, :] = jnp.concatenate(
            [both[first : first + ROWS_SHARE], jnp.zeros((8 - ROWS_SHARE, TILE), F32)], 0
        )


def pair_sums(pieces, held):
    held[...] = jnp.sum(pieces[...], 0)


def first_adjoint(
    tiles, duals, side, payload, dual, table_out, pairs, chunks, table, done, total
):
    copies, first = [], 0
    for k, slots in enumerate(PIECES):
        part = pl.ds(first, slots)
        copies.append(pltpu.make_async_copy(tiles.at[part], chunks.at[part], done.at[k]))
        copies[k].start()
        first += slots
    table_out[...] = side[TABLE:, :].astype(jnp.int32)
    read = pltpu.make_async_copy(table_out, table, done.at[len(PIECES)])
    read.start()
    for k in range(N):
        dual[k * ROWS_SHARE : (k + 1) * ROWS_SHARE, :] = duals[k]
    total[...] = jnp.zeros_like(total)
    payload[COL_BLOCKS:, :] = side[COL_SIDE:ROW_SIDE, :]
    read.wait()

    def tile_pair(slot):
        tile = jnp.where(slot < table[COUNT, 0], chunks[slot], 0.0)
        lead = tile.astype(BF16)
        pair = jnp.concatenate([lead, (tile - lead.astype(F32)).astype(BF16)], 0)
        pairs[slot] = pair
        return pair

    first = 0
    for k, slots in enumerate(PIECES):
        copies[k].wait()
        adjoint_slots(table, tile_pair, dual, total, first, slots)
        first += slots
    payload[0:COL_BLOCKS, :] = total[:, 0, :]


def first_forward(
    table, own, opposite, right, left, pairs, kept, given, primal, start, cost, free, extended, total
):
    y, x = table[AT_Y, 0], table[AT_X, 0]
    for j, (ref, dy) in enumerate(((own, 0), (opposite, 2), (right, 3), (left, 1))):
        for k, dx in enumerate((0, 2, 3, 1)):
            device = ((y + dy) & 3) * 4 + ((x + dx) & 3)
            block = pl.ds(pl.multiple_of(device * COLS_SHARE, COLS_SHARE), COLS_SHARE)
            for m, out in enumerate((start, cost, free)):
                first = COL_BLOCKS + (3 * k + m) * COLS_SHARE
                out[block, :] = ref[first : first + COLS_SHARE, :]
    gradient = sum_four((own, opposite, right, left), slice(0, COL_BLOCKS))
    primal[...] = clamp_primal(start[...] - 0.4 * (cost[...] - gradient), free[...])
    extended[...] = 2.0 * primal[...] - start[...]
    forward_product(table, lambda slot: pairs[slot], [extended], total)
    mine = pl.multiple_of(table[AT_CORE, 0] * HALF, HALF)
    kept[...] = total[pl.ds(mine, HALF), 0, :]
    given[...] = total[pl.ds(HALF - mine, HALF), 0, :]


def second_adjoint(table, held, other, start, pairs, gradient, dual, rhs, ineq, image, total):
    first = table[AT_CORE, 0] == 0
    mine, theirs = held[...], other[...]
    for core, half in enumerate((jnp.where(first, mine, theirs), jnp.where(first, theirs, mine))):
        image[core * HALF : (core + 1) * HALF, :] = half[0:HALF]
        for k in range(8):
            block = slice((2 * k + core) * ROWS_SHARE, (2 * k + core + 1) * ROWS_SHARE)
            share = slice(k * ROWS_SHARE, (k + 1) * ROWS_SHARE)
            rhs[block, :] = half[HALF : 2 * HALF][share]
            ineq[block, :] = half[2 * HALF :][share]
    dual[...] = clamp_dual(start[...] + 0.4 * (rhs[...] - image[...]), ineq[...])
    adjoint_product(table, lambda slot: pairs[slot], dual, total)
    gradient[...] = total[:, 0, :]


def second_forward(
    table, own, opposite, right, left, before, cost, free, pairs, kept, given, primal, gradient, primal_mine, extended, total
):
    gradient[...] = sum_four((own, opposite, right, left), slice(0, COL_BLOCKS))
    primal[...] = clamp_primal(before[...] - 0.4 * (cost[...] - gradient[...]), free[...])
    extended[...] = 2.0 * primal[...] - before[...]
    primal_mine[...] = primal[
        pl.ds(pl.multiple_of(index_row(table) * COLS_SHARE, COLS_SHARE), COLS_SHARE), :
    ]
    forward_product(table, lambda slot: pairs[slot], [extended, primal], total)
    mine = pl.multiple_of(table[AT_CORE, 0] * HALF, HALF)
    for k, part in enumerate((0, 4)):
        rows = slice(k * HALF, (k + 1) * HALF)
        kept[rows, :] = total[pl.ds(mine, HALF), part, :]
        given[rows, :] = total[pl.ds(HALF - mine, HALF), part, :]


def third_adjoint(
    table, held, other, before, rhs, ineq, pairs, payload, mine, dual, image, total
):
    half = pl.multiple_of(table[AT_CORE, 0] * HALF, HALF)
    image[pl.ds(half, HALF), :] = held[0:HALF, :]
    image[pl.ds(HALF - half, HALF), :] = other[0:HALF, :]
    dual[...] = clamp_dual(before[...] + 0.4 * (rhs[...] - image[...]), ineq[...])
    mine[...] = dual[pl.ds(index_col(table) * ROWS_SHARE, ROWS_SHARE), :]
    adjoint_product(table, lambda slot: pairs[slot], dual, total)
    payload[0:COL_BLOCKS, :] = total[:, 0, :]
    share = pl.ds(half + table[AT_Z, 0] * ROWS_SHARE, ROWS_SHARE)
    plain = held[HALF : HALF + ROWS_SHARE, :]
    bound, kind, last = rhs[share, :], ineq[share, :], dual[share, :]
    terms = []
    for product in (plain, 0.5 * (3.0 * plain - image[share, :])):
        residual = bound - product
        residual = jnp.where(kind > 0.5, jnp.maximum(residual, 0.0), residual)
        terms.append(jnp.sum(residual * residual, 0, keepdims=True))
    for value in (last, 0.5 * (before[share, :] + last)):
        terms.append(jnp.sum(bound * value, 0, keepdims=True))
    payload[COL_BLOCKS : COL_BLOCKS + 8, :] = jnp.concatenate(terms + terms, 0)


def column_terms(own, opposite, right, left, earlier, before, primal, cost, free, terms):
    four = (own, opposite, right, left)
    adjoint = sum_four(four, slice(0, COL_BLOCKS))
    row_terms = sum_four(four, slice(COL_BLOCKS, COL_BLOCKS + 8))
    price, kind = cost[...], free[...]
    squares, gaps = [], []
    for k, (gradient, value) in enumerate(
        (
            (adjoint, primal[...]),
            (0.5 * (earlier[...] + adjoint), 0.5 * (before[...] + primal[...])),
        )
    ):
        low = jnp.minimum(price - gradient, 0.0)
        violation = jnp.where(kind > 0.5, low, 0.0)
        box = jnp.where(kind > 0.5, 0.0, low)
        squares.append(jnp.sum(violation * violation, 0, keepdims=True))
        column = jnp.sum(price * value, 0, keepdims=True) - jnp.sum(box, 0, keepdims=True)
        gaps.append(column - row_terms[2 + k : 3 + k])
    rows = jnp.concatenate([row_terms[0:2]] + squares + gaps + squares, 0)
    sums = jnp.broadcast_to(jnp.sum(rows, 1, keepdims=True), rows.shape)
    places = [lax.broadcasted_iota(jnp.int32, rows.shape, k) for k in range(2)]
    line = jnp.sum(jnp.where(places[0] == places[1], sums, 0.0), 0, keepdims=True)
    terms[...] = jnp.broadcast_to(line[None], terms.shape)


def measures(gathered, primal_residual, dual_residual, gap):
    line = jnp.sum(gathered[...], 0)
    lane = lax.broadcasted_iota(jnp.int32, line.shape, 1)
    for k, (out, size) in enumerate(
        ((primal_residual, NROWS), (dual_residual, NCOLS), (gap, NCOLS))
    ):
        for j in range(2):
            out[j] = jnp.sum(jnp.where(lane == 2 * k + j, line, 0.0)) * (1.0 / size)


def shift(values, axis, step):
    return lax.ppermute(values, axis, [(k, (k + step) % 4) for k in range(4)])


def four_of(values, axis):
    return values, shift(values, axis, 2), shift(values, axis, 1), shift(values, axis, -1)


def four_over_row(values):
    total = call(sums, "sums", [(values.shape, F32)], four_of(values, "x"))
    return four_of(total[0], "y")


def swap_cores(values):
    return lax.ppermute(values, "core", [(0, 1), (1, 0)])


def exchange(copies, axes):
    return lax.all_to_all(copies, axes, 0, 0)


def shards(
    tiles, tile_rows, tile_cols, tile_count, row_types, var_types, rhs, cost, primal_start, dual_start
):
    tiles = tiles.reshape(SLOTS, TILE, TILE)
    blocks, columns, half = (ROW_BLOCKS, TILE), (COL_BLOCKS, TILE), (HALF, TILE)
    row_total = [pltpu.VMEM((ROW_BLOCKS, 8, TILE), F32)]
    col_total = [pltpu.VMEM((COL_BLOCKS, 8, TILE), F32)]

    duals, side = call(
        pack,
        "pack",
        [((N, ROWS_SHARE, TILE), F32), ((SIDE, TILE), F32)],
        (tile_count, tile_rows, tile_cols, row_types, rhs, dual_start, var_types, cost, primal_start),
        smem=1,
        hbm=8,
        scratch=[
            pltpu.VMEM((2, SLOTS), jnp.int32),
            pltpu.VMEM((2 * COLS_SHARE, TILE), jnp.int32),
            pltpu.VMEM((ROWS_SHARE, TILE), F32),
            pltpu.SemaphoreType.DMA((8,)),
        ],
        vmem=PACK_VMEM,
    )

    payload, dual0, table, pairs = call(
        first_adjoint,
        "first_adjoint",
        [
            ((COL_BLOCKS + 3 * COLS_SHARE, TILE), F32),
            (blocks, F32),
            ((8, TILE), jnp.int32),
            ((SLOTS, 2 * TILE, TILE), BF16),
        ],
        (tiles, exchange(duals, ("z", "core")), side),
        hbm=1,
        scratch=[
            pltpu.VMEM((SLOTS, TILE, TILE), F32),
            pltpu.SMEM((8, TILE), jnp.int32),
            pltpu.SemaphoreType.DMA((len(PIECES) + 1,)),
        ]
        + col_total,
        vmem=FIRST_VMEM,
    )
    payload = call(
        x_sums, "x_sums", [((COL_BLOCKS + 12 * COLS_SHARE, TILE), F32)], four_of(payload, "x")
    )

    kept, given, primal1, start_full, cost_full, free = call(
        first_forward,
        "first_forward",
        [(half, F32)] * 2 + [(columns, F32)] * 4,
        (table, *four_of(payload[0], "y"), pairs),
        smem=1,
        scratch=[pltpu.VMEM(columns, F32)] + row_total,
    )
    copies = call(
        image_copies,
        "image_copies",
        [((8, HALF + 2 * ROWS_SHARE, TILE), F32)],
        (kept, swap_cores(given), side),
    )
    held = call(
        image_sums, "image_sums", [((3 * HALF, TILE), F32)], (exchange(copies[0], "z"),)
    )[0]

    gradient, dual1, rhs_full, ineq = call(
        second_adjoint,
        "second_adjoint",
        [(columns, F32)] + [(blocks, F32)] * 3,
        (table, held, swap_cores(held), dual0, pairs),
        smem=1,
        scratch=[pltpu.VMEM(blocks, F32)] + col_total,
    )

    kept, given, primal2, gradient2, primal_mine = call(
        second_forward,
        "second_forward",
        [(blocks, F32)] * 2 + [(columns, F32)] * 2 + [((COLS_SHARE, TILE), F32)],
        (table, *four_over_row(gradient), primal1, cost_full, free, pairs),
        smem=1,
        scratch=[pltpu.VMEM(columns, F32)] + row_total,
    )
    copies = call(
        pair_copies, "pair_copies", [((8, HALF + 8, TILE), F32)], (kept, swap_cores(given))
    )
    held = call(pair_sums, "pair_sums", [((HALF + 8, TILE), F32)], (exchange(copies[0], "z"),))[0]

    payload, dual_mine = call(
        third_adjoint,
        "third_adjoint",
        [((COL_BLOCKS + 8, TILE), F32), ((ROWS_SHARE, TILE), F32)],
        (table, held, swap_cores(held), dual1, rhs_full, ineq, pairs),
        smem=1,
        scratch=[pltpu.VMEM(blocks, F32)] * 2 + col_total,
    )
    terms = call(
        column_terms,
        "column_terms",
        [((N, 1, TILE), F32)],
        (*four_over_row(payload), gradient2, primal1, primal2, cost_full, free),
    )
    primal_residual, dual_residual, gap = call(
        measures,
        "measures",
        [((2,), F32)] * 3,
        (exchange(terms[0], ("z", "core")),),
        smem_out=True,
    )
    return primal_mine[None], dual_mine[None], primal_residual, dual_residual, gap


def solution(mesh):
    rings = Mesh(mesh.devices.reshape(4, 4, 8, 2), ("y", "x", "z", "core"))
    row, col = ("y", "x"), ("z", "core")
    in_specs = (
        P(row, col, None, None, None),
        P(row, col, None),
        P(row, col, None),
        P(row, col),
        P(row, col, None),
        P(col, row, None),
        P(row, col, None),
        P(col, row, None),
        P(col, row, None),
        P(row, col, None),
    )
    out_specs = (P(col, row, None), P(row, col, None), P(), P(), P())
    return jax.shard_map(shards, mesh=rings, in_specs=in_specs, out_specs=out_specs, check_vma=False)
```

time: 137 us -> 129 us (0.942)
  blocking collectives: 57.2 us -> 52.2 us
  Pallas kernels: 17.1 us -> 12.9 us
  starting transfers between devices: 28.7 us -> 31.3 us
    all_to_all x4, blocking collectives: 57.2 us -> 52.2 us  [exchange(): return lax.all_to_all(copies, axes, 0, 0)]
    pallas_call x15, Pallas kernels: 17.1 us -> 12.9 us  [call(): pl.pallas_call(kernel, name=name, out_shape=shapes, in_specs=[SMEM] * sme...]
    ppermute x18, starting transfers between devices: 21.3 us -> 22.7 us  [shift(): return lax.ppermute(values, axis, [(k, (k + step) % 4) for k in range(4)])]
  transfers between devices with their start and end apart: 22 -> 22, of which waited for: 17 -> 16; matrix products, arithmetic and copies ran while one was open for 0% -> 0% of each run, Pallas kernels for 0% -> 0%
where the time goes in v4:
time: 129 us
  blocking collectives  52.2 us (40%)
  starting transfers between devices  31.3 us (24%)
  waiting for transfers between devices  30 us (23%)
  Pallas kernels  12.9 us (10%)
  between operations  1.51 us (1%)
    all_to_all x4, blocking collectives, exchange(): return lax.all_to_all(copies, axes, 0, 0)  52.2 us
    ppermute x18, waiting for transfers between devices, shift(): return lax.ppermute(values, axis, [(k, (k + step) % 4) for k in range(4)])  26.5 us
    ppermute x18, starting transfers between devices, shift(): return lax.ppermute(values, axis, [(k, (k + step) % 4) for k in range(4)])  22.7 us
    pallas_call x15, Pallas kernels, call(): pl.pallas_call(kernel, name=name, out_shape=shapes, in_specs=[SMEM] * sme...  12.9 us
    ppermute x4, starting transfers between devices, swap_cores(): return lax.ppermute(values, 'core', [(0, 1), (1, 0)])  8.68 us
    ppermute x4, waiting for transfers between devices, swap_cores(): return lax.ppermute(values, 'core', [(0, 1), (1, 0)])  3.42 us
  transfers between devices with their start and end apart: 22, of which 16 were waited for; matrix products, arithmetic and copies ran while one was open for 0% of the time, Pallas kernels for 0%

profile of v4, /device:TPU:1, one launch (start us, length us, event | category | flops | bytes accessed | tf_op | source)
XLA Modules:
  0.0 128.7 jit_solution(2193789467597195240)
XLA Ops:
  2.8 17.4 %all_to_all.20.duals = f32[16,4,128]{2,1,0:T(4,128)S(1)} all-to-all(f32[16,4,128]{2,1,0:T(4,128)} %get-tuple-element.30), channel_id=1, replica_groups=mesh['y'=4,'x'=4,'z'=8,'core'=2] {'z','core'}, dimensions={0} | all-to-all | bytes 65536 | tf_op jit(solution)/shard_map/all_to_all | solution.py:346
  20.9 2.8 %first_adjoint.1 = (f32[152,128]{1,0:T(8,128)S(1)}, f32[64,128]{1,0:T(8,128)S(1)}, s32[8,128]{1,0:T(8,128)S(1)}, bf16[64,256,128]{2,1,0:T(8,128)(2,1)S(1)}) custom-call(f32[64,128,128]{2,1,0:T(8,128)} %bitcast.3, f32[16,4,128]{2,1,0:T(4,128)S(1)} %all_to_all.20.duals, f32[40,128]{1,0:T(8,128)S(1)} %copy-done), custom_call_target="tpu_custom_call" | custom-call | tf_op jit(solution)/shard_map/first_adjoint/pallas_call | solution.py:34
  23.7 2.6 %collective-permute-start.2 = (f32[152,128]{1,0:T(8,128)S(1)}, f32[152,128]{1,0:T(8,128)S(1)}, u32[]{:S(2)}, u32[]{:S(2)}) collective-permute-start(f32[152,128]{1,0:T(8,128)S(1)} %get-tuple-element.33.own), channel_id=1, source_target_pairs={{0,48},{16,0},{32,16},{48,32},{1,49},{17,1},{33,17},{49,33},{2,50}... | collective-permute-start | bytes 233480 | tf_op jit(solution)/shard_map/ppermute | solution.py:329
  26.2 1.7 %collective-permute-start = (f32[152,128]{1,0:T(8,128)S(1)}, f32[152,128]{1,0:T(8,128)S(1)}, u32[]{:S(2)}, u32[]{:S(2)}) collective-permute-start(f32[152,128]{1,0:T(8,128)S(1)} %get-tuple-element.33.own), channel_id=1, source_target_pairs={{0,32},{16,48},{32,0},{48,16},{1,33},{17,49},{33,1},{49,17},{2,34}... | collective-permute-start | bytes 233480 | tf_op jit(solution)/shard_map/ppermute | solution.py:329
  28.0 3.7 %collective-permute-done.1.right = f32[152,128]{1,0:T(8,128)S(1)} collective-permute-done((f32[152,128]{1,0:T(8,128)S(1)}, f32[152,128]{1,0:T(8,128)S(1)}, u32[]{:S(2)}, u32[]{:S(2)}) %collective-permute-start.1) | collective-permute-done | bytes 77856 | tf_op jit(solution)/shard_map/ppermute | solution.py:329
  32.1 2.8 %collective-permute-start.5 = (f32[224,128]{1,0:T(8,128)S(1)}, f32[224,128]{1,0:T(8,128)S(1)}, u32[]{:S(2)}, u32[]{:S(2)}) collective-permute-start(f32[224,128]{1,0:T(8,128)S(1)} %x_sums.1.own), channel_id=1, source_target_pairs={{0,192},{64,0},{128,64},{192,128},{1,193},{65,1},{129,65},{193,129... | collective-permute-start | bytes 344072 | tf_op jit(solution)/shard_map/ppermute | solution.py:329
  35.0 1.6 %collective-permute-start.3 = (f32[224,128]{1,0:T(8,128)S(1)}, f32[224,128]{1,0:T(8,128)S(1)}, u32[]{:S(2)}, u32[]{:S(2)}) collective-permute-start(f32[224,128]{1,0:T(8,128)S(1)} %x_sums.1.own), channel_id=1, source_target_pairs={{0,128},{64,192},{128,0},{192,64},{1,129},{65,193},{129,1},{193,65... | collective-permute-start | bytes 344072 | tf_op jit(solution)/shard_map/ppermute | solution.py:329
  36.7 4.3 %collective-permute-done.4.right = f32[224,128]{1,0:T(8,128)S(1)} collective-permute-done((f32[224,128]{1,0:T(8,128)S(1)}, f32[224,128]{1,0:T(8,128)S(1)}, u32[]{:S(2)}, u32[]{:S(2)}) %collective-permute-start.4) | collective-permute-done | bytes 114720 | tf_op jit(solution)/shard_map/ppermute | solution.py:329
  41.0 2.3 %first_forward.1 = (f32[32,128]{1,0:T(8,128)S(1)}, f32[32,128]{1,0:T(8,128)S(1)}, f32[128,128]{1,0:T(8,128)S(1)}, f32[128,128]{1,0:T(8,128)}, f32[128,128]{1,0:T(8,128)S(1)}, /*index=5*/f32[128,128]{1,0:T(8,128)S(1)}) custom-call(s32[8,128]{1,0:T(8,128)S(1)} %get-tuple-element.32.table, f32[224,128]{1,0:T(8,128)S(1)} %x_sums.1.own, ...), custom_call_target="tpu_custom_call" | custom-call | tf_op jit(solution)/shard_map/first_forward/pallas_call | solution.py:34
  43.3 3.2 %collective-permute-start.6 = (f32[32,128]{1,0:T(8,128)S(1)}, f32[32,128]{1,0:T(8,128)S(1)}, u32[]{:S(2)}, u32[]{:S(2)}) collective-permute-start(f32[32,128]{1,0:T(8,128)S(1)} %get-tuple-element.36), channel_id=1, source_target_pairs={{0,1},{1,0},{2,3},{3,2},{4,5},{5,4},{6,7},{7,6},{8,9},{9,8},{10,11... | collective-permute-start | bytes 49160 | tf_op jit(solution)/shard_map/ppermute | solution.py:342
  47.4 11.6 %all_to_all.21.pieces = f32[8,40,128]{2,1,0:T(8,128)S(1)} all-to-all(f32[8,40,128]{2,1,0:T(8,128)S(1)} %image_copies.1), channel_id=1, replica_groups=mesh['y'=4,'x'=4,'z'=8,'core'=2] {'z'}, dimensions={0} | all-to-all | bytes 327680 | tf_op jit(solution)/shard_map/all_to_all | solution.py:346
  62.8 2.0 %collective-permute-start.10 = (f32[128,128]{1,0:T(8,128)S(1)}, f32[128,128]{1,0:T(8,128)S(1)}, u32[]{:S(2)}, u32[]{:S(2)}) collective-permute-start(f32[128,128]{1,0:T(8,128)S(1)} %get-tuple-element.38.own), channel_id=1, source_target_pairs={{0,48},{16,0},{32,16},{48,32},{1,49},{17,1},{33,17},{49,33},{2,50}... | collective-permute-start | bytes 196616 | tf_op jit(solution)/shard_map/ppermute | solution.py:329
  66.1 5.0 %collective-permute-done.9.right = f32[128,128]{1,0:T(8,128)S(1)} collective-permute-done((f32[128,128]{1,0:T(8,128)S(1)}, f32[128,128]{1,0:T(8,128)S(1)}, u32[]{:S(2)}, u32[]{:S(2)}) %collective-permute-start.9) | collective-permute-done | bytes 65568 | tf_op jit(solution)/shard_map/ppermute | solution.py:329
  71.1 2.1 %collective-permute-start.13 = (f32[128,128]{1,0:T(8,128)S(1)}, f32[128,128]{1,0:T(8,128)S(1)}, u32[]{:S(2)}, u32[]{:S(2)}) collective-permute-start(f32[128,128]{1,0:T(8,128)S(1)} %sums.2.own), channel_id=1, source_target_pairs={{0,192},{64,0},{128,64},{192,128},{1,193},{65,1},{129,65},{193,129... | collective-permute-start | bytes 196616 | tf_op jit(solution)/shard_map/ppermute | solution.py:329
  74.5 3.7 %collective-permute-done.12.right = f32[128,128]{1,0:T(8,128)S(1)} collective-permute-done((f32[128,128]{1,0:T(8,128)S(1)}, f32[128,128]{1,0:T(8,128)S(1)}, u32[]{:S(2)}, u32[]{:S(2)}) %collective-permute-start.12) | collective-permute-done | bytes 65568 | tf_op jit(solution)/shard_map/ppermute | solution.py:329
  78.2 2.3 %second_forward.1 = (f32[64,128]{1,0:T(8,128)S(1)}, f32[64,128]{1,0:T(8,128)S(1)}, f32[128,128]{1,0:T(8,128)S(1)}, f32[128,128]{1,0:T(8,128)S(1)}, f32[8,128]{1,0:T(8,128)}) custom-call(s32[8,128]{1,0:T(8,128)S(1)} %get-tuple-element.32.table, f32[128,128]{1,0:T(8,128)S(1)} %sums.2.own, f32[128,128]{1,0:T(8,128)S(1)} %collective-permute-done.11.opposite, ...), custom_call_target="tpu_custom_call" | custom-call | tf_op jit(solution)/shard_map/second_forward/pallas_call | solution.py:34
  80.5 2.2 %collective-permute-start.14 = (f32[64,128]{1,0:T(8,128)S(1)}, f32[64,128]{1,0:T(8,128)S(1)}, u32[]{:S(2)}, u32[]{:S(2)}) collective-permute-start(f32[64,128]{1,0:T(8,128)S(1)} %get-tuple-element.44), channel_id=1, source_target_pairs={{0,1},{1,0},{2,3},{3,2},{4,5},{5,4},{6,7},{7,6},{8,9},{9,8},{10,11... | collective-permute-start | bytes 98312 | tf_op jit(solution)/shard_map/ppermute | solution.py:342
  83.6 11.6 %all_to_all.22.pieces = f32[8,40,128]{2,1,0:T(8,128)S(1)} all-to-all(f32[8,40,128]{2,1,0:T(8,128)S(1)} %pair_copies.1), channel_id=1, replica_groups=mesh['y'=4,'x'=4,'z'=8,'core'=2] {'z'}, dimensions={0} | all-to-all | bytes 327680 | tf_op jit(solution)/shard_map/all_to_all | solution.py:346
  97.7 1.8 %third_adjoint.1 = (f32[136,128]{1,0:T(8,128)S(1)}, f32[4,128]{1,0:T(4,128)}) custom-call(s32[8,128]{1,0:T(8,128)S(1)} %get-tuple-element.32.table, f32[40,128]{1,0:T(8,128)S(1)} %pair_sums.1.held, f32[40,128]{1,0:T(8,128)S(1)} %collective-permute-done.15.other, f32[64,128]{1,0:T(8,128)S(1)} %get-tuple-element.45.before, ...), custom_call_target="tpu_custom_call" | custom-call | tf_op jit(solution)/shard_map/third_adjoint/pallas_call | solution.py:34
  99.5 2.2 %collective-permute-start.18 = (f32[136,128]{1,0:T(8,128)S(1)}, f32[136,128]{1,0:T(8,128)S(1)}, u32[]{:S(2)}, u32[]{:S(2)}) collective-permute-start(f32[136,128]{1,0:T(8,128)S(1)} %get-tuple-element.49.own), channel_id=1, source_target_pairs={{0,48},{16,0},{32,16},{48,32},{1,49},{17,1},{33,17},{49,33},{2,50}... | collective-permute-start | bytes 208904 | tf_op jit(solution)/shard_map/ppermute | solution.py:329
  103.1 5.1 %collective-permute-done.17.right = f32[136,128]{1,0:T(8,128)S(1)} collective-permute-done((f32[136,128]{1,0:T(8,128)S(1)}, f32[136,128]{1,0:T(8,128)S(1)}, u32[]{:S(2)}, u32[]{:S(2)}) %collective-permute-start.17) | collective-permute-done | bytes 69664 | tf_op jit(solution)/shard_map/ppermute | solution.py:329
  108.2 2.6 %collective-permute-start.21 = (f32[136,128]{1,0:T(8,128)S(1)}, f32[136,128]{1,0:T(8,128)S(1)}, u32[]{:S(2)}, u32[]{:S(2)}) collective-permute-start(f32[136,128]{1,0:T(8,128)S(1)} %sums.3.own), channel_id=1, source_target_pairs={{0,192},{64,0},{128,64},{192,128},{1,193},{65,1},{129,65},{193,129... | collective-permute-start | bytes 208904 | tf_op jit(solution)/shard_map/ppermute | solution.py:329
  112.2 3.7 %collective-permute-done.20.right = f32[136,128]{1,0:T(8,128)S(1)} collective-permute-done((f32[136,128]{1,0:T(8,128)S(1)}, f32[136,128]{1,0:T(8,128)S(1)}, u32[]{:S(2)}, u32[]{:S(2)}) %collective-permute-start.20) | collective-permute-done | bytes 69664 | tf_op jit(solution)/shard_map/ppermute | solution.py:329
  116.1 11.7 %all_to_all.23.gathered = f32[16,1,128]{2,1,0:T(1,128)S(1)} all-to-all(f32[16,1,128]{2,1,0:T(1,128)S(1)} %column_terms.1), channel_id=1, replica_groups=mesh['y'=4,'x'=4,'z'=8,'core'=2] {'z','core'}, dimensions={0} | all-to-all | bytes 16384 | tf_op jit(solution)/shard_map/all_to_all | solution.py:346
  (41 shorter events, 17.1 us)
Async XLA Ops:
  20.2 0.7 copy-start
  23.7 4.3 %collective-permute-start.2 = (f32[152,128]{1,0:T(8,128)S(1)}, f32[152,128]{1,0:T(8,128)S(1)}, u32[]{:S(2)}, u32[]{:S(2)}) collective-permute-start(f32[152,128]{1,0:T(8,128)S(1)} %get-tuple-element.33.own), channel_id=1, source_target_pairs={{0,48},{16,0},{32,16},{48,32},{1,49},{17,1},{33,17},{49,33},{2,50}... | collective-permute-start | bytes 233480 | tf_op jit(solution)/shard_map/ppermute | solution.py:329
  26.2 5.5 %collective-permute-start.1 = (f32[152,128]{1,0:T(8,128)S(1)}, f32[152,128]{1,0:T(8,128)S(1)}, u32[]{:S(2)}, u32[]{:S(2)}) collective-permute-start(f32[152,128]{1,0:T(8,128)S(1)} %get-tuple-element.33.own), channel_id=1, source_target_pairs={{0,16},{16,32},{32,48},{48,0},{1,17},{17,33},{33,49},{49,1},{2,18}... | collective-permute-start | bytes 233480 | tf_op jit(solution)/shard_map/ppermute | solution.py:329
  26.2 5.9 %collective-permute-start = (f32[152,128]{1,0:T(8,128)S(1)}, f32[152,128]{1,0:T(8,128)S(1)}, u32[]{:S(2)}, u32[]{:S(2)}) collective-permute-start(f32[152,128]{1,0:T(8,128)S(1)} %get-tuple-element.33.own), channel_id=1, source_target_pairs={{0,32},{16,48},{32,0},{48,16},{1,33},{17,49},{33,1},{49,17},{2,34}... | collective-permute-start | bytes 233480 | tf_op jit(solution)/shard_map/ppermute | solution.py:329
  32.1 4.6 %collective-permute-start.5 = (f32[224,128]{1,0:T(8,128)S(1)}, f32[224,128]{1,0:T(8,128)S(1)}, u32[]{:S(2)}, u32[]{:S(2)}) collective-permute-start(f32[224,128]{1,0:T(8,128)S(1)} %x_sums.1.own), channel_id=1, source_target_pairs={{0,192},{64,0},{128,64},{192,128},{1,193},{65,1},{129,65},{193,129... | collective-permute-start | bytes 344072 | tf_op jit(solution)/shard_map/ppermute | solution.py:329
  35.0 6.1 %collective-permute-start.4 = (f32[224,128]{1,0:T(8,128)S(1)}, f32[224,128]{1,0:T(8,128)S(1)}, u32[]{:S(2)}, u32[]{:S(2)}) collective-permute-start(f32[224,128]{1,0:T(8,128)S(1)} %x_sums.1.own), channel_id=1, source_target_pairs={{0,64},{64,128},{128,192},{192,0},{1,65},{65,129},{129,193},{193,1... | collective-permute-start | bytes 344072 | tf_op jit(solution)/shard_map/ppermute | solution.py:329
  35.0 6.1 %collective-permute-start.3 = (f32[224,128]{1,0:T(8,128)S(1)}, f32[224,128]{1,0:T(8,128)S(1)}, u32[]{:S(2)}, u32[]{:S(2)}) collective-permute-start(f32[224,128]{1,0:T(8,128)S(1)} %x_sums.1.own), channel_id=1, source_target_pairs={{0,128},{64,192},{128,0},{192,64},{1,129},{65,193},{129,1},{193,65... | collective-permute-start | bytes 344072 | tf_op jit(solution)/shard_map/ppermute | solution.py:329
  43.3 4.0 %collective-permute-start.6 = (f32[32,128]{1,0:T(8,128)S(1)}, f32[32,128]{1,0:T(8,128)S(1)}, u32[]{:S(2)}, u32[]{:S(2)}) collective-permute-start(f32[32,128]{1,0:T(8,128)S(1)} %get-tuple-element.36), channel_id=1, source_target_pairs={{0,1},{1,0},{2,3},{3,2},{4,5},{5,4},{6,7},{7,6},{8,9},{9,8},{10,11... | collective-permute-start | bytes 49160 | tf_op jit(solution)/shard_map/ppermute | solution.py:342
  59.0 2.5 %collective-permute-start.7 = (f32[96,128]{1,0:T(8,128)S(1)}, f32[96,128]{1,0:T(8,128)S(1)}, u32[]{:S(2)}, u32[]{:S(2)}) collective-permute-start(f32[96,128]{1,0:T(8,128)S(1)} %image_sums.1.held), channel_id=1, source_target_pairs={{0,1},{1,0},{2,3},{3,2},{4,5},{5,4},{6,7},{7,6},{8,9},{9,8},{10,11... | collective-permute-start | bytes 147464 | tf_op jit(solution)/shard_map/ppermute | solution.py:342
  62.8 3.3 %collective-permute-start.10 = (f32[128,128]{1,0:T(8,128)S(1)}, f32[128,128]{1,0:T(8,128)S(1)}, u32[]{:S(2)}, u32[]{:S(2)}) collective-permute-start(f32[128,128]{1,0:T(8,128)S(1)} %get-tuple-element.38.own), channel_id=1, source_target_pairs={{0,48},{16,0},{32,16},{48,32},{1,49},{17,1},{33,17},{49,33},{2,50}... | collective-permute-start | bytes 196616 | tf_op jit(solution)/shard_map/ppermute | solution.py:329
  64.7 6.3 %collective-permute-start.9 = (f32[128,128]{1,0:T(8,128)S(1)}, f32[128,128]{1,0:T(8,128)S(1)}, u32[]{:S(2)}, u32[]{:S(2)}) collective-permute-start(f32[128,128]{1,0:T(8,128)S(1)} %get-tuple-element.38.own), channel_id=1, source_target_pairs={{0,16},{16,32},{32,48},{48,0},{1,17},{17,33},{33,49},{49,1},{2,18}... | collective-permute-start | bytes 196616 | tf_op jit(solution)/shard_map/ppermute | solution.py:329
  64.7 6.3 %collective-permute-start.8 = (f32[128,128]{1,0:T(8,128)S(1)}, f32[128,128]{1,0:T(8,128)S(1)}, u32[]{:S(2)}, u32[]{:S(2)}) collective-permute-start(f32[128,128]{1,0:T(8,128)S(1)} %get-tuple-element.38.own), channel_id=1, source_target_pairs={{0,32},{16,48},{32,0},{48,16},{1,33},{17,49},{33,1},{49,17},{2,34}... | collective-permute-start | bytes 196616 | tf_op jit(solution)/shard_map/ppermute | solution.py:329
  71.1 3.4 %collective-permute-start.13 = (f32[128,128]{1,0:T(8,128)S(1)}, f32[128,128]{1,0:T(8,128)S(1)}, u32[]{:S(2)}, u32[]{:S(2)}) collective-permute-start(f32[128,128]{1,0:T(8,128)S(1)} %sums.2.own), channel_id=1, source_target_pairs={{0,192},{64,0},{128,64},{192,128},{1,193},{65,1},{129,65},{193,129... | collective-permute-start | bytes 196616 | tf_op jit(solution)/shard_map/ppermute | solution.py:329
  73.2 5.0 %collective-permute-start.12 = (f32[128,128]{1,0:T(8,128)S(1)}, f32[128,128]{1,0:T(8,128)S(1)}, u32[]{:S(2)}, u32[]{:S(2)}) collective-permute-start(f32[128,128]{1,0:T(8,128)S(1)} %sums.2.own), channel_id=1, source_target_pairs={{0,64},{64,128},{128,192},{192,0},{1,65},{65,129},{129,193},{193,1... | collective-permute-start | bytes 196616 | tf_op jit(solution)/shard_map/ppermute | solution.py:329
  73.2 5.0 %collective-permute-start.11 = (f32[128,128]{1,0:T(8,128)S(1)}, f32[128,128]{1,0:T(8,128)S(1)}, u32[]{:S(2)}, u32[]{:S(2)}) collective-permute-start(f32[128,128]{1,0:T(8,128)S(1)} %sums.2.own), channel_id=1, source_target_pairs={{0,128},{64,192},{128,0},{192,64},{1,129},{65,193},{129,1},{193,65... | collective-permute-start | bytes 196616 | tf_op jit(solution)/shard_map/ppermute | solution.py:329
  80.5 3.1 %collective-permute-start.14 = (f32[64,128]{1,0:T(8,128)S(1)}, f32[64,128]{1,0:T(8,128)S(1)}, u32[]{:S(2)}, u32[]{:S(2)}) collective-permute-start(f32[64,128]{1,0:T(8,128)S(1)} %get-tuple-element.44), channel_id=1, source_target_pairs={{0,1},{1,0},{2,3},{3,2},{4,5},{5,4},{6,7},{7,6},{8,9},{9,8},{10,11... | collective-permute-start | bytes 98312 | tf_op jit(solution)/shard_map/ppermute | solution.py:342
  95.2 2.5 %collective-permute-start.15 = (f32[40,128]{1,0:T(8,128)S(1)}, f32[40,128]{1,0:T(8,128)S(1)}, u32[]{:S(2)}, u32[]{:S(2)}) collective-permute-start(f32[40,128]{1,0:T(8,128)S(1)} %pair_sums.1.held), channel_id=1, source_target_pairs={{0,1},{1,0},{2,3},{3,2},{4,5},{5,4},{6,7},{7,6},{8,9},{9,8},{10,11... | collective-permute-start | bytes 61448 | tf_op jit(solution)/shard_map/ppermute | solution.py:342
  99.5 3.6 %collective-permute-start.18 = (f32[136,128]{1,0:T(8,128)S(1)}, f32[136,128]{1,0:T(8,128)S(1)}, u32[]{:S(2)}, u32[]{:S(2)}) collective-permute-start(f32[136,128]{1,0:T(8,128)S(1)} %get-tuple-element.49.own), channel_id=1, source_target_pairs={{0,48},{16,0},{32,16},{48,32},{1,49},{17,1},{33,17},{49,33},{2,50}... | collective-permute-start | bytes 208904 | tf_op jit(solution)/shard_map/ppermute | solution.py:329
  101.7 6.5 %collective-permute-start.17 = (f32[136,128]{1,0:T(8,128)S(1)}, f32[136,128]{1,0:T(8,128)S(1)}, u32[]{:S(2)}, u32[]{:S(2)}) collective-permute-start(f32[136,128]{1,0:T(8,128)S(1)} %get-tuple-element.49.own), channel_id=1, source_target_pairs={{0,16},{16,32},{32,48},{48,0},{1,17},{17,33},{33,49},{49,1},{2,18}... | collective-permute-start | bytes 208904 | tf_op jit(solution)/shard_map/ppermute | solution.py:329
  101.7 6.5 %collective-permute-start.16 = (f32[136,128]{1,0:T(8,128)S(1)}, f32[136,128]{1,0:T(8,128)S(1)}, u32[]{:S(2)}, u32[]{:S(2)}) collective-permute-start(f32[136,128]{1,0:T(8,128)S(1)} %get-tuple-element.49.own), channel_id=1, source_target_pairs={{0,32},{16,48},{32,0},{48,16},{1,33},{17,49},{33,1},{49,17},{2,34}... | collective-permute-start | bytes 208904 | tf_op jit(solution)/shard_map/ppermute | solution.py:329
  108.2 4.0 %collective-permute-start.21 = (f32[136,128]{1,0:T(8,128)S(1)}, f32[136,128]{1,0:T(8,128)S(1)}, u32[]{:S(2)}, u32[]{:S(2)}) collective-permute-start(f32[136,128]{1,0:T(8,128)S(1)} %sums.3.own), channel_id=1, source_target_pairs={{0,192},{64,0},{128,64},{192,128},{1,193},{65,1},{129,65},{193,129... | collective-permute-start | bytes 208904 | tf_op jit(solution)/shard_map/ppermute | solution.py:329
  110.9 5.1 %collective-permute-start.20 = (f32[136,128]{1,0:T(8,128)S(1)}, f32[136,128]{1,0:T(8,128)S(1)}, u32[]{:S(2)}, u32[]{:S(2)}) collective-permute-start(f32[136,128]{1,0:T(8,128)S(1)} %sums.3.own), channel_id=1, source_target_pairs={{0,64},{64,128},{128,192},{192,0},{1,65},{65,129},{129,193},{193,1... | collective-permute-start | bytes 208904 | tf_op jit(solution)/shard_map/ppermute | solution.py:329
  110.9 5.1 %collective-permute-start.19 = (f32[136,128]{1,0:T(8,128)S(1)}, f32[136,128]{1,0:T(8,128)S(1)}, u32[]{:S(2)}, u32[]{:S(2)}) collective-permute-start(f32[136,128]{1,0:T(8,128)S(1)} %sums.3.own), channel_id=1, source_target_pairs={{0,128},{64,192},{128,0},{192,64},{1,129},{65,193},{129,1},{193,65... | collective-permute-start | bytes 208904 | tf_op jit(solution)/shard_map/ppermute | solution.py:329

commit v5 on v4

--- a/solution.py
+++ b/solution.py
@@ -99,7 +99,7 @@
 
 
 def sum_four(refs, rows):
-    own, opposite, right, left = (ref[rows, :] for ref in refs)
+    own, right, left, opposite = (ref[rows, :] for ref in refs)
     return (own + opposite) + (right + left)
 
 
@@ -141,8 +141,8 @@
     duals[...] = jnp.broadcast_to(start[...][None], duals.shape)
 
 
-def x_sums(own, opposite, right, left, payload):
-    four = (own, opposite, right, left)
+def x_sums(own, right, left, opposite, payload):
+    four = (own, right, left, opposite)
     payload[0:COL_BLOCKS, :] = sum_four(four, slice(0, COL_BLOCKS))
     share = 3 * COLS_SHARE
     for k, ref in enumerate(four):
@@ -150,8 +150,8 @@
         payload[first : first + share, :] = ref[COL_BLOCKS : COL_BLOCKS + share, :]
 
 
-def sums(own, opposite, right, left, total):
-    total[...] = sum_four((own, opposite, right, left), slice(None))
+def sums(own, right, left, opposite, total):
+    total[...] = sum_four((own, right, left, opposite), slice(None))
 
 
 def image_copies(kept, received, side, copies):
@@ -216,17 +216,17 @@
 
 
 def first_forward(
-    table, own, opposite, right, left, pairs, kept, given, primal, start, cost, free, extended, total
+    table, own, right, left, opposite, pairs, kept, given, primal, start, cost, free, extended, total
 ):
     y, x = table[AT_Y, 0], table[AT_X, 0]
-    for j, (ref, dy) in enumerate(((own, 0), (opposite, 2), (right, 3), (left, 1))):
-        for k, dx in enumerate((0, 2, 3, 1)):
+    for j, (ref, dy) in enumerate(((own, 0), (right, 3), (left, 1), (opposite, 2))):
+        for k, dx in enumerate((0, 3, 1, 2)):
             device = ((y + dy) & 3) * 4 + ((x + dx) & 3)
             block = pl.ds(pl.multiple_of(device * COLS_SHARE, COLS_SHARE), COLS_SHARE)
             for m, out in enumerate((start, cost, free)):
                 first = COL_BLOCKS + (3 * k + m) * COLS_SHARE
                 out[block, :] = ref[first : first + COLS_SHARE, :]
-    gradient = sum_four((own, opposite, right, left), slice(0, COL_BLOCKS))
+    gradient = sum_four((own, right, left, opposite), slice(0, COL_BLOCKS))
     primal[...] = clamp_primal(start[...] - 0.4 * (cost[...] - gradient), free[...])
     extended[...] = 2.0 * primal[...] - start[...]
     forward_product(table, lambda slot: pairs[slot], [extended], total)
@@ -251,9 +251,9 @@
 
 
 def second_forward(
-    table, own, opposite, right, left, before, cost, free, pairs, kept, given, primal, gradient, primal_mine, extended, total
-):
-    gradient[...] = sum_four((own, opposite, right, left), slice(0, COL_BLOCKS))
+    table, own, right, left, opposite, before, cost, free, pairs, kept, given, primal, gradient, primal_mine, extended, total
+):
+    gradient[...] = sum_four((own, right, left, opposite), slice(0, COL_BLOCKS))
     primal[...] = clamp_primal(before[...] - 0.4 * (cost[...] - gradient[...]), free[...])
     extended[...] = 2.0 * primal[...] - before[...]
     primal_mine[...] = primal[
@@ -290,8 +290,8 @@
     payload[COL_BLOCKS : COL_BLOCKS + 8, :] = jnp.concatenate(terms + terms, 0)
 
 
-def column_terms(own, opposite, right, left, earlier, before, primal, cost, free, terms):
-    four = (own, opposite, right, left)
+def column_terms(own, right, left, opposite, earlier, before, primal, cost, free, terms):
+    four = (own, right, left, opposite)
     adjoint = sum_four(four, slice(0, COL_BLOCKS))
     row_terms = sum_four(four, slice(COL_BLOCKS, COL_BLOCKS + 8))
     price, kind = cost[...], free[...]
@@ -330,7 +330,7 @@
 
 
 def four_of(values, axis):
-    return values, shift(values, axis, 2), shift(values, axis, 1), shift(values, axis, -1)
+    return values, shift(values, axis, 1), shift(values, axis, -1), shift(values, axis, 2)
 
 
 def four_over_row(values):

time: 129 us -> 125 us (0.969)
  starting transfers between devices: 31.3 us -> 26.3 us
  blocking collectives: 52.2 us -> 53.6 us
    ppermute x18, starting transfers between devices: 22.7 us -> 16.6 us  [shift(): return lax.ppermute(values, axis, [(k, (k + step) % 4) for k in range(4)])]
    all_to_all x4, blocking collectives: 52.2 us -> 53.6 us  [exchange(): return lax.all_to_all(copies, axes, 0, 0)]
  transfers between devices with their start and end apart: 22 -> 22, of which waited for: 16 -> 18; matrix products, arithmetic and copies ran while one was open for 0% -> 0% of each run, Pallas kernels for 0% -> 0%
where the time goes in v5:
time: 125 us
  blocking collectives  53.6 us (43%)
  waiting for transfers between devices  29.7 us (24%)
  starting transfers between devices  26.3 us (21%)
  Pallas kernels  12.9 us (10%)
  between operations  1.52 us (1%)
    all_to_all x4, blocking collectives, exchange(): return lax.all_to_all(copies, axes, 0, 0)  53.6 us
    ppermute x18, waiting for transfers between devices, shift(): return lax.ppermute(values, axis, [(k, (k + step) % 4) for k in range(4)])  26.3 us
    ppermute x18, starting transfers between devices, shift(): return lax.ppermute(values, axis, [(k, (k + step) % 4) for k in range(4)])  16.6 us
    pallas_call x15, Pallas kernels, call(): pl.pallas_call(kernel, name=name, out_shape=shapes, in_specs=[SMEM] * sme...  12.9 us
    ppermute x4, starting transfers between devices, swap_cores(): return lax.ppermute(values, 'core', [(0, 1), (1, 0)])  9.74 us
    ppermute x4, waiting for transfers between devices, swap_cores(): return lax.ppermute(values, 'core', [(0, 1), (1, 0)])  3.42 us
  transfers between devices with their start and end apart: 22, of which 18 were waited for; matrix products, arithmetic and copies ran while one was open for 0% of the time, Pallas kernels for 0%

profile of v5, /device:TPU:1, one launch (start us, length us, event | category | flops | bytes accessed | tf_op | source)
XLA Modules:
  0.0 124.8 jit_solution(7802372106526629172)
XLA Ops:
  2.8 17.4 %all_to_all.20.duals = f32[16,4,128]{2,1,0:T(4,128)S(1)} all-to-all(f32[16,4,128]{2,1,0:T(4,128)} %get-tuple-element.30), channel_id=1, replica_groups=mesh['y'=4,'x'=4,'z'=8,'core'=2] {'z','core'}, dimensions={0} | all-to-all | bytes 65536 | tf_op jit(solution)/shard_map/all_to_all | solution.py:346
  20.9 2.8 %first_adjoint.1 = (f32[152,128]{1,0:T(8,128)S(1)}, f32[64,128]{1,0:T(8,128)S(1)}, s32[8,128]{1,0:T(8,128)S(1)}, bf16[64,256,128]{2,1,0:T(8,128)(2,1)S(1)}) custom-call(f32[64,128,128]{2,1,0:T(8,128)} %bitcast.3, f32[16,4,128]{2,1,0:T(4,128)S(1)} %all_to_all.20.duals, f32[40,128]{1,0:T(8,128)S(1)} %copy-done), custom_call_target="tpu_custom_call" | custom-call | tf_op jit(solution)/shard_map/first_adjoint/pallas_call | solution.py:34
  23.7 2.8 %collective-permute-start.2 = (f32[152,128]{1,0:T(8,128)S(1)}, f32[152,128]{1,0:T(8,128)S(1)}, u32[]{:S(2)}, u32[]{:S(2)}) collective-permute-start(f32[152,128]{1,0:T(8,128)S(1)} %get-tuple-element.33.own), channel_id=1, source_target_pairs={{0,32},{16,48},{32,0},{48,16},{1,33},{17,49},{33,1},{49,17},{2,34}... | collective-permute-start | bytes 233480 | tf_op jit(solution)/shard_map/ppermute | solution.py:329
  28.5 2.3 %collective-permute-done.1.left = f32[152,128]{1,0:T(8,128)S(1)} collective-permute-done((f32[152,128]{1,0:T(8,128)S(1)}, f32[152,128]{1,0:T(8,128)S(1)}, u32[]{:S(2)}, u32[]{:S(2)}) %collective-permute-start.1) | collective-permute-done | bytes 77856 | tf_op jit(solution)/shard_map/ppermute | solution.py:329
  31.9 3.0 %collective-permute-start.5 = (f32[224,128]{1,0:T(8,128)S(1)}, f32[224,128]{1,0:T(8,128)S(1)}, u32[]{:S(2)}, u32[]{:S(2)}) collective-permute-start(f32[224,128]{1,0:T(8,128)S(1)} %x_sums.1.own), channel_id=1, source_target_pairs={{0,128},{64,192},{128,0},{192,64},{1,129},{65,193},{129,1},{193,65... | collective-permute-start | bytes 344072 | tf_op jit(solution)/shard_map/ppermute | solution.py:329
  37.1 1.9 %collective-permute-done.4.left = f32[224,128]{1,0:T(8,128)S(1)} collective-permute-done((f32[224,128]{1,0:T(8,128)S(1)}, f32[224,128]{1,0:T(8,128)S(1)}, u32[]{:S(2)}, u32[]{:S(2)}) %collective-permute-start.4) | collective-permute-done | bytes 114720 | tf_op jit(solution)/shard_map/ppermute | solution.py:329
  39.0 2.3 %collective-permute-done.3.right = f32[224,128]{1,0:T(8,128)S(1)} collective-permute-done((f32[224,128]{1,0:T(8,128)S(1)}, f32[224,128]{1,0:T(8,128)S(1)}, u32[]{:S(2)}, u32[]{:S(2)}) %collective-permute-start.3) | collective-permute-done | bytes 114720 | tf_op jit(solution)/shard_map/ppermute | solution.py:329
  41.3 2.3 %first_forward.1 = (f32[32,128]{1,0:T(8,128)S(1)}, f32[32,128]{1,0:T(8,128)S(1)}, f32[128,128]{1,0:T(8,128)S(1)}, f32[128,128]{1,0:T(8,128)}, f32[128,128]{1,0:T(8,128)S(1)}, /*index=5*/f32[128,128]{1,0:T(8,128)S(1)}) custom-call(s32[8,128]{1,0:T(8,128)S(1)} %get-tuple-element.32.table, f32[224,128]{1,0:T(8,128)S(1)} %x_sums.1.own, ...), custom_call_target="tpu_custom_call" | custom-call | tf_op jit(solution)/shard_map/first_forward/pallas_call | solution.py:34
  43.5 3.0 %collective-permute-start.6 = (f32[32,128]{1,0:T(8,128)S(1)}, f32[32,128]{1,0:T(8,128)S(1)}, u32[]{:S(2)}, u32[]{:S(2)}) collective-permute-start(f32[32,128]{1,0:T(8,128)S(1)} %get-tuple-element.36), channel_id=1, source_target_pairs={{0,1},{1,0},{2,3},{3,2},{4,5},{5,4},{6,7},{7,6},{8,9},{9,8},{10,11... | collective-permute-start | bytes 49160 | tf_op jit(solution)/shard_map/ppermute | solution.py:342
  47.4 11.6 %all_to_all.21.pieces = f32[8,40,128]{2,1,0:T(8,128)S(1)} all-to-all(f32[8,40,128]{2,1,0:T(8,128)S(1)} %image_copies.1), channel_id=1, replica_groups=mesh['y'=4,'x'=4,'z'=8,'core'=2] {'z'}, dimensions={0} | all-to-all | bytes 327680 | tf_op jit(solution)/shard_map/all_to_all | solution.py:346
  59.0 1.6 %collective-permute-start.7 = (f32[96,128]{1,0:T(8,128)S(1)}, f32[96,128]{1,0:T(8,128)S(1)}, u32[]{:S(2)}, u32[]{:S(2)}) collective-permute-start(f32[96,128]{1,0:T(8,128)S(1)} %image_sums.1.held), channel_id=1, source_target_pairs={{0,1},{1,0},{2,3},{3,2},{4,5},{5,4},{6,7},{7,6},{8,9},{9,8},{10,11... | collective-permute-start | bytes 147464 | tf_op jit(solution)/shard_map/ppermute | solution.py:342
  64.9 2.6 %collective-permute-done.10.opposite = f32[128,128]{1,0:T(8,128)S(1)} collective-permute-done((f32[128,128]{1,0:T(8,128)S(1)}, f32[128,128]{1,0:T(8,128)S(1)}, u32[]{:S(2)}, u32[]{:S(2)}) %collective-permute-start.10) | collective-permute-done | bytes 65568 | tf_op jit(solution)/shard_map/ppermute | solution.py:329
  67.6 1.5 %collective-permute-done.8.right = f32[128,128]{1,0:T(8,128)S(1)} collective-permute-done((f32[128,128]{1,0:T(8,128)S(1)}, f32[128,128]{1,0:T(8,128)S(1)}, u32[]{:S(2)}, u32[]{:S(2)}) %collective-permute-start.8) | collective-permute-done | bytes 65568 | tf_op jit(solution)/shard_map/ppermute | solution.py:329
  71.7 2.1 %collective-permute-done.13.opposite = f32[128,128]{1,0:T(8,128)S(1)} collective-permute-done((f32[128,128]{1,0:T(8,128)S(1)}, f32[128,128]{1,0:T(8,128)S(1)}, u32[]{:S(2)}, u32[]{:S(2)}) %collective-permute-start.13) | collective-permute-done | bytes 65568 | tf_op jit(solution)/shard_map/ppermute | solution.py:329
  73.8 2.2 %collective-permute-done.11.right = f32[128,128]{1,0:T(8,128)S(1)} collective-permute-done((f32[128,128]{1,0:T(8,128)S(1)}, f32[128,128]{1,0:T(8,128)S(1)}, u32[]{:S(2)}, u32[]{:S(2)}) %collective-permute-start.11) | collective-permute-done | bytes 65568 | tf_op jit(solution)/shard_map/ppermute | solution.py:329
  76.0 2.3 %second_forward.1 = (f32[64,128]{1,0:T(8,128)S(1)}, f32[64,128]{1,0:T(8,128)S(1)}, f32[128,128]{1,0:T(8,128)S(1)}, f32[128,128]{1,0:T(8,128)S(1)}, f32[8,128]{1,0:T(8,128)}) custom-call(s32[8,128]{1,0:T(8,128)S(1)} %get-tuple-element.32.table, f32[128,128]{1,0:T(8,128)S(1)} %sums.2.own, f32[128,128]{1,0:T(8,128)S(1)} %collective-permute-done.11.right, ...), custom_call_target="tpu_custom_call" | custom-call | tf_op jit(solution)/shard_map/second_forward/pallas_call | solution.py:34
  78.3 3.5 %collective-permute-start.14 = (f32[64,128]{1,0:T(8,128)S(1)}, f32[64,128]{1,0:T(8,128)S(1)}, u32[]{:S(2)}, u32[]{:S(2)}) collective-permute-start(f32[64,128]{1,0:T(8,128)S(1)} %get-tuple-element.44), channel_id=1, source_target_pairs={{0,1},{1,0},{2,3},{3,2},{4,5},{5,4},{6,7},{7,6},{8,9},{9,8},{10,11... | collective-permute-start | bytes 98312 | tf_op jit(solution)/shard_map/ppermute | solution.py:342
  82.6 11.6 %all_to_all.22.pieces = f32[8,40,128]{2,1,0:T(8,128)S(1)} all-to-all(f32[8,40,128]{2,1,0:T(8,128)S(1)} %pair_copies.1), channel_id=1, replica_groups=mesh['y'=4,'x'=4,'z'=8,'core'=2] {'z'}, dimensions={0} | all-to-all | bytes 327680 | tf_op jit(solution)/shard_map/all_to_all | solution.py:346
  94.2 1.6 %collective-permute-start.15 = (f32[40,128]{1,0:T(8,128)S(1)}, f32[40,128]{1,0:T(8,128)S(1)}, u32[]{:S(2)}, u32[]{:S(2)}) collective-permute-start(f32[40,128]{1,0:T(8,128)S(1)} %pair_sums.1.held), channel_id=1, source_target_pairs={{0,1},{1,0},{2,3},{3,2},{4,5},{5,4},{6,7},{7,6},{8,9},{9,8},{10,11... | collective-permute-start | bytes 61448 | tf_op jit(solution)/shard_map/ppermute | solution.py:342
  96.7 1.8 %third_adjoint.1 = (f32[136,128]{1,0:T(8,128)S(1)}, f32[4,128]{1,0:T(4,128)}) custom-call(s32[8,128]{1,0:T(8,128)S(1)} %get-tuple-element.32.table, f32[40,128]{1,0:T(8,128)S(1)} %pair_sums.1.held, f32[40,128]{1,0:T(8,128)S(1)} %collective-permute-done.15.other, f32[64,128]{1,0:T(8,128)S(1)} %get-tuple-element.45.before, ...), custom_call_target="tpu_custom_call" | custom-call | tf_op jit(solution)/shard_map/third_adjoint/pallas_call | solution.py:34
  100.0 3.1 %collective-permute-done.18.opposite = f32[136,128]{1,0:T(8,128)S(1)} collective-permute-done((f32[136,128]{1,0:T(8,128)S(1)}, f32[136,128]{1,0:T(8,128)S(1)}, u32[]{:S(2)}, u32[]{:S(2)}) %collective-permute-start.18) | collective-permute-done | bytes 69664 | tf_op jit(solution)/shard_map/ppermute | solution.py:329
  103.1 1.5 %collective-permute-done.16.right = f32[136,128]{1,0:T(8,128)S(1)} collective-permute-done((f32[136,128]{1,0:T(8,128)S(1)}, f32[136,128]{1,0:T(8,128)S(1)}, u32[]{:S(2)}, u32[]{:S(2)}) %collective-permute-start.16) | collective-permute-done | bytes 69664 | tf_op jit(solution)/shard_map/ppermute | solution.py:329
  106.4 3.1 %collective-permute-done.21.opposite = f32[136,128]{1,0:T(8,128)S(1)} collective-permute-done((f32[136,128]{1,0:T(8,128)S(1)}, f32[136,128]{1,0:T(8,128)S(1)}, u32[]{:S(2)}, u32[]{:S(2)}) %collective-permute-start.21) | collective-permute-done | bytes 69664 | tf_op jit(solution)/shard_map/ppermute | solution.py:329
  110.9 13.1 %all_to_all.23.gathered = f32[16,1,128]{2,1,0:T(1,128)S(1)} all-to-all(f32[16,1,128]{2,1,0:T(1,128)S(1)} %column_terms.1), channel_id=1, replica_groups=mesh['y'=4,'x'=4,'z'=8,'core'=2] {'z','core'}, dimensions={0} | all-to-all | bytes 16384 | tf_op jit(solution)/shard_map/all_to_all | solution.py:346
  (41 shorter events, 22.2 us)
Async XLA Ops:
  20.2 0.7 copy-start
  23.7 4.8 %collective-permute-start.2 = (f32[152,128]{1,0:T(8,128)S(1)}, f32[152,128]{1,0:T(8,128)S(1)}, u32[]{:S(2)}, u32[]{:S(2)}) collective-permute-start(f32[152,128]{1,0:T(8,128)S(1)} %get-tuple-element.33.own), channel_id=1, source_target_pairs={{0,32},{16,48},{32,0},{48,16},{1,33},{17,49},{33,1},{49,17},{2,34}... | collective-permute-start | bytes 233480 | tf_op jit(solution)/shard_map/ppermute | solution.py:329
  26.5 4.3 %collective-permute-start.1 = (f32[152,128]{1,0:T(8,128)S(1)}, f32[152,128]{1,0:T(8,128)S(1)}, u32[]{:S(2)}, u32[]{:S(2)}) collective-permute-start(f32[152,128]{1,0:T(8,128)S(1)} %get-tuple-element.33.own), channel_id=1, source_target_pairs={{0,48},{16,0},{32,16},{48,32},{1,49},{17,1},{33,17},{49,33},{2,50}... | collective-permute-start | bytes 233480 | tf_op jit(solution)/shard_map/ppermute | solution.py:329
  27.4 4.5 %collective-permute-start = (f32[152,128]{1,0:T(8,128)S(1)}, f32[152,128]{1,0:T(8,128)S(1)}, u32[]{:S(2)}, u32[]{:S(2)}) collective-permute-start(f32[152,128]{1,0:T(8,128)S(1)} %get-tuple-element.33.own), channel_id=1, source_target_pairs={{0,16},{16,32},{32,48},{48,0},{1,17},{17,33},{33,49},{49,1},{2,18}... | collective-permute-start | bytes 233480 | tf_op jit(solution)/shard_map/ppermute | solution.py:329
  31.9 5.2 %collective-permute-start.5 = (f32[224,128]{1,0:T(8,128)S(1)}, f32[224,128]{1,0:T(8,128)S(1)}, u32[]{:S(2)}, u32[]{:S(2)}) collective-permute-start(f32[224,128]{1,0:T(8,128)S(1)} %x_sums.1.own), channel_id=1, source_target_pairs={{0,128},{64,192},{128,0},{192,64},{1,129},{65,193},{129,1},{193,65... | collective-permute-start | bytes 344072 | tf_op jit(solution)/shard_map/ppermute | solution.py:329
  34.9 4.1 %collective-permute-start.4 = (f32[224,128]{1,0:T(8,128)S(1)}, f32[224,128]{1,0:T(8,128)S(1)}, u32[]{:S(2)}, u32[]{:S(2)}) collective-permute-start(f32[224,128]{1,0:T(8,128)S(1)} %x_sums.1.own), channel_id=1, source_target_pairs={{0,192},{64,0},{128,64},{192,128},{1,193},{65,1},{129,65},{193,129... | collective-permute-start | bytes 344072 | tf_op jit(solution)/shard_map/ppermute | solution.py:329
  35.6 5.6 %collective-permute-start.3 = (f32[224,128]{1,0:T(8,128)S(1)}, f32[224,128]{1,0:T(8,128)S(1)}, u32[]{:S(2)}, u32[]{:S(2)}) collective-permute-start(f32[224,128]{1,0:T(8,128)S(1)} %x_sums.1.own), channel_id=1, source_target_pairs={{0,64},{64,128},{128,192},{192,0},{1,65},{65,129},{129,193},{193,1... | collective-permute-start | bytes 344072 | tf_op jit(solution)/shard_map/ppermute | solution.py:329
  43.5 3.9 %collective-permute-start.6 = (f32[32,128]{1,0:T(8,128)S(1)}, f32[32,128]{1,0:T(8,128)S(1)}, u32[]{:S(2)}, u32[]{:S(2)}) collective-permute-start(f32[32,128]{1,0:T(8,128)S(1)} %get-tuple-element.36), channel_id=1, source_target_pairs={{0,1},{1,0},{2,3},{3,2},{4,5},{5,4},{6,7},{7,6},{8,9},{9,8},{10,11... | collective-permute-start | bytes 49160 | tf_op jit(solution)/shard_map/ppermute | solution.py:342
  59.0 2.5 %collective-permute-start.7 = (f32[96,128]{1,0:T(8,128)S(1)}, f32[96,128]{1,0:T(8,128)S(1)}, u32[]{:S(2)}, u32[]{:S(2)}) collective-permute-start(f32[96,128]{1,0:T(8,128)S(1)} %image_sums.1.held), channel_id=1, source_target_pairs={{0,1},{1,0},{2,3},{3,2},{4,5},{5,4},{6,7},{7,6},{8,9},{9,8},{10,11... | collective-permute-start | bytes 147464 | tf_op jit(solution)/shard_map/ppermute | solution.py:342
  62.8 4.7 %collective-permute-start.10 = (f32[128,128]{1,0:T(8,128)S(1)}, f32[128,128]{1,0:T(8,128)S(1)}, u32[]{:S(2)}, u32[]{:S(2)}) collective-permute-start(f32[128,128]{1,0:T(8,128)S(1)} %get-tuple-element.38.own), channel_id=1, source_target_pairs={{0,32},{16,48},{32,0},{48,16},{1,33},{17,49},{33,1},{49,17},{2,34}... | collective-permute-start | bytes 196616 | tf_op jit(solution)/shard_map/ppermute | solution.py:329
  63.4 4.1 %collective-permute-start.9 = (f32[128,128]{1,0:T(8,128)S(1)}, f32[128,128]{1,0:T(8,128)S(1)}, u32[]{:S(2)}, u32[]{:S(2)}) collective-permute-start(f32[128,128]{1,0:T(8,128)S(1)} %get-tuple-element.38.own), channel_id=1, source_target_pairs={{0,48},{16,0},{32,16},{48,32},{1,49},{17,1},{33,17},{49,33},{2,50}... | collective-permute-start | bytes 196616 | tf_op jit(solution)/shard_map/ppermute | solution.py:329
  64.7 4.4 %collective-permute-start.8 = (f32[128,128]{1,0:T(8,128)S(1)}, f32[128,128]{1,0:T(8,128)S(1)}, u32[]{:S(2)}, u32[]{:S(2)}) collective-permute-start(f32[128,128]{1,0:T(8,128)S(1)} %get-tuple-element.38.own), channel_id=1, source_target_pairs={{0,16},{16,32},{32,48},{48,0},{1,17},{17,33},{33,49},{49,1},{2,18}... | collective-permute-start | bytes 196616 | tf_op jit(solution)/shard_map/ppermute | solution.py:329
  69.1 4.7 %collective-permute-start.13 = (f32[128,128]{1,0:T(8,128)S(1)}, f32[128,128]{1,0:T(8,128)S(1)}, u32[]{:S(2)}, u32[]{:S(2)}) collective-permute-start(f32[128,128]{1,0:T(8,128)S(1)} %sums.2.own), channel_id=1, source_target_pairs={{0,128},{64,192},{128,0},{192,64},{1,129},{65,193},{129,1},{193,65... | collective-permute-start | bytes 196616 | tf_op jit(solution)/shard_map/ppermute | solution.py:329
  70.2 3.6 %collective-permute-start.12 = (f32[128,128]{1,0:T(8,128)S(1)}, f32[128,128]{1,0:T(8,128)S(1)}, u32[]{:S(2)}, u32[]{:S(2)}) collective-permute-start(f32[128,128]{1,0:T(8,128)S(1)} %sums.2.own), channel_id=1, source_target_pairs={{0,192},{64,0},{128,64},{192,128},{1,193},{65,1},{129,65},{193,129... | collective-permute-start | bytes 196616 | tf_op jit(solution)/shard_map/ppermute | solution.py:329
  71.3 4.6 %collective-permute-start.11 = (f32[128,128]{1,0:T(8,128)S(1)}, f32[128,128]{1,0:T(8,128)S(1)}, u32[]{:S(2)}, u32[]{:S(2)}) collective-permute-start(f32[128,128]{1,0:T(8,128)S(1)} %sums.2.own), channel_id=1, source_target_pairs={{0,64},{64,128},{128,192},{192,0},{1,65},{65,129},{129,193},{193,1... | collective-permute-start | bytes 196616 | tf_op jit(solution)/shard_map/ppermute | solution.py:329
  78.3 4.3 %collective-permute-start.14 = (f32[64,128]{1,0:T(8,128)S(1)}, f32[64,128]{1,0:T(8,128)S(1)}, u32[]{:S(2)}, u32[]{:S(2)}) collective-permute-start(f32[64,128]{1,0:T(8,128)S(1)} %get-tuple-element.44), channel_id=1, source_target_pairs={{0,1},{1,0},{2,3},{3,2},{4,5},{5,4},{6,7},{7,6},{8,9},{9,8},{10,11... | collective-permute-start | bytes 98312 | tf_op jit(solution)/shard_map/ppermute | solution.py:342
  94.2 2.5 %collective-permute-start.15 = (f32[40,128]{1,0:T(8,128)S(1)}, f32[40,128]{1,0:T(8,128)S(1)}, u32[]{:S(2)}, u32[]{:S(2)}) collective-permute-start(f32[40,128]{1,0:T(8,128)S(1)} %pair_sums.1.held), channel_id=1, source_target_pairs={{0,1},{1,0},{2,3},{3,2},{4,5},{5,4},{6,7},{7,6},{8,9},{9,8},{10,11... | collective-permute-start | bytes 61448 | tf_op jit(solution)/shard_map/ppermute | solution.py:342
  98.5 4.7 %collective-permute-start.18 = (f32[136,128]{1,0:T(8,128)S(1)}, f32[136,128]{1,0:T(8,128)S(1)}, u32[]{:S(2)}, u32[]{:S(2)}) collective-permute-start(f32[136,128]{1,0:T(8,128)S(1)} %get-tuple-element.49.own), channel_id=1, source_target_pairs={{0,32},{16,48},{32,0},{48,16},{1,33},{17,49},{33,1},{49,17},{2,34}... | collective-permute-start | bytes 208904 | tf_op jit(solution)/shard_map/ppermute | solution.py:329
  98.5 4.7 %collective-permute-start.17 = (f32[136,128]{1,0:T(8,128)S(1)}, f32[136,128]{1,0:T(8,128)S(1)}, u32[]{:S(2)}, u32[]{:S(2)}) collective-permute-start(f32[136,128]{1,0:T(8,128)S(1)} %get-tuple-element.49.own), channel_id=1, source_target_pairs={{0,48},{16,0},{32,16},{48,32},{1,49},{17,1},{33,17},{49,33},{2,50}... | collective-permute-start | bytes 208904 | tf_op jit(solution)/shard_map/ppermute | solution.py:329
  100.0 4.7 %collective-permute-start.16 = (f32[136,128]{1,0:T(8,128)S(1)}, f32[136,128]{1,0:T(8,128)S(1)}, u32[]{:S(2)}, u32[]{:S(2)}) collective-permute-start(f32[136,128]{1,0:T(8,128)S(1)} %get-tuple-element.49.own), channel_id=1, source_target_pairs={{0,16},{16,32},{32,48},{48,0},{1,17},{17,33},{33,49},{49,1},{2,18}... | collective-permute-start | bytes 208904 | tf_op jit(solution)/shard_map/ppermute | solution.py:329
  104.7 4.8 %collective-permute-start.21 = (f32[136,128]{1,0:T(8,128)S(1)}, f32[136,128]{1,0:T(8,128)S(1)}, u32[]{:S(2)}, u32[]{:S(2)}) collective-permute-start(f32[136,128]{1,0:T(8,128)S(1)} %sums.3.own), channel_id=1, source_target_pairs={{0,128},{64,192},{128,0},{192,64},{1,129},{65,193},{129,1},{193,65... | collective-permute-start | bytes 208904 | tf_op jit(solution)/shard_map/ppermute | solution.py:329
  104.8 4.7 %collective-permute-start.20 = (f32[136,128]{1,0:T(8,128)S(1)}, f32[136,128]{1,0:T(8,128)S(1)}, u32[]{:S(2)}, u32[]{:S(2)}) collective-permute-start(f32[136,128]{1,0:T(8,128)S(1)} %sums.3.own), channel_id=1, source_target_pairs={{0,192},{64,0},{128,64},{192,128},{1,193},{65,1},{129,65},{193,129... | collective-permute-start | bytes 208904 | tf_op jit(solution)/shard_map/ppermute | solution.py:329
  106.3 4.4 %collective-permute-start.19 = (f32[136,128]{1,0:T(8,128)S(1)}, f32[136,128]{1,0:T(8,128)S(1)}, u32[]{:S(2)}, u32[]{:S(2)}) collective-permute-start(f32[136,128]{1,0:T(8,128)S(1)} %sums.3.own), channel_id=1, source_target_pairs={{0,64},{64,128},{128,192},{192,0},{1,65},{65,129},{129,193},{193,1... | collective-permute-start | bytes 208904 | tf_op jit(solution)/shard_map/ppermute | solution.py:329

commit v6 on v5

--- a/solution.py
+++ b/solution.py
@@ -22,7 +22,8 @@
 F32, BF16 = jnp.float32, jnp.bfloat16
 
 SLOT_ROWS, SLOT_COLS, COUNT, AT_Y, AT_X, AT_Z, AT_CORE = range(7)
-COL_SIDE, ROW_SIDE, TABLE, SIDE = 0, 24, 32, 40
+COL_KINDS, COST, ROW_SIDE, TABLE, SIDE = 8, 16, 24, 32, 40
+STEP = 0.4
 
 VMEM = pl.BlockSpec(memory_space=pltpu.VMEM)
 SMEM = pl.BlockSpec(memory_space=pltpu.SMEM)
@@ -90,8 +91,9 @@
     return jnp.where(ineq > 0.5, jnp.maximum(values, 0.0), values)
 
 
-def index_row(table):
-    return table[AT_Y, 0] * 4 + table[AT_X, 0]
+def own_columns(table):
+    index = table[AT_Y, 0] * 4 + table[AT_X, 0]
+    return pl.ds(pl.multiple_of(index * COLS_SHARE, COLS_SHARE), COLS_SHARE)
 
 
 def index_col(table):
@@ -116,7 +118,7 @@
                 (rhs.at[0], side.at[ROW_SIDE : ROW_SIDE + ROWS_SHARE]),
                 (row_kinds.at[0], kinds.at[0:ROWS_SHARE]),
                 (primal.at[0], side.at[0:COLS_SHARE]),
-                (cost.at[0], side.at[COLS_SHARE : 2 * COLS_SHARE]),
+                (cost.at[0], side.at[COST:ROW_SIDE]),
                 (col_kinds.at[0], kinds.at[COLS_SHARE : 2 * COLS_SHARE]),
             )
         )
@@ -136,7 +138,7 @@
     for copy in copies:
         copy.wait()
     side[TABLE : TABLE + COUNT, 0:SLOTS] = places[...].astype(F32)
-    side[2 * COLS_SHARE : ROW_SIDE, :] = kinds[COLS_SHARE:, :].astype(F32)
+    side[COL_KINDS:COST, :] = kinds[COLS_SHARE:, :].astype(F32)
     side[ROW_SIDE + ROWS_SHARE : TABLE, :] = kinds[0:ROWS_SHARE, :].astype(F32)
     duals[...] = jnp.broadcast_to(start[...][None], duals.shape)
 
@@ -144,7 +146,7 @@
 def x_sums(own, right, left, opposite, payload):
     four = (own, right, left, opposite)
     payload[0:COL_BLOCKS, :] = sum_four(four, slice(0, COL_BLOCKS))
-    share = 3 * COLS_SHARE
+    share = 2 * COLS_SHARE
     for k, ref in enumerate(four):
         first = COL_BLOCKS + k * share
         payload[first : first + share, :] = ref[COL_BLOCKS : COL_BLOCKS + share, :]
@@ -197,7 +199,7 @@
     for k in range(N):
         dual[k * ROWS_SHARE : (k + 1) * ROWS_SHARE, :] = duals[k]
     total[...] = jnp.zeros_like(total)
-    payload[COL_BLOCKS:, :] = side[COL_SIDE:ROW_SIDE, :]
+    payload[COL_BLOCKS:, :] = side[0:COST, :]
     read.wait()
 
     def tile_pair(slot):
@@ -213,21 +215,23 @@
         adjoint_slots(table, tile_pair, dual, total, first, slots)
         first += slots
     payload[0:COL_BLOCKS, :] = total[:, 0, :]
+    mine = own_columns(table)
+    payload[mine, :] += side[0:COLS_SHARE, :] * (1.0 / STEP) - side[COST:ROW_SIDE, :]
 
 
 def first_forward(
-    table, own, right, left, opposite, pairs, kept, given, primal, start, cost, free, extended, total
+    table, own, right, left, opposite, pairs, kept, given, primal, start, free, extended, total
 ):
     y, x = table[AT_Y, 0], table[AT_X, 0]
     for j, (ref, dy) in enumerate(((own, 0), (right, 3), (left, 1), (opposite, 2))):
         for k, dx in enumerate((0, 3, 1, 2)):
             device = ((y + dy) & 3) * 4 + ((x + dx) & 3)
             block = pl.ds(pl.multiple_of(device * COLS_SHARE, COLS_SHARE), COLS_SHARE)
-            for m, out in enumerate((start, cost, free)):
-                first = COL_BLOCKS + (3 * k + m) * COLS_SHARE
+            for m, out in enumerate((start, free)):
+                first = COL_BLOCKS + (2 * k + m) * COLS_SHARE
                 out[block, :] = ref[first : first + COLS_SHARE, :]
-    gradient = sum_four((own, right, left, opposite), slice(0, COL_BLOCKS))
-    primal[...] = clamp_primal(start[...] - 0.4 * (cost[...] - gradient), free[...])
+    ascent = sum_four((own, right, left, opposite), slice(0, COL_BLOCKS))
+    primal[...] = clamp_primal(STEP * ascent, free[...])
     extended[...] = 2.0 * primal[...] - start[...]
     forward_product(table, lambda slot: pairs[slot], [extended], total)
     mine = pl.multiple_of(table[AT_CORE, 0] * HALF, HALF)
@@ -235,7 +239,7 @@
     given[...] = total[pl.ds(HALF - mine, HALF), 0, :]
 
 
-def second_adjoint(table, held, other, start, pairs, gradient, dual, rhs, ineq, image, total):
+def second_adjoint(table, held, other, start, side, pairs, gradient, dual, rhs, ineq, image, total):
     first = table[AT_CORE, 0] == 0
     mine, theirs = held[...], other[...]
     for core, half in enumerate((jnp.where(first, mine, theirs), jnp.where(first, theirs, mine))):
@@ -245,20 +249,19 @@
             share = slice(k * ROWS_SHARE, (k + 1) * ROWS_SHARE)
             rhs[block, :] = half[HALF : 2 * HALF][share]
             ineq[block, :] = half[2 * HALF :][share]
-    dual[...] = clamp_dual(start[...] + 0.4 * (rhs[...] - image[...]), ineq[...])
+    dual[...] = clamp_dual(start[...] + STEP * (rhs[...] - image[...]), ineq[...])
     adjoint_product(table, lambda slot: pairs[slot], dual, total)
     gradient[...] = total[:, 0, :]
+    gradient[own_columns(table), :] -= side[COST:ROW_SIDE, :]
 
 
 def second_forward(
-    table, own, right, left, opposite, before, cost, free, pairs, kept, given, primal, gradient, primal_mine, extended, total
-):
-    gradient[...] = sum_four((own, right, left, opposite), slice(0, COL_BLOCKS))
-    primal[...] = clamp_primal(before[...] - 0.4 * (cost[...] - gradient[...]), free[...])
+    table, own, right, left, opposite, before, free, pairs, kept, given, primal, ascent, primal_mine, extended, total
+):
+    ascent[...] = sum_four((own, right, left, opposite), slice(0, COL_BLOCKS))
+    primal[...] = clamp_primal(before[...] + STEP * ascent[...], free[...])
     extended[...] = 2.0 * primal[...] - before[...]
-    primal_mine[...] = primal[
-        pl.ds(pl.multiple_of(index_row(table) * COLS_SHARE, COLS_SHARE), COLS_SHARE), :
-    ]
+    primal_mine[...] = primal[own_columns(table), :]
     forward_product(table, lambda slot: pairs[slot], [extended, primal], total)
     mine = pl.multiple_of(table[AT_CORE, 0] * HALF, HALF)
     for k, part in enumerate((0, 4)):
@@ -268,15 +271,13 @@
 
 
 def third_adjoint(
-    table, held, other, before, rhs, ineq, pairs, payload, mine, dual, image, total
+    table, held, other, before, rhs, ineq, side, primal1, primal2, pairs, payload, mine, dual, image, total
 ):
     half = pl.multiple_of(table[AT_CORE, 0] * HALF, HALF)
     image[pl.ds(half, HALF), :] = held[0:HALF, :]
     image[pl.ds(HALF - half, HALF), :] = other[0:HALF, :]
-    dual[...] = clamp_dual(before[...] + 0.4 * (rhs[...] - image[...]), ineq[...])
+    dual[...] = clamp_dual(before[...] + STEP * (rhs[...] - image[...]), ineq[...])
     mine[...] = dual[pl.ds(index_col(table) * ROWS_SHARE, ROWS_SHARE), :]
-    adjoint_product(table, lambda slot: pairs[slot], dual, total)
-    payload[0:COL_BLOCKS, :] = total[:, 0, :]
     share = pl.ds(half + table[AT_Z, 0] * ROWS_SHARE, ROWS_SHARE)
     plain = held[HALF : HALF + ROWS_SHARE, :]
     bound, kind, last = rhs[share, :], ineq[share, :], dual[share, :]
@@ -285,29 +286,32 @@
         residual = bound - product
         residual = jnp.where(kind > 0.5, jnp.maximum(residual, 0.0), residual)
         terms.append(jnp.sum(residual * residual, 0, keepdims=True))
-    for value in (last, 0.5 * (before[share, :] + last)):
-        terms.append(jnp.sum(bound * value, 0, keepdims=True))
+    columns = own_columns(table)
+    price, final = side[COST:ROW_SIDE, :], primal2[columns, :]
+    for primal, value in (
+        (final, last),
+        (0.5 * (primal1[columns, :] + final), 0.5 * (before[share, :] + last)),
+    ):
+        gain = jnp.sum(price * primal, 0, keepdims=True)
+        terms.append(gain - jnp.sum(bound * value, 0, keepdims=True))
     payload[COL_BLOCKS : COL_BLOCKS + 8, :] = jnp.concatenate(terms + terms, 0)
-
-
-def column_terms(own, right, left, opposite, earlier, before, primal, cost, free, terms):
+    adjoint_product(table, lambda slot: pairs[slot], dual, total)
+    payload[0:COL_BLOCKS, :] = total[:, 0, :]
+    payload[columns, :] -= price
+
+
+def column_terms(own, right, left, opposite, earlier, free, terms):
     four = (own, right, left, opposite)
-    adjoint = sum_four(four, slice(0, COL_BLOCKS))
+    ascent = sum_four(four, slice(0, COL_BLOCKS))
     row_terms = sum_four(four, slice(COL_BLOCKS, COL_BLOCKS + 8))
-    price, kind = cost[...], free[...]
+    kind = free[...]
     squares, gaps = [], []
-    for k, (gradient, value) in enumerate(
-        (
-            (adjoint, primal[...]),
-            (0.5 * (earlier[...] + adjoint), 0.5 * (before[...] + primal[...])),
-        )
-    ):
-        low = jnp.minimum(price - gradient, 0.0)
+    for k, reduced in enumerate((-ascent, -0.5 * (earlier[...] + ascent))):
+        low = jnp.minimum(reduced, 0.0)
         violation = jnp.where(kind > 0.5, low, 0.0)
         box = jnp.where(kind > 0.5, 0.0, low)
         squares.append(jnp.sum(violation * violation, 0, keepdims=True))
-        column = jnp.sum(price * value, 0, keepdims=True) - jnp.sum(box, 0, keepdims=True)
-        gaps.append(column - row_terms[2 + k : 3 + k])
+        gaps.append(row_terms[2 + k : 3 + k] - jnp.sum(box, 0, keepdims=True))
     rows = jnp.concatenate([row_terms[0:2]] + squares + gaps + squares, 0)
     sums = jnp.broadcast_to(jnp.sum(rows, 1, keepdims=True), rows.shape)
     places = [lax.broadcasted_iota(jnp.int32, rows.shape, k) for k in range(2)]
@@ -374,7 +378,7 @@
         first_adjoint,
         "first_adjoint",
         [
-            ((COL_BLOCKS + 3 * COLS_SHARE, TILE), F32),
+            ((COL_BLOCKS + 2 * COLS_SHARE, TILE), F32),
             (blocks, F32),
             ((8, TILE), jnp.int32),
             ((SLOTS, 2 * TILE, TILE), BF16),
@@ -390,13 +394,13 @@
         vmem=FIRST_VMEM,
     )
     payload = call(
-        x_sums, "x_sums", [((COL_BLOCKS + 12 * COLS_SHARE, TILE), F32)], four_of(payload, "x")
-    )
-
-    kept, given, primal1, start_full, cost_full, free = call(
+        x_sums, "x_sums", [((COL_BLOCKS + 8 * COLS_SHARE, TILE), F32)], four_of(payload, "x")
+    )
+
+    kept, given, primal1, _, free = call(
         first_forward,
         "first_forward",
-        [(half, F32)] * 2 + [(columns, F32)] * 4,
+        [(half, F32)] * 2 + [(columns, F32)] * 3,
         (table, *four_of(payload[0], "y"), pairs),
         smem=1,
         scratch=[pltpu.VMEM(columns, F32)] + row_total,
@@ -415,16 +419,16 @@
         second_adjoint,
         "second_adjoint",
         [(columns, F32)] + [(blocks, F32)] * 3,
-        (table, held, swap_cores(held), dual0, pairs),
+        (table, held, swap_cores(held), dual0, side, pairs),
         smem=1,
         scratch=[pltpu.VMEM(blocks, F32)] + col_total,
     )
 
-    kept, given, primal2, gradient2, primal_mine = call(
+    kept, given, primal2, ascent2, primal_mine = call(
         second_forward,
         "second_forward",
         [(blocks, F32)] * 2 + [(columns, F32)] * 2 + [((COLS_SHARE, TILE), F32)],
-        (table, *four_over_row(gradient), primal1, cost_full, free, pairs),
+        (table, *four_over_row(gradient), primal1, free, pairs),
         smem=1,
         scratch=[pltpu.VMEM(columns, F32)] + row_total,
     )
@@ -437,7 +441,7 @@
         third_adjoint,
         "third_adjoint",
         [((COL_BLOCKS + 8, TILE), F32), ((ROWS_SHARE, TILE), F32)],
-        (table, held, swap_cores(held), dual1, rhs_full, ineq, pairs),
+        (table, held, swap_cores(held), dual1, rhs_full, ineq, side, primal1, primal2, pairs),
         smem=1,
         scratch=[pltpu.VMEM(blocks, F32)] * 2 + col_total,
     )
@@ -445,7 +449,7 @@
         column_terms,
         "column_terms",
         [((N, 1, TILE), F32)],
-        (*four_over_row(payload), gradient2, primal1, primal2, cost_full, free),
+        (*four_over_row(payload), ascent2, free),
     )
     primal_residual, dual_residual, gap = call(
         measures,

time: 125 us -> 124 us (level)
  no operation moved by 1% of the time
where the time goes in v6:
time: 124 us
  blocking collectives  53.3 us (43%)
  waiting for transfers between devices  29.2 us (24%)
  starting transfers between devices  26.1 us (21%)
  Pallas kernels  12.9 us (10%)
  between operations  1.52 us (1%)
    all_to_all x4, blocking collectives, exchange(): return lax.all_to_all(copies, axes, 0, 0)  53.3 us
    ppermute x18, waiting for transfers between devices, shift(): return lax.ppermute(values, axis, [(k, (k + step) % 4) for k in range(4)])  25.8 us
    ppermute x18, starting transfers between devices, shift(): return lax.ppermute(values, axis, [(k, (k + step) % 4) for k in range(4)])  16 us
    pallas_call x15, Pallas kernels, call(): pl.pallas_call(kernel, name=name, out_shape=shapes, in_specs=[SMEM] * sme...  12.9 us
    ppermute x4, starting transfers between devices, swap_cores(): return lax.ppermute(values, 'core', [(0, 1), (1, 0)])  10.2 us
    ppermute x4, waiting for transfers between devices, swap_cores(): return lax.ppermute(values, 'core', [(0, 1), (1, 0)])  3.42 us
  transfers between devices with their start and end apart: 22, of which 18 were waited for; matrix products, arithmetic and copies ran while one was open for 0% of the time, Pallas kernels for 0%

profile of v6, /device:TPU:1, one launch (start us, length us, event | category | flops | bytes accessed | tf_op | source)
XLA Modules:
  0.0 123.8 jit_solution(40049234051378475)
XLA Ops:
  1.3 1.5 %pack.1 = (f32[16,4,128]{2,1,0:T(4,128)}, f32[40,128]{1,0:T(8,128)}) custom-call(s32[1,1]{1,0:T(1,128)S(6)} %copy.15.count, s32[1,1,64]{2,1,0:T(1,128)} %rows.1, s32[1,1,64]{2,1,0:T(1,128)} %cols.1, s32[1,4,128]{2,1,0:T(4,128)} %row_kinds.1, f32[1,4,128]{2,1,0:T(4,128)} %rhs.1, f32[1,4,128]{2,1,0:T(4,128)} %dual.1, s32[1,8,128]{2,1,0:T(8,128)} %col_kinds.1, ...), custom_call_target="tpu_custom_call" | custom-call | tf_op jit(solution)/shard_map/pack/pallas_call | solution.py:35
  2.8 17.4 %all_to_all.20.duals = f32[16,4,128]{2,1,0:T(4,128)S(1)} all-to-all(f32[16,4,128]{2,1,0:T(4,128)} %get-tuple-element.29), channel_id=1, replica_groups=mesh['y'=4,'x'=4,'z'=8,'core'=2] {'z','core'}, dimensions={0} | all-to-all | bytes 65536 | tf_op jit(solution)/shard_map/all_to_all | solution.py:350
  20.9 2.8 %first_adjoint.1 = (f32[144,128]{1,0:T(8,128)S(1)}, f32[64,128]{1,0:T(8,128)S(1)}, s32[8,128]{1,0:T(8,128)S(1)}, bf16[64,256,128]{2,1,0:T(8,128)(2,1)S(1)}) custom-call(f32[64,128,128]{2,1,0:T(8,128)} %bitcast.3, f32[16,4,128]{2,1,0:T(4,128)S(1)} %all_to_all.20.duals, f32[40,128]{1,0:T(8,128)S(1)} %copy-done), custom_call_target="tpu_custom_call" | custom-call | tf_op jit(solution)/shard_map/first_adjoint/pallas_call | solution.py:35
  23.7 2.8 %collective-permute-start.2 = (f32[144,128]{1,0:T(8,128)S(1)}, f32[144,128]{1,0:T(8,128)S(1)}, u32[]{:S(2)}, u32[]{:S(2)}) collective-permute-start(f32[144,128]{1,0:T(8,128)S(1)} %get-tuple-element.32.own), channel_id=1, source_target_pairs={{0,32},{16,48},{32,0},{48,16},{1,33},{17,49},{33,1},{49,17},{2,34}... | collective-permute-start | bytes 221192 | tf_op jit(solution)/shard_map/ppermute | solution.py:333
  28.5 2.1 %collective-permute-done.1.left = f32[144,128]{1,0:T(8,128)S(1)} collective-permute-done((f32[144,128]{1,0:T(8,128)S(1)}, f32[144,128]{1,0:T(8,128)S(1)}, u32[]{:S(2)}, u32[]{:S(2)}) %collective-permute-start.1) | collective-permute-done | bytes 73760 | tf_op jit(solution)/shard_map/ppermute | solution.py:333
  31.8 3.0 %collective-permute-start.5 = (f32[192,128]{1,0:T(8,128)S(1)}, f32[192,128]{1,0:T(8,128)S(1)}, u32[]{:S(2)}, u32[]{:S(2)}) collective-permute-start(f32[192,128]{1,0:T(8,128)S(1)} %x_sums.1.own), channel_id=1, source_target_pairs={{0,128},{64,192},{128,0},{192,64},{1,129},{65,193},{129,1},{193,65... | collective-permute-start | bytes 294920 | tf_op jit(solution)/shard_map/ppermute | solution.py:333
  38.3 2.6 %collective-permute-done.3.right = f32[192,128]{1,0:T(8,128)S(1)} collective-permute-done((f32[192,128]{1,0:T(8,128)S(1)}, f32[192,128]{1,0:T(8,128)S(1)}, u32[]{:S(2)}, u32[]{:S(2)}) %collective-permute-start.3) | collective-permute-done | bytes 98336 | tf_op jit(solution)/shard_map/ppermute | solution.py:333
  40.9 2.3 %first_forward.1 = (f32[32,128]{1,0:T(8,128)S(1)}, f32[32,128]{1,0:T(8,128)S(1)}, f32[128,128]{1,0:T(8,128)S(1)}, f32[128,128]{1,0:T(8,128)}, f32[128,128]{1,0:T(8,128)S(1)}) custom-call(s32[8,128]{1,0:T(8,128)S(1)} %get-tuple-element.31.table, f32[192,128]{1,0:T(8,128)S(1)} %x_sums.1.own, f32[192,128]{1,0:T(8,128)S(1)} %collective-permute-done.3.right, ...), custom_call_target="tpu_custom_call" | custom-call | tf_op jit(solution)/shard_map/first_forward/pallas_call | solution.py:35
  43.1 3.2 %collective-permute-start.6 = (f32[32,128]{1,0:T(8,128)S(1)}, f32[32,128]{1,0:T(8,128)S(1)}, u32[]{:S(2)}, u32[]{:S(2)}) collective-permute-start(f32[32,128]{1,0:T(8,128)S(1)} %get-tuple-element.35), channel_id=1, source_target_pairs={{0,1},{1,0},{2,3},{3,2},{4,5},{5,4},{6,7},{7,6},{8,9},{9,8},{10,11... | collective-permute-start | bytes 49160 | tf_op jit(solution)/shard_map/ppermute | solution.py:346
  47.2 11.6 %all_to_all.21.pieces = f32[8,40,128]{2,1,0:T(8,128)S(1)} all-to-all(f32[8,40,128]{2,1,0:T(8,128)S(1)} %image_copies.1), channel_id=1, replica_groups=mesh['y'=4,'x'=4,'z'=8,'core'=2] {'z'}, dimensions={0} | all-to-all | bytes 327680 | tf_op jit(solution)/shard_map/all_to_all | solution.py:350
  58.8 1.6 %collective-permute-start.7 = (f32[96,128]{1,0:T(8,128)S(1)}, f32[96,128]{1,0:T(8,128)S(1)}, u32[]{:S(2)}, u32[]{:S(2)}) collective-permute-start(f32[96,128]{1,0:T(8,128)S(1)} %image_sums.1.held), channel_id=1, source_target_pairs={{0,1},{1,0},{2,3},{3,2},{4,5},{5,4},{6,7},{7,6},{8,9},{9,8},{10,11... | collective-permute-start | bytes 147464 | tf_op jit(solution)/shard_map/ppermute | solution.py:346
  64.6 2.8 %collective-permute-done.10.opposite = f32[128,128]{1,0:T(8,128)S(1)} collective-permute-done((f32[128,128]{1,0:T(8,128)S(1)}, f32[128,128]{1,0:T(8,128)S(1)}, u32[]{:S(2)}, u32[]{:S(2)}) %collective-permute-start.10) | collective-permute-done | bytes 65568 | tf_op jit(solution)/shard_map/ppermute | solution.py:333
  67.4 1.5 %collective-permute-done.8.right = f32[128,128]{1,0:T(8,128)S(1)} collective-permute-done((f32[128,128]{1,0:T(8,128)S(1)}, f32[128,128]{1,0:T(8,128)S(1)}, u32[]{:S(2)}, u32[]{:S(2)}) %collective-permute-start.8) | collective-permute-done | bytes 65568 | tf_op jit(solution)/shard_map/ppermute | solution.py:333
  71.1 2.6 %collective-permute-done.13.opposite = f32[128,128]{1,0:T(8,128)S(1)} collective-permute-done((f32[128,128]{1,0:T(8,128)S(1)}, f32[128,128]{1,0:T(8,128)S(1)}, u32[]{:S(2)}, u32[]{:S(2)}) %collective-permute-start.13) | collective-permute-done | bytes 65568 | tf_op jit(solution)/shard_map/ppermute | solution.py:333
  73.6 1.6 %collective-permute-done.11.right = f32[128,128]{1,0:T(8,128)S(1)} collective-permute-done((f32[128,128]{1,0:T(8,128)S(1)}, f32[128,128]{1,0:T(8,128)S(1)}, u32[]{:S(2)}, u32[]{:S(2)}) %collective-permute-start.11) | collective-permute-done | bytes 65568 | tf_op jit(solution)/shard_map/ppermute | solution.py:333
  75.2 2.3 %second_forward.1 = (f32[64,128]{1,0:T(8,128)S(1)}, f32[64,128]{1,0:T(8,128)S(1)}, f32[128,128]{1,0:T(8,128)S(1)}, f32[128,128]{1,0:T(8,128)S(1)}, f32[8,128]{1,0:T(8,128)}) custom-call(s32[8,128]{1,0:T(8,128)S(1)} %get-tuple-element.31.table, f32[128,128]{1,0:T(8,128)S(1)} %sums.2.own, f32[128,128]{1,0:T(8,128)S(1)} %collective-permute-done.11.right, ...), custom_call_target="tpu_custom_call" | custom-call | tf_op jit(solution)/shard_map/second_forward/pallas_call | solution.py:35
  77.5 3.7 %collective-permute-start.14 = (f32[64,128]{1,0:T(8,128)S(1)}, f32[64,128]{1,0:T(8,128)S(1)}, u32[]{:S(2)}, u32[]{:S(2)}) collective-permute-start(f32[64,128]{1,0:T(8,128)S(1)} %get-tuple-element.42), channel_id=1, source_target_pairs={{0,1},{1,0},{2,3},{3,2},{4,5},{5,4},{6,7},{7,6},{8,9},{9,8},{10,11... | collective-permute-start | bytes 98312 | tf_op jit(solution)/shard_map/ppermute | solution.py:346
  82.1 11.6 %all_to_all.22.pieces = f32[8,40,128]{2,1,0:T(8,128)S(1)} all-to-all(f32[8,40,128]{2,1,0:T(8,128)S(1)} %pair_copies.1), channel_id=1, replica_groups=mesh['y'=4,'x'=4,'z'=8,'core'=2] {'z'}, dimensions={0} | all-to-all | bytes 327680 | tf_op jit(solution)/shard_map/all_to_all | solution.py:350
  93.7 1.6 %collective-permute-start.15 = (f32[40,128]{1,0:T(8,128)S(1)}, f32[40,128]{1,0:T(8,128)S(1)}, u32[]{:S(2)}, u32[]{:S(2)}) collective-permute-start(f32[40,128]{1,0:T(8,128)S(1)} %pair_sums.1.held), channel_id=1, source_target_pairs={{0,1},{1,0},{2,3},{3,2},{4,5},{5,4},{6,7},{7,6},{8,9},{9,8},{10,11... | collective-permute-start | bytes 61448 | tf_op jit(solution)/shard_map/ppermute | solution.py:346
  96.2 1.8 %third_adjoint.1 = (f32[136,128]{1,0:T(8,128)S(1)}, f32[4,128]{1,0:T(4,128)}) custom-call(s32[8,128]{1,0:T(8,128)S(1)} %get-tuple-element.31.table, f32[40,128]{1,0:T(8,128)S(1)} %pair_sums.1.held, f32[40,128]{1,0:T(8,128)S(1)} %collective-permute-done.15.other, f32[64,128]{1,0:T(8,128)S(1)} %get-tuple-element.43.before, ...), custom_call_target="tpu_custom_call" | custom-call | tf_op jit(solution)/shard_map/third_adjoint/pallas_call | solution.py:35
  99.4 3.2 %collective-permute-done.18.opposite = f32[136,128]{1,0:T(8,128)S(1)} collective-permute-done((f32[136,128]{1,0:T(8,128)S(1)}, f32[136,128]{1,0:T(8,128)S(1)}, u32[]{:S(2)}, u32[]{:S(2)}) %collective-permute-start.18) | collective-permute-done | bytes 69664 | tf_op jit(solution)/shard_map/ppermute | solution.py:333
  102.6 1.5 %collective-permute-done.16.right = f32[136,128]{1,0:T(8,128)S(1)} collective-permute-done((f32[136,128]{1,0:T(8,128)S(1)}, f32[136,128]{1,0:T(8,128)S(1)}, u32[]{:S(2)}, u32[]{:S(2)}) %collective-permute-start.16) | collective-permute-done | bytes 69664 | tf_op jit(solution)/shard_map/ppermute | solution.py:333
  105.9 3.1 %collective-permute-done.21.opposite = f32[136,128]{1,0:T(8,128)S(1)} collective-permute-done((f32[136,128]{1,0:T(8,128)S(1)}, f32[136,128]{1,0:T(8,128)S(1)}, u32[]{:S(2)}, u32[]{:S(2)}) %collective-permute-start.21) | collective-permute-done | bytes 69664 | tf_op jit(solution)/shard_map/ppermute | solution.py:333
  110.2 12.7 %all_to_all.23.gathered = f32[16,1,128]{2,1,0:T(1,128)S(1)} all-to-all(f32[16,1,128]{2,1,0:T(1,128)S(1)} %column_terms.1), channel_id=1, replica_groups=mesh['y'=4,'x'=4,'z'=8,'core'=2] {'z','core'}, dimensions={0} | all-to-all | bytes 16384 | tf_op jit(solution)/shard_map/all_to_all | solution.py:350
  (41 shorter events, 21.3 us)
Async XLA Ops:
  20.2 0.7 copy-start
  23.7 4.8 %collective-permute-start.2 = (f32[144,128]{1,0:T(8,128)S(1)}, f32[144,128]{1,0:T(8,128)S(1)}, u32[]{:S(2)}, u32[]{:S(2)}) collective-permute-start(f32[144,128]{1,0:T(8,128)S(1)} %get-tuple-element.32.own), channel_id=1, source_target_pairs={{0,32},{16,48},{32,0},{48,16},{1,33},{17,49},{33,1},{49,17},{2,34}... | collective-permute-start | bytes 221192 | tf_op jit(solution)/shard_map/ppermute | solution.py:333
  26.5 4.1 %collective-permute-start.1 = (f32[144,128]{1,0:T(8,128)S(1)}, f32[144,128]{1,0:T(8,128)S(1)}, u32[]{:S(2)}, u32[]{:S(2)}) collective-permute-start(f32[144,128]{1,0:T(8,128)S(1)} %get-tuple-element.32.own), channel_id=1, source_target_pairs={{0,48},{16,0},{32,16},{48,32},{1,49},{17,1},{33,17},{49,33},{2,50}... | collective-permute-start | bytes 221192 | tf_op jit(solution)/shard_map/ppermute | solution.py:333
  27.4 4.4 %collective-permute-start = (f32[144,128]{1,0:T(8,128)S(1)}, f32[144,128]{1,0:T(8,128)S(1)}, u32[]{:S(2)}, u32[]{:S(2)}) collective-permute-start(f32[144,128]{1,0:T(8,128)S(1)} %get-tuple-element.32.own), channel_id=1, source_target_pairs={{0,16},{16,32},{32,48},{48,0},{1,17},{17,33},{33,49},{49,1},{2,18}... | collective-permute-start | bytes 221192 | tf_op jit(solution)/shard_map/ppermute | solution.py:333
  31.8 5.1 %collective-permute-start.5 = (f32[192,128]{1,0:T(8,128)S(1)}, f32[192,128]{1,0:T(8,128)S(1)}, u32[]{:S(2)}, u32[]{:S(2)}) collective-permute-start(f32[192,128]{1,0:T(8,128)S(1)} %x_sums.1.own), channel_id=1, source_target_pairs={{0,128},{64,192},{128,0},{192,64},{1,129},{65,193},{129,1},{193,65... | collective-permute-start | bytes 294920 | tf_op jit(solution)/shard_map/ppermute | solution.py:333
  34.8 3.5 %collective-permute-start.4 = (f32[192,128]{1,0:T(8,128)S(1)}, f32[192,128]{1,0:T(8,128)S(1)}, u32[]{:S(2)}, u32[]{:S(2)}) collective-permute-start(f32[192,128]{1,0:T(8,128)S(1)} %x_sums.1.own), channel_id=1, source_target_pairs={{0,192},{64,0},{128,64},{192,128},{1,193},{65,1},{129,65},{193,129... | collective-permute-start | bytes 294920 | tf_op jit(solution)/shard_map/ppermute | solution.py:333
  35.6 5.3 %collective-permute-start.3 = (f32[192,128]{1,0:T(8,128)S(1)}, f32[192,128]{1,0:T(8,128)S(1)}, u32[]{:S(2)}, u32[]{:S(2)}) collective-permute-start(f32[192,128]{1,0:T(8,128)S(1)} %x_sums.1.own), channel_id=1, source_target_pairs={{0,64},{64,128},{128,192},{192,0},{1,65},{65,129},{129,193},{193,1... | collective-permute-start | bytes 294920 | tf_op jit(solution)/shard_map/ppermute | solution.py:333
  43.1 4.1 %collective-permute-start.6 = (f32[32,128]{1,0:T(8,128)S(1)}, f32[32,128]{1,0:T(8,128)S(1)}, u32[]{:S(2)}, u32[]{:S(2)}) collective-permute-start(f32[32,128]{1,0:T(8,128)S(1)} %get-tuple-element.35), channel_id=1, source_target_pairs={{0,1},{1,0},{2,3},{3,2},{4,5},{5,4},{6,7},{7,6},{8,9},{9,8},{10,11... | collective-permute-start | bytes 49160 | tf_op jit(solution)/shard_map/ppermute | solution.py:346
  58.8 2.5 %collective-permute-start.7 = (f32[96,128]{1,0:T(8,128)S(1)}, f32[96,128]{1,0:T(8,128)S(1)}, u32[]{:S(2)}, u32[]{:S(2)}) collective-permute-start(f32[96,128]{1,0:T(8,128)S(1)} %image_sums.1.held), channel_id=1, source_target_pairs={{0,1},{1,0},{2,3},{3,2},{4,5},{5,4},{6,7},{7,6},{8,9},{9,8},{10,11... | collective-permute-start | bytes 147464 | tf_op jit(solution)/shard_map/ppermute | solution.py:346
  62.7 4.7 %collective-permute-start.10 = (f32[128,128]{1,0:T(8,128)S(1)}, f32[128,128]{1,0:T(8,128)S(1)}, u32[]{:S(2)}, u32[]{:S(2)}) collective-permute-start(f32[128,128]{1,0:T(8,128)S(1)} %get-tuple-element.37.own), channel_id=1, source_target_pairs={{0,32},{16,48},{32,0},{48,16},{1,33},{17,49},{33,1},{49,17},{2,34}... | collective-permute-start | bytes 196616 | tf_op jit(solution)/shard_map/ppermute | solution.py:333
  63.1 4.2 %collective-permute-start.9 = (f32[128,128]{1,0:T(8,128)S(1)}, f32[128,128]{1,0:T(8,128)S(1)}, u32[]{:S(2)}, u32[]{:S(2)}) collective-permute-start(f32[128,128]{1,0:T(8,128)S(1)} %get-tuple-element.37.own), channel_id=1, source_target_pairs={{0,48},{16,0},{32,16},{48,32},{1,49},{17,1},{33,17},{49,33},{2,50}... | collective-permute-start | bytes 196616 | tf_op jit(solution)/shard_map/ppermute | solution.py:333
  64.5 4.4 %collective-permute-start.8 = (f32[128,128]{1,0:T(8,128)S(1)}, f32[128,128]{1,0:T(8,128)S(1)}, u32[]{:S(2)}, u32[]{:S(2)}) collective-permute-start(f32[128,128]{1,0:T(8,128)S(1)} %get-tuple-element.37.own), channel_id=1, source_target_pairs={{0,16},{16,32},{32,48},{48,0},{1,17},{17,33},{33,49},{49,1},{2,18}... | collective-permute-start | bytes 196616 | tf_op jit(solution)/shard_map/ppermute | solution.py:333
  68.9 4.7 %collective-permute-start.13 = (f32[128,128]{1,0:T(8,128)S(1)}, f32[128,128]{1,0:T(8,128)S(1)}, u32[]{:S(2)}, u32[]{:S(2)}) collective-permute-start(f32[128,128]{1,0:T(8,128)S(1)} %sums.2.own), channel_id=1, source_target_pairs={{0,128},{64,192},{128,0},{192,64},{1,129},{65,193},{129,1},{193,65... | collective-permute-start | bytes 196616 | tf_op jit(solution)/shard_map/ppermute | solution.py:333
  69.6 4.0 %collective-permute-start.12 = (f32[128,128]{1,0:T(8,128)S(1)}, f32[128,128]{1,0:T(8,128)S(1)}, u32[]{:S(2)}, u32[]{:S(2)}) collective-permute-start(f32[128,128]{1,0:T(8,128)S(1)} %sums.2.own), channel_id=1, source_target_pairs={{0,192},{64,0},{128,64},{192,128},{1,193},{65,1},{129,65},{193,129... | collective-permute-start | bytes 196616 | tf_op jit(solution)/shard_map/ppermute | solution.py:333
  70.9 4.3 %collective-permute-start.11 = (f32[128,128]{1,0:T(8,128)S(1)}, f32[128,128]{1,0:T(8,128)S(1)}, u32[]{:S(2)}, u32[]{:S(2)}) collective-permute-start(f32[128,128]{1,0:T(8,128)S(1)} %sums.2.own), channel_id=1, source_target_pairs={{0,64},{64,128},{128,192},{192,0},{1,65},{65,129},{129,193},{193,1... | collective-permute-start | bytes 196616 | tf_op jit(solution)/shard_map/ppermute | solution.py:333
  77.5 4.6 %collective-permute-start.14 = (f32[64,128]{1,0:T(8,128)S(1)}, f32[64,128]{1,0:T(8,128)S(1)}, u32[]{:S(2)}, u32[]{:S(2)}) collective-permute-start(f32[64,128]{1,0:T(8,128)S(1)} %get-tuple-element.42), channel_id=1, source_target_pairs={{0,1},{1,0},{2,3},{3,2},{4,5},{5,4},{6,7},{7,6},{8,9},{9,8},{10,11... | collective-permute-start | bytes 98312 | tf_op jit(solution)/shard_map/ppermute | solution.py:346
  93.7 2.5 %collective-permute-start.15 = (f32[40,128]{1,0:T(8,128)S(1)}, f32[40,128]{1,0:T(8,128)S(1)}, u32[]{:S(2)}, u32[]{:S(2)}) collective-permute-start(f32[40,128]{1,0:T(8,128)S(1)} %pair_sums.1.held), channel_id=1, source_target_pairs={{0,1},{1,0},{2,3},{3,2},{4,5},{5,4},{6,7},{7,6},{8,9},{9,8},{10,11... | collective-permute-start | bytes 61448 | tf_op jit(solution)/shard_map/ppermute | solution.py:346
  98.0 4.7 %collective-permute-start.18 = (f32[136,128]{1,0:T(8,128)S(1)}, f32[136,128]{1,0:T(8,128)S(1)}, u32[]{:S(2)}, u32[]{:S(2)}) collective-permute-start(f32[136,128]{1,0:T(8,128)S(1)} %get-tuple-element.48.own), channel_id=1, source_target_pairs={{0,32},{16,48},{32,0},{48,16},{1,33},{17,49},{33,1},{49,17},{2,34}... | collective-permute-start | bytes 208904 | tf_op jit(solution)/shard_map/ppermute | solution.py:333
  98.0 4.7 %collective-permute-start.17 = (f32[136,128]{1,0:T(8,128)S(1)}, f32[136,128]{1,0:T(8,128)S(1)}, u32[]{:S(2)}, u32[]{:S(2)}) collective-permute-start(f32[136,128]{1,0:T(8,128)S(1)} %get-tuple-element.48.own), channel_id=1, source_target_pairs={{0,48},{16,0},{32,16},{48,32},{1,49},{17,1},{33,17},{49,33},{2,50}... | collective-permute-start | bytes 208904 | tf_op jit(solution)/shard_map/ppermute | solution.py:333
  99.3 4.9 %collective-permute-start.16 = (f32[136,128]{1,0:T(8,128)S(1)}, f32[136,128]{1,0:T(8,128)S(1)}, u32[]{:S(2)}, u32[]{:S(2)}) collective-permute-start(f32[136,128]{1,0:T(8,128)S(1)} %get-tuple-element.48.own), channel_id=1, source_target_pairs={{0,16},{16,32},{32,48},{48,0},{1,17},{17,33},{33,49},{49,1},{2,18}... | collective-permute-start | bytes 208904 | tf_op jit(solution)/shard_map/ppermute | solution.py:333
  104.2 4.8 %collective-permute-start.21 = (f32[136,128]{1,0:T(8,128)S(1)}, f32[136,128]{1,0:T(8,128)S(1)}, u32[]{:S(2)}, u32[]{:S(2)}) collective-permute-start(f32[136,128]{1,0:T(8,128)S(1)} %sums.3.own), channel_id=1, source_target_pairs={{0,128},{64,192},{128,0},{192,64},{1,129},{65,193},{129,1},{193,65... | collective-permute-start | bytes 208904 | tf_op jit(solution)/shard_map/ppermute | solution.py:333
  104.3 4.7 %collective-permute-start.20 = (f32[136,128]{1,0:T(8,128)S(1)}, f32[136,128]{1,0:T(8,128)S(1)}, u32[]{:S(2)}, u32[]{:S(2)}) collective-permute-start(f32[136,128]{1,0:T(8,128)S(1)} %sums.3.own), channel_id=1, source_target_pairs={{0,192},{64,0},{128,64},{192,128},{1,193},{65,1},{129,65},{193,129... | collective-permute-start | bytes 208904 | tf_op jit(solution)/shard_map/ppermute | solution.py:333
  105.7 4.4 %collective-permute-start.19 = (f32[136,128]{1,0:T(8,128)S(1)}, f32[136,128]{1,0:T(8,128)S(1)}, u32[]{:S(2)}, u32[]{:S(2)}) collective-permute-start(f32[136,128]{1,0:T(8,128)S(1)} %sums.3.own), channel_id=1, source_target_pairs={{0,64},{64,128},{128,192},{192,0},{1,65},{65,129},{129,193},{193,1... | collective-permute-start | bytes 208904 | tf_op jit(solution)/shard_map/ppermute | solution.py:333

commit v7 on v6

--- a/solution.py
+++ b/solution.py
@@ -18,7 +18,7 @@
 NCOLS = float(N * COL_BLOCKS * TILE)
 PACK_VMEM = 60 * 2**20
 FIRST_VMEM = 48 * 2**20
-PIECES = (4, 12, 16, 32)
+PIECES = (8, 16, 16, 16, 8)
 F32, BF16 = jnp.float32, jnp.bfloat16
 
 SLOT_ROWS, SLOT_COLS, COUNT, AT_Y, AT_X, AT_Z, AT_CORE = range(7)
@@ -30,7 +30,7 @@
 HBM = pl.BlockSpec(memory_space=pltpu.HBM)
 
 
-def call(kernel, name, out_shapes, args, smem=0, hbm=0, smem_out=False, scratch=(), vmem=8 * 2**20):
+def call(kernel, name, out_shapes, args, smem=0, hbm=0, smem_out=False, scratch=(), vmem=8 * 2**20, cost=None):
     shapes = tuple(jax.ShapeDtypeStruct(s, d) for s, d in out_shapes)
     return pl.pallas_call(
         kernel,
@@ -40,6 +40,7 @@
         out_specs=tuple([SMEM if smem_out else VMEM] * len(shapes)),
         scratch_shapes=list(scratch),
         compiler_params=pltpu.CompilerParams(vmem_limit_bytes=vmem),
+        cost_estimate=cost,
     )(*args)
 
 
@@ -72,10 +73,8 @@
     def body(slot, carry):
         parts = [split(ref[pl.ds(table[SLOT_COLS, slot], 1), :], copies) for ref in primal_refs]
         lhs = jnp.concatenate([p[0] for p in parts] + [p[1] for p in parts], 0).astype(BF16)
-        product = lax.dot_general(
-            lhs, tile_pair(slot), (((1,), (1,)), ((), ())), preferred_element_type=F32
-        )
-        product = product[:, :TILE] + product[:, TILE:]
+        lhs = jnp.concatenate([lhs, lhs], 1)
+        product = jnp.dot(lhs, tile_pair(slot), preferred_element_type=F32)
         total[table[SLOT_ROWS, slot]] += product[0:8] + product[8:16]
         return carry
 
@@ -143,6 +142,13 @@
     duals[...] = jnp.broadcast_to(start[...][None], duals.shape)
 
 
+def turn(pairs, turned):
+    for slot in range(SLOTS):
+        for part in range(2):
+            rows = slice(part * TILE, (part + 1) * TILE)
+            turned[slot, rows, :] = pairs[slot, rows, :].T
+
+
 def x_sums(own, right, left, opposite, payload):
     four = (own, right, left, opposite)
     payload[0:COL_BLOCKS, :] = sum_four(four, slice(0, COL_BLOCKS))
@@ -220,7 +226,7 @@
 
 
 def first_forward(
-    table, own, right, left, opposite, pairs, kept, given, primal, start, free, extended, total
+    table, own, right, left, opposite, turned, kept, given, primal, start, free, extended, total
 ):
     y, x = table[AT_Y, 0], table[AT_X, 0]
     for j, (ref, dy) in enumerate(((own, 0), (right, 3), (left, 1), (opposite, 2))):
@@ -233,7 +239,7 @@
     ascent = sum_four((own, right, left, opposite), slice(0, COL_BLOCKS))
     primal[...] = clamp_primal(STEP * ascent, free[...])
     extended[...] = 2.0 * primal[...] - start[...]
-    forward_product(table, lambda slot: pairs[slot], [extended], total)
+    forward_product(table, lambda slot: turned[slot], [extended], total)
     mine = pl.multiple_of(table[AT_CORE, 0] * HALF, HALF)
     kept[...] = total[pl.ds(mine, HALF), 0, :]
     given[...] = total[pl.ds(HALF - mine, HALF), 0, :]
@@ -256,13 +262,13 @@
 
 
 def second_forward(
-    table, own, right, left, opposite, before, free, pairs, kept, given, primal, ascent, primal_mine, extended, total
+    table, own, right, left, opposite, before, free, turned, kept, given, primal, ascent, primal_mine, extended, total
 ):
     ascent[...] = sum_four((own, right, left, opposite), slice(0, COL_BLOCKS))
     primal[...] = clamp_primal(before[...] + STEP * ascent[...], free[...])
     extended[...] = 2.0 * primal[...] - before[...]
     primal_mine[...] = primal[own_columns(table), :]
-    forward_product(table, lambda slot: pairs[slot], [extended, primal], total)
+    forward_product(table, lambda slot: turned[slot], [extended, primal], total)
     mine = pl.multiple_of(table[AT_CORE, 0] * HALF, HALF)
     for k, part in enumerate((0, 4)):
         rows = slice(k * HALF, (k + 1) * HALF)
@@ -393,6 +399,13 @@
         + col_total,
         vmem=FIRST_VMEM,
     )
+    turned = call(
+        turn,
+        "turn",
+        [((SLOTS, 2 * TILE, TILE), BF16)],
+        (pairs,),
+        cost=pl.CostEstimate(flops=0, bytes_accessed=2**23, transcendentals=0),
+    )[0]
     payload = call(
         x_sums, "x_sums", [((COL_BLOCKS + 8 * COLS_SHARE, TILE), F32)], four_of(payload, "x")
     )
@@ -401,7 +414,7 @@
         first_forward,
         "first_forward",
         [(half, F32)] * 2 + [(columns, F32)] * 3,
-        (table, *four_of(payload[0], "y"), pairs),
+        (table, *four_of(payload[0], "y"), turned),
         smem=1,
         scratch=[pltpu.VMEM(columns, F32)] + row_total,
     )
@@ -428,7 +441,7 @@
         second_forward,
         "second_forward",
         [(blocks, F32)] * 2 + [(columns, F32)] * 2 + [((COLS_SHARE, TILE), F32)],
-        (table, *four_over_row(gradient), primal1, free, pairs),
+        (table, *four_over_row(gradient), primal1, free, turned),
         smem=1,
         scratch=[pltpu.VMEM(columns, F32)] + row_total,
     )

time: 124 us -> 123 us (level)
    pallas_call x15 -> x16, Pallas kernels: 12.9 us -> 13 us  [call(): pl.pallas_call(kernel, name=name, out_shape=shapes, in_specs=[SMEM] * sme...]
  transfers between devices with their start and end apart: 22 -> 22, of which waited for: 18 -> 17; matrix products, arithmetic and copies ran while one was open for 0% -> 0% of each run, Pallas kernels for 0% -> 1%
where the time goes in v7:
time: 123 us
  blocking collectives  53.3 us (43%)
  waiting for transfers between devices  28.1 us (23%)
  starting transfers between devices  26.1 us (21%)
  Pallas kernels  13 us (11%)
  between operations  1.53 us (1%)
    all_to_all x4, blocking collectives, exchange(): return lax.all_to_all(copies, axes, 0, 0)  53.3 us
    ppermute x18, waiting for transfers between devices, shift(): return lax.ppermute(values, axis, [(k, (k + step) % 4) for k in range(4)])  24.6 us
    ppermute x18, starting transfers between devices, shift(): return lax.ppermute(values, axis, [(k, (k + step) % 4) for k in range(4)])  16 us
    pallas_call x16, Pallas kernels, call(): pl.pallas_call(kernel, name=name, out_shape=shapes, in_specs=[SMEM] * sme...  13 us
    ppermute x4, starting transfers between devices, swap_cores(): return lax.ppermute(values, 'core', [(0, 1), (1, 0)])  10.2 us
    ppermute x4, waiting for transfers between devices, swap_cores(): return lax.ppermute(values, 'core', [(0, 1), (1, 0)])  3.42 us
  transfers between devices with their start and end apart: 22, of which 17 were waited for; matrix products, arithmetic and copies ran while one was open for 0% of the time, Pallas kernels for 1%

profile of v7, /device:TPU:1, one launch (start us, length us, event | category | flops | bytes accessed | tf_op | source)
XLA Modules:
  0.0 122.7 jit_solution(14666945988355597897)
XLA Ops:
  1.3 1.5 %pack.1 = (f32[16,4,128]{2,1,0:T(4,128)}, f32[40,128]{1,0:T(8,128)}) custom-call(s32[1,1]{1,0:T(1,128)S(6)} %copy.15.count, s32[1,1,64]{2,1,0:T(1,128)} %rows.1, s32[1,1,64]{2,1,0:T(1,128)} %cols.1, s32[1,4,128]{2,1,0:T(4,128)} %row_kinds.1, f32[1,4,128]{2,1,0:T(4,128)} %rhs.1, f32[1,4,128]{2,1,0:T(4,128)} %dual.1, s32[1,8,128]{2,1,0:T(8,128)} %col_kinds.1, ...), custom_call_target="tpu_custom_call" | custom-call | tf_op jit(solution)/shard_map/pack/pallas_call | solution.py:35
  2.8 17.4 %all_to_all.20.duals = f32[16,4,128]{2,1,0:T(4,128)S(1)} all-to-all(f32[16,4,128]{2,1,0:T(4,128)} %get-tuple-element.29), channel_id=1, replica_groups=mesh['y'=4,'x'=4,'z'=8,'core'=2] {'z','core'}, dimensions={0} | all-to-all | bytes 65536 | tf_op jit(solution)/shard_map/all_to_all | solution.py:356
  20.9 2.6 %first_adjoint.1 = (f32[144,128]{1,0:T(8,128)S(1)}, f32[64,128]{1,0:T(8,128)S(1)}, s32[8,128]{1,0:T(8,128)S(1)}, bf16[64,256,128]{2,1,0:T(8,128)(2,1)S(1)}) custom-call(f32[64,128,128]{2,1,0:T(8,128)} %bitcast.3, f32[16,4,128]{2,1,0:T(4,128)S(1)} %all_to_all.20.duals, f32[40,128]{1,0:T(8,128)S(1)} %copy-done), custom_call_target="tpu_custom_call" | custom-call | tf_op jit(solution)/shard_map/first_adjoint/pallas_call | solution.py:35
  23.5 2.8 %collective-permute-start.2 = (f32[144,128]{1,0:T(8,128)S(1)}, f32[144,128]{1,0:T(8,128)S(1)}, u32[]{:S(2)}, u32[]{:S(2)}) collective-permute-start(f32[144,128]{1,0:T(8,128)S(1)} %get-tuple-element.32.own), channel_id=1, source_target_pairs={{0,32},{16,48},{32,0},{48,16},{1,33},{17,49},{33,1},{49,17},{2,34}... | collective-permute-start | bytes 221192 | tf_op jit(solution)/shard_map/ppermute | solution.py:339
  28.3 2.2 %collective-permute-done.1.left = f32[144,128]{1,0:T(8,128)S(1)} collective-permute-done((f32[144,128]{1,0:T(8,128)S(1)}, f32[144,128]{1,0:T(8,128)S(1)}, u32[]{:S(2)}, u32[]{:S(2)}) %collective-permute-start.1) | collective-permute-done | bytes 73760 | tf_op jit(solution)/shard_map/ppermute | solution.py:339
  31.6 3.0 %collective-permute-start.5 = (f32[192,128]{1,0:T(8,128)S(1)}, f32[192,128]{1,0:T(8,128)S(1)}, u32[]{:S(2)}, u32[]{:S(2)}) collective-permute-start(f32[192,128]{1,0:T(8,128)S(1)} %x_sums.1.own), channel_id=1, source_target_pairs={{0,128},{64,192},{128,0},{192,64},{1,129},{65,193},{129,1},{193,65... | collective-permute-start | bytes 294920 | tf_op jit(solution)/shard_map/ppermute | solution.py:339
  38.1 2.6 %collective-permute-done.3.right = f32[192,128]{1,0:T(8,128)S(1)} collective-permute-done((f32[192,128]{1,0:T(8,128)S(1)}, f32[192,128]{1,0:T(8,128)S(1)}, u32[]{:S(2)}, u32[]{:S(2)}) %collective-permute-start.3) | collective-permute-done | bytes 98336 | tf_op jit(solution)/shard_map/ppermute | solution.py:339
  40.7 1.8 %first_forward.1 = (f32[32,128]{1,0:T(8,128)S(1)}, f32[32,128]{1,0:T(8,128)S(1)}, f32[128,128]{1,0:T(8,128)S(1)}, f32[128,128]{1,0:T(8,128)}, f32[128,128]{1,0:T(8,128)S(1)}) custom-call(s32[8,128]{1,0:T(8,128)S(1)} %get-tuple-element.31.table, f32[192,128]{1,0:T(8,128)S(1)} %x_sums.1.own, f32[192,128]{1,0:T(8,128)S(1)} %collective-permute-done.3.right, ...), custom_call_target="tpu_custom_call" | custom-call | tf_op jit(solution)/shard_map/first_forward/pallas_call | solution.py:35
  42.5 3.2 %collective-permute-start.6 = (f32[32,128]{1,0:T(8,128)S(1)}, f32[32,128]{1,0:T(8,128)S(1)}, u32[]{:S(2)}, u32[]{:S(2)}) collective-permute-start(f32[32,128]{1,0:T(8,128)S(1)} %get-tuple-element.35), channel_id=1, source_target_pairs={{0,1},{1,0},{2,3},{3,2},{4,5},{5,4},{6,7},{7,6},{8,9},{9,8},{10,11... | collective-permute-start | bytes 49160 | tf_op jit(solution)/shard_map/ppermute | solution.py:352
  46.6 11.6 %all_to_all.21.pieces = f32[8,40,128]{2,1,0:T(8,128)S(1)} all-to-all(f32[8,40,128]{2,1,0:T(8,128)S(1)} %image_copies.1), channel_id=1, replica_groups=mesh['y'=4,'x'=4,'z'=8,'core'=2] {'z'}, dimensions={0} | all-to-all | bytes 327680 | tf_op jit(solution)/shard_map/all_to_all | solution.py:356
  58.2 1.6 %collective-permute-start.7 = (f32[96,128]{1,0:T(8,128)S(1)}, f32[96,128]{1,0:T(8,128)S(1)}, u32[]{:S(2)}, u32[]{:S(2)}) collective-permute-start(f32[96,128]{1,0:T(8,128)S(1)} %image_sums.1.held), channel_id=1, source_target_pairs={{0,1},{1,0},{2,3},{3,2},{4,5},{5,4},{6,7},{7,6},{8,9},{9,8},{10,11... | collective-permute-start | bytes 147464 | tf_op jit(solution)/shard_map/ppermute | solution.py:352
  64.0 2.8 %collective-permute-done.10.opposite = f32[128,128]{1,0:T(8,128)S(1)} collective-permute-done((f32[128,128]{1,0:T(8,128)S(1)}, f32[128,128]{1,0:T(8,128)S(1)}, u32[]{:S(2)}, u32[]{:S(2)}) %collective-permute-start.10) | collective-permute-done | bytes 65568 | tf_op jit(solution)/shard_map/ppermute | solution.py:339
  66.7 1.5 %collective-permute-done.8.right = f32[128,128]{1,0:T(8,128)S(1)} collective-permute-done((f32[128,128]{1,0:T(8,128)S(1)}, f32[128,128]{1,0:T(8,128)S(1)}, u32[]{:S(2)}, u32[]{:S(2)}) %collective-permute-start.8) | collective-permute-done | bytes 65568 | tf_op jit(solution)/shard_map/ppermute | solution.py:339
  70.4 2.6 %collective-permute-done.13.opposite = f32[128,128]{1,0:T(8,128)S(1)} collective-permute-done((f32[128,128]{1,0:T(8,128)S(1)}, f32[128,128]{1,0:T(8,128)S(1)}, u32[]{:S(2)}, u32[]{:S(2)}) %collective-permute-start.13) | collective-permute-done | bytes 65568 | tf_op jit(solution)/shard_map/ppermute | solution.py:339
  73.0 1.6 %collective-permute-done.11.right = f32[128,128]{1,0:T(8,128)S(1)} collective-permute-done((f32[128,128]{1,0:T(8,128)S(1)}, f32[128,128]{1,0:T(8,128)S(1)}, u32[]{:S(2)}, u32[]{:S(2)}) %collective-permute-start.11) | collective-permute-done | bytes 65568 | tf_op jit(solution)/shard_map/ppermute | solution.py:339
  74.6 1.8 %second_forward.1 = (f32[64,128]{1,0:T(8,128)S(1)}, f32[64,128]{1,0:T(8,128)S(1)}, f32[128,128]{1,0:T(8,128)S(1)}, f32[128,128]{1,0:T(8,128)S(1)}, f32[8,128]{1,0:T(8,128)}) custom-call(s32[8,128]{1,0:T(8,128)S(1)} %get-tuple-element.31.table, f32[128,128]{1,0:T(8,128)S(1)} %sums.2.own, f32[128,128]{1,0:T(8,128)S(1)} %collective-permute-done.11.right, ...), custom_call_target="tpu_custom_call" | custom-call | tf_op jit(solution)/shard_map/second_forward/pallas_call | solution.py:35
  76.4 3.7 %collective-permute-start.14 = (f32[64,128]{1,0:T(8,128)S(1)}, f32[64,128]{1,0:T(8,128)S(1)}, u32[]{:S(2)}, u32[]{:S(2)}) collective-permute-start(f32[64,128]{1,0:T(8,128)S(1)} %get-tuple-element.42), channel_id=1, source_target_pairs={{0,1},{1,0},{2,3},{3,2},{4,5},{5,4},{6,7},{7,6},{8,9},{9,8},{10,11... | collective-permute-start | bytes 98312 | tf_op jit(solution)/shard_map/ppermute | solution.py:352
  81.0 11.6 %all_to_all.22.pieces = f32[8,40,128]{2,1,0:T(8,128)S(1)} all-to-all(f32[8,40,128]{2,1,0:T(8,128)S(1)} %pair_copies.1), channel_id=1, replica_groups=mesh['y'=4,'x'=4,'z'=8,'core'=2] {'z'}, dimensions={0} | all-to-all | bytes 327680 | tf_op jit(solution)/shard_map/all_to_all | solution.py:356
  92.6 1.6 %collective-permute-start.15 = (f32[40,128]{1,0:T(8,128)S(1)}, f32[40,128]{1,0:T(8,128)S(1)}, u32[]{:S(2)}, u32[]{:S(2)}) collective-permute-start(f32[40,128]{1,0:T(8,128)S(1)} %pair_sums.1.held), channel_id=1, source_target_pairs={{0,1},{1,0},{2,3},{3,2},{4,5},{5,4},{6,7},{7,6},{8,9},{9,8},{10,11... | collective-permute-start | bytes 61448 | tf_op jit(solution)/shard_map/ppermute | solution.py:352
  95.1 1.8 %third_adjoint.1 = (f32[136,128]{1,0:T(8,128)S(1)}, f32[4,128]{1,0:T(4,128)}) custom-call(s32[8,128]{1,0:T(8,128)S(1)} %get-tuple-element.31.table, f32[40,128]{1,0:T(8,128)S(1)} %pair_sums.1.held, f32[40,128]{1,0:T(8,128)S(1)} %collective-permute-done.15.other, f32[64,128]{1,0:T(8,128)S(1)} %get-tuple-element.43.before, ...), custom_call_target="tpu_custom_call" | custom-call | tf_op jit(solution)/shard_map/third_adjoint/pallas_call | solution.py:35
  98.3 3.2 %collective-permute-done.18.opposite = f32[136,128]{1,0:T(8,128)S(1)} collective-permute-done((f32[136,128]{1,0:T(8,128)S(1)}, f32[136,128]{1,0:T(8,128)S(1)}, u32[]{:S(2)}, u32[]{:S(2)}) %collective-permute-start.18) | collective-permute-done | bytes 69664 | tf_op jit(solution)/shard_map/ppermute | solution.py:339
  101.5 1.5 %collective-permute-done.16.right = f32[136,128]{1,0:T(8,128)S(1)} collective-permute-done((f32[136,128]{1,0:T(8,128)S(1)}, f32[136,128]{1,0:T(8,128)S(1)}, u32[]{:S(2)}, u32[]{:S(2)}) %collective-permute-start.16) | collective-permute-done | bytes 69664 | tf_op jit(solution)/shard_map/ppermute | solution.py:339
  104.8 3.1 %collective-permute-done.21.opposite = f32[136,128]{1,0:T(8,128)S(1)} collective-permute-done((f32[136,128]{1,0:T(8,128)S(1)}, f32[136,128]{1,0:T(8,128)S(1)}, u32[]{:S(2)}, u32[]{:S(2)}) %collective-permute-start.21) | collective-permute-done | bytes 69664 | tf_op jit(solution)/shard_map/ppermute | solution.py:339
  109.1 12.8 %all_to_all.23.gathered = f32[16,1,128]{2,1,0:T(1,128)S(1)} all-to-all(f32[16,1,128]{2,1,0:T(1,128)S(1)} %column_terms.1), channel_id=1, replica_groups=mesh['y'=4,'x'=4,'z'=8,'core'=2] {'z','core'}, dimensions={0} | all-to-all | bytes 16384 | tf_op jit(solution)/shard_map/all_to_all | solution.py:356
  (42 shorter events, 21.3 us)
Async XLA Ops:
  20.2 0.7 copy-start
  23.5 4.8 %collective-permute-start.2 = (f32[144,128]{1,0:T(8,128)S(1)}, f32[144,128]{1,0:T(8,128)S(1)}, u32[]{:S(2)}, u32[]{:S(2)}) collective-permute-start(f32[144,128]{1,0:T(8,128)S(1)} %get-tuple-element.32.own), channel_id=1, source_target_pairs={{0,32},{16,48},{32,0},{48,16},{1,33},{17,49},{33,1},{49,17},{2,34}... | collective-permute-start | bytes 221192 | tf_op jit(solution)/shard_map/ppermute | solution.py:339
  26.3 4.1 %collective-permute-start.1 = (f32[144,128]{1,0:T(8,128)S(1)}, f32[144,128]{1,0:T(8,128)S(1)}, u32[]{:S(2)}, u32[]{:S(2)}) collective-permute-start(f32[144,128]{1,0:T(8,128)S(1)} %get-tuple-element.32.own), channel_id=1, source_target_pairs={{0,48},{16,0},{32,16},{48,32},{1,49},{17,1},{33,17},{49,33},{2,50}... | collective-permute-start | bytes 221192 | tf_op jit(solution)/shard_map/ppermute | solution.py:339
  27.2 4.4 %collective-permute-start = (f32[144,128]{1,0:T(8,128)S(1)}, f32[144,128]{1,0:T(8,128)S(1)}, u32[]{:S(2)}, u32[]{:S(2)}) collective-permute-start(f32[144,128]{1,0:T(8,128)S(1)} %get-tuple-element.32.own), channel_id=1, source_target_pairs={{0,16},{16,32},{32,48},{48,0},{1,17},{17,33},{33,49},{49,1},{2,18}... | collective-permute-start | bytes 221192 | tf_op jit(solution)/shard_map/ppermute | solution.py:339
  31.6 5.6 %collective-permute-start.5 = (f32[192,128]{1,0:T(8,128)S(1)}, f32[192,128]{1,0:T(8,128)S(1)}, u32[]{:S(2)}, u32[]{:S(2)}) collective-permute-start(f32[192,128]{1,0:T(8,128)S(1)} %x_sums.1.own), channel_id=1, source_target_pairs={{0,128},{64,192},{128,0},{192,64},{1,129},{65,193},{129,1},{193,65... | collective-permute-start | bytes 294920 | tf_op jit(solution)/shard_map/ppermute | solution.py:339
  34.6 3.5 %collective-permute-start.4 = (f32[192,128]{1,0:T(8,128)S(1)}, f32[192,128]{1,0:T(8,128)S(1)}, u32[]{:S(2)}, u32[]{:S(2)}) collective-permute-start(f32[192,128]{1,0:T(8,128)S(1)} %x_sums.1.own), channel_id=1, source_target_pairs={{0,192},{64,0},{128,64},{192,128},{1,193},{65,1},{129,65},{193,129... | collective-permute-start | bytes 294920 | tf_op jit(solution)/shard_map/ppermute | solution.py:339
  35.4 5.3 %collective-permute-start.3 = (f32[192,128]{1,0:T(8,128)S(1)}, f32[192,128]{1,0:T(8,128)S(1)}, u32[]{:S(2)}, u32[]{:S(2)}) collective-permute-start(f32[192,128]{1,0:T(8,128)S(1)} %x_sums.1.own), channel_id=1, source_target_pairs={{0,64},{64,128},{128,192},{192,0},{1,65},{65,129},{129,193},{193,1... | collective-permute-start | bytes 294920 | tf_op jit(solution)/shard_map/ppermute | solution.py:339
  42.5 4.1 %collective-permute-start.6 = (f32[32,128]{1,0:T(8,128)S(1)}, f32[32,128]{1,0:T(8,128)S(1)}, u32[]{:S(2)}, u32[]{:S(2)}) collective-permute-start(f32[32,128]{1,0:T(8,128)S(1)} %get-tuple-element.35), channel_id=1, source_target_pairs={{0,1},{1,0},{2,3},{3,2},{4,5},{5,4},{6,7},{7,6},{8,9},{9,8},{10,11... | collective-permute-start | bytes 49160 | tf_op jit(solution)/shard_map/ppermute | solution.py:352
  58.2 2.5 %collective-permute-start.7 = (f32[96,128]{1,0:T(8,128)S(1)}, f32[96,128]{1,0:T(8,128)S(1)}, u32[]{:S(2)}, u32[]{:S(2)}) collective-permute-start(f32[96,128]{1,0:T(8,128)S(1)} %image_sums.1.held), channel_id=1, source_target_pairs={{0,1},{1,0},{2,3},{3,2},{4,5},{5,4},{6,7},{7,6},{8,9},{9,8},{10,11... | collective-permute-start | bytes 147464 | tf_op jit(solution)/shard_map/ppermute | solution.py:352
  62.0 4.7 %collective-permute-start.10 = (f32[128,128]{1,0:T(8,128)S(1)}, f32[128,128]{1,0:T(8,128)S(1)}, u32[]{:S(2)}, u32[]{:S(2)}) collective-permute-start(f32[128,128]{1,0:T(8,128)S(1)} %get-tuple-element.37.own), channel_id=1, source_target_pairs={{0,32},{16,48},{32,0},{48,16},{1,33},{17,49},{33,1},{49,17},{2,34}... | collective-permute-start | bytes 196616 | tf_op jit(solution)/shard_map/ppermute | solution.py:339
  62.5 4.2 %collective-permute-start.9 = (f32[128,128]{1,0:T(8,128)S(1)}, f32[128,128]{1,0:T(8,128)S(1)}, u32[]{:S(2)}, u32[]{:S(2)}) collective-permute-start(f32[128,128]{1,0:T(8,128)S(1)} %get-tuple-element.37.own), channel_id=1, source_target_pairs={{0,48},{16,0},{32,16},{48,32},{1,49},{17,1},{33,17},{49,33},{2,50}... | collective-permute-start | bytes 196616 | tf_op jit(solution)/shard_map/ppermute | solution.py:339
  63.9 4.4 %collective-permute-start.8 = (f32[128,128]{1,0:T(8,128)S(1)}, f32[128,128]{1,0:T(8,128)S(1)}, u32[]{:S(2)}, u32[]{:S(2)}) collective-permute-start(f32[128,128]{1,0:T(8,128)S(1)} %get-tuple-element.37.own), channel_id=1, source_target_pairs={{0,16},{16,32},{32,48},{48,0},{1,17},{17,33},{33,49},{49,1},{2,18}... | collective-permute-start | bytes 196616 | tf_op jit(solution)/shard_map/ppermute | solution.py:339
  68.3 4.7 %collective-permute-start.13 = (f32[128,128]{1,0:T(8,128)S(1)}, f32[128,128]{1,0:T(8,128)S(1)}, u32[]{:S(2)}, u32[]{:S(2)}) collective-permute-start(f32[128,128]{1,0:T(8,128)S(1)} %sums.2.own), channel_id=1, source_target_pairs={{0,128},{64,192},{128,0},{192,64},{1,129},{65,193},{129,1},{193,65... | collective-permute-start | bytes 196616 | tf_op jit(solution)/shard_map/ppermute | solution.py:339
  68.9 4.0 %collective-permute-start.12 = (f32[128,128]{1,0:T(8,128)S(1)}, f32[128,128]{1,0:T(8,128)S(1)}, u32[]{:S(2)}, u32[]{:S(2)}) collective-permute-start(f32[128,128]{1,0:T(8,128)S(1)} %sums.2.own), channel_id=1, source_target_pairs={{0,192},{64,0},{128,64},{192,128},{1,193},{65,1},{129,65},{193,129... | collective-permute-start | bytes 196616 | tf_op jit(solution)/shard_map/ppermute | solution.py:339
  70.2 4.3 %collective-permute-start.11 = (f32[128,128]{1,0:T(8,128)S(1)}, f32[128,128]{1,0:T(8,128)S(1)}, u32[]{:S(2)}, u32[]{:S(2)}) collective-permute-start(f32[128,128]{1,0:T(8,128)S(1)} %sums.2.own), channel_id=1, source_target_pairs={{0,64},{64,128},{128,192},{192,0},{1,65},{65,129},{129,193},{193,1... | collective-permute-start | bytes 196616 | tf_op jit(solution)/shard_map/ppermute | solution.py:339
  76.4 4.6 %collective-permute-start.14 = (f32[64,128]{1,0:T(8,128)S(1)}, f32[64,128]{1,0:T(8,128)S(1)}, u32[]{:S(2)}, u32[]{:S(2)}) collective-permute-start(f32[64,128]{1,0:T(8,128)S(1)} %get-tuple-element.42), channel_id=1, source_target_pairs={{0,1},{1,0},{2,3},{3,2},{4,5},{5,4},{6,7},{7,6},{8,9},{9,8},{10,11... | collective-permute-start | bytes 98312 | tf_op jit(solution)/shard_map/ppermute | solution.py:352
  92.6 2.5 %collective-permute-start.15 = (f32[40,128]{1,0:T(8,128)S(1)}, f32[40,128]{1,0:T(8,128)S(1)}, u32[]{:S(2)}, u32[]{:S(2)}) collective-permute-start(f32[40,128]{1,0:T(8,128)S(1)} %pair_sums.1.held), channel_id=1, source_target_pairs={{0,1},{1,0},{2,3},{3,2},{4,5},{5,4},{6,7},{7,6},{8,9},{9,8},{10,11... | collective-permute-start | bytes 61448 | tf_op jit(solution)/shard_map/ppermute | solution.py:352
  96.9 4.7 %collective-permute-start.18 = (f32[136,128]{1,0:T(8,128)S(1)}, f32[136,128]{1,0:T(8,128)S(1)}, u32[]{:S(2)}, u32[]{:S(2)}) collective-permute-start(f32[136,128]{1,0:T(8,128)S(1)} %get-tuple-element.48.own), channel_id=1, source_target_pairs={{0,32},{16,48},{32,0},{48,16},{1,33},{17,49},{33,1},{49,17},{2,34}... | collective-permute-start | bytes 208904 | tf_op jit(solution)/shard_map/ppermute | solution.py:339
  96.9 4.7 %collective-permute-start.17 = (f32[136,128]{1,0:T(8,128)S(1)}, f32[136,128]{1,0:T(8,128)S(1)}, u32[]{:S(2)}, u32[]{:S(2)}) collective-permute-start(f32[136,128]{1,0:T(8,128)S(1)} %get-tuple-element.48.own), channel_id=1, source_target_pairs={{0,48},{16,0},{32,16},{48,32},{1,49},{17,1},{33,17},{49,33},{2,50}... | collective-permute-start | bytes 208904 | tf_op jit(solution)/shard_map/ppermute | solution.py:339
  98.2 4.9 %collective-permute-start.16 = (f32[136,128]{1,0:T(8,128)S(1)}, f32[136,128]{1,0:T(8,128)S(1)}, u32[]{:S(2)}, u32[]{:S(2)}) collective-permute-start(f32[136,128]{1,0:T(8,128)S(1)} %get-tuple-element.48.own), channel_id=1, source_target_pairs={{0,16},{16,32},{32,48},{48,0},{1,17},{17,33},{33,49},{49,1},{2,18}... | collective-permute-start | bytes 208904 | tf_op jit(solution)/shard_map/ppermute | solution.py:339
  103.1 4.8 %collective-permute-start.21 = (f32[136,128]{1,0:T(8,128)S(1)}, f32[136,128]{1,0:T(8,128)S(1)}, u32[]{:S(2)}, u32[]{:S(2)}) collective-permute-start(f32[136,128]{1,0:T(8,128)S(1)} %sums.3.own), channel_id=1, source_target_pairs={{0,128},{64,192},{128,0},{192,64},{1,129},{65,193},{129,1},{193,65... | collective-permute-start | bytes 208904 | tf_op jit(solution)/shard_map/ppermute | solution.py:339
  103.2 4.7 %collective-permute-start.20 = (f32[136,128]{1,0:T(8,128)S(1)}, f32[136,128]{1,0:T(8,128)S(1)}, u32[]{:S(2)}, u32[]{:S(2)}) collective-permute-start(f32[136,128]{1,0:T(8,128)S(1)} %sums.3.own), channel_id=1, source_target_pairs={{0,192},{64,0},{128,64},{192,128},{1,193},{65,1},{129,65},{193,129... | collective-permute-start | bytes 208904 | tf_op jit(solution)/shard_map/ppermute | solution.py:339
  104.6 4.4 %collective-permute-start.19 = (f32[136,128]{1,0:T(8,128)S(1)}, f32[136,128]{1,0:T(8,128)S(1)}, u32[]{:S(2)}, u32[]{:S(2)}) collective-permute-start(f32[136,128]{1,0:T(8,128)S(1)} %sums.3.own), channel_id=1, source_target_pairs={{0,64},{64,128},{128,192},{192,0},{1,65},{65,129},{129,193},{193,1... | collective-permute-start | bytes 208904 | tf_op jit(solution)/shard_map/ppermute | solution.py:339

commit v8 on v7

--- a/solution.py
+++ b/solution.py
@@ -149,7 +149,7 @@
             turned[slot, rows, :] = pairs[slot, rows, :].T
 
 
-def x_sums(own, right, left, opposite, payload):
+def ring_sums(own, right, left, opposite, payload):
     four = (own, right, left, opposite)
     payload[0:COL_BLOCKS, :] = sum_four(four, slice(0, COL_BLOCKS))
     share = 2 * COLS_SHARE
@@ -228,10 +228,12 @@
 def first_forward(
     table, own, right, left, opposite, turned, kept, given, primal, start, free, extended, total
 ):
-    y, x = table[AT_Y, 0], table[AT_X, 0]
-    for j, (ref, dy) in enumerate(((own, 0), (right, 3), (left, 1), (opposite, 2))):
-        for k, dx in enumerate((0, 3, 1, 2)):
-            device = ((y + dy) & 3) * 4 + ((x + dx) & 3)
+    y, x, second = table[AT_Y, 0], table[AT_X, 0], table[AT_CORE, 0] == 1
+    for j, (ref, late) in enumerate(((own, 0), (right, 3), (left, 1), (opposite, 2))):
+        for k, early in enumerate((0, 3, 1, 2)):
+            to_y = (y + jnp.where(second, early, late)) & 3
+            to_x = (x + jnp.where(second, late, early)) & 3
+            device = to_y * 4 + to_x
             block = pl.ds(pl.multiple_of(device * COLS_SHARE, COLS_SHARE), COLS_SHARE)
             for m, out in enumerate((start, free)):
                 first = COL_BLOCKS + (2 * k + m) * COLS_SHARE
@@ -335,17 +337,23 @@
             out[j] = jnp.sum(jnp.where(lane == 2 * k + j, line, 0.0)) * (1.0 / size)
 
 
-def shift(values, axis, step):
-    return lax.ppermute(values, axis, [(k, (k + step) % 4) for k in range(4)])
-
-
-def four_of(values, axis):
-    return values, shift(values, axis, 1), shift(values, axis, -1), shift(values, axis, 2)
+def shift(values, phase, step):
+    pairs = []
+    for y in range(4):
+        for x in range(4):
+            for core in range(2):
+                to_y, to_x = (y, (x + step) % 4) if core == phase else ((y + step) % 4, x)
+                pairs.append(((y * 4 + x) * 2 + core, (to_y * 4 + to_x) * 2 + core))
+    return lax.ppermute(values, ("y", "x", "core"), pairs)
+
+
+def four_of(values, phase):
+    return values, shift(values, phase, 1), shift(values, phase, -1), shift(values, phase, 2)
 
 
 def four_over_row(values):
-    total = call(sums, "sums", [(values.shape, F32)], four_of(values, "x"))
-    return four_of(total[0], "y")
+    total = call(sums, "sums", [(values.shape, F32)], four_of(values, 0))
+    return four_of(total[0], 1)
 
 
 def swap_cores(values):
@@ -407,14 +415,14 @@
         cost=pl.CostEstimate(flops=0, bytes_accessed=2**23, transcendentals=0),
     )[0]
     payload = call(
-        x_sums, "x_sums", [((COL_BLOCKS + 8 * COLS_SHARE, TILE), F32)], four_of(payload, "x")
+        ring_sums, "ring_sums", [((COL_BLOCKS + 8 * COLS_SHARE, TILE), F32)], four_of(payload, 0)
     )
 
     kept, given, primal1, _, free = call(
         first_forward,
         "first_forward",
         [(half, F32)] * 2 + [(columns, F32)] * 3,
-        (table, *four_of(payload[0], "y"), turned),
+        (table, *four_of(payload[0], 1), turned),
         smem=1,
         scratch=[pltpu.VMEM(columns, F32)] + row_total,
     )

time: 123 us -> 122 us (level)
  waiting for transfers between devices: 28.1 us -> 26.8 us
    ppermute x18, waiting for transfers between devices: 24.6 us -> 23.4 us  [shift(): return lax.ppermute(values, ('y', 'x', 'core'), pairs)]
where the time goes in v8:
time: 122 us
  blocking collectives  53.2 us (44%)
  waiting for transfers between devices  26.8 us (22%)
  starting transfers between devices  26.5 us (22%)
  Pallas kernels  12.9 us (11%)
  between operations  1.53 us (1%)
    all_to_all x4, blocking collectives, exchange(): return lax.all_to_all(copies, axes, 0, 0)  53.2 us
    ppermute x18, waiting for transfers between devices, shift(): return lax.ppermute(values, ('y', 'x', 'core'), pairs)  23.4 us
    ppermute x18, starting transfers between devices, shift(): return lax.ppermute(values, ('y', 'x', 'core'), pairs)  15.7 us
    pallas_call x16, Pallas kernels, call(): pl.pallas_call(kernel, name=name, out_shape=shapes, in_specs=[SMEM] * sme...  12.9 us
    ppermute x4, starting transfers between devices, swap_cores(): return lax.ppermute(values, 'core', [(0, 1), (1, 0)])  10.8 us
    ppermute x4, waiting for transfers between devices, swap_cores(): return lax.ppermute(values, 'core', [(0, 1), (1, 0)])  3.42 us
  transfers between devices with their start and end apart: 22, of which 17 were waited for; matrix products, arithmetic and copies ran while one was open for 0% of the time, Pallas kernels for 1%

profile of v8, /device:TPU:1, one launch (start us, length us, event | category | flops | bytes accessed | tf_op | source)
XLA Modules:
  0.0 121.8 jit_solution(922886607297780890)
XLA Ops:
  2.8 17.4 %all_to_all.20.duals = f32[16,4,128]{2,1,0:T(4,128)S(1)} all-to-all(f32[16,4,128]{2,1,0:T(4,128)} %get-tuple-element.29), channel_id=1, replica_groups=mesh['y'=4,'x'=4,'z'=8,'core'=2] {'z','core'}, dimensions={0} | all-to-all | bytes 65536 | tf_op jit(solution)/shard_map/all_to_all | solution.py:364
  20.9 2.6 %first_adjoint.1 = (f32[144,128]{1,0:T(8,128)S(1)}, f32[64,128]{1,0:T(8,128)S(1)}, s32[8,128]{1,0:T(8,128)S(1)}, bf16[64,256,128]{2,1,0:T(8,128)(2,1)S(1)}) custom-call(f32[64,128,128]{2,1,0:T(8,128)} %bitcast.3, f32[16,4,128]{2,1,0:T(4,128)S(1)} %all_to_all.20.duals, f32[40,128]{1,0:T(8,128)S(1)} %copy-done), custom_call_target="tpu_custom_call" | custom-call | tf_op jit(solution)/shard_map/first_adjoint/pallas_call | solution.py:35
  23.5 3.0 %collective-permute-start.2 = (f32[144,128]{1,0:T(8,128)S(1)}, f32[144,128]{1,0:T(8,128)S(1)}, u32[]{:S(2)}, u32[]{:S(2)}) collective-permute-start(f32[144,128]{1,0:T(8,128)S(1)} %get-tuple-element.32.own), channel_id=1, source_target_pairs={{0,32},{1,129},{16,48},{17,145},{32,0},{33,161},{48,16},{49,177},{... | collective-permute-start | bytes 221192 | tf_op jit(solution)/shard_map/ppermute | solution.py:347
  29.7 2.0 %collective-permute-done.right = f32[144,128]{1,0:T(8,128)S(1)} collective-permute-done((f32[144,128]{1,0:T(8,128)S(1)}, f32[144,128]{1,0:T(8,128)S(1)}, u32[]{:S(2)}, u32[]{:S(2)}) %collective-permute-start) | collective-permute-done | bytes 73760 | tf_op jit(solution)/shard_map/ppermute | solution.py:347
  31.7 2.8 %collective-permute-start.5 = (f32[192,128]{1,0:T(8,128)S(1)}, f32[192,128]{1,0:T(8,128)S(1)}, u32[]{:S(2)}, u32[]{:S(2)}) collective-permute-start(f32[192,128]{1,0:T(8,128)S(1)} %ring_sums.1.own), channel_id=1, source_target_pairs={{0,128},{1,33},{16,144},{17,49},{32,160},{33,1},{48,176},{49,17},{... | collective-permute-start | bytes 294920 | tf_op jit(solution)/shard_map/ppermute | solution.py:347
  38.0 2.1 %collective-permute-done.3.right = f32[192,128]{1,0:T(8,128)S(1)} collective-permute-done((f32[192,128]{1,0:T(8,128)S(1)}, f32[192,128]{1,0:T(8,128)S(1)}, u32[]{:S(2)}, u32[]{:S(2)}) %collective-permute-start.3) | collective-permute-done | bytes 98336 | tf_op jit(solution)/shard_map/ppermute | solution.py:347
  40.1 1.8 %first_forward.1 = (f32[32,128]{1,0:T(8,128)S(1)}, f32[32,128]{1,0:T(8,128)S(1)}, f32[128,128]{1,0:T(8,128)S(1)}, f32[128,128]{1,0:T(8,128)}, f32[128,128]{1,0:T(8,128)S(1)}) custom-call(s32[8,128]{1,0:T(8,128)S(1)} %get-tuple-element.31.table, f32[192,128]{1,0:T(8,128)S(1)} %ring_sums.1.own, f32[192,128]{1,0:T(8,128)S(1)} %collective-permute-done.3.right, ...), custom_call_target="tpu_custom_call" | custom-call | tf_op jit(solution)/shard_map/first_forward/pallas_call | solution.py:35
  41.9 3.8 %collective-permute-start.6 = (f32[32,128]{1,0:T(8,128)S(1)}, f32[32,128]{1,0:T(8,128)S(1)}, u32[]{:S(2)}, u32[]{:S(2)}) collective-permute-start(f32[32,128]{1,0:T(8,128)S(1)} %get-tuple-element.35), channel_id=1, source_target_pairs={{0,1},{1,0},{2,3},{3,2},{4,5},{5,4},{6,7},{7,6},{8,9},{9,8},{10,11... | collective-permute-start | bytes 49160 | tf_op jit(solution)/shard_map/ppermute | solution.py:360
  46.6 11.6 %all_to_all.21.pieces = f32[8,40,128]{2,1,0:T(8,128)S(1)} all-to-all(f32[8,40,128]{2,1,0:T(8,128)S(1)} %image_copies.1), channel_id=1, replica_groups=mesh['y'=4,'x'=4,'z'=8,'core'=2] {'z'}, dimensions={0} | all-to-all | bytes 327680 | tf_op jit(solution)/shard_map/all_to_all | solution.py:364
  58.2 1.6 %collective-permute-start.7 = (f32[96,128]{1,0:T(8,128)S(1)}, f32[96,128]{1,0:T(8,128)S(1)}, u32[]{:S(2)}, u32[]{:S(2)}) collective-permute-start(f32[96,128]{1,0:T(8,128)S(1)} %image_sums.1.held), channel_id=1, source_target_pairs={{0,1},{1,0},{2,3},{3,2},{4,5},{5,4},{6,7},{7,6},{8,9},{9,8},{10,11... | collective-permute-start | bytes 147464 | tf_op jit(solution)/shard_map/ppermute | solution.py:360
  62.3 1.7 %collective-permute-start.9 = (f32[128,128]{1,0:T(8,128)S(1)}, f32[128,128]{1,0:T(8,128)S(1)}, u32[]{:S(2)}, u32[]{:S(2)}) collective-permute-start(f32[128,128]{1,0:T(8,128)S(1)} %get-tuple-element.37.own), channel_id=1, source_target_pairs={{0,48},{1,193},{16,0},{17,209},{32,16},{33,225},{48,32},{49,241},{... | collective-permute-start | bytes 196616 | tf_op jit(solution)/shard_map/ppermute | solution.py:347
  64.0 2.7 %collective-permute-done.10.opposite = f32[128,128]{1,0:T(8,128)S(1)} collective-permute-done((f32[128,128]{1,0:T(8,128)S(1)}, f32[128,128]{1,0:T(8,128)S(1)}, u32[]{:S(2)}, u32[]{:S(2)}) %collective-permute-start.10) | collective-permute-done | bytes 65568 | tf_op jit(solution)/shard_map/ppermute | solution.py:347
  66.7 1.6 %collective-permute-done.8.right = f32[128,128]{1,0:T(8,128)S(1)} collective-permute-done((f32[128,128]{1,0:T(8,128)S(1)}, f32[128,128]{1,0:T(8,128)S(1)}, u32[]{:S(2)}, u32[]{:S(2)}) %collective-permute-start.8) | collective-permute-done | bytes 65568 | tf_op jit(solution)/shard_map/ppermute | solution.py:347
  68.4 1.8 %collective-permute-start.12 = (f32[128,128]{1,0:T(8,128)S(1)}, f32[128,128]{1,0:T(8,128)S(1)}, u32[]{:S(2)}, u32[]{:S(2)}) collective-permute-start(f32[128,128]{1,0:T(8,128)S(1)} %sums.2.own), channel_id=1, source_target_pairs={{0,192},{1,49},{16,208},{17,1},{32,224},{33,17},{48,240},{49,33},{... | collective-permute-start | bytes 196616 | tf_op jit(solution)/shard_map/ppermute | solution.py:347
  70.2 2.8 %collective-permute-done.13.opposite = f32[128,128]{1,0:T(8,128)S(1)} collective-permute-done((f32[128,128]{1,0:T(8,128)S(1)}, f32[128,128]{1,0:T(8,128)S(1)}, u32[]{:S(2)}, u32[]{:S(2)}) %collective-permute-start.13) | collective-permute-done | bytes 65568 | tf_op jit(solution)/shard_map/ppermute | solution.py:347
  73.0 1.5 %collective-permute-done.11.right = f32[128,128]{1,0:T(8,128)S(1)} collective-permute-done((f32[128,128]{1,0:T(8,128)S(1)}, f32[128,128]{1,0:T(8,128)S(1)}, u32[]{:S(2)}, u32[]{:S(2)}) %collective-permute-start.11) | collective-permute-done | bytes 65568 | tf_op jit(solution)/shard_map/ppermute | solution.py:347
  74.5 1.8 %second_forward.1 = (f32[64,128]{1,0:T(8,128)S(1)}, f32[64,128]{1,0:T(8,128)S(1)}, f32[128,128]{1,0:T(8,128)S(1)}, f32[128,128]{1,0:T(8,128)S(1)}, f32[8,128]{1,0:T(8,128)}) custom-call(s32[8,128]{1,0:T(8,128)S(1)} %get-tuple-element.31.table, f32[128,128]{1,0:T(8,128)S(1)} %sums.2.own, f32[128,128]{1,0:T(8,128)S(1)} %collective-permute-done.11.right, ...), custom_call_target="tpu_custom_call" | custom-call | tf_op jit(solution)/shard_map/second_forward/pallas_call | solution.py:35
  76.3 3.8 %collective-permute-start.14 = (f32[64,128]{1,0:T(8,128)S(1)}, f32[64,128]{1,0:T(8,128)S(1)}, u32[]{:S(2)}, u32[]{:S(2)}) collective-permute-start(f32[64,128]{1,0:T(8,128)S(1)} %get-tuple-element.42), channel_id=1, source_target_pairs={{0,1},{1,0},{2,3},{3,2},{4,5},{5,4},{6,7},{7,6},{8,9},{9,8},{10,11... | collective-permute-start | bytes 98312 | tf_op jit(solution)/shard_map/ppermute | solution.py:360
  81.0 11.6 %all_to_all.22.pieces = f32[8,40,128]{2,1,0:T(8,128)S(1)} all-to-all(f32[8,40,128]{2,1,0:T(8,128)S(1)} %pair_copies.1), channel_id=1, replica_groups=mesh['y'=4,'x'=4,'z'=8,'core'=2] {'z'}, dimensions={0} | all-to-all | bytes 327680 | tf_op jit(solution)/shard_map/all_to_all | solution.py:364
  92.6 1.6 %collective-permute-start.15 = (f32[40,128]{1,0:T(8,128)S(1)}, f32[40,128]{1,0:T(8,128)S(1)}, u32[]{:S(2)}, u32[]{:S(2)}) collective-permute-start(f32[40,128]{1,0:T(8,128)S(1)} %pair_sums.1.held), channel_id=1, source_target_pairs={{0,1},{1,0},{2,3},{3,2},{4,5},{5,4},{6,7},{7,6},{8,9},{9,8},{10,11... | collective-permute-start | bytes 61448 | tf_op jit(solution)/shard_map/ppermute | solution.py:360
  95.1 1.8 %third_adjoint.1 = (f32[136,128]{1,0:T(8,128)S(1)}, f32[4,128]{1,0:T(4,128)}) custom-call(s32[8,128]{1,0:T(8,128)S(1)} %get-tuple-element.31.table, f32[40,128]{1,0:T(8,128)S(1)} %pair_sums.1.held, f32[40,128]{1,0:T(8,128)S(1)} %collective-permute-done.15.other, f32[64,128]{1,0:T(8,128)S(1)} %get-tuple-element.43.before, ...), custom_call_target="tpu_custom_call" | custom-call | tf_op jit(solution)/shard_map/third_adjoint/pallas_call | solution.py:35
  98.3 3.2 %collective-permute-done.18.opposite = f32[136,128]{1,0:T(8,128)S(1)} collective-permute-done((f32[136,128]{1,0:T(8,128)S(1)}, f32[136,128]{1,0:T(8,128)S(1)}, u32[]{:S(2)}, u32[]{:S(2)}) %collective-permute-start.18) | collective-permute-done | bytes 69664 | tf_op jit(solution)/shard_map/ppermute | solution.py:347
  104.2 3.1 %collective-permute-done.21.opposite = f32[136,128]{1,0:T(8,128)S(1)} collective-permute-done((f32[136,128]{1,0:T(8,128)S(1)}, f32[136,128]{1,0:T(8,128)S(1)}, u32[]{:S(2)}, u32[]{:S(2)}) %collective-permute-start.21) | collective-permute-done | bytes 69664 | tf_op jit(solution)/shard_map/ppermute | solution.py:347
  108.2 12.7 %all_to_all.23.gathered = f32[16,1,128]{2,1,0:T(1,128)S(1)} all-to-all(f32[16,1,128]{2,1,0:T(1,128)S(1)} %column_terms.1), channel_id=1, replica_groups=mesh['y'=4,'x'=4,'z'=8,'core'=2] {'z','core'}, dimensions={0} | all-to-all | bytes 16384 | tf_op jit(solution)/shard_map/all_to_all | solution.py:364
  (42 shorter events, 19.8 us)
Async XLA Ops:
  20.2 0.7 copy-start
  23.5 4.8 %collective-permute-start.2 = (f32[144,128]{1,0:T(8,128)S(1)}, f32[144,128]{1,0:T(8,128)S(1)}, u32[]{:S(2)}, u32[]{:S(2)}) collective-permute-start(f32[144,128]{1,0:T(8,128)S(1)} %get-tuple-element.32.own), channel_id=1, source_target_pairs={{0,32},{1,129},{16,48},{17,145},{32,0},{33,161},{48,16},{49,177},{... | collective-permute-start | bytes 221192 | tf_op jit(solution)/shard_map/ppermute | solution.py:347
  26.5 3.2 %collective-permute-start.1 = (f32[144,128]{1,0:T(8,128)S(1)}, f32[144,128]{1,0:T(8,128)S(1)}, u32[]{:S(2)}, u32[]{:S(2)}) collective-permute-start(f32[144,128]{1,0:T(8,128)S(1)} %get-tuple-element.32.own), channel_id=1, source_target_pairs={{0,48},{1,193},{16,0},{17,209},{32,16},{33,225},{48,32},{49,241},{... | collective-permute-start | bytes 221192 | tf_op jit(solution)/shard_map/ppermute | solution.py:347
  27.3 4.4 %collective-permute-start = (f32[144,128]{1,0:T(8,128)S(1)}, f32[144,128]{1,0:T(8,128)S(1)}, u32[]{:S(2)}, u32[]{:S(2)}) collective-permute-start(f32[144,128]{1,0:T(8,128)S(1)} %get-tuple-element.32.own), channel_id=1, source_target_pairs={{0,16},{1,65},{16,32},{17,81},{32,48},{33,97},{48,0},{49,113},{64,... | collective-permute-start | bytes 221192 | tf_op jit(solution)/shard_map/ppermute | solution.py:347
  31.7 5.4 %collective-permute-start.5 = (f32[192,128]{1,0:T(8,128)S(1)}, f32[192,128]{1,0:T(8,128)S(1)}, u32[]{:S(2)}, u32[]{:S(2)}) collective-permute-start(f32[192,128]{1,0:T(8,128)S(1)} %ring_sums.1.own), channel_id=1, source_target_pairs={{0,128},{1,33},{16,144},{17,49},{32,160},{33,1},{48,176},{49,17},{... | collective-permute-start | bytes 294920 | tf_op jit(solution)/shard_map/ppermute | solution.py:347
  34.5 3.5 %collective-permute-start.4 = (f32[192,128]{1,0:T(8,128)S(1)}, f32[192,128]{1,0:T(8,128)S(1)}, u32[]{:S(2)}, u32[]{:S(2)}) collective-permute-start(f32[192,128]{1,0:T(8,128)S(1)} %ring_sums.1.own), channel_id=1, source_target_pairs={{0,192},{1,49},{16,208},{17,1},{32,224},{33,17},{48,240},{49,33},{... | collective-permute-start | bytes 294920 | tf_op jit(solution)/shard_map/ppermute | solution.py:347
  35.4 4.7 %collective-permute-start.3 = (f32[192,128]{1,0:T(8,128)S(1)}, f32[192,128]{1,0:T(8,128)S(1)}, u32[]{:S(2)}, u32[]{:S(2)}) collective-permute-start(f32[192,128]{1,0:T(8,128)S(1)} %ring_sums.1.own), channel_id=1, source_target_pairs={{0,64},{1,17},{16,80},{17,33},{32,96},{33,49},{48,112},{49,1},{64,... | collective-permute-start | bytes 294920 | tf_op jit(solution)/shard_map/ppermute | solution.py:347
  41.9 4.7 %collective-permute-start.6 = (f32[32,128]{1,0:T(8,128)S(1)}, f32[32,128]{1,0:T(8,128)S(1)}, u32[]{:S(2)}, u32[]{:S(2)}) collective-permute-start(f32[32,128]{1,0:T(8,128)S(1)} %get-tuple-element.35), channel_id=1, source_target_pairs={{0,1},{1,0},{2,3},{3,2},{4,5},{5,4},{6,7},{7,6},{8,9},{9,8},{10,11... | collective-permute-start | bytes 49160 | tf_op jit(solution)/shard_map/ppermute | solution.py:360
  58.2 2.5 %collective-permute-start.7 = (f32[96,128]{1,0:T(8,128)S(1)}, f32[96,128]{1,0:T(8,128)S(1)}, u32[]{:S(2)}, u32[]{:S(2)}) collective-permute-start(f32[96,128]{1,0:T(8,128)S(1)} %image_sums.1.held), channel_id=1, source_target_pairs={{0,1},{1,0},{2,3},{3,2},{4,5},{5,4},{6,7},{7,6},{8,9},{9,8},{10,11... | collective-permute-start | bytes 147464 | tf_op jit(solution)/shard_map/ppermute | solution.py:360
  62.0 4.7 %collective-permute-start.10 = (f32[128,128]{1,0:T(8,128)S(1)}, f32[128,128]{1,0:T(8,128)S(1)}, u32[]{:S(2)}, u32[]{:S(2)}) collective-permute-start(f32[128,128]{1,0:T(8,128)S(1)} %get-tuple-element.37.own), channel_id=1, source_target_pairs={{0,32},{1,129},{16,48},{17,145},{32,0},{33,161},{48,16},{49,177},{... | collective-permute-start | bytes 196616 | tf_op jit(solution)/shard_map/ppermute | solution.py:347
  62.3 4.4 %collective-permute-start.9 = (f32[128,128]{1,0:T(8,128)S(1)}, f32[128,128]{1,0:T(8,128)S(1)}, u32[]{:S(2)}, u32[]{:S(2)}) collective-permute-start(f32[128,128]{1,0:T(8,128)S(1)} %get-tuple-element.37.own), channel_id=1, source_target_pairs={{0,48},{1,193},{16,0},{17,209},{32,16},{33,225},{48,32},{49,241},{... | collective-permute-start | bytes 196616 | tf_op jit(solution)/shard_map/ppermute | solution.py:347
  64.0 4.3 %collective-permute-start.8 = (f32[128,128]{1,0:T(8,128)S(1)}, f32[128,128]{1,0:T(8,128)S(1)}, u32[]{:S(2)}, u32[]{:S(2)}) collective-permute-start(f32[128,128]{1,0:T(8,128)S(1)} %get-tuple-element.37.own), channel_id=1, source_target_pairs={{0,16},{1,65},{16,32},{17,81},{32,48},{33,97},{48,0},{49,113},{64,... | collective-permute-start | bytes 196616 | tf_op jit(solution)/shard_map/ppermute | solution.py:347
  68.3 4.7 %collective-permute-start.13 = (f32[128,128]{1,0:T(8,128)S(1)}, f32[128,128]{1,0:T(8,128)S(1)}, u32[]{:S(2)}, u32[]{:S(2)}) collective-permute-start(f32[128,128]{1,0:T(8,128)S(1)} %sums.2.own), channel_id=1, source_target_pairs={{0,128},{1,33},{16,144},{17,49},{32,160},{33,1},{48,176},{49,17},{... | collective-permute-start | bytes 196616 | tf_op jit(solution)/shard_map/ppermute | solution.py:347
  68.4 4.6 %collective-permute-start.12 = (f32[128,128]{1,0:T(8,128)S(1)}, f32[128,128]{1,0:T(8,128)S(1)}, u32[]{:S(2)}, u32[]{:S(2)}) collective-permute-start(f32[128,128]{1,0:T(8,128)S(1)} %sums.2.own), channel_id=1, source_target_pairs={{0,192},{1,49},{16,208},{17,1},{32,224},{33,17},{48,240},{49,33},{... | collective-permute-start | bytes 196616 | tf_op jit(solution)/shard_map/ppermute | solution.py:347
  70.2 4.3 %collective-permute-start.11 = (f32[128,128]{1,0:T(8,128)S(1)}, f32[128,128]{1,0:T(8,128)S(1)}, u32[]{:S(2)}, u32[]{:S(2)}) collective-permute-start(f32[128,128]{1,0:T(8,128)S(1)} %sums.2.own), channel_id=1, source_target_pairs={{0,64},{1,17},{16,80},{17,33},{32,96},{33,49},{48,112},{49,1},{64,... | collective-permute-start | bytes 196616 | tf_op jit(solution)/shard_map/ppermute | solution.py:347
  76.3 4.6 %collective-permute-start.14 = (f32[64,128]{1,0:T(8,128)S(1)}, f32[64,128]{1,0:T(8,128)S(1)}, u32[]{:S(2)}, u32[]{:S(2)}) collective-permute-start(f32[64,128]{1,0:T(8,128)S(1)} %get-tuple-element.42), channel_id=1, source_target_pairs={{0,1},{1,0},{2,3},{3,2},{4,5},{5,4},{6,7},{7,6},{8,9},{9,8},{10,11... | collective-permute-start | bytes 98312 | tf_op jit(solution)/shard_map/ppermute | solution.py:360
  92.6 2.5 %collective-permute-start.15 = (f32[40,128]{1,0:T(8,128)S(1)}, f32[40,128]{1,0:T(8,128)S(1)}, u32[]{:S(2)}, u32[]{:S(2)}) collective-permute-start(f32[40,128]{1,0:T(8,128)S(1)} %pair_sums.1.held), channel_id=1, source_target_pairs={{0,1},{1,0},{2,3},{3,2},{4,5},{5,4},{6,7},{7,6},{8,9},{9,8},{10,11... | collective-permute-start | bytes 61448 | tf_op jit(solution)/shard_map/ppermute | solution.py:360
  96.9 4.7 %collective-permute-start.18 = (f32[136,128]{1,0:T(8,128)S(1)}, f32[136,128]{1,0:T(8,128)S(1)}, u32[]{:S(2)}, u32[]{:S(2)}) collective-permute-start(f32[136,128]{1,0:T(8,128)S(1)} %get-tuple-element.48.own), channel_id=1, source_target_pairs={{0,32},{1,129},{16,48},{17,145},{32,0},{33,161},{48,16},{49,177},{... | collective-permute-start | bytes 208904 | tf_op jit(solution)/shard_map/ppermute | solution.py:347
  96.9 4.7 %collective-permute-start.17 = (f32[136,128]{1,0:T(8,128)S(1)}, f32[136,128]{1,0:T(8,128)S(1)}, u32[]{:S(2)}, u32[]{:S(2)}) collective-permute-start(f32[136,128]{1,0:T(8,128)S(1)} %get-tuple-element.48.own), channel_id=1, source_target_pairs={{0,48},{1,193},{16,0},{17,209},{32,16},{33,225},{48,32},{49,241},{... | collective-permute-start | bytes 208904 | tf_op jit(solution)/shard_map/ppermute | solution.py:347
  97.8 4.7 %collective-permute-start.16 = (f32[136,128]{1,0:T(8,128)S(1)}, f32[136,128]{1,0:T(8,128)S(1)}, u32[]{:S(2)}, u32[]{:S(2)}) collective-permute-start(f32[136,128]{1,0:T(8,128)S(1)} %get-tuple-element.48.own), channel_id=1, source_target_pairs={{0,16},{1,65},{16,32},{17,81},{32,48},{33,97},{48,0},{49,113},{64,... | collective-permute-start | bytes 208904 | tf_op jit(solution)/shard_map/ppermute | solution.py:347
  102.6 4.8 %collective-permute-start.21 = (f32[136,128]{1,0:T(8,128)S(1)}, f32[136,128]{1,0:T(8,128)S(1)}, u32[]{:S(2)}, u32[]{:S(2)}) collective-permute-start(f32[136,128]{1,0:T(8,128)S(1)} %sums.3.own), channel_id=1, source_target_pairs={{0,128},{1,33},{16,144},{17,49},{32,160},{33,1},{48,176},{49,17},{... | collective-permute-start | bytes 208904 | tf_op jit(solution)/shard_map/ppermute | solution.py:347
  102.7 4.7 %collective-permute-start.20 = (f32[136,128]{1,0:T(8,128)S(1)}, f32[136,128]{1,0:T(8,128)S(1)}, u32[]{:S(2)}, u32[]{:S(2)}) collective-permute-start(f32[136,128]{1,0:T(8,128)S(1)} %sums.3.own), channel_id=1, source_target_pairs={{0,192},{1,49},{16,208},{17,1},{32,224},{33,17},{48,240},{49,33},{... | collective-permute-start | bytes 208904 | tf_op jit(solution)/shard_map/ppermute | solution.py:347
  103.4 4.7 %collective-permute-start.19 = (f32[136,128]{1,0:T(8,128)S(1)}, f32[136,128]{1,0:T(8,128)S(1)}, u32[]{:S(2)}, u32[]{:S(2)}) collective-permute-start(f32[136,128]{1,0:T(8,128)S(1)} %sums.3.own), channel_id=1, source_target_pairs={{0,64},{1,17},{16,80},{17,33},{32,96},{33,49},{48,112},{49,1},{64,... | collective-permute-start | bytes 208904 | tf_op jit(solution)/shard_map/ppermute | solution.py:347

commit v9 on v8

--- a/solution.py
+++ b/solution.py
@@ -23,6 +23,7 @@
 
 SLOT_ROWS, SLOT_COLS, COUNT, AT_Y, AT_X, AT_Z, AT_CORE = range(7)
 COL_KINDS, COST, ROW_SIDE, TABLE, SIDE = 8, 16, 24, 32, 40
+HANDED = 12288
 STEP = 0.4
 
 VMEM = pl.BlockSpec(memory_space=pltpu.VMEM)
@@ -30,14 +31,16 @@
 HBM = pl.BlockSpec(memory_space=pltpu.HBM)
 
 
-def call(kernel, name, out_shapes, args, smem=0, hbm=0, smem_out=False, scratch=(), vmem=8 * 2**20, cost=None):
+def call(kernel, name, out_shapes, args, smem=0, hbm=0, smem_out=False, hbm_out=(), scratch=(), vmem=8 * 2**20, cost=None):
     shapes = tuple(jax.ShapeDtypeStruct(s, d) for s, d in out_shapes)
     return pl.pallas_call(
         kernel,
         name=name,
         out_shape=shapes,
         in_specs=[SMEM] * smem + [HBM] * hbm + [VMEM] * (len(args) - smem - hbm),
-        out_specs=tuple([SMEM if smem_out else VMEM] * len(shapes)),
+        out_specs=tuple(
+            HBM if k in hbm_out else SMEM if smem_out else VMEM for k in range(len(shapes))
+        ),
         scratch_shapes=list(scratch),
         compiler_params=pltpu.CompilerParams(vmem_limit_bytes=vmem),
         cost_estimate=cost,
@@ -105,7 +108,7 @@
 
 
 def pack(
-    count, rows, cols, row_kinds, rhs, dual, col_kinds, cost, primal, duals, side, places, kinds, start, done
+    count, rows, cols, row_kinds, rhs, dual, col_kinds, cost, primal, duals, handed, side, places, kinds, start, done
 ):
     copies = [
         pltpu.make_async_copy(source, target, done.at[k])
@@ -139,7 +142,10 @@
     side[TABLE : TABLE + COUNT, 0:SLOTS] = places[...].astype(F32)
     side[COL_KINDS:COST, :] = kinds[COLS_SHARE:, :].astype(F32)
     side[ROW_SIDE + ROWS_SHARE : TABLE, :] = kinds[0:ROWS_SHARE, :].astype(F32)
+    hand = pltpu.make_async_copy(side, handed.at[0:SIDE], done.at[8])
+    hand.start()
     duals[...] = jnp.broadcast_to(start[...][None], duals.shape)
+    hand.wait()
 
 
 def turn(pairs, turned):
@@ -191,20 +197,23 @@
 
 
 def first_adjoint(
-    tiles, duals, side, payload, dual, table_out, pairs, chunks, table, done, total
+    tiles, handed, duals, payload, dual, side, table_out, pairs, chunks, table, done, total
 ):
+    share = pltpu.make_async_copy(handed.at[0:SIDE], side, done.at[len(PIECES) + 1])
+    share.start()
     copies, first = [], 0
     for k, slots in enumerate(PIECES):
         part = pl.ds(first, slots)
         copies.append(pltpu.make_async_copy(tiles.at[part], chunks.at[part], done.at[k]))
         copies[k].start()
         first += slots
+    for k in range(N):
+        dual[k * ROWS_SHARE : (k + 1) * ROWS_SHARE, :] = duals[k]
+    total[...] = jnp.zeros_like(total)
+    share.wait()
     table_out[...] = side[TABLE:, :].astype(jnp.int32)
     read = pltpu.make_async_copy(table_out, table, done.at[len(PIECES)])
     read.start()
-    for k in range(N):
-        dual[k * ROWS_SHARE : (k + 1) * ROWS_SHARE, :] = duals[k]
-    total[...] = jnp.zeros_like(total)
     payload[COL_BLOCKS:, :] = side[0:COST, :]
     read.wait()
 
@@ -278,34 +287,40 @@
         given[rows, :] = total[pl.ds(HALF - mine, HALF), part, :]
 
 
+def row_terms(table, held, before, rhs, ineq, side, primal1, primal2, terms):
+    offset = table[AT_Z, 0] * ROWS_SHARE
+    share = pl.ds(table[AT_CORE, 0] * HALF + offset, ROWS_SHARE)
+    image, plain = held[pl.ds(offset, ROWS_SHARE), :], held[HALF : HALF + ROWS_SHARE, :]
+    earlier, bound, kind = before[share, :], rhs[share, :], ineq[share, :]
+    last = clamp_dual(earlier + STEP * (bound - image), kind)
+    rows = []
+    for product in (plain, 0.5 * (3.0 * plain - image)):
+        residual = bound - product
+        residual = jnp.where(kind > 0.5, jnp.maximum(residual, 0.0), residual)
+        rows.append(jnp.sum(residual * residual, 0, keepdims=True))
+    columns = own_columns(table)
+    price, final = side[COST:ROW_SIDE, :], primal2[columns, :]
+    for primal, value in (
+        (final, last),
+        (0.5 * (primal1[columns, :] + final), 0.5 * (earlier + last)),
+    ):
+        gain = jnp.sum(price * primal, 0, keepdims=True)
+        rows.append(gain - jnp.sum(bound * value, 0, keepdims=True))
+    terms[...] = jnp.concatenate(rows + rows, 0)
+
+
 def third_adjoint(
-    table, held, other, before, rhs, ineq, side, primal1, primal2, pairs, payload, mine, dual, image, total
+    table, held, other, before, rhs, ineq, side, terms, pairs, payload, mine, dual, image, total
 ):
     half = pl.multiple_of(table[AT_CORE, 0] * HALF, HALF)
     image[pl.ds(half, HALF), :] = held[0:HALF, :]
     image[pl.ds(HALF - half, HALF), :] = other[0:HALF, :]
     dual[...] = clamp_dual(before[...] + STEP * (rhs[...] - image[...]), ineq[...])
     mine[...] = dual[pl.ds(index_col(table) * ROWS_SHARE, ROWS_SHARE), :]
-    share = pl.ds(half + table[AT_Z, 0] * ROWS_SHARE, ROWS_SHARE)
-    plain = held[HALF : HALF + ROWS_SHARE, :]
-    bound, kind, last = rhs[share, :], ineq[share, :], dual[share, :]
-    terms = []
-    for product in (plain, 0.5 * (3.0 * plain - image[share, :])):
-        residual = bound - product
-        residual = jnp.where(kind > 0.5, jnp.maximum(residual, 0.0), residual)
-        terms.append(jnp.sum(residual * residual, 0, keepdims=True))
-    columns = own_columns(table)
-    price, final = side[COST:ROW_SIDE, :], primal2[columns, :]
-    for primal, value in (
-        (final, last),
-        (0.5 * (primal1[columns, :] + final), 0.5 * (before[share, :] + last)),
-    ):
-        gain = jnp.sum(price * primal, 0, keepdims=True)
-        terms.append(gain - jnp.sum(bound * value, 0, keepdims=True))
-    payload[COL_BLOCKS : COL_BLOCKS + 8, :] = jnp.concatenate(terms + terms, 0)
     adjoint_product(table, lambda slot: pairs[slot], dual, total)
     payload[0:COL_BLOCKS, :] = total[:, 0, :]
-    payload[columns, :] -= price
+    payload[COL_BLOCKS : COL_BLOCKS + 8, :] = terms[...]
+    payload[own_columns(table), :] -= side[COST:ROW_SIDE, :]
 
 
 def column_terms(own, right, left, opposite, earlier, free, terms):
@@ -372,37 +387,40 @@
     row_total = [pltpu.VMEM((ROW_BLOCKS, 8, TILE), F32)]
     col_total = [pltpu.VMEM((COL_BLOCKS, 8, TILE), F32)]
 
-    duals, side = call(
+    duals, handed = call(
         pack,
         "pack",
-        [((N, ROWS_SHARE, TILE), F32), ((SIDE, TILE), F32)],
+        [((N, ROWS_SHARE, TILE), F32), ((HANDED, TILE), F32)],
         (tile_count, tile_rows, tile_cols, row_types, rhs, dual_start, var_types, cost, primal_start),
         smem=1,
         hbm=8,
+        hbm_out=(1,),
         scratch=[
+            pltpu.VMEM((SIDE, TILE), F32),
             pltpu.VMEM((2, SLOTS), jnp.int32),
             pltpu.VMEM((2 * COLS_SHARE, TILE), jnp.int32),
             pltpu.VMEM((ROWS_SHARE, TILE), F32),
-            pltpu.SemaphoreType.DMA((8,)),
+            pltpu.SemaphoreType.DMA((9,)),
         ],
         vmem=PACK_VMEM,
     )
 
-    payload, dual0, table, pairs = call(
+    payload, dual0, side, table, pairs = call(
         first_adjoint,
         "first_adjoint",
         [
             ((COL_BLOCKS + 2 * COLS_SHARE, TILE), F32),
             (blocks, F32),
+            ((SIDE, TILE), F32),
             ((8, TILE), jnp.int32),
             ((SLOTS, 2 * TILE, TILE), BF16),
         ],
-        (tiles, exchange(duals, ("z", "core")), side),
-        hbm=1,
+        (tiles, handed, exchange(duals, ("z", "core"))),
+        hbm=2,
         scratch=[
             pltpu.VMEM((SLOTS, TILE, TILE), F32),
             pltpu.SMEM((8, TILE), jnp.int32),
-            pltpu.SemaphoreType.DMA((len(PIECES) + 1,)),
+            pltpu.SemaphoreType.DMA((len(PIECES) + 2,)),
         ]
         + col_total,
         vmem=FIRST_VMEM,
@@ -457,12 +475,21 @@
         pair_copies, "pair_copies", [((8, HALF + 8, TILE), F32)], (kept, swap_cores(given))
     )
     held = call(pair_sums, "pair_sums", [((HALF + 8, TILE), F32)], (exchange(copies[0], "z"),))[0]
+    other = swap_cores(held)
+    terms = call(
+        row_terms,
+        "row_terms",
+        [((8, TILE), F32)],
+        (table, held, dual1, rhs_full, ineq, side, primal1, primal2),
+        smem=1,
+        cost=pl.CostEstimate(flops=0, bytes_accessed=2**21, transcendentals=0),
+    )[0]
 
     payload, dual_mine = call(
         third_adjoint,
         "third_adjoint",
         [((COL_BLOCKS + 8, TILE), F32), ((ROWS_SHARE, TILE), F32)],
-        (table, held, swap_cores(held), dual1, rhs_full, ineq, side, primal1, primal2, pairs),
+        (table, held, other, dual1, rhs_full, ineq, side, terms, pairs),
         smem=1,
         scratch=[pltpu.VMEM(blocks, F32)] * 2 + col_total,
     )

time: 122 us -> 122 us (level)
  Pallas kernels: 12.9 us -> 14.3 us
    pallas_call x16 -> x17, Pallas kernels: 12.9 us -> 14.3 us  [call(): pl.pallas_call(kernel, name=name, out_shape=shapes, in_specs=[SMEM] * sme...]
where the time goes in v9:
time: 122 us
  blocking collectives  53.2 us (44%)
  starting transfers between devices  26.5 us (22%)
  waiting for transfers between devices  26.2 us (21%)
  Pallas kernels  14.3 us (12%)
  between operations  1.54 us (1%)
    all_to_all x4, blocking collectives, exchange(): return lax.all_to_all(copies, axes, 0, 0)  53.2 us
    ppermute x18, waiting for transfers between devices, shift(): return lax.ppermute(values, ('y', 'x', 'core'), pairs)  23.4 us
    ppermute x18, starting transfers between devices, shift(): return lax.ppermute(values, ('y', 'x', 'core'), pairs)  15.7 us
    pallas_call x17, Pallas kernels, call(): pl.pallas_call(kernel, name=name, out_shape=shapes, in_specs=[SMEM] * sme...  14.3 us
    ppermute x4, starting transfers between devices, swap_cores(): return lax.ppermute(values, 'core', [(0, 1), (1, 0)])  10.8 us
    ppermute x4, waiting for transfers between devices, swap_cores(): return lax.ppermute(values, 'core', [(0, 1), (1, 0)])  2.8 us
  transfers between devices with their start and end apart: 22, of which 17 were waited for; matrix products, arithmetic and copies ran while one was open for 0% of the time, Pallas kernels for 1%

profile of v9, /device:TPU:1, one launch (start us, length us, event | category | flops | bytes accessed | tf_op | source)
XLA Modules:
  0.0 121.8 jit_solution(3998972183376044637)
XLA Ops:
  1.3 2.1 %pack.1 = (f32[16,4,128]{2,1,0:T(4,128)}, f32[12288,128]{1,0:T(8,128)}) custom-call(s32[1,1]{1,0:T(1,128)S(6)} %copy.15.count, s32[1,1,64]{2,1,0:T(1,128)} %rows.1, s32[1,1,64]{2,1,0:T(1,128)} %cols.1, s32[1,4,128]{2,1,0:T(4,128)} %row_kinds.1, f32[1,4,128]{2,1,0:T(4,128)} %rhs.1, f32[1,4,128]{2,1,0:T(4,128)} %dual.1, s32[1,8,128]{2,1,0:T(8,128)} %col_kinds.1, ...), custom_call_target="tpu_custom_call" | custom-call | tf_op jit(solution)/shard_map/pack/pallas_call | solution.py:36
  3.4 17.4 %all_to_all.20.duals = f32[16,4,128]{2,1,0:T(4,128)S(1)} all-to-all(f32[16,4,128]{2,1,0:T(4,128)} %get-tuple-element.31), channel_id=1, replica_groups=mesh['y'=4,'x'=4,'z'=8,'core'=2] {'z','core'}, dimensions={0} | all-to-all | bytes 65536 | tf_op jit(solution)/shard_map/all_to_all | solution.py:379
  20.8 2.7 %first_adjoint.1 = (f32[144,128]{1,0:T(8,128)S(1)}, f32[64,128]{1,0:T(8,128)S(1)}, f32[40,128]{1,0:T(8,128)S(1)}, s32[8,128]{1,0:T(8,128)S(1)}, bf16[64,256,128]{2,1,0:T(8,128)(2,1)S(1)}) custom-call(f32[64,128,128]{2,1,0:T(8,128)} %bitcast.3, f32[12288,128]{1,0:T(8,128)} %get-tuple-element.30.handed, f32[16,4,128]{2,1,0:T(4,128)S(1)} %all_to_all.20.duals), custom_call_target="tpu_custom_call" | custom-call | tf_op jit(solution)/shard_map/first_adjoint/pallas_call | solution.py:36
  23.5 3.0 %collective-permute-start.2 = (f32[144,128]{1,0:T(8,128)S(1)}, f32[144,128]{1,0:T(8,128)S(1)}, u32[]{:S(2)}, u32[]{:S(2)}) collective-permute-start(f32[144,128]{1,0:T(8,128)S(1)} %get-tuple-element.33.own), channel_id=1, source_target_pairs={{0,32},{1,129},{16,48},{17,145},{32,0},{33,161},{48,16},{49,177},{... | collective-permute-start | bytes 221192 | tf_op jit(solution)/shard_map/ppermute | solution.py:362
  29.7 2.0 %collective-permute-done.right = f32[144,128]{1,0:T(8,128)S(1)} collective-permute-done((f32[144,128]{1,0:T(8,128)S(1)}, f32[144,128]{1,0:T(8,128)S(1)}, u32[]{:S(2)}, u32[]{:S(2)}) %collective-permute-start) | collective-permute-done | bytes 73760 | tf_op jit(solution)/shard_map/ppermute | solution.py:362
  31.7 2.8 %collective-permute-start.5 = (f32[192,128]{1,0:T(8,128)S(1)}, f32[192,128]{1,0:T(8,128)S(1)}, u32[]{:S(2)}, u32[]{:S(2)}) collective-permute-start(f32[192,128]{1,0:T(8,128)S(1)} %ring_sums.1.own), channel_id=1, source_target_pairs={{0,128},{1,33},{16,144},{17,49},{32,160},{33,1},{48,176},{49,17},{... | collective-permute-start | bytes 294920 | tf_op jit(solution)/shard_map/ppermute | solution.py:362
  38.0 2.1 %collective-permute-done.3.right = f32[192,128]{1,0:T(8,128)S(1)} collective-permute-done((f32[192,128]{1,0:T(8,128)S(1)}, f32[192,128]{1,0:T(8,128)S(1)}, u32[]{:S(2)}, u32[]{:S(2)}) %collective-permute-start.3) | collective-permute-done | bytes 98336 | tf_op jit(solution)/shard_map/ppermute | solution.py:362
  40.1 1.8 %first_forward.1 = (f32[32,128]{1,0:T(8,128)S(1)}, f32[32,128]{1,0:T(8,128)S(1)}, f32[128,128]{1,0:T(8,128)S(1)}, f32[128,128]{1,0:T(8,128)}, f32[128,128]{1,0:T(8,128)S(1)}) custom-call(s32[8,128]{1,0:T(8,128)S(1)} %get-tuple-element.32.table, f32[192,128]{1,0:T(8,128)S(1)} %ring_sums.1.own, f32[192,128]{1,0:T(8,128)S(1)} %collective-permute-done.3.right, ...), custom_call_target="tpu_custom_call" | custom-call | tf_op jit(solution)/shard_map/first_forward/pallas_call | solution.py:36
  41.9 3.8 %collective-permute-start.6 = (f32[32,128]{1,0:T(8,128)S(1)}, f32[32,128]{1,0:T(8,128)S(1)}, u32[]{:S(2)}, u32[]{:S(2)}) collective-permute-start(f32[32,128]{1,0:T(8,128)S(1)} %get-tuple-element.36), channel_id=1, source_target_pairs={{0,1},{1,0},{2,3},{3,2},{4,5},{5,4},{6,7},{7,6},{8,9},{9,8},{10,11... | collective-permute-start | bytes 49160 | tf_op jit(solution)/shard_map/ppermute | solution.py:375
  46.6 11.6 %all_to_all.21.pieces = f32[8,40,128]{2,1,0:T(8,128)S(1)} all-to-all(f32[8,40,128]{2,1,0:T(8,128)S(1)} %image_copies.1), channel_id=1, replica_groups=mesh['y'=4,'x'=4,'z'=8,'core'=2] {'z'}, dimensions={0} | all-to-all | bytes 327680 | tf_op jit(solution)/shard_map/all_to_all | solution.py:379
  58.2 1.6 %collective-permute-start.7 = (f32[96,128]{1,0:T(8,128)S(1)}, f32[96,128]{1,0:T(8,128)S(1)}, u32[]{:S(2)}, u32[]{:S(2)}) collective-permute-start(f32[96,128]{1,0:T(8,128)S(1)} %image_sums.1.held), channel_id=1, source_target_pairs={{0,1},{1,0},{2,3},{3,2},{4,5},{5,4},{6,7},{7,6},{8,9},{9,8},{10,11... | collective-permute-start | bytes 147464 | tf_op jit(solution)/shard_map/ppermute | solution.py:375
  62.3 1.7 %collective-permute-start.9 = (f32[128,128]{1,0:T(8,128)S(1)}, f32[128,128]{1,0:T(8,128)S(1)}, u32[]{:S(2)}, u32[]{:S(2)}) collective-permute-start(f32[128,128]{1,0:T(8,128)S(1)} %get-tuple-element.39.own), channel_id=1, source_target_pairs={{0,48},{1,193},{16,0},{17,209},{32,16},{33,225},{48,32},{49,241},{... | collective-permute-start | bytes 196616 | tf_op jit(solution)/shard_map/ppermute | solution.py:362
  64.0 2.7 %collective-permute-done.10.opposite = f32[128,128]{1,0:T(8,128)S(1)} collective-permute-done((f32[128,128]{1,0:T(8,128)S(1)}, f32[128,128]{1,0:T(8,128)S(1)}, u32[]{:S(2)}, u32[]{:S(2)}) %collective-permute-start.10) | collective-permute-done | bytes 65568 | tf_op jit(solution)/shard_map/ppermute | solution.py:362
  66.7 1.6 %collective-permute-done.8.right = f32[128,128]{1,0:T(8,128)S(1)} collective-permute-done((f32[128,128]{1,0:T(8,128)S(1)}, f32[128,128]{1,0:T(8,128)S(1)}, u32[]{:S(2)}, u32[]{:S(2)}) %collective-permute-start.8) | collective-permute-done | bytes 65568 | tf_op jit(solution)/shard_map/ppermute | solution.py:362
  68.4 1.8 %collective-permute-start.12 = (f32[128,128]{1,0:T(8,128)S(1)}, f32[128,128]{1,0:T(8,128)S(1)}, u32[]{:S(2)}, u32[]{:S(2)}) collective-permute-start(f32[128,128]{1,0:T(8,128)S(1)} %sums.2.own), channel_id=1, source_target_pairs={{0,192},{1,49},{16,208},{17,1},{32,224},{33,17},{48,240},{49,33},{... | collective-permute-start | bytes 196616 | tf_op jit(solution)/shard_map/ppermute | solution.py:362
  70.2 2.8 %collective-permute-done.13.opposite = f32[128,128]{1,0:T(8,128)S(1)} collective-permute-done((f32[128,128]{1,0:T(8,128)S(1)}, f32[128,128]{1,0:T(8,128)S(1)}, u32[]{:S(2)}, u32[]{:S(2)}) %collective-permute-start.13) | collective-permute-done | bytes 65568 | tf_op jit(solution)/shard_map/ppermute | solution.py:362
  74.5 1.8 %second_forward.1 = (f32[64,128]{1,0:T(8,128)S(1)}, f32[64,128]{1,0:T(8,128)S(1)}, f32[128,128]{1,0:T(8,128)S(1)}, f32[128,128]{1,0:T(8,128)S(1)}, f32[8,128]{1,0:T(8,128)}) custom-call(s32[8,128]{1,0:T(8,128)S(1)} %get-tuple-element.32.table, f32[128,128]{1,0:T(8,128)S(1)} %sums.2.own, f32[128,128]{1,0:T(8,128)S(1)} %collective-permute-done.11.right, ...), custom_call_target="tpu_custom_call" | custom-call | tf_op jit(solution)/shard_map/second_forward/pallas_call | solution.py:36
  76.4 3.8 %collective-permute-start.14 = (f32[64,128]{1,0:T(8,128)S(1)}, f32[64,128]{1,0:T(8,128)S(1)}, u32[]{:S(2)}, u32[]{:S(2)}) collective-permute-start(f32[64,128]{1,0:T(8,128)S(1)} %get-tuple-element.44), channel_id=1, source_target_pairs={{0,1},{1,0},{2,3},{3,2},{4,5},{5,4},{6,7},{7,6},{8,9},{9,8},{10,11... | collective-permute-start | bytes 98312 | tf_op jit(solution)/shard_map/ppermute | solution.py:375
  81.0 11.6 %all_to_all.22.pieces = f32[8,40,128]{2,1,0:T(8,128)S(1)} all-to-all(f32[8,40,128]{2,1,0:T(8,128)S(1)} %pair_copies.1), channel_id=1, replica_groups=mesh['y'=4,'x'=4,'z'=8,'core'=2] {'z'}, dimensions={0} | all-to-all | bytes 327680 | tf_op jit(solution)/shard_map/all_to_all | solution.py:379
  92.6 1.6 %collective-permute-start.15 = (f32[40,128]{1,0:T(8,128)S(1)}, f32[40,128]{1,0:T(8,128)S(1)}, u32[]{:S(2)}, u32[]{:S(2)}) collective-permute-start(f32[40,128]{1,0:T(8,128)S(1)} %pair_sums.1.held), channel_id=1, source_target_pairs={{0,1},{1,0},{2,3},{3,2},{4,5},{5,4},{6,7},{7,6},{8,9},{9,8},{10,11... | collective-permute-start | bytes 61448 | tf_op jit(solution)/shard_map/ppermute | solution.py:375
  95.1 1.8 %third_adjoint.1 = (f32[136,128]{1,0:T(8,128)S(1)}, f32[4,128]{1,0:T(4,128)}) custom-call(s32[8,128]{1,0:T(8,128)S(1)} %get-tuple-element.32.table, f32[40,128]{1,0:T(8,128)S(1)} %pair_sums.1.held, f32[40,128]{1,0:T(8,128)S(1)} %collective-permute-done.15.other, f32[64,128]{1,0:T(8,128)S(1)} %get-tuple-element.45.before, ...), custom_call_target="tpu_custom_call" | custom-call | tf_op jit(solution)/shard_map/third_adjoint/pallas_call | solution.py:36
  98.4 3.2 %collective-permute-done.18.opposite = f32[136,128]{1,0:T(8,128)S(1)} collective-permute-done((f32[136,128]{1,0:T(8,128)S(1)}, f32[136,128]{1,0:T(8,128)S(1)}, u32[]{:S(2)}, u32[]{:S(2)}) %collective-permute-start.18) | collective-permute-done | bytes 69664 | tf_op jit(solution)/shard_map/ppermute | solution.py:362
  104.3 3.1 %collective-permute-done.21.opposite = f32[136,128]{1,0:T(8,128)S(1)} collective-permute-done((f32[136,128]{1,0:T(8,128)S(1)}, f32[136,128]{1,0:T(8,128)S(1)}, u32[]{:S(2)}, u32[]{:S(2)}) %collective-permute-start.21) | collective-permute-done | bytes 69664 | tf_op jit(solution)/shard_map/ppermute | solution.py:362
  108.3 12.7 %all_to_all.23.gathered = f32[16,1,128]{2,1,0:T(1,128)S(1)} all-to-all(f32[16,1,128]{2,1,0:T(1,128)S(1)} %column_terms.1), channel_id=1, replica_groups=mesh['y'=4,'x'=4,'z'=8,'core'=2] {'z','core'}, dimensions={0} | all-to-all | bytes 16384 | tf_op jit(solution)/shard_map/all_to_all | solution.py:379
  (41 shorter events, 19.1 us)
Async XLA Ops:
  23.5 4.8 %collective-permute-start.2 = (f32[144,128]{1,0:T(8,128)S(1)}, f32[144,128]{1,0:T(8,128)S(1)}, u32[]{:S(2)}, u32[]{:S(2)}) collective-permute-start(f32[144,128]{1,0:T(8,128)S(1)} %get-tuple-element.33.own), channel_id=1, source_target_pairs={{0,32},{1,129},{16,48},{17,145},{32,0},{33,161},{48,16},{49,177},{... | collective-permute-start | bytes 221192 | tf_op jit(solution)/shard_map/ppermute | solution.py:362
  26.5 3.2 %collective-permute-start.1 = (f32[144,128]{1,0:T(8,128)S(1)}, f32[144,128]{1,0:T(8,128)S(1)}, u32[]{:S(2)}, u32[]{:S(2)}) collective-permute-start(f32[144,128]{1,0:T(8,128)S(1)} %get-tuple-element.33.own), channel_id=1, source_target_pairs={{0,48},{1,193},{16,0},{17,209},{32,16},{33,225},{48,32},{49,241},{... | collective-permute-start | bytes 221192 | tf_op jit(solution)/shard_map/ppermute | solution.py:362
  27.3 4.4 %collective-permute-start = (f32[144,128]{1,0:T(8,128)S(1)}, f32[144,128]{1,0:T(8,128)S(1)}, u32[]{:S(2)}, u32[]{:S(2)}) collective-permute-start(f32[144,128]{1,0:T(8,128)S(1)} %get-tuple-element.33.own), channel_id=1, source_target_pairs={{0,16},{1,65},{16,32},{17,81},{32,48},{33,97},{48,0},{49,113},{64,... | collective-permute-start | bytes 221192 | tf_op jit(solution)/shard_map/ppermute | solution.py:362
  31.7 5.4 %collective-permute-start.5 = (f32[192,128]{1,0:T(8,128)S(1)}, f32[192,128]{1,0:T(8,128)S(1)}, u32[]{:S(2)}, u32[]{:S(2)}) collective-permute-start(f32[192,128]{1,0:T(8,128)S(1)} %ring_sums.1.own), channel_id=1, source_target_pairs={{0,128},{1,33},{16,144},{17,49},{32,160},{33,1},{48,176},{49,17},{... | collective-permute-start | bytes 294920 | tf_op jit(solution)/shard_map/ppermute | solution.py:362
  34.6 3.5 %collective-permute-start.4 = (f32[192,128]{1,0:T(8,128)S(1)}, f32[192,128]{1,0:T(8,128)S(1)}, u32[]{:S(2)}, u32[]{:S(2)}) collective-permute-start(f32[192,128]{1,0:T(8,128)S(1)} %ring_sums.1.own), channel_id=1, source_target_pairs={{0,192},{1,49},{16,208},{17,1},{32,224},{33,17},{48,240},{49,33},{... | collective-permute-start | bytes 294920 | tf_op jit(solution)/shard_map/ppermute | solution.py:362
  35.4 4.7 %collective-permute-start.3 = (f32[192,128]{1,0:T(8,128)S(1)}, f32[192,128]{1,0:T(8,128)S(1)}, u32[]{:S(2)}, u32[]{:S(2)}) collective-permute-start(f32[192,128]{1,0:T(8,128)S(1)} %ring_sums.1.own), channel_id=1, source_target_pairs={{0,64},{1,17},{16,80},{17,33},{32,96},{33,49},{48,112},{49,1},{64,... | collective-permute-start | bytes 294920 | tf_op jit(solution)/shard_map/ppermute | solution.py:362
  41.9 4.7 %collective-permute-start.6 = (f32[32,128]{1,0:T(8,128)S(1)}, f32[32,128]{1,0:T(8,128)S(1)}, u32[]{:S(2)}, u32[]{:S(2)}) collective-permute-start(f32[32,128]{1,0:T(8,128)S(1)} %get-tuple-element.36), channel_id=1, source_target_pairs={{0,1},{1,0},{2,3},{3,2},{4,5},{5,4},{6,7},{7,6},{8,9},{9,8},{10,11... | collective-permute-start | bytes 49160 | tf_op jit(solution)/shard_map/ppermute | solution.py:375
  58.2 2.5 %collective-permute-start.7 = (f32[96,128]{1,0:T(8,128)S(1)}, f32[96,128]{1,0:T(8,128)S(1)}, u32[]{:S(2)}, u32[]{:S(2)}) collective-permute-start(f32[96,128]{1,0:T(8,128)S(1)} %image_sums.1.held), channel_id=1, source_target_pairs={{0,1},{1,0},{2,3},{3,2},{4,5},{5,4},{6,7},{7,6},{8,9},{9,8},{10,11... | collective-permute-start | bytes 147464 | tf_op jit(solution)/shard_map/ppermute | solution.py:375
  62.0 4.7 %collective-permute-start.10 = (f32[128,128]{1,0:T(8,128)S(1)}, f32[128,128]{1,0:T(8,128)S(1)}, u32[]{:S(2)}, u32[]{:S(2)}) collective-permute-start(f32[128,128]{1,0:T(8,128)S(1)} %get-tuple-element.39.own), channel_id=1, source_target_pairs={{0,32},{1,129},{16,48},{17,145},{32,0},{33,161},{48,16},{49,177},{... | collective-permute-start | bytes 196616 | tf_op jit(solution)/shard_map/ppermute | solution.py:362
  62.3 4.4 %collective-permute-start.9 = (f32[128,128]{1,0:T(8,128)S(1)}, f32[128,128]{1,0:T(8,128)S(1)}, u32[]{:S(2)}, u32[]{:S(2)}) collective-permute-start(f32[128,128]{1,0:T(8,128)S(1)} %get-tuple-element.39.own), channel_id=1, source_target_pairs={{0,48},{1,193},{16,0},{17,209},{32,16},{33,225},{48,32},{49,241},{... | collective-permute-start | bytes 196616 | tf_op jit(solution)/shard_map/ppermute | solution.py:362
  64.0 4.3 %collective-permute-start.8 = (f32[128,128]{1,0:T(8,128)S(1)}, f32[128,128]{1,0:T(8,128)S(1)}, u32[]{:S(2)}, u32[]{:S(2)}) collective-permute-start(f32[128,128]{1,0:T(8,128)S(1)} %get-tuple-element.39.own), channel_id=1, source_target_pairs={{0,16},{1,65},{16,32},{17,81},{32,48},{33,97},{48,0},{49,113},{64,... | collective-permute-start | bytes 196616 | tf_op jit(solution)/shard_map/ppermute | solution.py:362
  68.3 4.7 %collective-permute-start.13 = (f32[128,128]{1,0:T(8,128)S(1)}, f32[128,128]{1,0:T(8,128)S(1)}, u32[]{:S(2)}, u32[]{:S(2)}) collective-permute-start(f32[128,128]{1,0:T(8,128)S(1)} %sums.2.own), channel_id=1, source_target_pairs={{0,128},{1,33},{16,144},{17,49},{32,160},{33,1},{48,176},{49,17},{... | collective-permute-start | bytes 196616 | tf_op jit(solution)/shard_map/ppermute | solution.py:362
  68.4 4.6 %collective-permute-start.12 = (f32[128,128]{1,0:T(8,128)S(1)}, f32[128,128]{1,0:T(8,128)S(1)}, u32[]{:S(2)}, u32[]{:S(2)}) collective-permute-start(f32[128,128]{1,0:T(8,128)S(1)} %sums.2.own), channel_id=1, source_target_pairs={{0,192},{1,49},{16,208},{17,1},{32,224},{33,17},{48,240},{49,33},{... | collective-permute-start | bytes 196616 | tf_op jit(solution)/shard_map/ppermute | solution.py:362
  70.2 4.3 %collective-permute-start.11 = (f32[128,128]{1,0:T(8,128)S(1)}, f32[128,128]{1,0:T(8,128)S(1)}, u32[]{:S(2)}, u32[]{:S(2)}) collective-permute-start(f32[128,128]{1,0:T(8,128)S(1)} %sums.2.own), channel_id=1, source_target_pairs={{0,64},{1,17},{16,80},{17,33},{32,96},{33,49},{48,112},{49,1},{64,... | collective-permute-start | bytes 196616 | tf_op jit(solution)/shard_map/ppermute | solution.py:362
  76.4 4.6 %collective-permute-start.14 = (f32[64,128]{1,0:T(8,128)S(1)}, f32[64,128]{1,0:T(8,128)S(1)}, u32[]{:S(2)}, u32[]{:S(2)}) collective-permute-start(f32[64,128]{1,0:T(8,128)S(1)} %get-tuple-element.44), channel_id=1, source_target_pairs={{0,1},{1,0},{2,3},{3,2},{4,5},{5,4},{6,7},{7,6},{8,9},{9,8},{10,11... | collective-permute-start | bytes 98312 | tf_op jit(solution)/shard_map/ppermute | solution.py:375
  92.6 2.5 %collective-permute-start.15 = (f32[40,128]{1,0:T(8,128)S(1)}, f32[40,128]{1,0:T(8,128)S(1)}, u32[]{:S(2)}, u32[]{:S(2)}) collective-permute-start(f32[40,128]{1,0:T(8,128)S(1)} %pair_sums.1.held), channel_id=1, source_target_pairs={{0,1},{1,0},{2,3},{3,2},{4,5},{5,4},{6,7},{7,6},{8,9},{9,8},{10,11... | collective-permute-start | bytes 61448 | tf_op jit(solution)/shard_map/ppermute | solution.py:375
  96.9 4.7 %collective-permute-start.18 = (f32[136,128]{1,0:T(8,128)S(1)}, f32[136,128]{1,0:T(8,128)S(1)}, u32[]{:S(2)}, u32[]{:S(2)}) collective-permute-start(f32[136,128]{1,0:T(8,128)S(1)} %get-tuple-element.50.own), channel_id=1, source_target_pairs={{0,32},{1,129},{16,48},{17,145},{32,0},{33,161},{48,16},{49,177},{... | collective-permute-start | bytes 208904 | tf_op jit(solution)/shard_map/ppermute | solution.py:362
  96.9 4.7 %collective-permute-start.17 = (f32[136,128]{1,0:T(8,128)S(1)}, f32[136,128]{1,0:T(8,128)S(1)}, u32[]{:S(2)}, u32[]{:S(2)}) collective-permute-start(f32[136,128]{1,0:T(8,128)S(1)} %get-tuple-element.50.own), channel_id=1, source_target_pairs={{0,48},{1,193},{16,0},{17,209},{32,16},{33,225},{48,32},{49,241},{... | collective-permute-start | bytes 208904 | tf_op jit(solution)/shard_map/ppermute | solution.py:362
  97.9 4.7 %collective-permute-start.16 = (f32[136,128]{1,0:T(8,128)S(1)}, f32[136,128]{1,0:T(8,128)S(1)}, u32[]{:S(2)}, u32[]{:S(2)}) collective-permute-start(f32[136,128]{1,0:T(8,128)S(1)} %get-tuple-element.50.own), channel_id=1, source_target_pairs={{0,16},{1,65},{16,32},{17,81},{32,48},{33,97},{48,0},{49,113},{64,... | collective-permute-start | bytes 208904 | tf_op jit(solution)/shard_map/ppermute | solution.py:362
  102.6 4.8 %collective-permute-start.21 = (f32[136,128]{1,0:T(8,128)S(1)}, f32[136,128]{1,0:T(8,128)S(1)}, u32[]{:S(2)}, u32[]{:S(2)}) collective-permute-start(f32[136,128]{1,0:T(8,128)S(1)} %sums.3.own), channel_id=1, source_target_pairs={{0,128},{1,33},{16,144},{17,49},{32,160},{33,1},{48,176},{49,17},{... | collective-permute-start | bytes 208904 | tf_op jit(solution)/shard_map/ppermute | solution.py:362
  102.7 4.7 %collective-permute-start.20 = (f32[136,128]{1,0:T(8,128)S(1)}, f32[136,128]{1,0:T(8,128)S(1)}, u32[]{:S(2)}, u32[]{:S(2)}) collective-permute-start(f32[136,128]{1,0:T(8,128)S(1)} %sums.3.own), channel_id=1, source_target_pairs={{0,192},{1,49},{16,208},{17,1},{32,224},{33,17},{48,240},{49,33},{... | collective-permute-start | bytes 208904 | tf_op jit(solution)/shard_map/ppermute | solution.py:362
  103.5 4.7 %collective-permute-start.19 = (f32[136,128]{1,0:T(8,128)S(1)}, f32[136,128]{1,0:T(8,128)S(1)}, u32[]{:S(2)}, u32[]{:S(2)}) collective-permute-start(f32[136,128]{1,0:T(8,128)S(1)} %sums.3.own), channel_id=1, source_target_pairs={{0,64},{1,17},{16,80},{17,33},{32,96},{33,49},{48,112},{49,1},{64,... | collective-permute-start | bytes 208904 | tf_op jit(solution)/shard_map/ppermute | solution.py:362

commit v10 on v9

--- a/solution.py
+++ b/solution.py
@@ -23,7 +23,6 @@
 
 SLOT_ROWS, SLOT_COLS, COUNT, AT_Y, AT_X, AT_Z, AT_CORE = range(7)
 COL_KINDS, COST, ROW_SIDE, TABLE, SIDE = 8, 16, 24, 32, 40
-HANDED = 12288
 STEP = 0.4
 
 VMEM = pl.BlockSpec(memory_space=pltpu.VMEM)
@@ -108,7 +107,7 @@
 
 
 def pack(
-    count, rows, cols, row_kinds, rhs, dual, col_kinds, cost, primal, duals, handed, side, places, kinds, start, done
+    count, rows, cols, row_kinds, rhs, dual, col_kinds, cost, primal, duals, side, places, kinds, start, done
 ):
     copies = [
         pltpu.make_async_copy(source, target, done.at[k])
@@ -142,10 +141,7 @@
     side[TABLE : TABLE + COUNT, 0:SLOTS] = places[...].astype(F32)
     side[COL_KINDS:COST, :] = kinds[COLS_SHARE:, :].astype(F32)
     side[ROW_SIDE + ROWS_SHARE : TABLE, :] = kinds[0:ROWS_SHARE, :].astype(F32)
-    hand = pltpu.make_async_copy(side, handed.at[0:SIDE], done.at[8])
-    hand.start()
     duals[...] = jnp.broadcast_to(start[...][None], duals.shape)
-    hand.wait()
 
 
 def turn(pairs, turned):
@@ -197,23 +193,20 @@
 
 
 def first_adjoint(
-    tiles, handed, duals, payload, dual, side, table_out, pairs, chunks, table, done, total
+    tiles, duals, side, payload, dual, table_out, pairs, chunks, table, done, total
 ):
-    share = pltpu.make_async_copy(handed.at[0:SIDE], side, done.at[len(PIECES) + 1])
-    share.start()
     copies, first = [], 0
     for k, slots in enumerate(PIECES):
         part = pl.ds(first, slots)
         copies.append(pltpu.make_async_copy(tiles.at[part], chunks.at[part], done.at[k]))
         copies[k].start()
         first += slots
+    table_out[...] = side[TABLE:, :].astype(jnp.int32)
+    read = pltpu.make_async_copy(table_out, table, done.at[len(PIECES)])
+    read.start()
     for k in range(N):
         dual[k * ROWS_SHARE : (k + 1) * ROWS_SHARE, :] = duals[k]
     total[...] = jnp.zeros_like(total)
-    share.wait()
-    table_out[...] = side[TABLE:, :].astype(jnp.int32)
-    read = pltpu.make_async_copy(table_out, table, done.at[len(PIECES)])
-    read.start()
     payload[COL_BLOCKS:, :] = side[0:COST, :]
     read.wait()
 
@@ -235,7 +228,7 @@
 
 
 def first_forward(
-    table, own, right, left, opposite, turned, kept, given, primal, start, free, extended, total
+    table, own, right, left, opposite, turned, kept, given, primal, free, start, extended, total
 ):
     y, x, second = table[AT_Y, 0], table[AT_X, 0], table[AT_CORE, 0] == 1
     for j, (ref, late) in enumerate(((own, 0), (right, 3), (left, 1), (opposite, 2))):
@@ -273,18 +266,21 @@
 
 
 def second_forward(
-    table, own, right, left, opposite, before, free, turned, kept, given, primal, ascent, primal_mine, extended, total
+    table, own, right, left, opposite, before, free, turned, kept, given, primal, ascent, primal_mine, extended, part, done, total
 ):
     ascent[...] = sum_four((own, right, left, opposite), slice(0, COL_BLOCKS))
     primal[...] = clamp_primal(before[...] + STEP * ascent[...], free[...])
     extended[...] = 2.0 * primal[...] - before[...]
-    primal_mine[...] = primal[own_columns(table), :]
+    part[...] = primal[own_columns(table), :]
+    copy = pltpu.make_async_copy(part, primal_mine, done)
+    copy.start()
     forward_product(table, lambda slot: turned[slot], [extended, primal], total)
     mine = pl.multiple_of(table[AT_CORE, 0] * HALF, HALF)
     for k, part in enumerate((0, 4)):
         rows = slice(k * HALF, (k + 1) * HALF)
         kept[rows, :] = total[pl.ds(mine, HALF), part, :]
         given[rows, :] = total[pl.ds(HALF - mine, HALF), part, :]
+    copy.wait()
 
 
 def row_terms(table, held, before, rhs, ineq, side, primal1, primal2, terms):
@@ -310,17 +306,20 @@
 
 
 def third_adjoint(
-    table, held, other, before, rhs, ineq, side, terms, pairs, payload, mine, dual, image, total
+    table, held, other, before, rhs, ineq, side, terms, pairs, payload, mine, image, dual, part, done, total
 ):
     half = pl.multiple_of(table[AT_CORE, 0] * HALF, HALF)
     image[pl.ds(half, HALF), :] = held[0:HALF, :]
     image[pl.ds(HALF - half, HALF), :] = other[0:HALF, :]
     dual[...] = clamp_dual(before[...] + STEP * (rhs[...] - image[...]), ineq[...])
-    mine[...] = dual[pl.ds(index_col(table) * ROWS_SHARE, ROWS_SHARE), :]
+    part[...] = dual[pl.ds(index_col(table) * ROWS_SHARE, ROWS_SHARE), :]
+    copy = pltpu.make_async_copy(part, mine, done)
+    copy.start()
     adjoint_product(table, lambda slot: pairs[slot], dual, total)
     payload[0:COL_BLOCKS, :] = total[:, 0, :]
     payload[COL_BLOCKS : COL_BLOCKS + 8, :] = terms[...]
     payload[own_columns(table), :] -= side[COST:ROW_SIDE, :]
+    copy.wait()
 
 
 def column_terms(own, right, left, opposite, earlier, free, terms):
@@ -387,40 +386,37 @@
     row_total = [pltpu.VMEM((ROW_BLOCKS, 8, TILE), F32)]
     col_total = [pltpu.VMEM((COL_BLOCKS, 8, TILE), F32)]
 
-    duals, handed = call(
+    duals, side = call(
         pack,
         "pack",
-        [((N, ROWS_SHARE, TILE), F32), ((HANDED, TILE), F32)],
+        [((N, ROWS_SHARE, TILE), F32), ((SIDE, TILE), F32)],
         (tile_count, tile_rows, tile_cols, row_types, rhs, dual_start, var_types, cost, primal_start),
         smem=1,
         hbm=8,
-        hbm_out=(1,),
         scratch=[
-            pltpu.VMEM((SIDE, TILE), F32),
             pltpu.VMEM((2, SLOTS), jnp.int32),
             pltpu.VMEM((2 * COLS_SHARE, TILE), jnp.int32),
             pltpu.VMEM((ROWS_SHARE, TILE), F32),
-            pltpu.SemaphoreType.DMA((9,)),
+            pltpu.SemaphoreType.DMA((8,)),
         ],
         vmem=PACK_VMEM,
     )
 
-    payload, dual0, side, table, pairs = call(
+    payload, dual0, table, pairs = call(
         first_adjoint,
         "first_adjoint",
         [
             ((COL_BLOCKS + 2 * COLS_SHARE, TILE), F32),
             (blocks, F32),
-            ((SIDE, TILE), F32),
             ((8, TILE), jnp.int32),
             ((SLOTS, 2 * TILE, TILE), BF16),
         ],
-        (tiles, handed, exchange(duals, ("z", "core"))),
-        hbm=2,
+        (tiles, exchange(duals, ("z", "core")), side),
+        hbm=1,
         scratch=[
             pltpu.VMEM((SLOTS, TILE, TILE), F32),
             pltpu.SMEM((8, TILE), jnp.int32),
-            pltpu.SemaphoreType.DMA((len(PIECES) + 2,)),
+            pltpu.SemaphoreType.DMA((len(PIECES) + 1,)),
         ]
         + col_total,
         vmem=FIRST_VMEM,
@@ -436,13 +432,13 @@
         ring_sums, "ring_sums", [((COL_BLOCKS + 8 * COLS_SHARE, TILE), F32)], four_of(payload, 0)
     )
 
-    kept, given, primal1, _, free = call(
+    kept, given, primal1, free = call(
         first_forward,
         "first_forward",
-        [(half, F32)] * 2 + [(columns, F32)] * 3,
+        [(half, F32)] * 2 + [(columns, F32)] * 2,
         (table, *four_of(payload[0], 1), turned),
         smem=1,
-        scratch=[pltpu.VMEM(columns, F32)] + row_total,
+        scratch=[pltpu.VMEM(columns, F32)] * 2 + row_total,
     )
     copies = call(
         image_copies,
@@ -469,7 +465,9 @@
         [(blocks, F32)] * 2 + [(columns, F32)] * 2 + [((COLS_SHARE, TILE), F32)],
         (table, *four_over_row(gradient), primal1, free, turned),
         smem=1,
-        scratch=[pltpu.VMEM(columns, F32)] + row_total,
+        hbm_out=(4,),
+        scratch=[pltpu.VMEM(columns, F32), pltpu.VMEM((COLS_SHARE, TILE), F32), pltpu.SemaphoreType.DMA]
+        + row_total,
     )
     copies = call(
         pair_copies, "pair_copies", [((8, HALF + 8, TILE), F32)], (kept, swap_cores(given))
@@ -491,7 +489,10 @@
         [((COL_BLOCKS + 8, TILE), F32), ((ROWS_SHARE, TILE), F32)],
         (table, held, other, dual1, rhs_full, ineq, side, terms, pairs),
         smem=1,
-        scratch=[pltpu.VMEM(blocks, F32)] * 2 + col_total,
+        hbm_out=(1,),
+        scratch=[pltpu.VMEM(blocks, F32)] * 2
+        + [pltpu.VMEM((ROWS_SHARE, TILE), F32), pltpu.SemaphoreType.DMA]
+        + col_total,
     )
     terms = call(
         column_terms,

time: 122 us -> 122 us (level)
  no operation moved by 1% of the time
where the time goes in v10:
time: 122 us
  blocking collectives  53.2 us (44%)
  starting transfers between devices  26.9 us (22%)
  waiting for transfers between devices  26.1 us (21%)
  Pallas kernels  13.1 us (11%)
  between operations  1.57 us (1%)
    all_to_all x4, blocking collectives, exchange(): return lax.all_to_all(copies, axes, 0, 0)  53.2 us
    ppermute x18, waiting for transfers between devices, shift(): return lax.ppermute(values, ('y', 'x', 'core'), pairs)  23.3 us
    ppermute x18, starting transfers between devices, shift(): return lax.ppermute(values, ('y', 'x', 'core'), pairs)  15.9 us
    pallas_call x17, Pallas kernels, call(): pl.pallas_call(kernel, name=name, out_shape=shapes, in_specs=[SMEM] * sme...  13.1 us
    ppermute x4, starting transfers between devices, swap_cores(): return lax.ppermute(values, 'core', [(0, 1), (1, 0)])  11 us
    ppermute x4, waiting for transfers between devices, swap_cores(): return lax.ppermute(values, 'core', [(0, 1), (1, 0)])  2.8 us
  transfers between devices with their start and end apart: 22, of which 17 were waited for; matrix products, arithmetic and copies ran while one was open for 0% of the time, Pallas kernels for 1%

profile of v10, /device:TPU:1, one launch (start us, length us, event | category | flops | bytes accessed | tf_op | source)
XLA Modules:
  0.0 121.6 jit_solution(1692483038429374907)
XLA Ops:
  1.3 1.5 %pack.1 = (f32[16,4,128]{2,1,0:T(4,128)}, f32[40,128]{1,0:T(8,128)}) custom-call(s32[1,1]{1,0:T(1,128)S(6)} %copy.15.count, s32[1,1,64]{2,1,0:T(1,128)} %rows.1, s32[1,1,64]{2,1,0:T(1,128)} %cols.1, s32[1,4,128]{2,1,0:T(4,128)} %row_kinds.1, f32[1,4,128]{2,1,0:T(4,128)} %rhs.1, f32[1,4,128]{2,1,0:T(4,128)} %dual.1, s32[1,8,128]{2,1,0:T(8,128)} %col_kinds.1, ...), custom_call_target="tpu_custom_call" | custom-call | tf_op jit(solution)/shard_map/pack/pallas_call | solution.py:35
  2.8 17.4 %all_to_all.20.duals = f32[16,4,128]{2,1,0:T(4,128)S(1)} all-to-all(f32[16,4,128]{2,1,0:T(4,128)} %get-tuple-element.29), channel_id=1, replica_groups=mesh['y'=4,'x'=4,'z'=8,'core'=2] {'z','core'}, dimensions={0} | all-to-all | bytes 65536 | tf_op jit(solution)/shard_map/all_to_all | solution.py:378
  20.9 2.6 %first_adjoint.1 = (f32[144,128]{1,0:T(8,128)S(1)}, f32[64,128]{1,0:T(8,128)S(1)}, s32[8,128]{1,0:T(8,128)S(1)}, bf16[64,256,128]{2,1,0:T(8,128)(2,1)S(1)}) custom-call(f32[64,128,128]{2,1,0:T(8,128)} %bitcast.3, f32[16,4,128]{2,1,0:T(4,128)S(1)} %all_to_all.20.duals, f32[40,128]{1,0:T(8,128)S(1)} %copy-done), custom_call_target="tpu_custom_call" | custom-call | tf_op jit(solution)/shard_map/first_adjoint/pallas_call | solution.py:35
  23.5 3.0 %collective-permute-start.2 = (f32[144,128]{1,0:T(8,128)S(1)}, f32[144,128]{1,0:T(8,128)S(1)}, u32[]{:S(2)}, u32[]{:S(2)}) collective-permute-start(f32[144,128]{1,0:T(8,128)S(1)} %get-tuple-element.32.own), channel_id=1, source_target_pairs={{0,32},{1,129},{16,48},{17,145},{32,0},{33,161},{48,16},{49,177},{... | collective-permute-start | bytes 221192 | tf_op jit(solution)/shard_map/ppermute | solution.py:361
  29.7 2.0 %collective-permute-done.right = f32[144,128]{1,0:T(8,128)S(1)} collective-permute-done((f32[144,128]{1,0:T(8,128)S(1)}, f32[144,128]{1,0:T(8,128)S(1)}, u32[]{:S(2)}, u32[]{:S(2)}) %collective-permute-start) | collective-permute-done | bytes 73760 | tf_op jit(solution)/shard_map/ppermute | solution.py:361
  31.7 2.8 %collective-permute-start.5 = (f32[192,128]{1,0:T(8,128)S(1)}, f32[192,128]{1,0:T(8,128)S(1)}, u32[]{:S(2)}, u32[]{:S(2)}) collective-permute-start(f32[192,128]{1,0:T(8,128)S(1)} %ring_sums.1.own), channel_id=1, source_target_pairs={{0,128},{1,33},{16,144},{17,49},{32,160},{33,1},{48,176},{49,17},{... | collective-permute-start | bytes 294920 | tf_op jit(solution)/shard_map/ppermute | solution.py:361
  38.0 2.1 %collective-permute-done.3.right = f32[192,128]{1,0:T(8,128)S(1)} collective-permute-done((f32[192,128]{1,0:T(8,128)S(1)}, f32[192,128]{1,0:T(8,128)S(1)}, u32[]{:S(2)}, u32[]{:S(2)}) %collective-permute-start.3) | collective-permute-done | bytes 98336 | tf_op jit(solution)/shard_map/ppermute | solution.py:361
  41.4 3.9 %collective-permute-start.6 = (f32[32,128]{1,0:T(8,128)S(1)}, f32[32,128]{1,0:T(8,128)S(1)}, u32[]{:S(2)}, u32[]{:S(2)}) collective-permute-start(f32[32,128]{1,0:T(8,128)S(1)} %get-tuple-element.35), channel_id=1, source_target_pairs={{0,1},{1,0},{2,3},{3,2},{4,5},{5,4},{6,7},{7,6},{8,9},{9,8},{10,11... | collective-permute-start | bytes 49160 | tf_op jit(solution)/shard_map/ppermute | solution.py:374
  46.2 11.6 %all_to_all.21.pieces = f32[8,40,128]{2,1,0:T(8,128)S(1)} all-to-all(f32[8,40,128]{2,1,0:T(8,128)S(1)} %image_copies.1), channel_id=1, replica_groups=mesh['y'=4,'x'=4,'z'=8,'core'=2] {'z'}, dimensions={0} | all-to-all | bytes 327680 | tf_op jit(solution)/shard_map/all_to_all | solution.py:378
  57.8 1.6 %collective-permute-start.7 = (f32[96,128]{1,0:T(8,128)S(1)}, f32[96,128]{1,0:T(8,128)S(1)}, u32[]{:S(2)}, u32[]{:S(2)}) collective-permute-start(f32[96,128]{1,0:T(8,128)S(1)} %image_sums.1.held), channel_id=1, source_target_pairs={{0,1},{1,0},{2,3},{3,2},{4,5},{5,4},{6,7},{7,6},{8,9},{9,8},{10,11... | collective-permute-start | bytes 147464 | tf_op jit(solution)/shard_map/ppermute | solution.py:374
  61.9 1.7 %collective-permute-start.9 = (f32[128,128]{1,0:T(8,128)S(1)}, f32[128,128]{1,0:T(8,128)S(1)}, u32[]{:S(2)}, u32[]{:S(2)}) collective-permute-start(f32[128,128]{1,0:T(8,128)S(1)} %get-tuple-element.37.own), channel_id=1, source_target_pairs={{0,48},{1,193},{16,0},{17,209},{32,16},{33,225},{48,32},{49,241},{... | collective-permute-start | bytes 196616 | tf_op jit(solution)/shard_map/ppermute | solution.py:361
  63.6 2.7 %collective-permute-done.10.opposite = f32[128,128]{1,0:T(8,128)S(1)} collective-permute-done((f32[128,128]{1,0:T(8,128)S(1)}, f32[128,128]{1,0:T(8,128)S(1)}, u32[]{:S(2)}, u32[]{:S(2)}) %collective-permute-start.10) | collective-permute-done | bytes 65568 | tf_op jit(solution)/shard_map/ppermute | solution.py:361
  66.3 1.6 %collective-permute-done.8.right = f32[128,128]{1,0:T(8,128)S(1)} collective-permute-done((f32[128,128]{1,0:T(8,128)S(1)}, f32[128,128]{1,0:T(8,128)S(1)}, u32[]{:S(2)}, u32[]{:S(2)}) %collective-permute-start.8) | collective-permute-done | bytes 65568 | tf_op jit(solution)/shard_map/ppermute | solution.py:361
  68.1 1.8 %collective-permute-start.12 = (f32[128,128]{1,0:T(8,128)S(1)}, f32[128,128]{1,0:T(8,128)S(1)}, u32[]{:S(2)}, u32[]{:S(2)}) collective-permute-start(f32[128,128]{1,0:T(8,128)S(1)} %sums.2.own), channel_id=1, source_target_pairs={{0,192},{1,49},{16,208},{17,1},{32,224},{33,17},{48,240},{49,33},{... | collective-permute-start | bytes 196616 | tf_op jit(solution)/shard_map/ppermute | solution.py:361
  69.8 2.8 %collective-permute-done.13.opposite = f32[128,128]{1,0:T(8,128)S(1)} collective-permute-done((f32[128,128]{1,0:T(8,128)S(1)}, f32[128,128]{1,0:T(8,128)S(1)}, u32[]{:S(2)}, u32[]{:S(2)}) %collective-permute-start.13) | collective-permute-done | bytes 65568 | tf_op jit(solution)/shard_map/ppermute | solution.py:361
  72.6 1.5 %collective-permute-done.11.right = f32[128,128]{1,0:T(8,128)S(1)} collective-permute-done((f32[128,128]{1,0:T(8,128)S(1)}, f32[128,128]{1,0:T(8,128)S(1)}, u32[]{:S(2)}, u32[]{:S(2)}) %collective-permute-start.11) | collective-permute-done | bytes 65568 | tf_op jit(solution)/shard_map/ppermute | solution.py:361
  74.1 1.8 %second_forward.1 = (f32[64,128]{1,0:T(8,128)S(1)}, f32[64,128]{1,0:T(8,128)S(1)}, f32[128,128]{1,0:T(8,128)S(1)}, f32[128,128]{1,0:T(8,128)S(1)}, f32[8,128]{1,0:T(8,128)}) custom-call(s32[8,128]{1,0:T(8,128)S(1)} %get-tuple-element.31.table, f32[128,128]{1,0:T(8,128)S(1)} %sums.2.own, f32[128,128]{1,0:T(8,128)S(1)} %collective-permute-done.11.right, ...), custom_call_target="tpu_custom_call" | custom-call | tf_op jit(solution)/shard_map/second_forward/pallas_call | solution.py:35
  76.0 3.9 %collective-permute-start.14 = (f32[64,128]{1,0:T(8,128)S(1)}, f32[64,128]{1,0:T(8,128)S(1)}, u32[]{:S(2)}, u32[]{:S(2)}) collective-permute-start(f32[64,128]{1,0:T(8,128)S(1)} %get-tuple-element.42), channel_id=1, source_target_pairs={{0,1},{1,0},{2,3},{3,2},{4,5},{5,4},{6,7},{7,6},{8,9},{9,8},{10,11... | collective-permute-start | bytes 98312 | tf_op jit(solution)/shard_map/ppermute | solution.py:374
  80.7 11.6 %all_to_all.22.pieces = f32[8,40,128]{2,1,0:T(8,128)S(1)} all-to-all(f32[8,40,128]{2,1,0:T(8,128)S(1)} %pair_copies.1), channel_id=1, replica_groups=mesh['y'=4,'x'=4,'z'=8,'core'=2] {'z'}, dimensions={0} | all-to-all | bytes 327680 | tf_op jit(solution)/shard_map/all_to_all | solution.py:378
  92.3 1.6 %collective-permute-start.15 = (f32[40,128]{1,0:T(8,128)S(1)}, f32[40,128]{1,0:T(8,128)S(1)}, u32[]{:S(2)}, u32[]{:S(2)}) collective-permute-start(f32[40,128]{1,0:T(8,128)S(1)} %pair_sums.1.held), channel_id=1, source_target_pairs={{0,1},{1,0},{2,3},{3,2},{4,5},{5,4},{6,7},{7,6},{8,9},{9,8},{10,11... | collective-permute-start | bytes 61448 | tf_op jit(solution)/shard_map/ppermute | solution.py:374
  94.8 1.8 %third_adjoint.1 = (f32[136,128]{1,0:T(8,128)S(1)}, f32[4,128]{1,0:T(4,128)}) custom-call(s32[8,128]{1,0:T(8,128)S(1)} %get-tuple-element.31.table, f32[40,128]{1,0:T(8,128)S(1)} %pair_sums.1.held, f32[40,128]{1,0:T(8,128)S(1)} %collective-permute-done.15.other, f32[64,128]{1,0:T(8,128)S(1)} %get-tuple-element.43.before, ...), custom_call_target="tpu_custom_call" | custom-call | tf_op jit(solution)/shard_map/third_adjoint/pallas_call | solution.py:35
  98.3 3.1 %collective-permute-done.18.opposite = f32[136,128]{1,0:T(8,128)S(1)} collective-permute-done((f32[136,128]{1,0:T(8,128)S(1)}, f32[136,128]{1,0:T(8,128)S(1)}, u32[]{:S(2)}, u32[]{:S(2)}) %collective-permute-start.18) | collective-permute-done | bytes 69664 | tf_op jit(solution)/shard_map/ppermute | solution.py:361
  104.1 3.1 %collective-permute-done.21.opposite = f32[136,128]{1,0:T(8,128)S(1)} collective-permute-done((f32[136,128]{1,0:T(8,128)S(1)}, f32[136,128]{1,0:T(8,128)S(1)}, u32[]{:S(2)}, u32[]{:S(2)}) %collective-permute-start.21) | collective-permute-done | bytes 69664 | tf_op jit(solution)/shard_map/ppermute | solution.py:361
  108.1 12.7 %all_to_all.23.gathered = f32[16,1,128]{2,1,0:T(1,128)S(1)} all-to-all(f32[16,1,128]{2,1,0:T(1,128)S(1)} %column_terms.1), channel_id=1, replica_groups=mesh['y'=4,'x'=4,'z'=8,'core'=2] {'z','core'}, dimensions={0} | all-to-all | bytes 16384 | tf_op jit(solution)/shard_map/all_to_all | solution.py:378
  (43 shorter events, 19.8 us)
Async XLA Ops:
  20.2 0.7 copy-start
  23.5 4.8 %collective-permute-start.2 = (f32[144,128]{1,0:T(8,128)S(1)}, f32[144,128]{1,0:T(8,128)S(1)}, u32[]{:S(2)}, u32[]{:S(2)}) collective-permute-start(f32[144,128]{1,0:T(8,128)S(1)} %get-tuple-element.32.own), channel_id=1, source_target_pairs={{0,32},{1,129},{16,48},{17,145},{32,0},{33,161},{48,16},{49,177},{... | collective-permute-start | bytes 221192 | tf_op jit(solution)/shard_map/ppermute | solution.py:361
  26.5 3.2 %collective-permute-start.1 = (f32[144,128]{1,0:T(8,128)S(1)}, f32[144,128]{1,0:T(8,128)S(1)}, u32[]{:S(2)}, u32[]{:S(2)}) collective-permute-start(f32[144,128]{1,0:T(8,128)S(1)} %get-tuple-element.32.own), channel_id=1, source_target_pairs={{0,48},{1,193},{16,0},{17,209},{32,16},{33,225},{48,32},{49,241},{... | collective-permute-start | bytes 221192 | tf_op jit(solution)/shard_map/ppermute | solution.py:361
  27.3 4.4 %collective-permute-start = (f32[144,128]{1,0:T(8,128)S(1)}, f32[144,128]{1,0:T(8,128)S(1)}, u32[]{:S(2)}, u32[]{:S(2)}) collective-permute-start(f32[144,128]{1,0:T(8,128)S(1)} %get-tuple-element.32.own), channel_id=1, source_target_pairs={{0,16},{1,65},{16,32},{17,81},{32,48},{33,97},{48,0},{49,113},{64,... | collective-permute-start | bytes 221192 | tf_op jit(solution)/shard_map/ppermute | solution.py:361
  31.7 5.4 %collective-permute-start.5 = (f32[192,128]{1,0:T(8,128)S(1)}, f32[192,128]{1,0:T(8,128)S(1)}, u32[]{:S(2)}, u32[]{:S(2)}) collective-permute-start(f32[192,128]{1,0:T(8,128)S(1)} %ring_sums.1.own), channel_id=1, source_target_pairs={{0,128},{1,33},{16,144},{17,49},{32,160},{33,1},{48,176},{49,17},{... | collective-permute-start | bytes 294920 | tf_op jit(solution)/shard_map/ppermute | solution.py:361
  34.5 3.5 %collective-permute-start.4 = (f32[192,128]{1,0:T(8,128)S(1)}, f32[192,128]{1,0:T(8,128)S(1)}, u32[]{:S(2)}, u32[]{:S(2)}) collective-permute-start(f32[192,128]{1,0:T(8,128)S(1)} %ring_sums.1.own), channel_id=1, source_target_pairs={{0,192},{1,49},{16,208},{17,1},{32,224},{33,17},{48,240},{49,33},{... | collective-permute-start | bytes 294920 | tf_op jit(solution)/shard_map/ppermute | solution.py:361
  35.4 4.7 %collective-permute-start.3 = (f32[192,128]{1,0:T(8,128)S(1)}, f32[192,128]{1,0:T(8,128)S(1)}, u32[]{:S(2)}, u32[]{:S(2)}) collective-permute-start(f32[192,128]{1,0:T(8,128)S(1)} %ring_sums.1.own), channel_id=1, source_target_pairs={{0,64},{1,17},{16,80},{17,33},{32,96},{33,49},{48,112},{49,1},{64,... | collective-permute-start | bytes 294920 | tf_op jit(solution)/shard_map/ppermute | solution.py:361
  41.4 4.7 %collective-permute-start.6 = (f32[32,128]{1,0:T(8,128)S(1)}, f32[32,128]{1,0:T(8,128)S(1)}, u32[]{:S(2)}, u32[]{:S(2)}) collective-permute-start(f32[32,128]{1,0:T(8,128)S(1)} %get-tuple-element.35), channel_id=1, source_target_pairs={{0,1},{1,0},{2,3},{3,2},{4,5},{5,4},{6,7},{7,6},{8,9},{9,8},{10,11... | collective-permute-start | bytes 49160 | tf_op jit(solution)/shard_map/ppermute | solution.py:374
  57.8 2.5 %collective-permute-start.7 = (f32[96,128]{1,0:T(8,128)S(1)}, f32[96,128]{1,0:T(8,128)S(1)}, u32[]{:S(2)}, u32[]{:S(2)}) collective-permute-start(f32[96,128]{1,0:T(8,128)S(1)} %image_sums.1.held), channel_id=1, source_target_pairs={{0,1},{1,0},{2,3},{3,2},{4,5},{5,4},{6,7},{7,6},{8,9},{9,8},{10,11... | collective-permute-start | bytes 147464 | tf_op jit(solution)/shard_map/ppermute | solution.py:374
  61.6 4.7 %collective-permute-start.10 = (f32[128,128]{1,0:T(8,128)S(1)}, f32[128,128]{1,0:T(8,128)S(1)}, u32[]{:S(2)}, u32[]{:S(2)}) collective-permute-start(f32[128,128]{1,0:T(8,128)S(1)} %get-tuple-element.37.own), channel_id=1, source_target_pairs={{0,32},{1,129},{16,48},{17,145},{32,0},{33,161},{48,16},{49,177},{... | collective-permute-start | bytes 196616 | tf_op jit(solution)/shard_map/ppermute | solution.py:361
  61.9 4.4 %collective-permute-start.9 = (f32[128,128]{1,0:T(8,128)S(1)}, f32[128,128]{1,0:T(8,128)S(1)}, u32[]{:S(2)}, u32[]{:S(2)}) collective-permute-start(f32[128,128]{1,0:T(8,128)S(1)} %get-tuple-element.37.own), channel_id=1, source_target_pairs={{0,48},{1,193},{16,0},{17,209},{32,16},{33,225},{48,32},{49,241},{... | collective-permute-start | bytes 196616 | tf_op jit(solution)/shard_map/ppermute | solution.py:361
  63.6 4.3 %collective-permute-start.8 = (f32[128,128]{1,0:T(8,128)S(1)}, f32[128,128]{1,0:T(8,128)S(1)}, u32[]{:S(2)}, u32[]{:S(2)}) collective-permute-start(f32[128,128]{1,0:T(8,128)S(1)} %get-tuple-element.37.own), channel_id=1, source_target_pairs={{0,16},{1,65},{16,32},{17,81},{32,48},{33,97},{48,0},{49,113},{64,... | collective-permute-start | bytes 196616 | tf_op jit(solution)/shard_map/ppermute | solution.py:361
  67.9 4.7 %collective-permute-start.13 = (f32[128,128]{1,0:T(8,128)S(1)}, f32[128,128]{1,0:T(8,128)S(1)}, u32[]{:S(2)}, u32[]{:S(2)}) collective-permute-start(f32[128,128]{1,0:T(8,128)S(1)} %sums.2.own), channel_id=1, source_target_pairs={{0,128},{1,33},{16,144},{17,49},{32,160},{33,1},{48,176},{49,17},{... | collective-permute-start | bytes 196616 | tf_op jit(solution)/shard_map/ppermute | solution.py:361
  68.1 4.6 %collective-permute-start.12 = (f32[128,128]{1,0:T(8,128)S(1)}, f32[128,128]{1,0:T(8,128)S(1)}, u32[]{:S(2)}, u32[]{:S(2)}) collective-permute-start(f32[128,128]{1,0:T(8,128)S(1)} %sums.2.own), channel_id=1, source_target_pairs={{0,192},{1,49},{16,208},{17,1},{32,224},{33,17},{48,240},{49,33},{... | collective-permute-start | bytes 196616 | tf_op jit(solution)/shard_map/ppermute | solution.py:361
  69.8 4.3 %collective-permute-start.11 = (f32[128,128]{1,0:T(8,128)S(1)}, f32[128,128]{1,0:T(8,128)S(1)}, u32[]{:S(2)}, u32[]{:S(2)}) collective-permute-start(f32[128,128]{1,0:T(8,128)S(1)} %sums.2.own), channel_id=1, source_target_pairs={{0,64},{1,17},{16,80},{17,33},{32,96},{33,49},{48,112},{49,1},{64,... | collective-permute-start | bytes 196616 | tf_op jit(solution)/shard_map/ppermute | solution.py:361
  76.0 4.7 %collective-permute-start.14 = (f32[64,128]{1,0:T(8,128)S(1)}, f32[64,128]{1,0:T(8,128)S(1)}, u32[]{:S(2)}, u32[]{:S(2)}) collective-permute-start(f32[64,128]{1,0:T(8,128)S(1)} %get-tuple-element.42), channel_id=1, source_target_pairs={{0,1},{1,0},{2,3},{3,2},{4,5},{5,4},{6,7},{7,6},{8,9},{9,8},{10,11... | collective-permute-start | bytes 98312 | tf_op jit(solution)/shard_map/ppermute | solution.py:374
  92.3 2.5 %collective-permute-start.15 = (f32[40,128]{1,0:T(8,128)S(1)}, f32[40,128]{1,0:T(8,128)S(1)}, u32[]{:S(2)}, u32[]{:S(2)}) collective-permute-start(f32[40,128]{1,0:T(8,128)S(1)} %pair_sums.1.held), channel_id=1, source_target_pairs={{0,1},{1,0},{2,3},{3,2},{4,5},{5,4},{6,7},{7,6},{8,9},{9,8},{10,11... | collective-permute-start | bytes 61448 | tf_op jit(solution)/shard_map/ppermute | solution.py:374
  96.6 4.8 %collective-permute-start.18 = (f32[136,128]{1,0:T(8,128)S(1)}, f32[136,128]{1,0:T(8,128)S(1)}, u32[]{:S(2)}, u32[]{:S(2)}) collective-permute-start(f32[136,128]{1,0:T(8,128)S(1)} %get-tuple-element.48.own), channel_id=1, source_target_pairs={{0,32},{1,129},{16,48},{17,145},{32,0},{33,161},{48,16},{49,177},{... | collective-permute-start | bytes 208904 | tf_op jit(solution)/shard_map/ppermute | solution.py:361
  96.7 4.7 %collective-permute-start.17 = (f32[136,128]{1,0:T(8,128)S(1)}, f32[136,128]{1,0:T(8,128)S(1)}, u32[]{:S(2)}, u32[]{:S(2)}) collective-permute-start(f32[136,128]{1,0:T(8,128)S(1)} %get-tuple-element.48.own), channel_id=1, source_target_pairs={{0,48},{1,193},{16,0},{17,209},{32,16},{33,225},{48,32},{49,241},{... | collective-permute-start | bytes 208904 | tf_op jit(solution)/shard_map/ppermute | solution.py:361
  97.7 4.7 %collective-permute-start.16 = (f32[136,128]{1,0:T(8,128)S(1)}, f32[136,128]{1,0:T(8,128)S(1)}, u32[]{:S(2)}, u32[]{:S(2)}) collective-permute-start(f32[136,128]{1,0:T(8,128)S(1)} %get-tuple-element.48.own), channel_id=1, source_target_pairs={{0,16},{1,65},{16,32},{17,81},{32,48},{33,97},{48,0},{49,113},{64,... | collective-permute-start | bytes 208904 | tf_op jit(solution)/shard_map/ppermute | solution.py:361
  102.4 4.8 %collective-permute-start.21 = (f32[136,128]{1,0:T(8,128)S(1)}, f32[136,128]{1,0:T(8,128)S(1)}, u32[]{:S(2)}, u32[]{:S(2)}) collective-permute-start(f32[136,128]{1,0:T(8,128)S(1)} %sums.3.own), channel_id=1, source_target_pairs={{0,128},{1,33},{16,144},{17,49},{32,160},{33,1},{48,176},{49,17},{... | collective-permute-start | bytes 208904 | tf_op jit(solution)/shard_map/ppermute | solution.py:361
  102.5 4.7 %collective-permute-start.20 = (f32[136,128]{1,0:T(8,128)S(1)}, f32[136,128]{1,0:T(8,128)S(1)}, u32[]{:S(2)}, u32[]{:S(2)}) collective-permute-start(f32[136,128]{1,0:T(8,128)S(1)} %sums.3.own), channel_id=1, source_target_pairs={{0,192},{1,49},{16,208},{17,1},{32,224},{33,17},{48,240},{49,33},{... | collective-permute-start | bytes 208904 | tf_op jit(solution)/shard_map/ppermute | solution.py:361
  103.3 4.7 %collective-permute-start.19 = (f32[136,128]{1,0:T(8,128)S(1)}, f32[136,128]{1,0:T(8,128)S(1)}, u32[]{:S(2)}, u32[]{:S(2)}) collective-permute-start(f32[136,128]{1,0:T(8,128)S(1)} %sums.3.own), channel_id=1, source_target_pairs={{0,64},{1,17},{16,80},{17,33},{32,96},{33,49},{48,112},{49,1},{64,... | collective-permute-start | bytes 208904 | tf_op jit(solution)/shard_map/ppermute | solution.py:361

commit v11 on v10

--- a/solution.py
+++ b/solution.py
@@ -30,16 +30,14 @@
 HBM = pl.BlockSpec(memory_space=pltpu.HBM)
 
 
-def call(kernel, name, out_shapes, args, smem=0, hbm=0, smem_out=False, hbm_out=(), scratch=(), vmem=8 * 2**20, cost=None):
+def call(kernel, name, out_shapes, args, smem=0, hbm=0, smem_out=0, scratch=(), vmem=8 * 2**20, cost=None):
     shapes = tuple(jax.ShapeDtypeStruct(s, d) for s, d in out_shapes)
     return pl.pallas_call(
         kernel,
         name=name,
         out_shape=shapes,
         in_specs=[SMEM] * smem + [HBM] * hbm + [VMEM] * (len(args) - smem - hbm),
-        out_specs=tuple(
-            HBM if k in hbm_out else SMEM if smem_out else VMEM for k in range(len(shapes))
-        ),
+        out_specs=tuple([SMEM] * smem_out + [VMEM] * (len(shapes) - smem_out)),
         scratch_shapes=list(scratch),
         compiler_params=pltpu.CompilerParams(vmem_limit_bytes=vmem),
         cost_estimate=cost,
@@ -266,21 +264,18 @@
 
 
 def second_forward(
-    table, own, right, left, opposite, before, free, turned, kept, given, primal, ascent, primal_mine, extended, part, done, total
+    table, own, right, left, opposite, before, free, turned, kept, given, primal, ascent, primal_mine, extended, total
 ):
     ascent[...] = sum_four((own, right, left, opposite), slice(0, COL_BLOCKS))
     primal[...] = clamp_primal(before[...] + STEP * ascent[...], free[...])
     extended[...] = 2.0 * primal[...] - before[...]
-    part[...] = primal[own_columns(table), :]
-    copy = pltpu.make_async_copy(part, primal_mine, done)
-    copy.start()
+    primal_mine[...] = primal[own_columns(table), :]
     forward_product(table, lambda slot: turned[slot], [extended, primal], total)
     mine = pl.multiple_of(table[AT_CORE, 0] * HALF, HALF)
     for k, part in enumerate((0, 4)):
         rows = slice(k * HALF, (k + 1) * HALF)
         kept[rows, :] = total[pl.ds(mine, HALF), part, :]
         given[rows, :] = total[pl.ds(HALF - mine, HALF), part, :]
-    copy.wait()
 
 
 def row_terms(table, held, before, rhs, ineq, side, primal1, primal2, terms):
@@ -306,20 +301,17 @@
 
 
 def third_adjoint(
-    table, held, other, before, rhs, ineq, side, terms, pairs, payload, mine, image, dual, part, done, total
+    table, held, other, before, rhs, ineq, side, terms, pairs, payload, mine, dual, image, total
 ):
     half = pl.multiple_of(table[AT_CORE, 0] * HALF, HALF)
     image[pl.ds(half, HALF), :] = held[0:HALF, :]
     image[pl.ds(HALF - half, HALF), :] = other[0:HALF, :]
     dual[...] = clamp_dual(before[...] + STEP * (rhs[...] - image[...]), ineq[...])
-    part[...] = dual[pl.ds(index_col(table) * ROWS_SHARE, ROWS_SHARE), :]
-    copy = pltpu.make_async_copy(part, mine, done)
-    copy.start()
+    mine[...] = dual[pl.ds(index_col(table) * ROWS_SHARE, ROWS_SHARE), :]
     adjoint_product(table, lambda slot: pairs[slot], dual, total)
     payload[0:COL_BLOCKS, :] = total[:, 0, :]
     payload[COL_BLOCKS : COL_BLOCKS + 8, :] = terms[...]
     payload[own_columns(table), :] -= side[COST:ROW_SIDE, :]
-    copy.wait()
 
 
 def column_terms(own, right, left, opposite, earlier, free, terms):
@@ -341,7 +333,11 @@
     terms[...] = jnp.broadcast_to(line[None], terms.shape)
 
 
-def measures(gathered, primal_residual, dual_residual, gap):
+def measures(
+    gathered, primal_part, dual_part, primal_residual, dual_residual, gap, primal_mine, dual_mine
+):
+    primal_mine[...] = primal_part[...]
+    dual_mine[...] = dual_part[...]
     line = jnp.sum(gathered[...], 0)
     lane = lax.broadcasted_iota(jnp.int32, line.shape, 1)
     for k, (out, size) in enumerate(
@@ -459,15 +455,13 @@
         scratch=[pltpu.VMEM(blocks, F32)] + col_total,
     )
 
-    kept, given, primal2, ascent2, primal_mine = call(
+    kept, given, primal2, ascent2, primal_part = call(
         second_forward,
         "second_forward",
         [(blocks, F32)] * 2 + [(columns, F32)] * 2 + [((COLS_SHARE, TILE), F32)],
         (table, *four_over_row(gradient), primal1, free, turned),
         smem=1,
-        hbm_out=(4,),
-        scratch=[pltpu.VMEM(columns, F32), pltpu.VMEM((COLS_SHARE, TILE), F32), pltpu.SemaphoreType.DMA]
-        + row_total,
+        scratch=[pltpu.VMEM(columns, F32)] + row_total,
     )
     copies = call(
         pair_copies, "pair_copies", [((8, HALF + 8, TILE), F32)], (kept, swap_cores(given))
@@ -483,16 +477,13 @@
         cost=pl.CostEstimate(flops=0, bytes_accessed=2**21, transcendentals=0),
     )[0]
 
-    payload, dual_mine = call(
+    payload, dual_part = call(
         third_adjoint,
         "third_adjoint",
         [((COL_BLOCKS + 8, TILE), F32), ((ROWS_SHARE, TILE), F32)],
         (table, held, other, dual1, rhs_full, ineq, side, terms, pairs),
         smem=1,
-        hbm_out=(1,),
-        scratch=[pltpu.VMEM(blocks, F32)] * 2
-        + [pltpu.VMEM((ROWS_SHARE, TILE), F32), pltpu.SemaphoreType.DMA]
-        + col_total,
+        scratch=[pltpu.VMEM(blocks, F32)] * 2 + col_total,
     )
     terms = call(
         column_terms,
@@ -500,12 +491,12 @@
         [((N, 1, TILE), F32)],
         (*four_over_row(payload), ascent2, free),
     )
-    primal_residual, dual_residual, gap = call(
+    primal_residual, dual_residual, gap, primal_mine, dual_mine = call(
         measures,
         "measures",
-        [((2,), F32)] * 3,
-        (exchange(terms[0], ("z", "core")),),
-        smem_out=True,
+        [((2,), F32)] * 3 + [((COLS_SHARE, TILE), F32), ((ROWS_SHARE, TILE), F32)],
+        (exchange(terms[0], ("z", "core")), primal_part, dual_part),
+        smem_out=3,
     )
     return primal_mine[None], dual_mine[None], primal_residual, dual_residual, gap
 

time: 122 us -> 121 us (level)
  no operation moved by 1% of the time
where the time goes in v11:
time: 121 us
  blocking collectives  53.2 us (44%)
  starting transfers between devices  26.9 us (22%)
  waiting for transfers between devices  26.1 us (22%)
  Pallas kernels  12.2 us (10%)
  between operations  1.57 us (1%)
    all_to_all x4, blocking collectives, exchange(): return lax.all_to_all(copies, axes, 0, 0)  53.2 us
    ppermute x18, waiting for transfers between devices, shift(): return lax.ppermute(values, ('y', 'x', 'core'), pairs)  23.3 us
    ppermute x18, starting transfers between devices, shift(): return lax.ppermute(values, ('y', 'x', 'core'), pairs)  15.9 us
    pallas_call x17, Pallas kernels, call(): pl.pallas_call(kernel, name=name, out_shape=shapes, in_specs=[SMEM] * sme...  12.2 us
    ppermute x4, starting transfers between devices, swap_cores(): return lax.ppermute(values, 'core', [(0, 1), (1, 0)])  11 us
    ppermute x4, waiting for transfers between devices, swap_cores(): return lax.ppermute(values, 'core', [(0, 1), (1, 0)])  2.8 us
  transfers between devices with their start and end apart: 22, of which 17 were waited for; matrix products, arithmetic and copies ran while one was open for 0% of the time, Pallas kernels for 1%

profile of v11, /device:TPU:1, one launch (start us, length us, event | category | flops | bytes accessed | tf_op | source)
XLA Modules:
  0.0 120.6 jit_solution(7573310026400526053)
XLA Ops:
  1.3 1.5 %pack.1 = (f32[16,4,128]{2,1,0:T(4,128)}, f32[40,128]{1,0:T(8,128)}) custom-call(s32[1,1]{1,0:T(1,128)S(6)} %copy.15.count, s32[1,1,64]{2,1,0:T(1,128)} %rows.1, s32[1,1,64]{2,1,0:T(1,128)} %cols.1, s32[1,4,128]{2,1,0:T(4,128)} %row_kinds.1, f32[1,4,128]{2,1,0:T(4,128)} %rhs.1, f32[1,4,128]{2,1,0:T(4,128)} %dual.1, s32[1,8,128]{2,1,0:T(8,128)} %col_kinds.1, ...), custom_call_target="tpu_custom_call" | custom-call | tf_op jit(solution)/shard_map/pack/pallas_call | solution.py:35
  2.8 17.4 %all_to_all.20.duals = f32[16,4,128]{2,1,0:T(4,128)S(1)} all-to-all(f32[16,4,128]{2,1,0:T(4,128)} %get-tuple-element.31), channel_id=1, replica_groups=mesh['y'=4,'x'=4,'z'=8,'core'=2] {'z','core'}, dimensions={0} | all-to-all | bytes 65536 | tf_op jit(solution)/shard_map/all_to_all | solution.py:374
  20.9 2.6 %first_adjoint.1 = (f32[144,128]{1,0:T(8,128)S(1)}, f32[64,128]{1,0:T(8,128)S(1)}, s32[8,128]{1,0:T(8,128)S(1)}, bf16[64,256,128]{2,1,0:T(8,128)(2,1)S(1)}) custom-call(f32[64,128,128]{2,1,0:T(8,128)} %bitcast.3, f32[16,4,128]{2,1,0:T(4,128)S(1)} %all_to_all.20.duals, f32[40,128]{1,0:T(8,128)S(1)} %copy-done), custom_call_target="tpu_custom_call" | custom-call | tf_op jit(solution)/shard_map/first_adjoint/pallas_call | solution.py:35
  23.5 3.0 %collective-permute-start.2 = (f32[144,128]{1,0:T(8,128)S(1)}, f32[144,128]{1,0:T(8,128)S(1)}, u32[]{:S(2)}, u32[]{:S(2)}) collective-permute-start(f32[144,128]{1,0:T(8,128)S(1)} %get-tuple-element.34.own), channel_id=1, source_target_pairs={{0,32},{1,129},{16,48},{17,145},{32,0},{33,161},{48,16},{49,177},{... | collective-permute-start | bytes 221192 | tf_op jit(solution)/shard_map/ppermute | solution.py:357
  28.3 1.4 %collective-permute-done.1.left = f32[144,128]{1,0:T(8,128)S(1)} collective-permute-done((f32[144,128]{1,0:T(8,128)S(1)}, f32[144,128]{1,0:T(8,128)S(1)}, u32[]{:S(2)}, u32[]{:S(2)}) %collective-permute-start.1) | collective-permute-done | bytes 73760 | tf_op jit(solution)/shard_map/ppermute | solution.py:357
  29.7 2.0 %collective-permute-done.right = f32[144,128]{1,0:T(8,128)S(1)} collective-permute-done((f32[144,128]{1,0:T(8,128)S(1)}, f32[144,128]{1,0:T(8,128)S(1)}, u32[]{:S(2)}, u32[]{:S(2)}) %collective-permute-start) | collective-permute-done | bytes 73760 | tf_op jit(solution)/shard_map/ppermute | solution.py:357
  31.7 2.8 %collective-permute-start.5 = (f32[192,128]{1,0:T(8,128)S(1)}, f32[192,128]{1,0:T(8,128)S(1)}, u32[]{:S(2)}, u32[]{:S(2)}) collective-permute-start(f32[192,128]{1,0:T(8,128)S(1)} %ring_sums.1.own), channel_id=1, source_target_pairs={{0,128},{1,33},{16,144},{17,49},{32,160},{33,1},{48,176},{49,17},{... | collective-permute-start | bytes 294920 | tf_op jit(solution)/shard_map/ppermute | solution.py:357
  38.0 2.1 %collective-permute-done.3.right = f32[192,128]{1,0:T(8,128)S(1)} collective-permute-done((f32[192,128]{1,0:T(8,128)S(1)}, f32[192,128]{1,0:T(8,128)S(1)}, u32[]{:S(2)}, u32[]{:S(2)}) %collective-permute-start.3) | collective-permute-done | bytes 98336 | tf_op jit(solution)/shard_map/ppermute | solution.py:357
  41.4 3.9 %collective-permute-start.6 = (f32[32,128]{1,0:T(8,128)S(1)}, f32[32,128]{1,0:T(8,128)S(1)}, u32[]{:S(2)}, u32[]{:S(2)}) collective-permute-start(f32[32,128]{1,0:T(8,128)S(1)} %get-tuple-element.37), channel_id=1, source_target_pairs={{0,1},{1,0},{2,3},{3,2},{4,5},{5,4},{6,7},{7,6},{8,9},{9,8},{10,11... | collective-permute-start | bytes 49160 | tf_op jit(solution)/shard_map/ppermute | solution.py:370
  46.2 11.6 %all_to_all.21.pieces = f32[8,40,128]{2,1,0:T(8,128)S(1)} all-to-all(f32[8,40,128]{2,1,0:T(8,128)S(1)} %image_copies.1), channel_id=1, replica_groups=mesh['y'=4,'x'=4,'z'=8,'core'=2] {'z'}, dimensions={0} | all-to-all | bytes 327680 | tf_op jit(solution)/shard_map/all_to_all | solution.py:374
  57.8 1.6 %collective-permute-start.7 = (f32[96,128]{1,0:T(8,128)S(1)}, f32[96,128]{1,0:T(8,128)S(1)}, u32[]{:S(2)}, u32[]{:S(2)}) collective-permute-start(f32[96,128]{1,0:T(8,128)S(1)} %image_sums.1.held), channel_id=1, source_target_pairs={{0,1},{1,0},{2,3},{3,2},{4,5},{5,4},{6,7},{7,6},{8,9},{9,8},{10,11... | collective-permute-start | bytes 147464 | tf_op jit(solution)/shard_map/ppermute | solution.py:370
  61.9 1.7 %collective-permute-start.9 = (f32[128,128]{1,0:T(8,128)S(1)}, f32[128,128]{1,0:T(8,128)S(1)}, u32[]{:S(2)}, u32[]{:S(2)}) collective-permute-start(f32[128,128]{1,0:T(8,128)S(1)} %get-tuple-element.39.own), channel_id=1, source_target_pairs={{0,48},{1,193},{16,0},{17,209},{32,16},{33,225},{48,32},{49,241},{... | collective-permute-start | bytes 196616 | tf_op jit(solution)/shard_map/ppermute | solution.py:357
  63.6 2.7 %collective-permute-done.10.opposite = f32[128,128]{1,0:T(8,128)S(1)} collective-permute-done((f32[128,128]{1,0:T(8,128)S(1)}, f32[128,128]{1,0:T(8,128)S(1)}, u32[]{:S(2)}, u32[]{:S(2)}) %collective-permute-start.10) | collective-permute-done | bytes 65568 | tf_op jit(solution)/shard_map/ppermute | solution.py:357
  66.3 1.6 %collective-permute-done.8.right = f32[128,128]{1,0:T(8,128)S(1)} collective-permute-done((f32[128,128]{1,0:T(8,128)S(1)}, f32[128,128]{1,0:T(8,128)S(1)}, u32[]{:S(2)}, u32[]{:S(2)}) %collective-permute-start.8) | collective-permute-done | bytes 65568 | tf_op jit(solution)/shard_map/ppermute | solution.py:357
  68.1 1.8 %collective-permute-start.12 = (f32[128,128]{1,0:T(8,128)S(1)}, f32[128,128]{1,0:T(8,128)S(1)}, u32[]{:S(2)}, u32[]{:S(2)}) collective-permute-start(f32[128,128]{1,0:T(8,128)S(1)} %sums.2.own), channel_id=1, source_target_pairs={{0,192},{1,49},{16,208},{17,1},{32,224},{33,17},{48,240},{49,33},{... | collective-permute-start | bytes 196616 | tf_op jit(solution)/shard_map/ppermute | solution.py:357
  69.8 2.8 %collective-permute-done.13.opposite = f32[128,128]{1,0:T(8,128)S(1)} collective-permute-done((f32[128,128]{1,0:T(8,128)S(1)}, f32[128,128]{1,0:T(8,128)S(1)}, u32[]{:S(2)}, u32[]{:S(2)}) %collective-permute-start.13) | collective-permute-done | bytes 65568 | tf_op jit(solution)/shard_map/ppermute | solution.py:357
  72.6 1.5 %collective-permute-done.11.right = f32[128,128]{1,0:T(8,128)S(1)} collective-permute-done((f32[128,128]{1,0:T(8,128)S(1)}, f32[128,128]{1,0:T(8,128)S(1)}, u32[]{:S(2)}, u32[]{:S(2)}) %collective-permute-start.11) | collective-permute-done | bytes 65568 | tf_op jit(solution)/shard_map/ppermute | solution.py:357
  74.1 1.4 %second_forward.1 = (f32[64,128]{1,0:T(8,128)S(1)}, f32[64,128]{1,0:T(8,128)S(1)}, f32[128,128]{1,0:T(8,128)S(1)}, f32[128,128]{1,0:T(8,128)S(1)}, f32[8,128]{1,0:T(8,128)S(1)}) custom-call(s32[8,128]{1,0:T(8,128)S(1)} %get-tuple-element.33.table, f32[128,128]{1,0:T(8,128)S(1)} %sums.2.own, f32[128,128]{1,0:T(8,128)S(1)} %collective-permute-done.11.right, ...), custom_call_target="tpu_custom_call" | custom-call | tf_op jit(solution)/shard_map/second_forward/pallas_call | solution.py:35
  75.5 3.9 %collective-permute-start.14 = (f32[64,128]{1,0:T(8,128)S(1)}, f32[64,128]{1,0:T(8,128)S(1)}, u32[]{:S(2)}, u32[]{:S(2)}) collective-permute-start(f32[64,128]{1,0:T(8,128)S(1)} %get-tuple-element.43), channel_id=1, source_target_pairs={{0,1},{1,0},{2,3},{3,2},{4,5},{5,4},{6,7},{7,6},{8,9},{9,8},{10,11... | collective-permute-start | bytes 98312 | tf_op jit(solution)/shard_map/ppermute | solution.py:370
  80.2 11.6 %all_to_all.22.pieces = f32[8,40,128]{2,1,0:T(8,128)S(1)} all-to-all(f32[8,40,128]{2,1,0:T(8,128)S(1)} %pair_copies.1), channel_id=1, replica_groups=mesh['y'=4,'x'=4,'z'=8,'core'=2] {'z'}, dimensions={0} | all-to-all | bytes 327680 | tf_op jit(solution)/shard_map/all_to_all | solution.py:374
  91.8 1.6 %collective-permute-start.15 = (f32[40,128]{1,0:T(8,128)S(1)}, f32[40,128]{1,0:T(8,128)S(1)}, u32[]{:S(2)}, u32[]{:S(2)}) collective-permute-start(f32[40,128]{1,0:T(8,128)S(1)} %pair_sums.1.held), channel_id=1, source_target_pairs={{0,1},{1,0},{2,3},{3,2},{4,5},{5,4},{6,7},{7,6},{8,9},{9,8},{10,11... | collective-permute-start | bytes 61448 | tf_op jit(solution)/shard_map/ppermute | solution.py:370
  97.3 3.1 %collective-permute-done.18.opposite = f32[136,128]{1,0:T(8,128)S(1)} collective-permute-done((f32[136,128]{1,0:T(8,128)S(1)}, f32[136,128]{1,0:T(8,128)S(1)}, u32[]{:S(2)}, u32[]{:S(2)}) %collective-permute-start.18) | collective-permute-done | bytes 69664 | tf_op jit(solution)/shard_map/ppermute | solution.py:357
  103.1 3.1 %collective-permute-done.21.opposite = f32[136,128]{1,0:T(8,128)S(1)} collective-permute-done((f32[136,128]{1,0:T(8,128)S(1)}, f32[136,128]{1,0:T(8,128)S(1)}, u32[]{:S(2)}, u32[]{:S(2)}) %collective-permute-start.21) | collective-permute-done | bytes 69664 | tf_op jit(solution)/shard_map/ppermute | solution.py:357
  107.1 12.7 %all_to_all.23.gathered = f32[16,1,128]{2,1,0:T(1,128)S(1)} all-to-all(f32[16,1,128]{2,1,0:T(1,128)S(1)} %column_terms.1), channel_id=1, replica_groups=mesh['y'=4,'x'=4,'z'=8,'core'=2] {'z','core'}, dimensions={0} | all-to-all | bytes 16384 | tf_op jit(solution)/shard_map/all_to_all | solution.py:374
  (43 shorter events, 19.8 us)
Async XLA Ops:
  20.2 0.7 copy-start
  23.5 4.8 %collective-permute-start.2 = (f32[144,128]{1,0:T(8,128)S(1)}, f32[144,128]{1,0:T(8,128)S(1)}, u32[]{:S(2)}, u32[]{:S(2)}) collective-permute-start(f32[144,128]{1,0:T(8,128)S(1)} %get-tuple-element.34.own), channel_id=1, source_target_pairs={{0,32},{1,129},{16,48},{17,145},{32,0},{33,161},{48,16},{49,177},{... | collective-permute-start | bytes 221192 | tf_op jit(solution)/shard_map/ppermute | solution.py:357
  26.5 3.2 %collective-permute-start.1 = (f32[144,128]{1,0:T(8,128)S(1)}, f32[144,128]{1,0:T(8,128)S(1)}, u32[]{:S(2)}, u32[]{:S(2)}) collective-permute-start(f32[144,128]{1,0:T(8,128)S(1)} %get-tuple-element.34.own), channel_id=1, source_target_pairs={{0,48},{1,193},{16,0},{17,209},{32,16},{33,225},{48,32},{49,241},{... | collective-permute-start | bytes 221192 | tf_op jit(solution)/shard_map/ppermute | solution.py:357
  27.3 4.4 %collective-permute-start = (f32[144,128]{1,0:T(8,128)S(1)}, f32[144,128]{1,0:T(8,128)S(1)}, u32[]{:S(2)}, u32[]{:S(2)}) collective-permute-start(f32[144,128]{1,0:T(8,128)S(1)} %get-tuple-element.34.own), channel_id=1, source_target_pairs={{0,16},{1,65},{16,32},{17,81},{32,48},{33,97},{48,0},{49,113},{64,... | collective-permute-start | bytes 221192 | tf_op jit(solution)/shard_map/ppermute | solution.py:357
  31.7 5.4 %collective-permute-start.5 = (f32[192,128]{1,0:T(8,128)S(1)}, f32[192,128]{1,0:T(8,128)S(1)}, u32[]{:S(2)}, u32[]{:S(2)}) collective-permute-start(f32[192,128]{1,0:T(8,128)S(1)} %ring_sums.1.own), channel_id=1, source_target_pairs={{0,128},{1,33},{16,144},{17,49},{32,160},{33,1},{48,176},{49,17},{... | collective-permute-start | bytes 294920 | tf_op jit(solution)/shard_map/ppermute | solution.py:357
  34.5 3.5 %collective-permute-start.4 = (f32[192,128]{1,0:T(8,128)S(1)}, f32[192,128]{1,0:T(8,128)S(1)}, u32[]{:S(2)}, u32[]{:S(2)}) collective-permute-start(f32[192,128]{1,0:T(8,128)S(1)} %ring_sums.1.own), channel_id=1, source_target_pairs={{0,192},{1,49},{16,208},{17,1},{32,224},{33,17},{48,240},{49,33},{... | collective-permute-start | bytes 294920 | tf_op jit(solution)/shard_map/ppermute | solution.py:357
  35.4 4.7 %collective-permute-start.3 = (f32[192,128]{1,0:T(8,128)S(1)}, f32[192,128]{1,0:T(8,128)S(1)}, u32[]{:S(2)}, u32[]{:S(2)}) collective-permute-start(f32[192,128]{1,0:T(8,128)S(1)} %ring_sums.1.own), channel_id=1, source_target_pairs={{0,64},{1,17},{16,80},{17,33},{32,96},{33,49},{48,112},{49,1},{64,... | collective-permute-start | bytes 294920 | tf_op jit(solution)/shard_map/ppermute | solution.py:357
  41.4 4.7 %collective-permute-start.6 = (f32[32,128]{1,0:T(8,128)S(1)}, f32[32,128]{1,0:T(8,128)S(1)}, u32[]{:S(2)}, u32[]{:S(2)}) collective-permute-start(f32[32,128]{1,0:T(8,128)S(1)} %get-tuple-element.37), channel_id=1, source_target_pairs={{0,1},{1,0},{2,3},{3,2},{4,5},{5,4},{6,7},{7,6},{8,9},{9,8},{10,11... | collective-permute-start | bytes 49160 | tf_op jit(solution)/shard_map/ppermute | solution.py:370
  57.8 2.5 %collective-permute-start.7 = (f32[96,128]{1,0:T(8,128)S(1)}, f32[96,128]{1,0:T(8,128)S(1)}, u32[]{:S(2)}, u32[]{:S(2)}) collective-permute-start(f32[96,128]{1,0:T(8,128)S(1)} %image_sums.1.held), channel_id=1, source_target_pairs={{0,1},{1,0},{2,3},{3,2},{4,5},{5,4},{6,7},{7,6},{8,9},{9,8},{10,11... | collective-permute-start | bytes 147464 | tf_op jit(solution)/shard_map/ppermute | solution.py:370
  61.6 4.7 %collective-permute-start.10 = (f32[128,128]{1,0:T(8,128)S(1)}, f32[128,128]{1,0:T(8,128)S(1)}, u32[]{:S(2)}, u32[]{:S(2)}) collective-permute-start(f32[128,128]{1,0:T(8,128)S(1)} %get-tuple-element.39.own), channel_id=1, source_target_pairs={{0,32},{1,129},{16,48},{17,145},{32,0},{33,161},{48,16},{49,177},{... | collective-permute-start | bytes 196616 | tf_op jit(solution)/shard_map/ppermute | solution.py:357
  61.9 4.4 %collective-permute-start.9 = (f32[128,128]{1,0:T(8,128)S(1)}, f32[128,128]{1,0:T(8,128)S(1)}, u32[]{:S(2)}, u32[]{:S(2)}) collective-permute-start(f32[128,128]{1,0:T(8,128)S(1)} %get-tuple-element.39.own), channel_id=1, source_target_pairs={{0,48},{1,193},{16,0},{17,209},{32,16},{33,225},{48,32},{49,241},{... | collective-permute-start | bytes 196616 | tf_op jit(solution)/shard_map/ppermute | solution.py:357
  63.6 4.3 %collective-permute-start.8 = (f32[128,128]{1,0:T(8,128)S(1)}, f32[128,128]{1,0:T(8,128)S(1)}, u32[]{:S(2)}, u32[]{:S(2)}) collective-permute-start(f32[128,128]{1,0:T(8,128)S(1)} %get-tuple-element.39.own), channel_id=1, source_target_pairs={{0,16},{1,65},{16,32},{17,81},{32,48},{33,97},{48,0},{49,113},{64,... | collective-permute-start | bytes 196616 | tf_op jit(solution)/shard_map/ppermute | solution.py:357
  67.9 4.7 %collective-permute-start.13 = (f32[128,128]{1,0:T(8,128)S(1)}, f32[128,128]{1,0:T(8,128)S(1)}, u32[]{:S(2)}, u32[]{:S(2)}) collective-permute-start(f32[128,128]{1,0:T(8,128)S(1)} %sums.2.own), channel_id=1, source_target_pairs={{0,128},{1,33},{16,144},{17,49},{32,160},{33,1},{48,176},{49,17},{... | collective-permute-start | bytes 196616 | tf_op jit(solution)/shard_map/ppermute | solution.py:357
  68.1 4.6 %collective-permute-start.12 = (f32[128,128]{1,0:T(8,128)S(1)}, f32[128,128]{1,0:T(8,128)S(1)}, u32[]{:S(2)}, u32[]{:S(2)}) collective-permute-start(f32[128,128]{1,0:T(8,128)S(1)} %sums.2.own), channel_id=1, source_target_pairs={{0,192},{1,49},{16,208},{17,1},{32,224},{33,17},{48,240},{49,33},{... | collective-permute-start | bytes 196616 | tf_op jit(solution)/shard_map/ppermute | solution.py:357
  69.8 4.3 %collective-permute-start.11 = (f32[128,128]{1,0:T(8,128)S(1)}, f32[128,128]{1,0:T(8,128)S(1)}, u32[]{:S(2)}, u32[]{:S(2)}) collective-permute-start(f32[128,128]{1,0:T(8,128)S(1)} %sums.2.own), channel_id=1, source_target_pairs={{0,64},{1,17},{16,80},{17,33},{32,96},{33,49},{48,112},{49,1},{64,... | collective-permute-start | bytes 196616 | tf_op jit(solution)/shard_map/ppermute | solution.py:357
  75.5 4.7 %collective-permute-start.14 = (f32[64,128]{1,0:T(8,128)S(1)}, f32[64,128]{1,0:T(8,128)S(1)}, u32[]{:S(2)}, u32[]{:S(2)}) collective-permute-start(f32[64,128]{1,0:T(8,128)S(1)} %get-tuple-element.43), channel_id=1, source_target_pairs={{0,1},{1,0},{2,3},{3,2},{4,5},{5,4},{6,7},{7,6},{8,9},{9,8},{10,11... | collective-permute-start | bytes 98312 | tf_op jit(solution)/shard_map/ppermute | solution.py:370
  91.8 2.5 %collective-permute-start.15 = (f32[40,128]{1,0:T(8,128)S(1)}, f32[40,128]{1,0:T(8,128)S(1)}, u32[]{:S(2)}, u32[]{:S(2)}) collective-permute-start(f32[40,128]{1,0:T(8,128)S(1)} %pair_sums.1.held), channel_id=1, source_target_pairs={{0,1},{1,0},{2,3},{3,2},{4,5},{5,4},{6,7},{7,6},{8,9},{9,8},{10,11... | collective-permute-start | bytes 61448 | tf_op jit(solution)/shard_map/ppermute | solution.py:370
  95.6 4.8 %collective-permute-start.18 = (f32[136,128]{1,0:T(8,128)S(1)}, f32[136,128]{1,0:T(8,128)S(1)}, u32[]{:S(2)}, u32[]{:S(2)}) collective-permute-start(f32[136,128]{1,0:T(8,128)S(1)} %get-tuple-element.48.own), channel_id=1, source_target_pairs={{0,32},{1,129},{16,48},{17,145},{32,0},{33,161},{48,16},{49,177},{... | collective-permute-start | bytes 208904 | tf_op jit(solution)/shard_map/ppermute | solution.py:357
  95.7 4.7 %collective-permute-start.17 = (f32[136,128]{1,0:T(8,128)S(1)}, f32[136,128]{1,0:T(8,128)S(1)}, u32[]{:S(2)}, u32[]{:S(2)}) collective-permute-start(f32[136,128]{1,0:T(8,128)S(1)} %get-tuple-element.48.own), channel_id=1, source_target_pairs={{0,48},{1,193},{16,0},{17,209},{32,16},{33,225},{48,32},{49,241},{... | collective-permute-start | bytes 208904 | tf_op jit(solution)/shard_map/ppermute | solution.py:357
  96.7 4.7 %collective-permute-start.16 = (f32[136,128]{1,0:T(8,128)S(1)}, f32[136,128]{1,0:T(8,128)S(1)}, u32[]{:S(2)}, u32[]{:S(2)}) collective-permute-start(f32[136,128]{1,0:T(8,128)S(1)} %get-tuple-element.48.own), channel_id=1, source_target_pairs={{0,16},{1,65},{16,32},{17,81},{32,48},{33,97},{48,0},{49,113},{64,... | collective-permute-start | bytes 208904 | tf_op jit(solution)/shard_map/ppermute | solution.py:357
  101.5 4.8 %collective-permute-start.21 = (f32[136,128]{1,0:T(8,128)S(1)}, f32[136,128]{1,0:T(8,128)S(1)}, u32[]{:S(2)}, u32[]{:S(2)}) collective-permute-start(f32[136,128]{1,0:T(8,128)S(1)} %sums.3.own), channel_id=1, source_target_pairs={{0,128},{1,33},{16,144},{17,49},{32,160},{33,1},{48,176},{49,17},{... | collective-permute-start | bytes 208904 | tf_op jit(solution)/shard_map/ppermute | solution.py:357
  101.6 4.7 %collective-permute-start.20 = (f32[136,128]{1,0:T(8,128)S(1)}, f32[136,128]{1,0:T(8,128)S(1)}, u32[]{:S(2)}, u32[]{:S(2)}) collective-permute-start(f32[136,128]{1,0:T(8,128)S(1)} %sums.3.own), channel_id=1, source_target_pairs={{0,192},{1,49},{16,208},{17,1},{32,224},{33,17},{48,240},{49,33},{... | collective-permute-start | bytes 208904 | tf_op jit(solution)/shard_map/ppermute | solution.py:357
  102.3 4.7 %collective-permute-start.19 = (f32[136,128]{1,0:T(8,128)S(1)}, f32[136,128]{1,0:T(8,128)S(1)}, u32[]{:S(2)}, u32[]{:S(2)}) collective-permute-start(f32[136,128]{1,0:T(8,128)S(1)} %sums.3.own), channel_id=1, source_target_pairs={{0,64},{1,17},{16,80},{17,33},{32,96},{33,49},{48,112},{49,1},{64,... | collective-permute-start | bytes 208904 | tf_op jit(solution)/shard_map/ppermute | solution.py:357
